TPU v7x, 32 devices: a whole 2x2x4 slice. The times are simulated.
32 devices in a mesh: rows: 8 (over y, x, core), vecs: 4 (over z).
Axes of the slice: x: 2, y: 2, z: 4, core: 2. Of those that a mesh axis runs over, the one named last changes fastest.
Arguments:
- vectors: float32 [1024, 512], P('rows', 'vecs'), may hold values from -6 to 6
- reflectors: float32 [3, 8, 128, 256], P(None, 'rows', 'vecs'), may hold values from -3 to 3
Outputs:
- transformed: float32 [1024, 512], P('rows', 'vecs')
All inputs are finite; a program needn't handle non-finite values.
Results may differ from a plain program's by a relative error of at most 0.0003.
Values sent between devices are 32-bit elements; how exact they have to be, the bound alone decides.
No kernel may reach another device: no remote copies, remote signals or barrier semaphores. Data moves between devices by JAX's collectives and lax.ppermute only.
A program may use at most 64 MiB of HBM per device.

v0:
```python
import jax
import jax.numpy as jnp
from jax import lax
from jax.sharding import PartitionSpec as P

HIGHEST = lax.Precision.HIGHEST


def from_behind(value, axis, steps):
    count = lax.axis_size(axis)
    leading, last = (max(0, -steps), min(count, count - steps))
    return lax.ppermute(value, axis, [(source, source + steps) for source in range(leading, last)])


def carried_in(part, axis, combine, identity):
    place = lax.axis_index(axis)
    gathered = jax.tree.map(lambda a: lax.all_gather(a, axis), part)
    state = jax.tree.map(lambda a, e: jnp.zeros_like(a) + jnp.asarray(e, a.dtype), part, identity)

    def one(hop, state):
        return combine(
            state, jax.tree.map(lambda a: lax.dynamic_index_in_dim(a, hop, 0, False), gathered)
        )

    return lax.fori_loop(0, place, one, state)


def inverse_factor(reflector):
    block_size = reflector.shape[0]
    gram_matrix = jnp.dot(reflector, reflector.T, precision=HIGHEST)
    half_diag = jnp.diag(gram_matrix) * 0.5
    nilpotent = jnp.triu(gram_matrix, 1) / half_diag[:, None]
    identity = jnp.eye(block_size, dtype=jnp.float32)
    power = -nilpotent
    result = identity + power
    reach = 2
    while reach < block_size:
        power = jnp.dot(power, power, precision=HIGHEST)
        result = jnp.dot(result, identity + power, precision=HIGHEST)
        reach = reach * 2
    return result / half_diag[None, :]


def reflect(window_rows, reflector, inv_matrix):
    weights = jnp.dot(reflector, window_rows, precision=HIGHEST)
    solved = jnp.dot(inv_matrix, weights, precision=HIGHEST)
    return window_rows - jnp.dot(reflector.T, solved, precision=HIGHEST)


def apply_blocks(slab_work, group_blocks, group_inverses):
    window_rows = slab_work
    updated = reflect(window_rows, group_blocks[0], group_inverses[0])
    slab_work = lax.dynamic_update_slice_in_dim(slab_work, updated, 0, 0)
    return slab_work


def compose(earlier, later):
    map_early, add_early = earlier
    map_late, add_late = later
    return (
        jnp.dot(map_late, map_early, precision=HIGHEST),
        jnp.dot(map_late, add_early, precision=HIGHEST) + add_late,
    )


def local(vectors, reflectors):
    rows_local, cols_local = vectors.shape
    block_size = reflectors.shape[3] // 2
    row_index = lax.axis_index("rows")
    row_count = lax.axis_size("rows")
    gathered = lax.all_gather(reflectors, "vecs", axis=2, tiled=True)
    row_pos = lax.broadcasted_iota(jnp.int32, gathered.shape, 3)
    block_pos = lax.broadcasted_iota(jnp.int32, gathered.shape, 1)
    cut_mask = (
        (row_index == row_count - 1)
        & (block_pos == gathered.shape[1] - 1)
        & (row_pos >= block_size)
    )
    gathered = jnp.where(cut_mask, jnp.zeros_like(gathered), gathered)
    inverses = jax.vmap(jax.vmap(inverse_factor))(gathered)
    identity = jnp.eye(block_size, dtype=jnp.float32)
    basis = jnp.concatenate([identity, jnp.zeros((rows_local, block_size), jnp.float32)], 0)
    is_first = row_index == 0
    current = vectors
    for group in range(gathered.shape[0]):
        top_rows = current
        below_rows = from_behind(top_rows, "rows", -1)
        slab_work = jnp.concatenate(
            [jnp.zeros((block_size, cols_local), jnp.float32), current[block_size:], below_rows], 0
        )
        joined = apply_blocks(
            jnp.concatenate([slab_work, basis], 1), gathered[group], inverses[group]
        )
        zero_carry = joined[:, :cols_local]
        carry_action = joined[:, cols_local:]
        step_map = carry_action[rows_local:]
        step_add = zero_carry[rows_local:]
        start_add = jnp.dot(step_map, top_rows, precision=HIGHEST) + step_add
        element = (
            jnp.where(is_first, jnp.zeros_like(step_map), step_map),
            jnp.where(is_first, start_add, step_add),
        )
        prefix_map = carried_in(
            element, "rows", compose, (identity, jnp.zeros((block_size, cols_local), jnp.float32))
        )
        carry_rows = jnp.where(is_first, top_rows, prefix_map[1])
        current = zero_carry[:rows_local] + jnp.dot(
            carry_action[:rows_local], carry_rows, precision=HIGHEST
        )
    return current


def solution(mesh):
    placed = (P("rows", "vecs"), P(None, "rows", "vecs", None))
    return jax.shard_map(
        local, mesh=mesh, in_specs=placed, out_specs=P("rows", "vecs"), check_vma=False
    )
```

profile of v0, /device:TPU:0, one launch (start us, length us, event | category | flops | bytes accessed | tf_op | source)
XLA Modules:
  0.0 105.2 jit_solution(14590100288948808028)
XLA Ops:
  0.0 1.3 %collective-permute-start = (f32[128,128]{1,0:T(8,128)}, f32[128,128]{1,0:T(8,128)S(1)}, u32[]{:S(2)}, u32[]{:S(2)}) collective-permute-start(f32[128,128]{1,0:T(8,128)} %param.8), channel_id=1, source_target_pairs={{4,0},{8,4},{12,8},{16,12},{20,16},{24,20},{28,24},{5,1},{9,5},{13... | collective-permute-start | bytes 196616 | tf_op jit(solution)/shard_map/ppermute | solution.py:12
  1.4 17.2 %all_gather.39 = f32[3,1,128,256]{3,2,1,0:T(8,128)S(1)} all-gather(f32[3,1,32,256]{3,2,1,0:T(8,128)} %param.9), channel_id=1, replica_groups=mesh['rows'=8,'vecs'=4] {'vecs'}, dimensions={2}, use_global_device_ids=true | all-gather | bytes 491520 | tf_op jit(solution)/shard_map/all_gather | solution.py:71
  18.6 0.5 fusion.12
  19.1 4.7 %copy.3 = f32[3,128,128]{0,2,1:T(8,128)} copy(f32[3,128,128]{2,1,0:T(8,128)S(1)} %fusion.12) | data formatting | bytes 393216 | tf_op jit(solution)/shard_map/vmap(vmap())/dot_general | solution.py:30
  23.7 1.8 %gather_fusion = f32[128,3]{1,0:T(8,128)S(1)} fusion(f32[3,128,128]{0,2,1:T(8,128)} %copy.3, s32[128]{0:T(128)S(1)} %or_bitcast_fusion), kind=kCustom, calls=%fused_computation | custom fusion | bytes 4096 | tf_op jit(solution)/shard_map/vmap(vmap(jit(_diag)))/jit(diagonal)/cond/branch_0_fun/gather | solution.py:31
  25.6 0.5 fusion.69
  26.4 0.4 fusion.27
  27.1 0.3 fusion.25
  28.4 0.3 fusion.21
  29.4 0.4 convolution_divide_fusion
  30.3 0.4 convolution_subtract_fusion.2
  31.0 10.7 %all-gather = f32[1024,128]{1,0:T(8,128)S(1)} all-gather(f32[128,128]{1,0:T(8,128)S(1)} %slice_select_fusion.2), channel_id=2, replica_groups=mesh['rows'=8,'vecs'=4] {'rows'}, dimensions={0}, use_global_device_ids=true | all-gather | bytes 589824 | tf_op jit(solution)/shard_map/all_gather | solution.py:17
  41.7 9.2 %all-gather.1 = f32[1024,128]{1,0:T(8,128)S(1)} all-gather(f32[128,128]{1,0:T(8,128)S(1)} %fusion.11), channel_id=3, replica_groups=mesh['rows'=8,'vecs'=4] {'rows'}, dimensions={0}, use_global_device_ids=true | all-gather | bytes 589824 | tf_op jit(solution)/shard_map/all_gather | solution.py:17
  51.1 1.3 %collective-permute-start.1 = (f32[128,128]{1,0:T(8,128)S(1)}, f32[128,128]{1,0:T(8,128)S(1)}, u32[]{:S(2)}, u32[]{:S(2)}) collective-permute-start(f32[128,128]{1,0:T(8,128)S(1)} %slice_add_fusion.2), channel_id=1, source_target_pairs={{4,0},{8,4},{12,8},{16,12},{20,16},{24,20},{28,24},{5,1},{9,5},{13... | collective-permute-start | bytes 196616 | tf_op jit(solution)/shard_map/ppermute | solution.py:12
  52.4 2.0 %collective-permute-done.1 = f32[128,128]{1,0:T(8,128)S(1)} collective-permute-done((f32[128,128]{1,0:T(8,128)S(1)}, f32[128,128]{1,0:T(8,128)S(1)}, u32[]{:S(2)}, u32[]{:S(2)}) %collective-permute-start.1) | collective-permute-done | bytes 65568 | tf_op jit(solution)/shard_map/ppermute | solution.py:12
  54.9 0.4 convolution_subtract_fusion.1
  55.6 12.7 %all-gather.3 = f32[1024,128]{1,0:T(8,128)S(1)} all-gather(f32[128,128]{1,0:T(8,128)S(1)} %fusion.10), channel_id=5, replica_groups=mesh['rows'=8,'vecs'=4] {'rows'}, dimensions={0}, use_global_device_ids=true | all-gather | bytes 589824 | tf_op jit(solution)/shard_map/all_gather | solution.py:17
  68.3 9.4 %all-gather.2 = f32[1024,128]{1,0:T(8,128)S(1)} all-gather(f32[128,128]{1,0:T(8,128)S(1)} %slice_select_fusion.1), channel_id=4, replica_groups=mesh['rows'=8,'vecs'=4] {'rows'}, dimensions={0}, use_global_device_ids=true | all-gather | bytes 589824 | tf_op jit(solution)/shard_map/all_gather | solution.py:17
  78.0 1.3 %collective-permute-start.2 = (f32[128,128]{1,0:T(8,128)S(1)}, f32[128,128]{1,0:T(8,128)S(1)}, u32[]{:S(2)}, u32[]{:S(2)}) collective-permute-start(f32[128,128]{1,0:T(8,128)S(1)} %slice_add_fusion.1), channel_id=1, source_target_pairs={{4,0},{8,4},{12,8},{16,12},{20,16},{24,20},{28,24},{5,1},{9,5},{13... | collective-permute-start | bytes 196616 | tf_op jit(solution)/shard_map/ppermute | solution.py:12
  79.3 2.0 %collective-permute-done.2 = f32[128,128]{1,0:T(8,128)S(1)} collective-permute-done((f32[128,128]{1,0:T(8,128)S(1)}, f32[128,128]{1,0:T(8,128)S(1)}, u32[]{:S(2)}, u32[]{:S(2)}) %collective-permute-start.2) | collective-permute-done | bytes 65568 | tf_op jit(solution)/shard_map/ppermute | solution.py:12
  81.8 0.4 convolution_subtract_fusion
  82.4 12.5 %all-gather.5 = f32[1024,128]{1,0:T(8,128)S(1)} all-gather(f32[128,128]{1,0:T(8,128)S(1)} %fusion.9), channel_id=7, replica_groups=mesh['rows'=8,'vecs'=4] {'rows'}, dimensions={0}, use_global_device_ids=true | all-gather | bytes 589824 | tf_op jit(solution)/shard_map/all_gather | solution.py:17
  94.9 9.4 %all-gather.4 = f32[1024,128]{1,0:T(8,128)S(1)} all-gather(f32[128,128]{1,0:T(8,128)S(1)} %slice_select_fusion), channel_id=6, replica_groups=mesh['rows'=8,'vecs'=4] {'rows'}, dimensions={0}, use_global_device_ids=true | all-gather | bytes 589824 | tf_op jit(solution)/shard_map/all_gather | solution.py:17
  104.4 0.8 slice_add_fusion
  (37 shorter events, 5.1 us)
Async XLA Ops:
  0.0 29.8 %collective-permute-start = (f32[128,128]{1,0:T(8,128)}, f32[128,128]{1,0:T(8,128)S(1)}, u32[]{:S(2)}, u32[]{:S(2)}) collective-permute-start(f32[128,128]{1,0:T(8,128)} %param.8), channel_id=1, source_target_pairs={{4,0},{8,4},{12,8},{16,12},{20,16},{24,20},{28,24},{5,1},{9,5},{13... | collective-permute-start | bytes 196616 | tf_op jit(solution)/shard_map/ppermute | solution.py:12
  19.1 11.7 %copy-start = (f32[128,128]{1,0:T(8,128)S(1)}, f32[128,128]{1,0:T(8,128)}, u32[]{:S(2)}) copy-start(f32[128,128]{1,0:T(8,128)} %param.8) | copy-start | bytes 196612
  51.1 3.3 %collective-permute-start.1 = (f32[128,128]{1,0:T(8,128)S(1)}, f32[128,128]{1,0:T(8,128)S(1)}, u32[]{:S(2)}, u32[]{:S(2)}) collective-permute-start(f32[128,128]{1,0:T(8,128)S(1)} %slice_add_fusion.2), channel_id=1, source_target_pairs={{4,0},{8,4},{12,8},{16,12},{20,16},{24,20},{28,24},{5,1},{9,5},{13... | collective-permute-start | bytes 196616 | tf_op jit(solution)/shard_map/ppermute | solution.py:12
  78.0 3.3 %collective-permute-start.2 = (f32[128,128]{1,0:T(8,128)S(1)}, f32[128,128]{1,0:T(8,128)S(1)}, u32[]{:S(2)}, u32[]{:S(2)}) collective-permute-start(f32[128,128]{1,0:T(8,128)S(1)} %slice_add_fusion.1), channel_id=1, source_target_pairs={{4,0},{8,4},{12,8},{16,12},{20,16},{24,20},{28,24},{5,1},{9,5},{13... | collective-permute-start | bytes 196616 | tf_op jit(solution)/shard_map/ppermute | solution.py:12
where the time goes:
time: 106 us; the launch traced here: 105 us
  blocking collectives  81.1 us (77%)
  matrix products  9.34 us (9%)
  local copies, waits for them, and re-layouts  6.49 us (6%)
  waiting for transfers between devices  3.95 us (4%)
  starting transfers between devices  3.86 us (4%)
    all_gather x6, blocking collectives, carried_in(): gathered = jax.tree.map(lambda a: lax.all_gather(a, axis), part)  63.9 us
    all_gather x1, blocking collectives, local(): gathered = lax.all_gather(reflectors, 'vecs', axis=2, tiled=True)  17.2 us
    dot_general x1, local copies, waits for them, and re-layouts, inverse_factor(): gram_matrix = jnp.dot(reflector, reflector.T, precision=HIGHEST)  4.65 us
    ppermute x3, waiting for transfers between devices, from_behind(): lax.ppermute(value, axis, [(source, source + steps) for source in range(l...  3.95 us
    ppermute x3, starting transfers between devices, from_behind(): lax.ppermute(value, axis, [(source, source + steps) for source in range(l...  3.86 us
  transfers between devices with their start and end apart: 3, of which 2 were waited for; matrix products, arithmetic and copies ran while one was open for 11% of the time, Pallas kernels for 0%

commit v1 on v0

v1 whole, which is shorter than its diff:
```python
import jax
import jax.numpy as jnp
from jax import lax
from jax.sharding import PartitionSpec as P

HIGHEST = lax.Precision.HIGHEST
PAIR = 2


def dot(left, right):
    return jnp.matmul(left, right, precision=HIGHEST)


def spread(value, axis, index, size):
    if size & (size - 1) or size > 8:
        gathered = lax.all_gather(value, axis)
        return [gathered[place] for place in range(size)]
    order = [value]
    for mask in range(1, size):
        order.append(lax.ppermute(value, axis, [(place, place ^ mask) for place in range(size)]))
    bit = 1
    while bit < size:
        flip = (index & bit) != 0
        order = [jnp.where(flip, order[place ^ bit], order[place]) for place in range(size)]
        bit *= 2
    return order


def block_mask(size, block):
    row = lax.broadcasted_iota(jnp.int32, (size, size), 0)
    col = lax.broadcasted_iota(jnp.int32, (size, size), 1)
    return (row // block) == (col // block)


def unit_upper_inverse(strict):
    size = strict.shape[-1]
    eye = jnp.eye(size, dtype=strict.dtype)
    block = min(8, size)
    near = jnp.where(block_mask(size, block), strict, 0.0)
    square = dot(near, near)
    fourth = dot(square, square)
    result = eye - near
    result = result + dot(result, square)
    result = result + dot(result, fourth)
    while block < size:
        step = 4 if 4 * block <= size else 2
        ring = block_mask(size, block * step) & ~block_mask(size, block)
        across = dot(result, jnp.where(ring, strict, 0.0))
        once = result - dot(across, result)
        if step == 4:
            once = once + dot(dot(across, across), once)
        result = once
        block *= step
    return result


def pair_operators(first, second):
    groups, block, _ = first.shape
    none = jnp.zeros((groups, block, block), first.dtype)
    joined = jnp.concatenate(
        [jnp.concatenate([none, second], 2), jnp.concatenate([first, none], 2)], 1
    )
    gram = jnp.einsum("gik,gjk->gij", joined, joined, precision=HIGHEST)
    size = 2 * block
    row = lax.broadcasted_iota(jnp.int32, (size, size), 0)
    col = lax.broadcasted_iota(jnp.int32, (size, size), 1)
    half_diag = 0.5 * jnp.sum(jnp.where(row == col, gram, 0.0), 2)
    strict = jnp.where(row < col, gram, 0.0) / half_diag[:, :, None]
    inverse = unit_upper_inverse(strict) / half_diag[:, None, :]
    solved = dot(inverse, joined)
    reached = jnp.einsum("gki,gkj->gij", joined, solved, precision=HIGHEST)
    return jnp.eye(3 * block, dtype=first.dtype) - reached


def local(vectors, reflectors):
    groups, _, _, window = reflectors.shape
    block = window // 2
    row_index = lax.axis_index("rows")
    row_count = lax.axis_size("rows")
    vec_index = lax.axis_index("vecs")
    vec_count = lax.axis_size("vecs")
    nodes = row_count // PAIR
    node = row_index // PAIR
    upper = (row_index % PAIR) == 0
    is_first = node == 0
    is_last = node == nodes - 1
    other_core = [(place, place ^ 1) for place in range(row_count)]

    def both(mine):
        theirs = lax.ppermute(mine, "rows", other_core)
        return jnp.where(upper, mine, theirs), jnp.where(upper, theirs, mine)

    top, low = both(vectors)
    below = lax.ppermute(
        top, "rows", [(place, place - PAIR) for place in range(PAIR, row_count)]
    )
    mine = jnp.concatenate(spread(reflectors[:, 0], "vecs", vec_index, vec_count), 1)
    first, second = both(mine)
    col = lax.broadcasted_iota(jnp.int32, second.shape, 2)
    second = jnp.where(is_last & (col >= block), 0.0, second)
    operators = pair_operators(first, second)

    def exchange(down, up, want_up):
        if nodes & (nodes - 1) or nodes > 4:
            members = [
                [place * PAIR + core for place in range(nodes)] for core in range(PAIR)
            ]
            earlier = lax.all_gather(down, "rows", axis_index_groups=members)
            earlier = [earlier[place] for place in range(nodes - 1)]
            later = lax.ppermute(
                up, "rows", [(place, place - PAIR) for place in range(PAIR, row_count)]
            )
            return earlier, later
        came = {}
        for mask in range(1, nodes):
            moves = [
                (place, place ^ mask)
                for place in range(nodes)
                if place ^ mask > place or (want_up and place ^ mask == place - 1)
            ]
            value = jnp.where((node ^ mask) > node, down, up) if want_up else down
            came[mask] = lax.ppermute(
                value,
                "rows",
                [
                    (source * PAIR + core, target * PAIR + core)
                    for source, target in moves
                    for core in range(PAIR)
                ],
            )
        earlier = []
        for place in range(nodes - 1):
            value = came[1]
            for mask in range(2, nodes):
                value = jnp.where((node ^ place) == mask, came[mask], value)
            earlier.append(value)
        later = came[1]
        for mask in range(2, nodes):
            later = jnp.where((node ^ (node + 1)) == mask, came[mask], later)
        return earlier, later

    for group in range(groups):
        operator = operators[group]
        last_group = group == groups - 1
        window_rows = jnp.concatenate(
            [jnp.where(is_first, top, 0.0), low, jnp.where(is_last, 0.0, below)], 0
        )
        fixed = dot(operator, window_rows)
        lead = operator[:, :block]
        down = jnp.concatenate([fixed[2 * block :], lead[2 * block :]], 0)
        up = jnp.concatenate([fixed[:block], lead[:block]], 0)
        earlier, later = exchange(down, up, not last_group)
        carry = jnp.zeros_like(top)
        for place, value in enumerate(earlier):
            if place == 0:
                step = value[:block]
            else:
                step = value[:block] + dot(value[block:], carry)
            carry = jnp.where(node > place, step, carry)
        result = fixed + dot(lead, carry)
        top = result[:block]
        low = result[block : 2 * block]
        if not last_group:
            below = later[:block] + dot(later[block:], result[2 * block :])
    return jnp.where(upper, top, low)


def solution(mesh):
    placed = (P("rows", "vecs"), P(None, "rows", "vecs", None))
    return jax.shard_map(
        local, mesh=mesh, in_specs=placed, out_specs=P("rows", "vecs"), check_vma=False
    )
```

time: 106 us -> 79.8 us (0.75)
  blocking collectives: 81.1 us -> 0 us
  starting transfers between devices: 3.86 us -> 28.9 us
  waiting for transfers between devices: 3.95 us -> 22.3 us
  matrix products: 9.34 us -> 25.8 us
  local copies, waits for them, and re-layouts: 6.49 us -> 0.18 us
  other arithmetic: 0.1 us -> 1.8 us
    all_gather x7 -> x0, blocking collectives: 81.1 us -> none  [the longest x6 63.9 us: carried_in(): gathered = jax.tree.map(lambda a: lax.all_gather(a, axis), part)]
    ppermute x3 -> x15, starting transfers between devices: 3.86 us -> 28.9 us  [the longest x9 21.8 us: exchange(): lax.ppermute(value, 'rows', [(source * PAIR + core, target * PAIR + core)...]
    ppermute x3 -> x15, waiting for transfers between devices: 3.95 us -> 22.3 us  [the longest x9 10.3 us: exchange(): lax.ppermute(value, 'rows', [(source * PAIR + core, target * PAIR + core)...]
    dot_general x28 -> x31, matrix products: 9.34 us -> 25.8 us  [the longest x29 22.3 us: dot(): return jnp.matmul(left, right, precision=HIGHEST)]
    dot_general x1 -> x0, local copies, waits for them, and re-layouts: 4.65 us -> none  [inverse_factor(): gram_matrix = jnp.dot(reflector, reflector.T, precision=HIGHEST)]
    gather x1 -> x0, local copies, waits for them, and re-layouts: 1.75 us -> none  [inverse_factor(): half_diag = jnp.diag(gram_matrix) * 0.5]
  transfers between devices with their start and end apart: 3 -> 15, of which waited for: 2 -> 9; matrix products, arithmetic and copies ran while one was open for 11% -> 1% of each run, Pallas kernels for 0% -> 0%
where the time goes in v1:
time: 79.8 us; the launch traced here: 79.5 us
  starting transfers between devices  28.9 us (36%)
  matrix products  25.8 us (32%)
  waiting for transfers between devices  22.3 us (28%)
  other arithmetic  1.8 us (2%)
    dot_general x29, matrix products, dot(): return jnp.matmul(left, right, precision=HIGHEST)  22.3 us
    ppermute x9, starting transfers between devices, exchange(): lax.ppermute(value, 'rows', [(source * PAIR + core, target * PAIR + core)...  21.8 us
    ppermute x9, waiting for transfers between devices, exchange(): lax.ppermute(value, 'rows', [(source * PAIR + core, target * PAIR + core)...  10.3 us
    ppermute x3, waiting for transfers between devices, spread(): lax.ppermute(value, axis, [(place, place ^ mask) for place in range(size)])  6.92 us
    ppermute x3, starting transfers between devices, spread(): lax.ppermute(value, axis, [(place, place ^ mask) for place in range(size)])  5.68 us
    ppermute x1, waiting for transfers between devices, local(): lax.ppermute(top, 'rows', [(place, place - PAIR) for place in range(PAIR,...  5.05 us
    dot_general x1, matrix products, pair_operators(): reached = jnp.einsum('gki,gkj->gij', joined, solved, precision=HIGHEST)  2.09 us
  transfers between devices with their start and end apart: 15, of which 9 were waited for; matrix products, arithmetic and copies ran while one was open for 1% of the time, Pallas kernels for 0%

profile of v1, /device:TPU:0, one launch (start us, length us, event | category | flops | bytes accessed | tf_op | source)
XLA Modules:
  0.0 79.5 jit_solution(12603696809753000697)
XLA Ops:
  0.0 5.0 %collective-permute-start = (f32[3,32,256]{2,1,0:T(8,128)}, f32[3,32,256]{2,1,0:T(8,128)S(1)}, u32[]{:S(2)}, u32[]{:S(2)}) collective-permute-start(f32[3,32,256]{2,1,0:T(8,128)} %bitcast.41), channel_id=1, source_target_pairs={{0,3},{1,2},{2,1},{3,0},{4,7},{5,6},{6,5},{7,4},{8,11},{9,10},{10,... | collective-permute-start | bytes 294920 | tf_op jit(solution)/shard_map/ppermute | solution.py:20
  6.6 2.4 %collective-permute-done = f32[3,32,256]{2,1,0:T(8,128)S(1)} collective-permute-done((f32[3,32,256]{2,1,0:T(8,128)}, f32[3,32,256]{2,1,0:T(8,128)S(1)}, u32[]{:S(2)}, u32[]{:S(2)}) %collective-permute-start) | collective-permute-done | bytes 98336 | tf_op jit(solution)/shard_map/ppermute | solution.py:20
  9.1 4.5 %collective-permute-done.1 = f32[3,32,256]{2,1,0:T(8,128)S(1)} collective-permute-done((f32[3,32,256]{2,1,0:T(8,128)}, f32[3,32,256]{2,1,0:T(8,128)S(1)}, u32[]{:S(2)}, u32[]{:S(2)}) %collective-permute-start.1) | collective-permute-done | bytes 98336 | tf_op jit(solution)/shard_map/ppermute | solution.py:20
  15.1 5.1 %collective-permute-done.5 = f32[128,128]{1,0:T(8,128)S(1)} collective-permute-done((f32[128,128]{1,0:T(8,128)S(1)}, f32[128,128]{1,0:T(8,128)S(1)}, u32[]{:S(2)}, u32[]{:S(2)}) %collective-permute-start.5) | collective-permute-done | bytes 65568 | tf_op jit(solution)/shard_map/ppermute | solution.py:94
  20.2 1.4 %select_reduce_fusion = (f32[3,256]{1,0:T(4,128)S(1)}, f32[3,256,256]{1,2,0:T(8,128)S(1)}) fusion(pred[256,256]{0,1:T(8,128)(4,1)S(1)} %iota_compare_fusion.4, f32[3,128,256]{2,1,0:T(8,128)S(1)} %get-tuple-element.11, f32[3,128,256]{2,1,0:T(8,128)S(1)} %get-tuple-element.10), kind=kOutput, calls=%fused_computation.22 | convolution fusion | flops 907836672 | bytes 1641472 | tf_op jit(solution)/shard_map/gik,gjk->gij/dot_general | solution.py:63
  21.6 1.7 %fusion.8 = f32[3,256,256]{2,1,0:T(8,128)S(1)} fusion(pred[256,256]{0,1:T(8,128)(4,1)S(1)} %get-tuple-element.46, f32[3,256,256]{1,2,0:T(8,128)S(1)} %get-tuple-element.48, f32[3,256]{1,0:T(4,128)S(1)} %broadcast_multiply_fusion, pred[256,256]{0,1:T(8,128)(4,1)S(1)} %get-tuple-element.61), kind=kOutput, calls=%fused_computation.24 | convolution fusion | flops 604569600 | bytes 1707008 | tf_op jit(solution)/shard_map/dot_general | solution.py:11
  24.2 1.5 %convolution_add_fusion.3 = f32[3,256,256]{1,2,0:T(8,128)S(1)} fusion(f32[3,256,256]{2,1,0:T(8,128)S(1)} %fusion.8, f32[256,256]{0,1:T(8,128)S(1)} %get-tuple-element.62, pred[256,256]{0,1:T(8,128)(4,1)S(1)} %get-tuple-element.46, f32[3,256,256]{1,2,0:T(8,128)S(1)} %get-tuple-element.48, f32[3,256]{1,0:T(4,128)S(1)} %broadcast_multiply_fusion, ...), kind=kOutput, calls=%fused_computation.7 | convolution fusion | flops 604962816 | bytes 2755584 | tf_op jit(solution)/shard_map/dot_general | solution.py:11
  25.7 1.4 %convolution_add_fusion.2 = f32[3,256,256]{1,2,0:T(8,128)S(1)} fusion(f32[3,256,256]{1,2,0:T(8,128)S(1)} %convolution_add_fusion.3, f32[3,256,256]{2,1,0:T(8,128)S(1)} %fusion.120), kind=kOutput, calls=%fused_computation.6 | convolution fusion | flops 604176384 | bytes 2359296 | tf_op jit(solution)/shard_map/dot_general | solution.py:11
  27.1 1.5 %fusion.5 = f32[3,256,256]{2,1,0:T(8,128)S(1)} fusion(f32[3,256,256]{1,2,0:T(8,128)S(1)} %convolution_add_fusion.2, pred[256,256]{0,1:T(8,128)(4,1)S(1)} %get-tuple-element.45, f32[3,256,256]{1,2,0:T(8,128)S(1)} %get-tuple-element.48, f32[3,256]{1,0:T(4,128)S(1)} %broadcast_multiply_fusion, pred[256,256]{0,1:T(8,128)(4,1)S(1)} %get-tuple-element.61), kind=kOutput, calls=%fused_computation.19 | convolution fusion | flops 604569600 | bytes 2493440 | tf_op jit(solution)/shard_map/dot_general | solution.py:11
  31.3 1.6 %fusion.3 = f32[3,256,256]{2,1,0:T(8,128)S(1)} fusion(f32[3,256,256]{1,2,0:T(8,128)S(1)} %convolution_add_fusion.1, pred[256,256]{0,1:T(8,128)(4,1)S(1)} %get-tuple-element.44, f32[3,256,256]{1,2,0:T(8,128)S(1)} %get-tuple-element.48, f32[3,256]{1,0:T(4,128)S(1)} %broadcast_multiply_fusion, pred[256,256]{0,1:T(8,128)(4,1)S(1)} %get-tuple-element.61), kind=kOutput, calls=%fused_computation.17 | convolution fusion | flops 604569600 | bytes 2493440 | tf_op jit(solution)/shard_map/dot_general | solution.py:11
  35.6 1.5 %fusion.1 = f32[3,256,256]{2,1,0:T(8,128)S(1)} fusion(f32[3,256,256]{1,2,0:T(8,128)S(1)} %convolution_add_fusion, pred[256,256]{0,1:T(8,128)(4,1)S(1)} %get-tuple-element.43, f32[3,256,256]{1,2,0:T(8,128)S(1)} %get-tuple-element.48, f32[3,256]{1,0:T(4,128)S(1)} %broadcast_multiply_fusion, pred[256,256]{0,1:T(8,128)(4,1)S(1)} %get-tuple-element.61), kind=kOutput, calls=%fused_computation.15 | convolution fusion | flops 604569600 | bytes 2493440 | tf_op jit(solution)/shard_map/dot_general | solution.py:11
  38.0 1.5 %fusion.11 = f32[3,256,384]{2,1,0:T(8,128)S(1)} fusion(f32[3,256,256]{1,2,0:T(8,128)S(1)} %fusion, f32[3,128,256]{2,1,0:T(8,128)S(1)} %get-tuple-element.11, f32[3,128,256]{2,1,0:T(8,128)S(1)} %get-tuple-element.10), kind=kOutput, calls=%fused_computation.27 | convolution fusion | flops 907444224 | bytes 2752512 | tf_op jit(solution)/shard_map/dot_general | solution.py:11
  39.5 2.1 %convolution_subtract_fusion = f32[3,384,384]{2,1,0:T(8,128)S(1)} fusion(f32[3,256,384]{2,1,0:T(8,128)S(1)} %fusion.11, f32[384,384]{1,0:T(8,128)S(1)} %fusion.19, f32[3,128,256]{2,1,0:T(8,128)S(1)} %get-tuple-element.11, f32[3,128,256]{2,1,0:T(8,128)S(1)} %get-tuple-element.10), kind=kOutput, calls=%fused_computation | convolution fusion | flops 1360871424 | bytes 4325376 | tf_op jit(solution)/shard_map/gki,gkj->gij/dot_general | solution.py:71
  42.4 2.4 %collective-permute-start.6 = (f32[256,128]{1,0:T(8,128)S(1)}, f32[256,128]{1,0:T(8,128)S(1)}, u32[]{:S(2)}, u32[]{:S(2)}) collective-permute-start(f32[256,128]{1,0:T(8,128)S(1)} %get-tuple-element.33), channel_id=1, source_target_pairs={{0,24},{4,28},{8,16},{12,20},{16,8},{20,12},{1,25},{5,29},{9,17},{... | collective-permute-start | bytes 393224 | tf_op jit(solution)/shard_map/ppermute | solution.py:122
  44.8 5.3 %collective-permute-start.7 = (f32[256,128]{1,0:T(8,128)S(1)}, f32[256,128]{1,0:T(8,128)S(1)}, u32[]{:S(2)}, u32[]{:S(2)}) collective-permute-start(f32[256,128]{1,0:T(8,128)S(1)} %get-tuple-element.31), channel_id=1, source_target_pairs={{0,16},{4,20},{8,24},{12,28},{1,17},{5,21},{9,25},{13,29},{2,18},{... | collective-permute-start | bytes 393224 | tf_op jit(solution)/shard_map/ppermute | solution.py:122
  50.2 2.4 %collective-permute-done.7 = f32[256,128]{1,0:T(8,128)S(1)} collective-permute-done((f32[256,128]{1,0:T(8,128)S(1)}, f32[256,128]{1,0:T(8,128)S(1)}, u32[]{:S(2)}, u32[]{:S(2)}) %collective-permute-start.7) | collective-permute-done | bytes 131104 | tf_op jit(solution)/shard_map/ppermute | solution.py:122
  52.6 2.5 %collective-permute-done.8 = f32[256,128]{1,0:T(8,128)S(1)} collective-permute-done((f32[256,128]{1,0:T(8,128)S(1)}, f32[256,128]{1,0:T(8,128)S(1)}, u32[]{:S(2)}, u32[]{:S(2)}) %collective-permute-start.8) | collective-permute-done | bytes 131104 | tf_op jit(solution)/shard_map/ppermute | solution.py:122
  56.9 1.8 %collective-permute-start.10 = (f32[256,128]{1,0:T(8,128)S(1)}, f32[256,128]{1,0:T(8,128)S(1)}, u32[]{:S(2)}, u32[]{:S(2)}) collective-permute-start(f32[256,128]{1,0:T(8,128)S(1)} %get-tuple-element.28), channel_id=1, source_target_pairs={{0,16},{4,20},{8,24},{12,28},{1,17},{5,21},{9,25},{13,29},{2,18},{... | collective-permute-start | bytes 393224 | tf_op jit(solution)/shard_map/ppermute | solution.py:122
  59.8 1.7 %collective-permute-start.9 = (f32[256,128]{1,0:T(8,128)S(1)}, f32[256,128]{1,0:T(8,128)S(1)}, u32[]{:S(2)}, u32[]{:S(2)}) collective-permute-start(f32[256,128]{1,0:T(8,128)S(1)} %get-tuple-element.30), channel_id=1, source_target_pairs={{0,24},{4,28},{8,16},{12,20},{16,8},{20,12},{1,25},{5,29},{9,17},{... | collective-permute-start | bytes 393224 | tf_op jit(solution)/shard_map/ppermute | solution.py:122
  62.3 2.1 %collective-permute-done.11 = f32[256,128]{1,0:T(8,128)S(1)} collective-permute-done((f32[256,128]{1,0:T(8,128)S(1)}, f32[256,128]{1,0:T(8,128)S(1)}, u32[]{:S(2)}, u32[]{:S(2)}) %collective-permute-start.11) | collective-permute-done | bytes 131104 | tf_op jit(solution)/shard_map/ppermute | solution.py:122
  66.1 5.0 %collective-permute-start.12 = (f32[256,128]{1,0:T(8,128)S(1)}, f32[256,128]{1,0:T(8,128)S(1)}, u32[]{:S(2)}, u32[]{:S(2)}) collective-permute-start(f32[256,128]{1,0:T(8,128)S(1)} %pad_maximum_fusion.5), channel_id=1, source_target_pairs={{0,24},{4,28},{8,16},{12,20},{1,25},{5,29},{9,17},{13,21},{2,26},{... | collective-permute-start | bytes 393224 | tf_op jit(solution)/shard_map/ppermute | solution.py:122
  71.1 1.3 %collective-permute-start.13 = (f32[256,128]{1,0:T(8,128)S(1)}, f32[256,128]{1,0:T(8,128)S(1)}, u32[]{:S(2)}, u32[]{:S(2)}) collective-permute-start(f32[256,128]{1,0:T(8,128)S(1)} %pad_maximum_fusion.5), channel_id=1, source_target_pairs={{0,16},{4,20},{8,24},{12,28},{1,17},{5,21},{9,25},{13,29},{2,18},{... | collective-permute-start | bytes 393224 | tf_op jit(solution)/shard_map/ppermute | solution.py:122
  72.4 3.1 %collective-permute-start.14 = (f32[256,128]{1,0:T(8,128)S(1)}, f32[256,128]{1,0:T(8,128)S(1)}, u32[]{:S(2)}, u32[]{:S(2)}) collective-permute-start(f32[256,128]{1,0:T(8,128)S(1)} %pad_maximum_fusion.5), channel_id=1, source_target_pairs={{0,8},{4,12},{16,24},{20,28},{1,9},{5,13},{17,25},{21,29},{2,10},{... | collective-permute-start | bytes 393224 | tf_op jit(solution)/shard_map/ppermute | solution.py:122
  75.7 2.4 %collective-permute-done.14 = f32[256,128]{1,0:T(8,128)S(1)} collective-permute-done((f32[256,128]{1,0:T(8,128)S(1)}, f32[256,128]{1,0:T(8,128)S(1)}, u32[]{:S(2)}, u32[]{:S(2)}) %collective-permute-start.14) | collective-permute-done | bytes 131104 | tf_op jit(solution)/shard_map/ppermute | solution.py:122
  (74 shorter events, 17.7 us)
Async XLA Ops:
  0.0 13.5 %copy-start = (f32[3,1,32,256]{3,2,1,0:T(8,128)S(1)}, f32[3,1,32,256]{3,2,1,0:T(8,128)}, u32[]{:S(2)}) copy-start(f32[3,1,32,256]{3,2,1,0:T(8,128)} %param.3) | copy-start | bytes 294916
  0.0 9.1 %collective-permute-start = (f32[3,32,256]{2,1,0:T(8,128)}, f32[3,32,256]{2,1,0:T(8,128)S(1)}, u32[]{:S(2)}, u32[]{:S(2)}) collective-permute-start(f32[3,32,256]{2,1,0:T(8,128)} %bitcast.41), channel_id=1, source_target_pairs={{0,3},{1,2},{2,1},{3,0},{4,7},{5,6},{6,5},{7,4},{8,11},{9,10},{10,... | collective-permute-start | bytes 294920 | tf_op jit(solution)/shard_map/ppermute | solution.py:20
  5.1 8.5 %collective-permute-start.1 = (f32[3,32,256]{2,1,0:T(8,128)}, f32[3,32,256]{2,1,0:T(8,128)S(1)}, u32[]{:S(2)}, u32[]{:S(2)}) collective-permute-start(f32[3,32,256]{2,1,0:T(8,128)} %bitcast.42), channel_id=1, source_target_pairs={{0,2},{1,3},{2,0},{3,1},{4,6},{5,7},{6,4},{7,5},{8,10},{9,11},{10,... | collective-permute-start | bytes 294920 | tf_op jit(solution)/shard_map/ppermute | solution.py:20
  5.1 8.5 %collective-permute-start.2 = (f32[3,32,256]{2,1,0:T(8,128)}, f32[3,32,256]{2,1,0:T(8,128)S(1)}, u32[]{:S(2)}, u32[]{:S(2)}) collective-permute-start(f32[3,32,256]{2,1,0:T(8,128)} %bitcast.43), channel_id=1, source_target_pairs={{0,1},{1,0},{2,3},{3,2},{4,5},{5,4},{6,7},{7,6},{8,9},{9,8},{10,11... | collective-permute-start | bytes 294920 | tf_op jit(solution)/shard_map/ppermute | solution.py:20
  5.7 8.0 %collective-permute-start.4 = (f32[128,128]{1,0:T(8,128)}, f32[128,128]{1,0:T(8,128)S(1)}, u32[]{:S(2)}, u32[]{:S(2)}) collective-permute-start(f32[128,128]{1,0:T(8,128)} %param.2), channel_id=1, source_target_pairs={{0,4},{4,0},{8,12},{12,8},{16,20},{20,16},{24,28},{28,24},{1,5},{5... | collective-permute-start | bytes 196616 | tf_op jit(solution)/shard_map/ppermute | solution.py:90
  5.8 7.9 %copy-start.1 = (f32[128,128]{1,0:T(8,128)S(1)}, f32[128,128]{1,0:T(8,128)}, u32[]{:S(2)}) copy-start(f32[128,128]{1,0:T(8,128)} %param.2) | copy-start | bytes 196612
  13.6 6.5 %collective-permute-start.3 = (f32[3,128,256]{2,1,0:T(8,128)S(1)}, f32[3,128,256]{2,1,0:T(8,128)S(1)}, u32[]{:S(2)}, u32[]{:S(2)}) collective-permute-start(f32[3,128,256]{2,1,0:T(8,128)S(1)} %pad_maximum_fusion), channel_id=1, source_target_pairs={{0,4},{4,0},{8,12},{12,8},{16,20},{20,16},{24,28},{28,24},{1,5},{5... | collective-permute-start | bytes 1179656 | tf_op jit(solution)/shard_map/ppermute | solution.py:90
  13.7 6.4 %collective-permute-start.5 = (f32[128,128]{1,0:T(8,128)S(1)}, f32[128,128]{1,0:T(8,128)S(1)}, u32[]{:S(2)}, u32[]{:S(2)}) collective-permute-start(f32[128,128]{1,0:T(8,128)S(1)} %get-tuple-element.6), channel_id=1, source_target_pairs={{8,0},{12,4},{16,8},{20,12},{24,16},{28,20},{9,1},{13,5},{17,9},{2... | collective-permute-start | bytes 196616 | tf_op jit(solution)/shard_map/ppermute | solution.py:94
  42.4 7.8 %collective-permute-start.6 = (f32[256,128]{1,0:T(8,128)S(1)}, f32[256,128]{1,0:T(8,128)S(1)}, u32[]{:S(2)}, u32[]{:S(2)}) collective-permute-start(f32[256,128]{1,0:T(8,128)S(1)} %get-tuple-element.33), channel_id=1, source_target_pairs={{0,24},{4,28},{8,16},{12,20},{16,8},{20,12},{1,25},{5,29},{9,17},{... | collective-permute-start | bytes 393224 | tf_op jit(solution)/shard_map/ppermute | solution.py:122
  44.8 7.8 %collective-permute-start.7 = (f32[256,128]{1,0:T(8,128)S(1)}, f32[256,128]{1,0:T(8,128)S(1)}, u32[]{:S(2)}, u32[]{:S(2)}) collective-permute-start(f32[256,128]{1,0:T(8,128)S(1)} %get-tuple-element.31), channel_id=1, source_target_pairs={{0,16},{4,20},{8,24},{12,28},{1,17},{5,21},{9,25},{13,29},{2,18},{... | collective-permute-start | bytes 393224 | tf_op jit(solution)/shard_map/ppermute | solution.py:122
  50.1 5.0 %collective-permute-start.8 = (f32[256,128]{1,0:T(8,128)S(1)}, f32[256,128]{1,0:T(8,128)S(1)}, u32[]{:S(2)}, u32[]{:S(2)}) collective-permute-start(f32[256,128]{1,0:T(8,128)S(1)} %get-tuple-element.32), channel_id=1, source_target_pairs={{0,8},{4,12},{8,0},{12,4},{16,24},{20,28},{24,16},{28,20},{1,9},{5... | collective-permute-start | bytes 393224 | tf_op jit(solution)/shard_map/ppermute | solution.py:122
  56.9 5.4 %collective-permute-start.10 = (f32[256,128]{1,0:T(8,128)S(1)}, f32[256,128]{1,0:T(8,128)S(1)}, u32[]{:S(2)}, u32[]{:S(2)}) collective-permute-start(f32[256,128]{1,0:T(8,128)S(1)} %get-tuple-element.28), channel_id=1, source_target_pairs={{0,16},{4,20},{8,24},{12,28},{1,17},{5,21},{9,25},{13,29},{2,18},{... | collective-permute-start | bytes 393224 | tf_op jit(solution)/shard_map/ppermute | solution.py:122
  58.7 5.7 %collective-permute-start.11 = (f32[256,128]{1,0:T(8,128)S(1)}, f32[256,128]{1,0:T(8,128)S(1)}, u32[]{:S(2)}, u32[]{:S(2)}) collective-permute-start(f32[256,128]{1,0:T(8,128)S(1)} %get-tuple-element.29), channel_id=1, source_target_pairs={{0,8},{4,12},{8,0},{12,4},{16,24},{20,28},{24,16},{28,20},{1,9},{5... | collective-permute-start | bytes 393224 | tf_op jit(solution)/shard_map/ppermute | solution.py:122
  59.8 4.6 %collective-permute-start.9 = (f32[256,128]{1,0:T(8,128)S(1)}, f32[256,128]{1,0:T(8,128)S(1)}, u32[]{:S(2)}, u32[]{:S(2)}) collective-permute-start(f32[256,128]{1,0:T(8,128)S(1)} %get-tuple-element.30), channel_id=1, source_target_pairs={{0,24},{4,28},{8,16},{12,20},{16,8},{20,12},{1,25},{5,29},{9,17},{... | collective-permute-start | bytes 393224 | tf_op jit(solution)/shard_map/ppermute | solution.py:122
  66.1 9.5 %collective-permute-start.12 = (f32[256,128]{1,0:T(8,128)S(1)}, f32[256,128]{1,0:T(8,128)S(1)}, u32[]{:S(2)}, u32[]{:S(2)}) collective-permute-start(f32[256,128]{1,0:T(8,128)S(1)} %pad_maximum_fusion.5), channel_id=1, source_target_pairs={{0,24},{4,28},{8,16},{12,20},{1,25},{5,29},{9,17},{13,21},{2,26},{... | collective-permute-start | bytes 393224 | tf_op jit(solution)/shard_map/ppermute | solution.py:122
  71.1 4.5 %collective-permute-start.13 = (f32[256,128]{1,0:T(8,128)S(1)}, f32[256,128]{1,0:T(8,128)S(1)}, u32[]{:S(2)}, u32[]{:S(2)}) collective-permute-start(f32[256,128]{1,0:T(8,128)S(1)} %pad_maximum_fusion.5), channel_id=1, source_target_pairs={{0,16},{4,20},{8,24},{12,28},{1,17},{5,21},{9,25},{13,29},{2,18},{... | collective-permute-start | bytes 393224 | tf_op jit(solution)/shard_map/ppermute | solution.py:122
  72.4 5.6 %collective-permute-start.14 = (f32[256,128]{1,0:T(8,128)S(1)}, f32[256,128]{1,0:T(8,128)S(1)}, u32[]{:S(2)}, u32[]{:S(2)}) collective-permute-start(f32[256,128]{1,0:T(8,128)S(1)} %pad_maximum_fusion.5), channel_id=1, source_target_pairs={{0,8},{4,12},{16,24},{20,28},{1,9},{5,13},{17,25},{21,29},{2,10},{... | collective-permute-start | bytes 393224 | tf_op jit(solution)/shard_map/ppermute | solution.py:122

commit v2 on v1

v2 whole, which is shorter than its diff:
```python
import jax
import jax.numpy as jnp
from jax import lax
from jax.experimental import pallas as pl
from jax.experimental.pallas import tpu as pltpu
from jax.sharding import PartitionSpec as P

PAIR = 2
F32, BF16 = jnp.float32, jnp.bfloat16
NN = ((1,), (0,))
NT = ((1,), (1,))
TN = ((0,), (0,))


def halves(value):
    high = value.astype(BF16)
    return high, (value - high.astype(F32)).astype(BF16)


def mm(left, right, dims=NN):
    left = left if isinstance(left, tuple) else halves(left)
    right = right if isinstance(right, tuple) else halves(right)

    def one(a, b):
        return lax.dot_general(a, b, (dims, ((), ())), preferred_element_type=F32)

    return one(left[0], right[0]) + (one(left[0], right[1]) + one(left[1], right[0]))


def same_block(shape, rows_block, cols_block, wrap):
    row = lax.broadcasted_iota(jnp.int32, shape, 0)
    col = lax.broadcasted_iota(jnp.int32, shape, 1)
    return (row // rows_block) == ((col % wrap) // cols_block)


def operators_kernel(flag_ref, first_ref, second_ref, out_ref):
    groups, block, window = first_ref.shape
    wide = 2 * block
    groups = range(groups)
    keep = flag_ref[0] == 0
    firsts, seconds, sfirst, ssecond = [], [], [], []
    col = lax.broadcasted_iota(jnp.int32, (block, window), 1)
    for g in groups:
        a = first_ref[g]
        b = jnp.where(keep | (col < block), second_ref[g], 0.0)
        firsts.append(a)
        seconds.append(b)
        sfirst.append(a * (2.0 / jnp.sum(a * a, 1, keepdims=True)))
        ssecond.append(b * (2.0 / jnp.sum(b * b, 1, keepdims=True)))
    above = lax.broadcasted_iota(jnp.int32, (block, wide), 0) < (
        lax.broadcasted_iota(jnp.int32, (block, wide), 1) % block
    )
    near, cross = [], []
    for g in groups:
        ha = halves(firsts[g])
        gq = mm(ssecond[g], halves(seconds[g]), NT)
        gp = mm(sfirst[g], ha, NT)
        near.append(jnp.where(above, jnp.concatenate([gq, gp], 1), 0.0))
        cross.append(
            mm(ssecond[g][:, :block], (ha[0][:, block:], ha[1][:, block:]), NT)
        )

    def diagonal(value, size):
        mask = same_block((wide, wide), size, size, wide)
        return tuple(
            jnp.where(mask, jnp.concatenate([part] * (wide // size), 0), jnp.zeros((), BF16))
            for part in halves(value)
        )

    def gather_blocks(value, size):
        total = None
        for place in range(block // size):
            part = value[place * size : (place + 1) * size]
            pcol = lax.broadcasted_iota(jnp.int32, part.shape, 1)
            part = jnp.where((pcol % block) // size == place, part, 0.0)
            total = part if total is None else total + part
        return total

    def widen(value, size):
        old = value.shape[0]
        tall = jnp.concatenate([value] * (size // old), 0)
        return jnp.where(same_block(tall.shape, old, old, size), tall, 0.0)

    def quad(result, ring, size):
        across = [mm(r, diagonal(b, size)) for r, b in zip(result, ring)]
        halved = [halves(x) for x in across]
        once = [r - mm(x, diagonal(r, size)) for r, x in zip(result, halved)]
        square = [mm(h, diagonal(x, size)) for h, x in zip(halved, across)]
        return [o + mm(s, diagonal(o, size)) for o, s in zip(once, square)]

    small = [gather_blocks(n, 16) for n in near]
    shape = small[0].shape
    row = lax.broadcasted_iota(jnp.int32, shape, 0)
    scol = lax.broadcasted_iota(jnp.int32, shape, 1)
    eye = jnp.where(row == scol % 16, 1.0, 0.0)
    inner = (row // 4) == (scol % 16) // 4
    tiny = [jnp.where(inner, n, 0.0) for n in small]
    square = [mm(n, diagonal(n, 16)) for n in tiny]
    result = [eye - n for n in tiny]
    result = [r + mm(r, diagonal(s, 16)) for r, s in zip(result, square)]
    result = quad(result, [jnp.where(inner, 0.0, n) for n in small], 16)
    middle = [gather_blocks(n, 64) for n in near]
    mmask = same_block(middle[0].shape, 16, 16, 64)
    result = [widen(r, 64) for r in result]
    result = quad(result, [jnp.where(mmask, 0.0, n) for n in middle], 64)
    result = [widen(r, block) for r in result]
    bmask = same_block((block, wide), 64, 64, block)
    across = [mm(r, diagonal(jnp.where(bmask, 0.0, n), block)) for r, n in zip(result, near)]
    result = [r - mm(x, diagonal(r, block)) for r, x in zip(result, across)]
    for g in groups:
        q, p = halves(result[g][:, :block]), halves(result[g][:, block:])
        link = mm(q, cross[g])
        link = mm(link, p)
        solved_p = mm(p, sfirst[g])
        low = halves(sfirst[g])
        solved_q = mm(q, ssecond[g])
        reach = mm(link, low)
        zero = jnp.zeros((block, block), F32)
        sq = jnp.concatenate([-reach[:, :block], solved_q[:, :block] - reach[:, block:], solved_q[:, block:]], 1)
        sp = jnp.concatenate([solved_p, zero], 1)
        solved = jnp.concatenate([sq, sp], 0)
        joined = jnp.concatenate(
            [
                jnp.concatenate([zero, seconds[g]], 1),
                jnp.concatenate([firsts[g], zero], 1),
            ],
            0,
        )
        moved = mm(joined, solved, TN)
        orow = lax.broadcasted_iota(jnp.int32, moved.shape, 0)
        ocol = lax.broadcasted_iota(jnp.int32, moved.shape, 1)
        out_ref[g] = jnp.where(orow == ocol, 1.0, 0.0) - moved


def pair_operators(first, second, is_last):
    groups, block, _ = first.shape
    return pl.pallas_call(
        operators_kernel,
        out_shape=jax.ShapeDtypeStruct((groups, 3 * block, 3 * block), F32),
        in_specs=[
            pl.BlockSpec(memory_space=pltpu.SMEM),
            pl.BlockSpec(memory_space=pltpu.VMEM),
            pl.BlockSpec(memory_space=pltpu.VMEM),
        ],
        out_specs=pl.BlockSpec(memory_space=pltpu.VMEM),
        compiler_params=pltpu.CompilerParams(vmem_limit_bytes=32 << 20),
    )(is_last.astype(jnp.int32).reshape(1), first, second)


def dot(left, right):
    return jnp.matmul(left, right, precision=lax.Precision.HIGHEST)


def spread(value, axis, index, size):
    if size & (size - 1) or size > 8:
        gathered = lax.all_gather(value, axis)
        return [gathered[place] for place in range(size)]
    order = [value]
    for mask in range(1, size):
        order.append(lax.ppermute(value, axis, [(place, place ^ mask) for place in range(size)]))
    bit = 1
    while bit < size:
        flip = (index & bit) != 0
        order = [jnp.where(flip, order[place ^ bit], order[place]) for place in range(size)]
        bit *= 2
    return order


def local(vectors, reflectors):
    groups, _, _, window = reflectors.shape
    block = window // 2
    row_index = lax.axis_index("rows")
    row_count = lax.axis_size("rows")
    vec_index = lax.axis_index("vecs")
    vec_count = lax.axis_size("vecs")
    nodes = row_count // PAIR
    node = row_index // PAIR
    upper = (row_index % PAIR) == 0
    is_first = node == 0
    is_last = node == nodes - 1

    def swap(value, masks):
        moves = [
            (place, ((place // PAIR) ^ masks[place % PAIR]) * PAIR + place % PAIR)
            for place in range(row_count)
        ]
        return lax.ppermute(value, "rows", moves)

    def across(value):
        return lax.ppermute(value, "rows", [(place, place ^ 1) for place in range(row_count)])

    def both(mine):
        theirs = across(mine)
        return jnp.where(upper, mine, theirs), jnp.where(upper, theirs, mine)

    def exchange(down, up, want_up):
        if nodes != 4:
            members = [
                [place * PAIR + core for place in range(nodes)] for core in range(PAIR)
            ]
            earlier = lax.all_gather(down, "rows", axis_index_groups=members)
            earlier = [earlier[place] for place in range(nodes - 1)]
            later = lax.ppermute(
                up, "rows", [(place, place - PAIR) for place in range(PAIR, row_count)]
            )
            return earlier, later
        near = swap(
            jnp.where(upper & ((node & 1) == 1), up, down) if want_up else down, (1, 2)
        )
        low_half = (node & 2) == 0
        far = swap(
            jnp.where(
                upper,
                jnp.where(low_half, down[:block], up[:block]),
                jnp.where(low_half, down[block:], up[block:]),
            ),
            (3, 3),
        )
        near_other = across(near)
        far_other = across(far)
        came = {
            1: jnp.where(upper, near, near_other),
            2: jnp.where(upper, near_other, near),
            3: jnp.concatenate(
                [jnp.where(upper, far, far_other), jnp.where(upper, far_other, far)], 0
            ),
        }
        earlier = []
        for place in range(nodes - 1):
            value = came[1]
            for mask in range(2, nodes):
                value = jnp.where((node ^ place) == mask, came[mask], value)
            earlier.append(value)
        later = came[1]
        for mask in range(2, nodes):
            later = jnp.where((node ^ (node + 1)) == mask, came[mask], later)
        return earlier, later

    top, low = both(vectors)
    if nodes == 4:
        below = jnp.where((node & 1) == 0, swap(top, (1, 1)), swap(top, (3, 3)))
    else:
        below = lax.ppermute(
            top, "rows", [(place, place - PAIR) for place in range(PAIR, row_count)]
        )
    mine = jnp.concatenate(spread(reflectors[:, 0], "vecs", vec_index, vec_count), 1)
    mine, below = lax.optimization_barrier((mine, below))
    first, second = both(mine)
    operators = pair_operators(first, second, is_last)

    for group in range(groups):
        operator = operators[group]
        last_group = group == groups - 1
        window_rows = jnp.concatenate(
            [jnp.where(is_first, top, 0.0), low, jnp.where(is_last, 0.0, below)], 0
        )
        fixed = dot(operator, window_rows)
        lead = operator[:, :block]
        down = jnp.concatenate([fixed[2 * block :], lead[2 * block :]], 0)
        up = jnp.concatenate([fixed[:block], lead[:block]], 0)
        earlier, later = exchange(down, up, not last_group)
        carry = jnp.zeros_like(top)
        for place, value in enumerate(earlier):
            if place == 0:
                step = value[:block]
            else:
                step = value[:block] + dot(value[block:], carry)
            carry = jnp.where(node > place, step, carry)
        result = fixed + dot(lead, carry)
        top = result[:block]
        low = result[block : 2 * block]
        if not last_group:
            below = later[:block] + dot(later[block:], result[2 * block :])
    return jnp.where(upper, top, low)


def solution(mesh):
    placed = (P("rows", "vecs"), P(None, "rows", "vecs", None))
    return jax.shard_map(
        local, mesh=mesh, in_specs=placed, out_specs=P("rows", "vecs"), check_vma=False
    )
```

time: 79.8 us -> 58.5 us (0.73)
  matrix products: 25.8 us -> 4.52 us
  starting transfers between devices: 28.9 us -> 18.3 us
  Pallas kernels: 0 us -> 5.68 us
  other arithmetic: 1.8 us -> 5.96 us
  local copies, waits for them, and re-layouts: 0.18 us -> 1.52 us
    dot_general x31 -> x14, matrix products: 25.8 us -> 4.52 us  [dot(): return jnp.matmul(left, right, precision=lax.Precision.HIGHEST)]
    ppermute x12 -> x16, starting transfers between devices: 23.2 us -> 13.1 us  [the longest x8 11.1 us: swap(): return lax.ppermute(value, 'rows', moves)]
    pallas_call x0 -> x1, Pallas kernels: none -> 5.68 us  [pair_operators(): pl.pallas_call(operators_kernel, out_shape=jax.ShapeDtypeStruct((groups,...]
    ppermute x3, waiting for transfers between devices: 6.92 us -> 3.66 us  [spread(): lax.ppermute(value, axis, [(place, place ^ mask) for place in range(size)])]
    ppermute x12 -> x16, waiting for transfers between devices: 15.3 us -> 18.3 us  [the longest x8 13.6 us: swap(): return lax.ppermute(value, 'rows', moves)]
    select_n x3 -> x7, other arithmetic: 0.13 us -> 1.68 us  [the longest x3 0.91 us: exchange(): jnp.where(upper, far_other, far)]
    select_n x3, other arithmetic: 0.04 us -> 1.52 us  [local(): jnp.where(is_first, top, 0.0)]
    unnamed x4 -> x8, local copies, waits for them, and re-layouts: 0.01 us -> 1.4 us
  transfers between devices with their start and end apart: 15 -> 19, of which waited for: 9 -> 10; matrix products, arithmetic and copies ran while one was open for 1% -> 6% of each run, Pallas kernels for 0% -> 0%
where the time goes in v2:
time: 58.5 us; the launch traced here: 58.2 us
  waiting for transfers between devices  21.9 us (37%)
  starting transfers between devices  18.3 us (31%)
  other arithmetic  5.96 us (10%)
  Pallas kernels  5.68 us (10%)
  matrix products  4.52 us (8%)
  local copies, waits for them, and re-layouts  1.52 us (3%)
    ppermute x8, waiting for transfers between devices, swap(): return lax.ppermute(value, 'rows', moves)  13.6 us
    ppermute x8, starting transfers between devices, swap(): return lax.ppermute(value, 'rows', moves)  11.1 us
    pallas_call x1, Pallas kernels, pair_operators(): pl.pallas_call(operators_kernel, out_shape=jax.ShapeDtypeStruct((groups,...  5.68 us
    ppermute x3, starting transfers between devices, spread(): lax.ppermute(value, axis, [(place, place ^ mask) for place in range(size)])  5.17 us
    ppermute x8, waiting for transfers between devices, across(): lax.ppermute(value, 'rows', [(place, place ^ 1) for place in range(row_co...  4.71 us
    dot_general x14, matrix products, dot(): return jnp.matmul(left, right, precision=lax.Precision.HIGHEST)  4.52 us
    ppermute x3, waiting for transfers between devices, spread(): lax.ppermute(value, axis, [(place, place ^ mask) for place in range(size)])  3.66 us
    ppermute x8, starting transfers between devices, across(): lax.ppermute(value, 'rows', [(place, place ^ 1) for place in range(row_co...  2.05 us
  transfers between devices with their start and end apart: 19, of which 10 were waited for; matrix products, arithmetic and copies ran while one was open for 6% of the time, Pallas kernels for 0%

profile of v2, /device:TPU:0, one launch (start us, length us, event | category | flops | bytes accessed | tf_op | source)
XLA Modules:
  0.0 58.2 jit_solution(14457974460265276757)
XLA Ops:
  0.5 2.6 %collective-permute-start.2 = (f32[3,32,256]{2,1,0:T(8,128)}, f32[3,32,256]{2,1,0:T(8,128)S(1)}, u32[]{:S(2)}, u32[]{:S(2)}) collective-permute-start(f32[3,32,256]{2,1,0:T(8,128)} %bitcast.18), channel_id=1, source_target_pairs={{0,1},{1,0},{2,3},{3,2},{4,5},{5,4},{6,7},{7,6},{8,9},{9,8},{10,11... | collective-permute-start | bytes 294920 | tf_op jit(solution)/shard_map/ppermute | solution.py:160
  3.0 2.6 %collective-permute-start.1 = (f32[3,32,256]{2,1,0:T(8,128)}, f32[3,32,256]{2,1,0:T(8,128)S(1)}, u32[]{:S(2)}, u32[]{:S(2)}) collective-permute-start(f32[3,32,256]{2,1,0:T(8,128)} %bitcast.19), channel_id=1, source_target_pairs={{0,2},{1,3},{2,0},{3,1},{4,6},{5,7},{6,4},{7,5},{8,10},{9,11},{10,... | collective-permute-start | bytes 294920 | tf_op jit(solution)/shard_map/ppermute | solution.py:160
  5.6 1.5 %broadcast_select_fusion.17 = (f32[128,128]{1,0:T(8,128)}, f32[128,128]{1,0:T(8,128)S(1)}, f32[128,128]{1,0:T(8,128)}) fusion(pred[]{:T(512)S(6)} %eq.31, f32[128,128]{1,0:T(8,128)} %param.2, f32[128,128]{1,0:T(8,128)S(1)} %collective-permute-done.3, pred[]{:T(512)S(6)} %eq.28), kind=kLoop, calls=%fused_computation.119 | loop fusion | flops 49152 | bytes 327682 | tf_op jit(solution)/shard_map/jit(_where)/select_n | solution.py:255
  7.1 2.7 %collective-permute-start.5 = (f32[128,128]{1,0:T(8,128)S(1)}, f32[128,128]{1,0:T(8,128)S(1)}, u32[]{:S(2)}, u32[]{:S(2)}) collective-permute-start(f32[128,128]{1,0:T(8,128)S(1)} %get-tuple-element.19), channel_id=1, source_target_pairs={{0,24},{4,28},{8,16},{12,20},{16,8},{20,12},{24,0},{28,4},{1,25},{... | collective-permute-start | bytes 196616 | tf_op jit(solution)/shard_map/ppermute | solution.py:187
  10.3 3.7 %collective-permute-done.1 = f32[3,32,256]{2,1,0:T(8,128)S(1)} collective-permute-done((f32[3,32,256]{2,1,0:T(8,128)}, f32[3,32,256]{2,1,0:T(8,128)S(1)}, u32[]{:S(2)}, u32[]{:S(2)}) %collective-permute-start.1) | collective-permute-done | bytes 98336 | tf_op jit(solution)/shard_map/ppermute | solution.py:160
  14.0 0.9 %broadcast_select_fusion.15 = (f32[3,32,256]{2,1,0:T(8,128)S(1)}, f32[3,32,256]{2,1,0:T(8,128)S(1)}, f32[3,32,256]{2,1,0:T(8,128)S(1)}, f32[3,32,256]{2,1,0:T(8,128)S(1)}) fusion(pred[]{:T(512)S(6)} %ne.20, f32[3,32,256]{2,1,0:T(8,128)S(1)} %collective-permute-done, f32[3,32,256]{2,1,0:T(8,128)S(1)} %collective-permute-done.1, pred[]{:T(512)S(6)} %ne.21, ...), kind=kLoop, calls=%fused_computation.117 | loop fusion | flops 196608 | bytes 786434 | tf_op jit(solution)/shard_map/jit(_where)/select_n | solution.py:164
  15.1 1.7 %collective-permute-done.6 = f32[3,128,256]{2,1,0:T(8,128)S(1)} collective-permute-done((f32[3,128,256]{2,1,0:T(8,128)S(1)}, f32[3,128,256]{2,1,0:T(8,128)S(1)}, u32[]{:S(2)}, u32[]{:S(2)}) %collective-permute-start.6) | collective-permute-done | bytes 393248 | tf_op jit(solution)/shard_map/ppermute | solution.py:190
  16.9 5.7 %shard_map.28 = f32[3,384,384]{2,1,0:T(8,128)S(1)} custom-call(s32[1]{0:T(128)} %bitcast.flag_ref, f32[3,128,256]{2,1,0:T(8,128)S(1)} %get-tuple-element.24.first_ref, f32[3,128,256]{2,1,0:T(8,128)S(1)} %get-tuple-element.23.second_ref), custom_call_target="tpu_custom_call" | custom-call | tf_op jit(solution)/shard_map/pallas_call | solution.py:137
  22.7 0.7 %copy-done.2 = f32[128,128]{1,0:T(8,128)S(1)} copy-done((f32[128,128]{1,0:T(8,128)S(1)}, f32[128,128]{1,0:T(8,128)}, u32[]{:S(2)}) %copy-start.2) | copy-done | bytes 65560
  24.1 0.7 %copy-done = f32[384,128]{1,0:T(8,128)} copy-done((f32[384,128]{1,0:T(8,128)}, f32[384,128]{1,0:T(8,128)S(1)}, u32[]{:S(2)}) %copy-start) | copy-done | bytes 196632
  24.8 0.7 %maximum_select_fusion = f32[256,128]{1,0:T(8,128)} fusion(f32[128,128]{1,0:T(8,128)S(1)} %get-tuple-element.31, f32[128,128]{1,0:T(8,128)S(1)} %get-tuple-element.42, f32[128,128]{1,0:T(8,128)S(1)} %get-tuple-element.30, f32[128,128]{1,0:T(8,128)S(1)} %get-tuple-element.41, pred[]{:T(512)S(6)} %and.38), kind=kLoop, calls=%fused_computation.39 | loop fusion | flops 98304 | bytes 393217 | tf_op jit(solution)/shard_map/jit(_where)/select_n | solution.py:208
  25.4 1.5 %collective-permute-start.9 = (f32[256,128]{1,0:T(8,128)}, f32[256,128]{1,0:T(8,128)}, u32[]{:S(2)}, u32[]{:S(2)}) collective-permute-start(f32[256,128]{1,0:T(8,128)} %maximum_select_fusion), channel_id=1, source_target_pairs={{0,8},{4,20},{8,0},{12,28},{16,24},{20,4},{24,16},{28,12},{1,9},{5... | collective-permute-start | bytes 393224 | tf_op jit(solution)/shard_map/ppermute | solution.py:187
  26.9 1.5 %collective-permute-start.7 = (f32[128,128]{1,0:T(8,128)S(1)}, f32[128,128]{1,0:T(8,128)}, u32[]{:S(2)}, u32[]{:S(2)}) collective-permute-start(f32[128,128]{1,0:T(8,128)S(1)} %get-tuple-element.32), channel_id=1, source_target_pairs={{0,24},{4,28},{8,16},{12,20},{16,8},{20,12},{24,0},{28,4},{1,25},{... | collective-permute-start | bytes 196616 | tf_op jit(solution)/shard_map/ppermute | solution.py:187
  28.4 4.7 %collective-permute-done.7 = f32[128,128]{1,0:T(8,128)} collective-permute-done((f32[128,128]{1,0:T(8,128)S(1)}, f32[128,128]{1,0:T(8,128)}, u32[]{:S(2)}, u32[]{:S(2)}) %collective-permute-start.7) | collective-permute-done | bytes 65568 | tf_op jit(solution)/shard_map/ppermute | solution.py:187
  33.6 1.1 %collective-permute-done.8 = f32[128,128]{1,0:T(8,128)} collective-permute-done((f32[128,128]{1,0:T(8,128)}, f32[128,128]{1,0:T(8,128)}, u32[]{:S(2)}, u32[]{:S(2)}) %collective-permute-start.8) | collective-permute-done | bytes 65568 | tf_op jit(solution)/shard_map/ppermute | solution.py:190
  34.7 0.9 %broadcast_select_fusion.23 = (f32[128,128]{1,0:T(8,128)S(1)}, f32[128,128]{1,0:T(8,128)S(1)}) fusion(f32[128,128]{1,0:T(8,128)} %collective-permute-done.8, f32[128,128]{1,0:T(8,128)} %collective-permute-done.7, pred[]{:T(512)S(6)} %eq.28), kind=kLoop, calls=%fused_computation.128 | loop fusion | flops 32768 | bytes 262145 | tf_op jit(solution)/shard_map/jit(_where)/select_n | solution.py:225
  35.6 0.9 %select_select_fusion.5 = (f32[256,128]{1,0:T(8,128)S(1)}, f32[256,128]{1,0:T(8,128)S(1)}, f32[256,128]{1,0:T(8,128)S(1)}) fusion(f32[128,128]{1,0:T(8,128)S(1)} %get-tuple-element.54, f32[128,128]{1,0:T(8,128)S(1)} %get-tuple-element.55, pred[]{:T(512)S(6)} %eq.71, pred[]{:T(512)S(6)} %eq.70, f32[256,128]{1,0:T(8,128)S(1)} %collective-permute-done.10, ...), kind=kLoop, calls=%fused_computation.47 | loop fusion | flops 163840 | bytes 786435 | tf_op jit(solution)/shard_map/jit(_where)/select_n | solution.py:236
  38.3 1.6 %collective-permute-start.13 = (f32[256,128]{1,0:T(8,128)S(1)}, f32[256,128]{1,0:T(8,128)S(1)}, u32[]{:S(2)}, u32[]{:S(2)}) collective-permute-start(f32[256,128]{1,0:T(8,128)S(1)} %maximum_select_fusion.1), channel_id=1, source_target_pairs={{0,8},{4,20},{8,0},{12,28},{16,24},{20,4},{24,16},{28,12},{1,9},{5... | collective-permute-start | bytes 393224 | tf_op jit(solution)/shard_map/ppermute | solution.py:187
  40.4 4.6 %collective-permute-done.11 = f32[128,128]{1,0:T(8,128)S(1)} collective-permute-done((f32[128,128]{1,0:T(8,128)S(1)}, f32[128,128]{1,0:T(8,128)S(1)}, u32[]{:S(2)}, u32[]{:S(2)}) %collective-permute-start.11) | collective-permute-done | bytes 65568 | tf_op jit(solution)/shard_map/ppermute | solution.py:187
  45.5 0.7 %collective-permute-done.12 = f32[128,128]{1,0:T(8,128)S(1)} collective-permute-done((f32[128,128]{1,0:T(8,128)S(1)}, f32[128,128]{1,0:T(8,128)S(1)}, u32[]{:S(2)}, u32[]{:S(2)}) %collective-permute-start.12) | collective-permute-done | bytes 65568 | tf_op jit(solution)/shard_map/ppermute | solution.py:190
  48.2 1.2 %collective-permute-start.17 = (f32[256,128]{1,0:T(8,128)S(1)}, f32[256,128]{1,0:T(8,128)S(1)}, u32[]{:S(2)}, u32[]{:S(2)}) collective-permute-start(f32[256,128]{1,0:T(8,128)S(1)} %pad_maximum_fusion.4), channel_id=1, source_target_pairs={{0,8},{4,20},{8,0},{12,28},{16,24},{20,4},{24,16},{28,12},{1,9},{5... | collective-permute-start | bytes 393224 | tf_op jit(solution)/shard_map/ppermute | solution.py:187
  49.5 1.5 %collective-permute-start.15 = (f32[128,128]{1,0:T(8,128)S(1)}, f32[128,128]{1,0:T(8,128)S(1)}, u32[]{:S(2)}, u32[]{:S(2)}) collective-permute-start(f32[128,128]{1,0:T(8,128)S(1)} %get-tuple-element.26), channel_id=1, source_target_pairs={{0,24},{4,28},{8,16},{12,20},{16,8},{20,12},{24,0},{28,4},{1,25},{... | collective-permute-start | bytes 196616 | tf_op jit(solution)/shard_map/ppermute | solution.py:187
  50.9 4.3 %collective-permute-done.15 = f32[128,128]{1,0:T(8,128)S(1)} collective-permute-done((f32[128,128]{1,0:T(8,128)S(1)}, f32[128,128]{1,0:T(8,128)S(1)}, u32[]{:S(2)}, u32[]{:S(2)}) %collective-permute-start.15) | collective-permute-done | bytes 65568 | tf_op jit(solution)/shard_map/ppermute | solution.py:187
  55.8 0.7 %collective-permute-done.16 = f32[128,128]{1,0:T(8,128)S(1)} collective-permute-done((f32[128,128]{1,0:T(8,128)S(1)}, f32[128,128]{1,0:T(8,128)S(1)}, u32[]{:S(2)}, u32[]{:S(2)}) %collective-permute-start.16) | collective-permute-done | bytes 65568 | tf_op jit(solution)/shard_map/ppermute | solution.py:190
  (62 shorter events, 9.4 us)
Async XLA Ops:
  0.0 5.6 %collective-permute-start.3 = (f32[128,128]{1,0:T(8,128)}, f32[128,128]{1,0:T(8,128)S(1)}, u32[]{:S(2)}, u32[]{:S(2)}) collective-permute-start(f32[128,128]{1,0:T(8,128)} %param.2), channel_id=1, source_target_pairs={{0,4},{4,0},{8,12},{12,8},{16,20},{20,16},{24,28},{28,24},{1,5},{5... | collective-permute-start | bytes 196616 | tf_op jit(solution)/shard_map/ppermute | solution.py:190
  0.5 9.9 %collective-permute-start.2 = (f32[3,32,256]{2,1,0:T(8,128)}, f32[3,32,256]{2,1,0:T(8,128)S(1)}, u32[]{:S(2)}, u32[]{:S(2)}) collective-permute-start(f32[3,32,256]{2,1,0:T(8,128)} %bitcast.18), channel_id=1, source_target_pairs={{0,1},{1,0},{2,3},{3,2},{4,5},{5,4},{6,7},{7,6},{8,9},{9,8},{10,11... | collective-permute-start | bytes 294920 | tf_op jit(solution)/shard_map/ppermute | solution.py:160
  3.0 11.0 %collective-permute-start.1 = (f32[3,32,256]{2,1,0:T(8,128)}, f32[3,32,256]{2,1,0:T(8,128)S(1)}, u32[]{:S(2)}, u32[]{:S(2)}) collective-permute-start(f32[3,32,256]{2,1,0:T(8,128)} %bitcast.19), channel_id=1, source_target_pairs={{0,2},{1,3},{2,0},{3,1},{4,6},{5,7},{6,4},{7,5},{8,10},{9,11},{10,... | collective-permute-start | bytes 294920 | tf_op jit(solution)/shard_map/ppermute | solution.py:160
  5.6 8.4 %collective-permute-start = (f32[3,32,256]{2,1,0:T(8,128)}, f32[3,32,256]{2,1,0:T(8,128)S(1)}, u32[]{:S(2)}, u32[]{:S(2)}) collective-permute-start(f32[3,32,256]{2,1,0:T(8,128)} %bitcast.20), channel_id=1, source_target_pairs={{0,3},{1,2},{2,1},{3,0},{4,7},{5,6},{6,5},{7,4},{8,11},{9,10},{10,... | collective-permute-start | bytes 294920 | tf_op jit(solution)/shard_map/ppermute | solution.py:160
  7.1 7.8 %collective-permute-start.5 = (f32[128,128]{1,0:T(8,128)S(1)}, f32[128,128]{1,0:T(8,128)S(1)}, u32[]{:S(2)}, u32[]{:S(2)}) collective-permute-start(f32[128,128]{1,0:T(8,128)S(1)} %get-tuple-element.19), channel_id=1, source_target_pairs={{0,24},{4,28},{8,16},{12,20},{16,8},{20,12},{24,0},{28,4},{1,25},{... | collective-permute-start | bytes 196616 | tf_op jit(solution)/shard_map/ppermute | solution.py:187
  9.8 5.2 %collective-permute-start.4 = (f32[128,128]{1,0:T(8,128)S(1)}, f32[128,128]{1,0:T(8,128)S(1)}, u32[]{:S(2)}, u32[]{:S(2)}) collective-permute-start(f32[128,128]{1,0:T(8,128)S(1)} %get-tuple-element.19), channel_id=1, source_target_pairs={{0,8},{4,12},{8,0},{12,4},{16,24},{20,28},{24,16},{28,20},{1,9},{5... | collective-permute-start | bytes 196616 | tf_op jit(solution)/shard_map/ppermute | solution.py:187
  15.0 1.8 %collective-permute-start.6 = (f32[3,128,256]{2,1,0:T(8,128)S(1)}, f32[3,128,256]{2,1,0:T(8,128)S(1)}, u32[]{:S(2)}, u32[]{:S(2)}) collective-permute-start(f32[3,128,256]{2,1,0:T(8,128)S(1)} %pad_maximum_fusion), channel_id=1, source_target_pairs={{0,4},{4,0},{8,12},{12,8},{16,20},{20,16},{24,28},{28,24},{1,5},{5... | collective-permute-start | bytes 1179656 | tf_op jit(solution)/shard_map/ppermute | solution.py:190
  22.5 0.8 %copy-start.2 = (f32[128,128]{1,0:T(8,128)S(1)}, f32[128,128]{1,0:T(8,128)}, u32[]{:S(2)}) copy-start(f32[128,128]{1,0:T(8,128)} %get-tuple-element.18) | copy-start | bytes 196612
  22.6 0.9 %copy-start.3 = (f32[128,128]{1,0:T(8,128)S(1)}, f32[128,128]{1,0:T(8,128)}, u32[]{:S(2)}) copy-start(f32[128,128]{1,0:T(8,128)} %get-tuple-element.56) | copy-start | bytes 196612
  24.1 0.7 %copy-start = (f32[384,128]{1,0:T(8,128)}, f32[384,128]{1,0:T(8,128)S(1)}, u32[]{:S(2)}) copy-start(f32[384,128]{1,0:T(8,128)S(1)} %fusion.3) | copy-start | bytes 589828
  25.4 7.7 %collective-permute-start.9 = (f32[256,128]{1,0:T(8,128)}, f32[256,128]{1,0:T(8,128)}, u32[]{:S(2)}, u32[]{:S(2)}) collective-permute-start(f32[256,128]{1,0:T(8,128)} %maximum_select_fusion), channel_id=1, source_target_pairs={{0,8},{4,20},{8,0},{12,28},{16,24},{20,4},{24,16},{28,12},{1,9},{5... | collective-permute-start | bytes 393224 | tf_op jit(solution)/shard_map/ppermute | solution.py:187
  26.9 6.1 %collective-permute-start.7 = (f32[128,128]{1,0:T(8,128)S(1)}, f32[128,128]{1,0:T(8,128)}, u32[]{:S(2)}, u32[]{:S(2)}) collective-permute-start(f32[128,128]{1,0:T(8,128)S(1)} %get-tuple-element.32), channel_id=1, source_target_pairs={{0,24},{4,28},{8,16},{12,20},{16,8},{20,12},{24,0},{28,4},{1,25},{... | collective-permute-start | bytes 196616 | tf_op jit(solution)/shard_map/ppermute | solution.py:187
  33.1 1.6 %collective-permute-start.8 = (f32[128,128]{1,0:T(8,128)}, f32[128,128]{1,0:T(8,128)}, u32[]{:S(2)}, u32[]{:S(2)}) collective-permute-start(f32[128,128]{1,0:T(8,128)} %collective-permute-done.7), channel_id=1, source_target_pairs={{0,4},{4,0},{8,12},{12,8},{16,20},{20,16},{24,28},{28,24},{1,5},{5... | collective-permute-start | bytes 196616 | tf_op jit(solution)/shard_map/ppermute | solution.py:190
  33.1 3.9 %copy-start.1 = (f32[384,128]{1,0:T(8,128)S(1)}, f32[384,128]{1,0:T(8,128)}, u32[]{:S(2)}) copy-start(f32[384,128]{1,0:T(8,128)} %copy-done) | copy-start | bytes 589828
  33.1 2.5 %collective-permute-start.10 = (f32[256,128]{1,0:T(8,128)}, f32[256,128]{1,0:T(8,128)S(1)}, u32[]{:S(2)}, u32[]{:S(2)}) collective-permute-start(f32[256,128]{1,0:T(8,128)} %collective-permute-done.9), channel_id=1, source_target_pairs={{0,4},{4,0},{8,12},{12,8},{16,20},{20,16},{24,28},{28,24},{1,5},{5... | collective-permute-start | bytes 393224 | tf_op jit(solution)/shard_map/ppermute | solution.py:190
  38.3 6.7 %collective-permute-start.13 = (f32[256,128]{1,0:T(8,128)S(1)}, f32[256,128]{1,0:T(8,128)S(1)}, u32[]{:S(2)}, u32[]{:S(2)}) collective-permute-start(f32[256,128]{1,0:T(8,128)S(1)} %maximum_select_fusion.1), channel_id=1, source_target_pairs={{0,8},{4,20},{8,0},{12,28},{16,24},{20,4},{24,16},{28,12},{1,9},{5... | collective-permute-start | bytes 393224 | tf_op jit(solution)/shard_map/ppermute | solution.py:187
  39.8 5.2 %collective-permute-start.11 = (f32[128,128]{1,0:T(8,128)S(1)}, f32[128,128]{1,0:T(8,128)S(1)}, u32[]{:S(2)}, u32[]{:S(2)}) collective-permute-start(f32[128,128]{1,0:T(8,128)S(1)} %get-tuple-element.29), channel_id=1, source_target_pairs={{0,24},{4,28},{8,16},{12,20},{16,8},{20,12},{24,0},{28,4},{1,25},{... | collective-permute-start | bytes 196616 | tf_op jit(solution)/shard_map/ppermute | solution.py:187
  45.0 1.3 %collective-permute-start.12 = (f32[128,128]{1,0:T(8,128)S(1)}, f32[128,128]{1,0:T(8,128)S(1)}, u32[]{:S(2)}, u32[]{:S(2)}) collective-permute-start(f32[128,128]{1,0:T(8,128)S(1)} %collective-permute-done.11), channel_id=1, source_target_pairs={{0,4},{4,0},{8,12},{12,8},{16,20},{20,16},{24,28},{28,24},{1,5},{5... | collective-permute-start | bytes 196616 | tf_op jit(solution)/shard_map/ppermute | solution.py:190
  45.0 1.5 %collective-permute-start.14 = (f32[256,128]{1,0:T(8,128)S(1)}, f32[256,128]{1,0:T(8,128)S(1)}, u32[]{:S(2)}, u32[]{:S(2)}) collective-permute-start(f32[256,128]{1,0:T(8,128)S(1)} %collective-permute-done.13), channel_id=1, source_target_pairs={{0,4},{4,0},{8,12},{12,8},{16,20},{20,16},{24,28},{28,24},{1,5},{5... | collective-permute-start | bytes 393224 | tf_op jit(solution)/shard_map/ppermute | solution.py:190
  48.2 7.1 %collective-permute-start.17 = (f32[256,128]{1,0:T(8,128)S(1)}, f32[256,128]{1,0:T(8,128)S(1)}, u32[]{:S(2)}, u32[]{:S(2)}) collective-permute-start(f32[256,128]{1,0:T(8,128)S(1)} %pad_maximum_fusion.4), channel_id=1, source_target_pairs={{0,8},{4,20},{8,0},{12,28},{16,24},{20,4},{24,16},{28,12},{1,9},{5... | collective-permute-start | bytes 393224 | tf_op jit(solution)/shard_map/ppermute | solution.py:187
  49.5 5.8 %collective-permute-start.15 = (f32[128,128]{1,0:T(8,128)S(1)}, f32[128,128]{1,0:T(8,128)S(1)}, u32[]{:S(2)}, u32[]{:S(2)}) collective-permute-start(f32[128,128]{1,0:T(8,128)S(1)} %get-tuple-element.26), channel_id=1, source_target_pairs={{0,24},{4,28},{8,16},{12,20},{16,8},{20,12},{24,0},{28,4},{1,25},{... | collective-permute-start | bytes 196616 | tf_op jit(solution)/shard_map/ppermute | solution.py:187
  55.3 1.3 %collective-permute-start.16 = (f32[128,128]{1,0:T(8,128)S(1)}, f32[128,128]{1,0:T(8,128)S(1)}, u32[]{:S(2)}, u32[]{:S(2)}) collective-permute-start(f32[128,128]{1,0:T(8,128)S(1)} %collective-permute-done.15), channel_id=1, source_target_pairs={{0,4},{4,0},{8,12},{12,8},{16,20},{20,16},{24,28},{28,24},{1,5},{5... | collective-permute-start | bytes 196616 | tf_op jit(solution)/shard_map/ppermute | solution.py:190
  55.3 1.5 %collective-permute-start.18 = (f32[256,128]{1,0:T(8,128)S(1)}, f32[256,128]{1,0:T(8,128)S(1)}, u32[]{:S(2)}, u32[]{:S(2)}) collective-permute-start(f32[256,128]{1,0:T(8,128)S(1)} %collective-permute-done.17), channel_id=1, source_target_pairs={{0,4},{4,0},{8,12},{12,8},{16,20},{20,16},{24,28},{28,24},{1,5},{5... | collective-permute-start | bytes 393224 | tf_op jit(solution)/shard_map/ppermute | solution.py:190

commit v3 on v2

v3 whole, which is shorter than its diff:
```python
import functools
import jax
import jax.numpy as jnp
from jax import lax
from jax.experimental import pallas as pl
from jax.experimental.pallas import tpu as pltpu
from jax.sharding import PartitionSpec as P

PAIR = 2
F32, BF16 = jnp.float32, jnp.bfloat16
NN = ((1,), (0,))
NT = ((1,), (1,))
TN = ((0,), (0,))


def halves(value):
    high = value.astype(BF16)
    return high, (value - high.astype(F32)).astype(BF16)


def mm(left, right, dims=NN):
    left = left if isinstance(left, tuple) else halves(left)
    right = right if isinstance(right, tuple) else halves(right)

    (lc,), (rc,) = dims
    return lax.dot_general(
        jnp.concatenate([left[0], left[0], left[1]], lc),
        jnp.concatenate([right[0], right[1], right[0]], rc),
        (dims, ((), ())),
        preferred_element_type=F32,
    )


def same_block(shape, rows_block, cols_block, wrap):
    row = lax.broadcasted_iota(jnp.int32, shape, 0)
    col = lax.broadcasted_iota(jnp.int32, shape, 1)
    return (row // rows_block) == ((col % wrap) // cols_block)


def pair_operators(refl_ref, keep, out_ref):
    _, groups, block, window = refl_ref.shape
    wide = 2 * block
    groups = range(groups)
    firsts, seconds, sfirst, ssecond = [], [], [], []
    col = lax.broadcasted_iota(jnp.int32, (block, window), 1)
    for g in groups:
        a = refl_ref[0, g]
        b = jnp.where(keep | (col < block), refl_ref[1, g], 0.0)
        firsts.append(a)
        seconds.append(b)
        sfirst.append(a * (2.0 / jnp.sum(a * a, 1, keepdims=True)))
        ssecond.append(b * (2.0 / jnp.sum(b * b, 1, keepdims=True)))
    above = lax.broadcasted_iota(jnp.int32, (block, wide), 0) < (
        lax.broadcasted_iota(jnp.int32, (block, wide), 1) % block
    )
    near, cross = [], []
    for g in groups:
        ha = halves(firsts[g])
        gq = mm(ssecond[g], halves(seconds[g]), NT)
        gp = mm(sfirst[g], ha, NT)
        near.append(jnp.where(above, jnp.concatenate([gq, gp], 1), 0.0))
        cross.append(
            mm(ssecond[g][:, :block], (ha[0][:, block:], ha[1][:, block:]), NT)
        )

    def diagonal(value, size):
        mask = same_block((wide, wide), size, size, wide)
        return tuple(
            jnp.where(mask, jnp.concatenate([part] * (wide // size), 0), jnp.zeros((), BF16))
            for part in halves(value)
        )

    def gather_blocks(value, size):
        total = None
        for place in range(block // size):
            part = value[place * size : (place + 1) * size]
            pcol = lax.broadcasted_iota(jnp.int32, part.shape, 1)
            part = jnp.where((pcol % block) // size == place, part, 0.0)
            total = part if total is None else total + part
        return total

    def widen(value, size):
        old = value.shape[0]
        tall = jnp.concatenate([value] * (size // old), 0)
        return jnp.where(same_block(tall.shape, old, old, size), tall, 0.0)

    def quad(result, ring, size):
        across = [mm(r, diagonal(b, size)) for r, b in zip(result, ring)]
        halved = [halves(x) for x in across]
        once = [r - mm(x, diagonal(r, size)) for r, x in zip(result, halved)]
        square = [mm(h, diagonal(x, size)) for h, x in zip(halved, across)]
        return [o + mm(s, diagonal(o, size)) for o, s in zip(once, square)]

    small = [gather_blocks(n, 16) for n in near]
    shape = small[0].shape
    row = lax.broadcasted_iota(jnp.int32, shape, 0)
    scol = lax.broadcasted_iota(jnp.int32, shape, 1)
    eye = jnp.where(row == scol % 16, 1.0, 0.0)
    inner = (row // 4) == (scol % 16) // 4
    tiny = [jnp.where(inner, n, 0.0) for n in small]
    square = [mm(n, diagonal(n, 16)) for n in tiny]
    result = [eye - n for n in tiny]
    result = [r + mm(r, diagonal(s, 16)) for r, s in zip(result, square)]
    result = quad(result, [jnp.where(inner, 0.0, n) for n in small], 16)
    middle = [gather_blocks(n, 64) for n in near]
    mmask = same_block(middle[0].shape, 16, 16, 64)
    result = [widen(r, 64) for r in result]
    result = quad(result, [jnp.where(mmask, 0.0, n) for n in middle], 64)
    result = [widen(r, block) for r in result]
    bmask = same_block((block, wide), 64, 64, block)
    across = [mm(r, diagonal(jnp.where(bmask, 0.0, n), block)) for r, n in zip(result, near)]
    result = [r - mm(x, diagonal(r, block)) for r, x in zip(result, across)]
    for g in groups:
        q, p = halves(result[g][:, :block]), halves(result[g][:, block:])
        link = mm(q, cross[g])
        link = mm(link, p)
        solved_p = mm(p, sfirst[g])
        low = halves(sfirst[g])
        solved_q = mm(q, ssecond[g])
        reach = mm(link, low)
        zero = jnp.zeros((block, block), F32)
        sq = jnp.concatenate([-reach[:, :block], solved_q[:, :block] - reach[:, block:], solved_q[:, block:]], 1)
        sp = jnp.concatenate([solved_p, zero], 1)
        solved = jnp.concatenate([sq, sp], 0)
        joined = jnp.concatenate(
            [
                jnp.concatenate([zero, seconds[g]], 1),
                jnp.concatenate([firsts[g], zero], 1),
            ],
            0,
        )
        moved = mm(joined, solved, TN)
        orow = lax.broadcasted_iota(jnp.int32, moved.shape, 0)
        ocol = lax.broadcasted_iota(jnp.int32, moved.shape, 1)
        out_ref[g] = jnp.where(orow == ocol, 1.0, 0.0) - moved


def payloads(node, core, fixed, lead, near_ref, far_ref):
    block = lead.shape[1]
    up, down = slice(0, block), slice(2 * block, None)
    send_up = (core == 0) & ((node & 1) == 1)
    near_ref[:block] = jnp.where(send_up, fixed[up], fixed[down])
    near_ref[block:] = jnp.where(send_up, lead[up], lead[down])
    low_half = (node & 2) == 0
    far_ref[...] = jnp.where(
        core == 0,
        jnp.where(low_half, fixed[down], fixed[up]),
        jnp.where(low_half, lead[down], lead[up]),
    )


def first_kernel(count, nodes, place_ref, *refs):
    mine, theirs = refs[:count], refs[count : 2 * count]
    own_ref, other_ref, near_ref, far_ref = refs[2 * count : 2 * count + 4]
    oper_ref, fixed_ref, out_near, out_far, refl_ref = refs[2 * count + 4 :]
    block = own_ref.shape[0]
    node, core, vec = place_ref[0], place_ref[1], place_ref[2]
    groups, rows, _ = mine[0].shape
    for step in range(count):
        at = pl.ds(pl.multiple_of((step ^ vec) * rows, rows), rows)
        for group in range(groups):
            refl_ref[core, group, at, :] = mine[step][group]
            refl_ref[1 - core, group, at, :] = theirs[step][group]
    pair_operators(refl_ref, node != nodes - 1, oper_ref)
    own, other = own_ref[...], other_ref[...]
    top = jnp.where(core == 0, own, other)
    low = jnp.where(core == 0, other, own)
    below = jnp.where((node & 1) == 0, near_ref[...], far_ref[...])
    window = jnp.concatenate(
        [
            jnp.where(node == 0, top, 0.0),
            low,
            jnp.where(node == nodes - 1, 0.0, below),
        ],
        0,
    )
    fixed = mm(oper_ref[0], window)
    fixed_ref[...] = fixed
    payloads(node, core, fixed, oper_ref[0, :, :block], out_near, out_far)


def next_kernel(group, place_ref, near_ref, far_ref, near2_ref, far2_ref, fixed_ref, oper_ref, *outs):
    block = far_ref.shape[0]
    node, core = place_ref[0], place_ref[1]
    here = core == 0
    near, near2, far, far2 = near_ref[...], near2_ref[...], far_ref[...], far2_ref[...]
    came1 = jnp.where(here, near, near2)
    came2 = jnp.where(here, near2, near)
    came3 = jnp.where(here, far, far2), jnp.where(here, far2, far)
    odd, high = (node & 1) == 1, (node & 2) == 2
    carry = jnp.where(high, jnp.where(odd, came3[0], came2[:block]), came1[:block])
    carry = jnp.where(node == 0, 0.0, carry)
    step = jnp.where(odd, came2[:block], came3[0]) + mm(
        jnp.where(odd, came2[block:], came3[1]), carry
    )
    carry = jnp.where(high, step, carry)
    step = came1[:block] + mm(came1[block:], carry)
    carry = jnp.where(node == 3, step, carry)
    result = fixed_ref[...] + mm(oper_ref[group, :, :block], carry)
    top, low, out = result[:block], result[block : 2 * block], result[2 * block :]
    if len(outs) == 1:
        outs[0][...] = jnp.where(here, top, low)
        return
    below = jnp.where(odd, came3[0], came1[:block]) + mm(
        jnp.where(odd, came3[1], came1[block:]), out
    )
    window = jnp.concatenate(
        [jnp.where(node == 0, top, 0.0), low, jnp.where(node == 3, 0.0, below)], 0
    )
    fixed = mm(oper_ref[group + 1], window)
    outs[0][...] = fixed
    payloads(node, core, fixed, oper_ref[group + 1, :, :block], outs[1], outs[2])


def call(kernel, outs, operands, scratch=()):
    vmem = pl.BlockSpec(memory_space=pltpu.VMEM)
    return pl.pallas_call(
        kernel,
        out_shape=[jax.ShapeDtypeStruct(shape, F32) for shape in outs],
        in_specs=[pl.BlockSpec(memory_space=pltpu.SMEM)] + [vmem] * (len(operands) - 1),
        out_specs=[vmem] * len(outs),
        scratch_shapes=list(scratch),
        compiler_params=pltpu.CompilerParams(vmem_limit_bytes=16 << 20),
    )(*operands)


def dot(left, right):
    return jnp.matmul(left, right, precision=lax.Precision.HIGHEST)


def spread(value, axis, size):
    if size & (size - 1) or size > 8:
        gathered = lax.all_gather(value, axis)
        return [gathered[place] for place in range(size)], False
    return [value] + [
        lax.ppermute(value, axis, [(place, place ^ mask) for place in range(size)])
        for mask in range(1, size)
    ], True


def many_pairs(fixed, operators, node, nodes, row_count):
    groups, _, block = operators.shape[0], None, operators.shape[1] // 3
    members = [[place * PAIR + core for place in range(nodes)] for core in range(PAIR)]
    for group in range(groups):
        lead = operators[group][:, :block]
        down = jnp.concatenate([fixed[2 * block :], lead[2 * block :]], 0)
        up = jnp.concatenate([fixed[:block], lead[:block]], 0)
        earlier = lax.all_gather(down, "rows", axis_index_groups=members)
        later = lax.ppermute(
            up, "rows", [(place, place - PAIR) for place in range(PAIR, row_count)]
        )
        carry = jnp.zeros((block, fixed.shape[1]), F32)
        for place in range(nodes - 1):
            step = earlier[place, :block] + dot(earlier[place, block:], carry)
            carry = jnp.where(node > place, step, carry)
        result = fixed + dot(lead, carry)
        if group < groups - 1:
            below = later[:block] + dot(later[block:], result[2 * block :])
            window = jnp.concatenate(
                [
                    jnp.where(node == 0, result[:block], 0.0),
                    result[block : 2 * block],
                    jnp.where(node == nodes - 1, 0.0, below),
                ],
                0,
            )
            fixed = dot(operators[group + 1], window)
    return result


def local(vectors, reflectors):
    groups, _, _, window = reflectors.shape
    block = window // 2
    cols = vectors.shape[1]
    row_index = lax.axis_index("rows")
    row_count = lax.axis_size("rows")
    vec_index = lax.axis_index("vecs")
    vec_count = lax.axis_size("vecs")
    nodes = row_count // PAIR
    node = row_index // PAIR
    core = row_index % PAIR

    def swap(value, masks):
        moves = [
            (place, ((place // PAIR) ^ masks[place % PAIR]) * PAIR + place % PAIR)
            for place in range(row_count)
        ]
        return lax.ppermute(value, "rows", moves)

    def across(value):
        return lax.ppermute(value, "rows", [(place, place ^ 1) for place in range(row_count)])

    mine, mixed = spread(reflectors[:, 0], "vecs", vec_count)
    other = across(vectors)
    top = jnp.where(core == 0, vectors, other)
    if nodes == 4:
        below = [swap(top, (1, 1)), swap(top, (3, 3))]
    else:
        below = [
            lax.ppermute(
                top, "rows", [(place, place - PAIR) for place in range(PAIR, row_count)]
            )
        ] * 2
    theirs = [across(piece) for piece in mine]
    place = jnp.stack([node, core, vec_index if mixed else 0]).astype(jnp.int32)
    operators, fixed, near, far = call(
        functools.partial(first_kernel, len(mine), nodes),
        [
            (groups, 3 * block, 3 * block),
            (3 * block, cols),
            (2 * block, cols),
            (block, cols),
        ],
        [place, *mine, *theirs, vectors, other, *below],
        [pltpu.VMEM((PAIR, groups, block, window), F32)],
    )
    if nodes != 4:
        result = many_pairs(fixed, operators, node, nodes, row_count)
        return jnp.where(core == 0, result[:block], result[block : 2 * block])
    for group in range(groups):
        near = swap(near, (1, 2))
        far = swap(far, (3, 3))
        operands = [place, near, far, across(near), across(far), fixed, operators]
        if group < groups - 1:
            fixed, near, far = call(
                functools.partial(next_kernel, group),
                [(3 * block, cols), (2 * block, cols), (block, cols)],
                operands,
            )
        else:
            (result,) = call(
                functools.partial(next_kernel, group), [(block, cols)], operands
            )
    return result


def solution(mesh):
    placed = (P("rows", "vecs"), P(None, "rows", "vecs", None))
    return jax.shard_map(
        local, mesh=mesh, in_specs=placed, out_specs=P("rows", "vecs"), check_vma=False
    )
```

time: 58.5 us -> 54.3 us (0.928)
  Pallas kernels: 5.68 us -> 11.7 us
  other arithmetic: 5.96 us -> 0.93 us
  matrix products: 4.52 us -> 0 us
    pallas_call x1 -> x4, Pallas kernels: 5.68 us -> 11.7 us  [call(): pl.pallas_call(kernel, out_shape=[jax.ShapeDtypeStruct(shape, F32) for sh...]
    select_n x19 -> x1, other arithmetic: 5.84 us -> 0.85 us  [local(): top = jnp.where(core == 0, vectors, other)]
    dot_general x14 -> x0, matrix products: 4.52 us -> none  [dot(): return jnp.matmul(left, right, precision=lax.Precision.HIGHEST)]
    ppermute x8 -> x11, starting transfers between devices: 2.05 us -> 1.04 us  [across(): lax.ppermute(value, 'rows', [(place, place ^ 1) for place in range(row_co...]
    unnamed x8 -> x4, local copies, waits for them, and re-layouts: 1.4 us -> 1.73 us
    ppermute x8 -> x11, waiting for transfers between devices: 4.71 us -> 4.62 us  [across(): lax.ppermute(value, 'rows', [(place, place ^ 1) for place in range(row_co...]
  transfers between devices with their start and end apart: 19 -> 22, of which waited for: 10 -> 12; matrix products, arithmetic and copies ran while one was open for 6% -> 2% of each run, Pallas kernels for 0% -> 0%
where the time goes in v3:
time: 54.3 us; the launch traced here: 54.1 us
  waiting for transfers between devices  21.6 us (40%)
  starting transfers between devices  18.1 us (33%)
  Pallas kernels  11.7 us (22%)
  local copies, waits for them, and re-layouts  1.73 us (3%)
  other arithmetic  0.93 us (2%)
    ppermute x8, waiting for transfers between devices, swap(): return lax.ppermute(value, 'rows', moves)  13 us
    pallas_call x4, Pallas kernels, call(): pl.pallas_call(kernel, out_shape=[jax.ShapeDtypeStruct(shape, F32) for sh...  11.7 us
    ppermute x8, starting transfers between devices, swap(): return lax.ppermute(value, 'rows', moves)  11.4 us
    ppermute x3, starting transfers between devices, spread(): lax.ppermute(value, axis, [(place, place ^ mask) for place in range(size)])  5.62 us
    ppermute x11, waiting for transfers between devices, across(): lax.ppermute(value, 'rows', [(place, place ^ 1) for place in range(row_co...  4.62 us
    ppermute x3, waiting for transfers between devices, spread(): lax.ppermute(value, axis, [(place, place ^ mask) for place in range(size)])  3.95 us
    unnamed x4, local copies, waits for them, and re-layouts  1.73 us
  transfers between devices with their start and end apart: 22, of which 12 were waited for; matrix products, arithmetic and copies ran while one was open for 2% of the time, Pallas kernels for 0%

profile of v3, /device:TPU:0, one launch (start us, length us, event | category | flops | bytes accessed | tf_op | source)
XLA Modules:
  0.0 54.1 jit_solution(11921275277762321856)
XLA Ops:
  0.5 5.0 %collective-permute-start.2 = (f32[3,32,256]{2,1,0:T(8,128)}, f32[3,32,256]{2,1,0:T(8,128)S(1)}, u32[]{:S(2)}, u32[]{:S(2)}) collective-permute-start(f32[3,32,256]{2,1,0:T(8,128)} %bitcast.5), channel_id=1, source_target_pairs={{0,3},{1,2},{2,1},{3,0},{4,7},{5,6},{6,5},{7,4},{8,11},{9,10},{10,... | collective-permute-start | bytes 294920 | tf_op jit(solution)/shard_map/ppermute | solution.py:236
  6.1 0.8 %broadcast_select_fusion = f32[128,128]{1,0:T(8,128)S(1)} fusion(f32[128,128]{1,0:T(8,128)} %refs_8_.1, f32[128,128]{1,0:T(8,128)S(1)} %collective-permute-done.7.refs_9_, pred[]{:T(512)S(6)} %eq.5), kind=kLoop, calls=%fused_computation | loop fusion | flops 16384 | bytes 196609 | tf_op jit(solution)/shard_map/jit(_where)/select_n | solution.py:295
  7.0 2.7 %collective-permute-start.9 = (f32[128,128]{1,0:T(8,128)S(1)}, f32[128,128]{1,0:T(8,128)S(1)}, u32[]{:S(2)}, u32[]{:S(2)}) collective-permute-start(f32[128,128]{1,0:T(8,128)S(1)} %broadcast_select_fusion), channel_id=1, source_target_pairs={{0,24},{4,28},{8,16},{12,20},{16,8},{20,12},{24,0},{28,4},{1,25},{... | collective-permute-start | bytes 196616 | tf_op jit(solution)/shard_map/ppermute | solution.py:288
  10.3 3.9 %collective-permute-done.1.refs_2_ = f32[3,32,256]{2,1,0:T(8,128)S(1)} collective-permute-done((f32[3,32,256]{2,1,0:T(8,128)}, f32[3,32,256]{2,1,0:T(8,128)S(1)}, u32[]{:S(2)}, u32[]{:S(2)}) %collective-permute-start.1) | collective-permute-done | bytes 98336 | tf_op jit(solution)/shard_map/ppermute | solution.py:236
  15.7 0.8 %copy-done = f32[128,128]{1,0:T(8,128)S(1)} copy-done((f32[128,128]{1,0:T(8,128)S(1)}, f32[128,128]{1,0:T(8,128)}, u32[]{:S(2)}) %copy-start) | copy-done | bytes 65560
  16.5 0.9 %copy-done.1 = f32[3,1,32,256]{3,2,1,0:T(8,128)S(1)} copy-done((f32[3,1,32,256]{3,2,1,0:T(8,128)S(1)}, f32[3,1,32,256]{3,2,1,0:T(8,128)}, u32[]{:S(2)}) %copy-start.1) | copy-done | bytes 98328
  17.4 6.3 %shard_map.28 = (f32[3,384,384]{2,1,0:T(8,128)S(1)}, f32[384,128]{1,0:T(8,128)S(1)}, f32[256,128]{1,0:T(8,128)S(1)}, f32[128,128]{1,0:T(8,128)S(1)}) custom-call(s32[3]{0:T(128)S(1)} %pad_add_fusion.place_ref, f32[3,32,256]{2,1,0:T(8,128)S(1)} %bitcast.8, f32[3,32,256]{2,1,0:T(8,128)S(1)} %collective-permute-done.refs_1_, ...), custom_call_target="tpu_custom_call" | custom-call | tf_op jit(solution)/shard_map/pallas_call | solution.py:217
  23.7 1.6 %collective-permute-start.10 = (f32[256,128]{1,0:T(8,128)S(1)}, f32[256,128]{1,0:T(8,128)S(1)}, u32[]{:S(2)}, u32[]{:S(2)}) collective-permute-start(f32[256,128]{1,0:T(8,128)S(1)} %get-tuple-element.15), channel_id=1, source_target_pairs={{0,8},{4,20},{8,0},{12,28},{16,24},{20,4},{24,16},{28,12},{1,9},{5... | collective-permute-start | bytes 393224 | tf_op jit(solution)/shard_map/ppermute | solution.py:288
  25.3 1.5 %collective-permute-start.11 = (f32[128,128]{1,0:T(8,128)S(1)}, f32[128,128]{1,0:T(8,128)S(1)}, u32[]{:S(2)}, u32[]{:S(2)}) collective-permute-start(f32[128,128]{1,0:T(8,128)S(1)} %get-tuple-element.16), channel_id=1, source_target_pairs={{0,24},{4,28},{8,16},{12,20},{16,8},{20,12},{24,0},{28,4},{1,25},{... | collective-permute-start | bytes 196616 | tf_op jit(solution)/shard_map/ppermute | solution.py:288
  26.8 2.7 %collective-permute-done.10.near_ref = f32[256,128]{1,0:T(8,128)S(1)} collective-permute-done((f32[256,128]{1,0:T(8,128)S(1)}, f32[256,128]{1,0:T(8,128)S(1)}, u32[]{:S(2)}, u32[]{:S(2)}) %collective-permute-start.10) | collective-permute-done | bytes 131104 | tf_op jit(solution)/shard_map/ppermute | solution.py:288
  29.5 1.7 %collective-permute-done.11.far_ref = f32[128,128]{1,0:T(8,128)S(1)} collective-permute-done((f32[128,128]{1,0:T(8,128)S(1)}, f32[128,128]{1,0:T(8,128)S(1)}, u32[]{:S(2)}, u32[]{:S(2)}) %collective-permute-start.11) | collective-permute-done | bytes 65568 | tf_op jit(solution)/shard_map/ppermute | solution.py:288
  31.1 1.3 %collective-permute-done.13.far2_ref = f32[128,128]{1,0:T(8,128)S(1)} collective-permute-done((f32[128,128]{1,0:T(8,128)S(1)}, f32[128,128]{1,0:T(8,128)S(1)}, u32[]{:S(2)}, u32[]{:S(2)}) %collective-permute-start.13) | collective-permute-done | bytes 65568 | tf_op jit(solution)/shard_map/ppermute | solution.py:291
  32.4 1.8 %shard_map.29 = (f32[384,128]{1,0:T(8,128)S(1)}, f32[256,128]{1,0:T(8,128)S(1)}, f32[128,128]{1,0:T(8,128)S(1)}) custom-call(s32[3]{0:T(128)S(1)} %pad_add_fusion.place_ref, f32[256,128]{1,0:T(8,128)S(1)} %collective-permute-done.10.near_ref, f32[128,128]{1,0:T(8,128)S(1)} %collective-permute-done.11.far_ref, ...), custom_call_target="tpu_custom_call" | custom-call | tf_op jit(solution)/shard_map/pallas_call | solution.py:217
  34.2 1.6 %collective-permute-start.14 = (f32[256,128]{1,0:T(8,128)S(1)}, f32[256,128]{1,0:T(8,128)S(1)}, u32[]{:S(2)}, u32[]{:S(2)}) collective-permute-start(f32[256,128]{1,0:T(8,128)S(1)} %get-tuple-element.19), channel_id=1, source_target_pairs={{0,8},{4,20},{8,0},{12,28},{16,24},{20,4},{24,16},{28,12},{1,9},{5... | collective-permute-start | bytes 393224 | tf_op jit(solution)/shard_map/ppermute | solution.py:288
  36.6 3.4 %collective-permute-done.14.near_ref = f32[256,128]{1,0:T(8,128)S(1)} collective-permute-done((f32[256,128]{1,0:T(8,128)S(1)}, f32[256,128]{1,0:T(8,128)S(1)}, u32[]{:S(2)}, u32[]{:S(2)}) %collective-permute-start.14) | collective-permute-done | bytes 131104 | tf_op jit(solution)/shard_map/ppermute | solution.py:288
  39.9 1.0 %collective-permute-done.15.far_ref = f32[128,128]{1,0:T(8,128)S(1)} collective-permute-done((f32[128,128]{1,0:T(8,128)S(1)}, f32[128,128]{1,0:T(8,128)S(1)}, u32[]{:S(2)}, u32[]{:S(2)}) %collective-permute-start.15) | collective-permute-done | bytes 65568 | tf_op jit(solution)/shard_map/ppermute | solution.py:288
  40.9 1.3 %collective-permute-done.17.far2_ref = f32[128,128]{1,0:T(8,128)S(1)} collective-permute-done((f32[128,128]{1,0:T(8,128)S(1)}, f32[128,128]{1,0:T(8,128)S(1)}, u32[]{:S(2)}, u32[]{:S(2)}) %collective-permute-start.17) | collective-permute-done | bytes 65568 | tf_op jit(solution)/shard_map/ppermute | solution.py:291
  42.2 1.8 %shard_map.30 = (f32[384,128]{1,0:T(8,128)S(1)}, f32[256,128]{1,0:T(8,128)S(1)}, f32[128,128]{1,0:T(8,128)S(1)}) custom-call(s32[3]{0:T(128)S(1)} %pad_add_fusion.place_ref, f32[256,128]{1,0:T(8,128)S(1)} %collective-permute-done.14.near_ref, f32[128,128]{1,0:T(8,128)S(1)} %collective-permute-done.15.far_ref, ...), custom_call_target="tpu_custom_call" | custom-call | tf_op jit(solution)/shard_map/pallas_call | solution.py:217
  44.0 1.2 %collective-permute-start.18 = (f32[256,128]{1,0:T(8,128)S(1)}, f32[256,128]{1,0:T(8,128)S(1)}, u32[]{:S(2)}, u32[]{:S(2)}) collective-permute-start(f32[256,128]{1,0:T(8,128)S(1)} %get-tuple-element.22), channel_id=1, source_target_pairs={{0,8},{4,20},{8,0},{12,28},{16,24},{20,4},{24,16},{28,12},{1,9},{5... | collective-permute-start | bytes 393224 | tf_op jit(solution)/shard_map/ppermute | solution.py:288
  45.2 1.5 %collective-permute-start.19 = (f32[128,128]{1,0:T(8,128)S(1)}, f32[128,128]{1,0:T(8,128)S(1)}, u32[]{:S(2)}, u32[]{:S(2)}) collective-permute-start(f32[128,128]{1,0:T(8,128)S(1)} %get-tuple-element.23), channel_id=1, source_target_pairs={{0,24},{4,28},{8,16},{12,20},{16,8},{20,12},{24,0},{28,4},{1,25},{... | collective-permute-start | bytes 196616 | tf_op jit(solution)/shard_map/ppermute | solution.py:288
  46.7 3.0 %collective-permute-done.18.near_ref = f32[256,128]{1,0:T(8,128)S(1)} collective-permute-done((f32[256,128]{1,0:T(8,128)S(1)}, f32[256,128]{1,0:T(8,128)S(1)}, u32[]{:S(2)}, u32[]{:S(2)}) %collective-permute-start.18) | collective-permute-done | bytes 131104 | tf_op jit(solution)/shard_map/ppermute | solution.py:288
  49.7 1.3 %collective-permute-done.19.far_ref = f32[128,128]{1,0:T(8,128)S(1)} collective-permute-done((f32[128,128]{1,0:T(8,128)S(1)}, f32[128,128]{1,0:T(8,128)S(1)}, u32[]{:S(2)}, u32[]{:S(2)}) %collective-permute-start.19) | collective-permute-done | bytes 65568 | tf_op jit(solution)/shard_map/ppermute | solution.py:288
  51.1 1.3 %collective-permute-done.21.far2_ref = f32[128,128]{1,0:T(8,128)S(1)} collective-permute-done((f32[128,128]{1,0:T(8,128)S(1)}, f32[128,128]{1,0:T(8,128)S(1)}, u32[]{:S(2)}, u32[]{:S(2)}) %collective-permute-start.21) | collective-permute-done | bytes 65568 | tf_op jit(solution)/shard_map/ppermute | solution.py:291
  52.3 1.7 %shard_map.31 = f32[128,128]{1,0:T(8,128)} custom-call(s32[3]{0:T(128)S(1)} %pad_add_fusion.place_ref, f32[256,128]{1,0:T(8,128)S(1)} %collective-permute-done.18.near_ref, f32[128,128]{1,0:T(8,128)S(1)} %collective-permute-done.19.far_ref, f32[256,128]{1,0:T(8,128)S(1)} %collective-permute-done.20.near2_ref, ...), custom_call_target="tpu_custom_call" | custom-call | tf_op jit(solution)/shard_map/pallas_call | solution.py:217
  (30 shorter events, 3.9 us)
Async XLA Ops:
  0.0 6.1 %collective-permute-start.7 = (f32[128,128]{1,0:T(8,128)}, f32[128,128]{1,0:T(8,128)S(1)}, u32[]{:S(2)}, u32[]{:S(2)}) collective-permute-start(f32[128,128]{1,0:T(8,128)} %refs_8_.1), channel_id=1, source_target_pairs={{0,4},{4,0},{8,12},{12,8},{16,20},{20,16},{24,28},{28,24},{1,5},{5... | collective-permute-start | bytes 196616 | tf_op jit(solution)/shard_map/ppermute | solution.py:291
  0.5 9.3 %collective-permute-start.3 = (f32[3,32,256]{2,1,0:T(8,128)}, f32[3,32,256]{2,1,0:T(8,128)S(1)}, u32[]{:S(2)}, u32[]{:S(2)}) collective-permute-start(f32[3,32,256]{2,1,0:T(8,128)} %bitcast.4), channel_id=1, source_target_pairs={{0,4},{4,0},{8,12},{12,8},{16,20},{20,16},{24,28},{28,24},{1,5},{5... | collective-permute-start | bytes 294920 | tf_op jit(solution)/shard_map/ppermute | solution.py:291
  0.5 9.7 %collective-permute-start.2 = (f32[3,32,256]{2,1,0:T(8,128)}, f32[3,32,256]{2,1,0:T(8,128)S(1)}, u32[]{:S(2)}, u32[]{:S(2)}) collective-permute-start(f32[3,32,256]{2,1,0:T(8,128)} %bitcast.5), channel_id=1, source_target_pairs={{0,3},{1,2},{2,1},{3,0},{4,7},{5,6},{6,5},{7,4},{8,11},{9,10},{10,... | collective-permute-start | bytes 294920 | tf_op jit(solution)/shard_map/ppermute | solution.py:236
  5.6 8.6 %collective-permute-start.1 = (f32[3,32,256]{2,1,0:T(8,128)}, f32[3,32,256]{2,1,0:T(8,128)S(1)}, u32[]{:S(2)}, u32[]{:S(2)}) collective-permute-start(f32[3,32,256]{2,1,0:T(8,128)} %bitcast.6), channel_id=1, source_target_pairs={{0,2},{1,3},{2,0},{3,1},{4,6},{5,7},{6,4},{7,5},{8,10},{9,11},{10,... | collective-permute-start | bytes 294920 | tf_op jit(solution)/shard_map/ppermute | solution.py:236
  5.6 8.6 %collective-permute-start = (f32[3,32,256]{2,1,0:T(8,128)}, f32[3,32,256]{2,1,0:T(8,128)S(1)}, u32[]{:S(2)}, u32[]{:S(2)}) collective-permute-start(f32[3,32,256]{2,1,0:T(8,128)} %bitcast.7), channel_id=1, source_target_pairs={{0,1},{1,0},{2,3},{3,2},{4,5},{5,4},{6,7},{7,6},{8,9},{9,8},{10,11... | collective-permute-start | bytes 294920 | tf_op jit(solution)/shard_map/ppermute | solution.py:236
  7.0 7.8 %collective-permute-start.9 = (f32[128,128]{1,0:T(8,128)S(1)}, f32[128,128]{1,0:T(8,128)S(1)}, u32[]{:S(2)}, u32[]{:S(2)}) collective-permute-start(f32[128,128]{1,0:T(8,128)S(1)} %broadcast_select_fusion), channel_id=1, source_target_pairs={{0,24},{4,28},{8,16},{12,20},{16,8},{20,12},{24,0},{28,4},{1,25},{... | collective-permute-start | bytes 196616 | tf_op jit(solution)/shard_map/ppermute | solution.py:288
  9.7 5.1 %collective-permute-start.8 = (f32[128,128]{1,0:T(8,128)S(1)}, f32[128,128]{1,0:T(8,128)S(1)}, u32[]{:S(2)}, u32[]{:S(2)}) collective-permute-start(f32[128,128]{1,0:T(8,128)S(1)} %broadcast_select_fusion), channel_id=1, source_target_pairs={{0,8},{4,12},{8,0},{12,4},{16,24},{20,28},{24,16},{28,20},{1,9},{5... | collective-permute-start | bytes 196616 | tf_op jit(solution)/shard_map/ppermute | solution.py:288
  10.3 4.6 %collective-permute-start.6 = (f32[3,32,256]{2,1,0:T(8,128)S(1)}, f32[3,32,256]{2,1,0:T(8,128)S(1)}, u32[]{:S(2)}, u32[]{:S(2)}) collective-permute-start(f32[3,32,256]{2,1,0:T(8,128)S(1)} %collective-permute-done.2.refs_3_), channel_id=1, source_target_pairs={{0,4},{4,0},{8,12},{12,8},{16,20},{20,16},{24,28},{28,24},{1,5},{5... | collective-permute-start | bytes 294920 | tf_op jit(solution)/shard_map/ppermute | solution.py:291
  14.2 1.3 %collective-permute-start.5 = (f32[3,32,256]{2,1,0:T(8,128)S(1)}, f32[3,32,256]{2,1,0:T(8,128)S(1)}, u32[]{:S(2)}, u32[]{:S(2)}) collective-permute-start(f32[3,32,256]{2,1,0:T(8,128)S(1)} %collective-permute-done.1.refs_2_), channel_id=1, source_target_pairs={{0,4},{4,0},{8,12},{12,8},{16,20},{20,16},{24,28},{28,24},{1,5},{5... | collective-permute-start | bytes 294920 | tf_op jit(solution)/shard_map/ppermute | solution.py:291
  14.2 1.5 %collective-permute-start.4 = (f32[3,32,256]{2,1,0:T(8,128)S(1)}, f32[3,32,256]{2,1,0:T(8,128)S(1)}, u32[]{:S(2)}, u32[]{:S(2)}) collective-permute-start(f32[3,32,256]{2,1,0:T(8,128)S(1)} %collective-permute-done.refs_1_), channel_id=1, source_target_pairs={{0,4},{4,0},{8,12},{12,8},{16,20},{20,16},{24,28},{28,24},{1,5},{5... | collective-permute-start | bytes 294920 | tf_op jit(solution)/shard_map/ppermute | solution.py:291
  15.7 0.8 %copy-start = (f32[128,128]{1,0:T(8,128)S(1)}, f32[128,128]{1,0:T(8,128)}, u32[]{:S(2)}) copy-start(f32[128,128]{1,0:T(8,128)} %refs_8_.1) | copy-start | bytes 196612
  16.5 0.9 %copy-start.1 = (f32[3,1,32,256]{3,2,1,0:T(8,128)S(1)}, f32[3,1,32,256]{3,2,1,0:T(8,128)}, u32[]{:S(2)}) copy-start(f32[3,1,32,256]{3,2,1,0:T(8,128)} %param.3) | copy-start | bytes 294916
  23.7 5.7 %collective-permute-start.10 = (f32[256,128]{1,0:T(8,128)S(1)}, f32[256,128]{1,0:T(8,128)S(1)}, u32[]{:S(2)}, u32[]{:S(2)}) collective-permute-start(f32[256,128]{1,0:T(8,128)S(1)} %get-tuple-element.15), channel_id=1, source_target_pairs={{0,8},{4,20},{8,0},{12,28},{16,24},{20,4},{24,16},{28,12},{1,9},{5... | collective-permute-start | bytes 393224 | tf_op jit(solution)/shard_map/ppermute | solution.py:288
  25.3 5.8 %collective-permute-start.11 = (f32[128,128]{1,0:T(8,128)S(1)}, f32[128,128]{1,0:T(8,128)S(1)}, u32[]{:S(2)}, u32[]{:S(2)}) collective-permute-start(f32[128,128]{1,0:T(8,128)S(1)} %get-tuple-element.16), channel_id=1, source_target_pairs={{0,24},{4,28},{8,16},{12,20},{16,8},{20,12},{24,0},{28,4},{1,25},{... | collective-permute-start | bytes 196616 | tf_op jit(solution)/shard_map/ppermute | solution.py:288
  29.5 2.9 %collective-permute-start.12 = (f32[256,128]{1,0:T(8,128)S(1)}, f32[256,128]{1,0:T(8,128)S(1)}, u32[]{:S(2)}, u32[]{:S(2)}) collective-permute-start(f32[256,128]{1,0:T(8,128)S(1)} %collective-permute-done.10.near_ref), channel_id=1, source_target_pairs={{0,4},{4,0},{8,12},{12,8},{16,20},{20,16},{24,28},{28,24},{1,5},{5... | collective-permute-start | bytes 393224 | tf_op jit(solution)/shard_map/ppermute | solution.py:291
  31.1 1.3 %collective-permute-start.13 = (f32[128,128]{1,0:T(8,128)S(1)}, f32[128,128]{1,0:T(8,128)S(1)}, u32[]{:S(2)}, u32[]{:S(2)}) collective-permute-start(f32[128,128]{1,0:T(8,128)S(1)} %collective-permute-done.11.far_ref), channel_id=1, source_target_pairs={{0,4},{4,0},{8,12},{12,8},{16,20},{20,16},{24,28},{28,24},{1,5},{5... | collective-permute-start | bytes 196616 | tf_op jit(solution)/shard_map/ppermute | solution.py:291
  34.2 5.7 %collective-permute-start.14 = (f32[256,128]{1,0:T(8,128)S(1)}, f32[256,128]{1,0:T(8,128)S(1)}, u32[]{:S(2)}, u32[]{:S(2)}) collective-permute-start(f32[256,128]{1,0:T(8,128)S(1)} %get-tuple-element.19), channel_id=1, source_target_pairs={{0,8},{4,20},{8,0},{12,28},{16,24},{20,4},{24,16},{28,12},{1,9},{5... | collective-permute-start | bytes 393224 | tf_op jit(solution)/shard_map/ppermute | solution.py:288
  35.8 5.2 %collective-permute-start.15 = (f32[128,128]{1,0:T(8,128)S(1)}, f32[128,128]{1,0:T(8,128)S(1)}, u32[]{:S(2)}, u32[]{:S(2)}) collective-permute-start(f32[128,128]{1,0:T(8,128)S(1)} %get-tuple-element.20), channel_id=1, source_target_pairs={{0,24},{4,28},{8,16},{12,20},{16,8},{20,12},{24,0},{28,4},{1,25},{... | collective-permute-start | bytes 196616 | tf_op jit(solution)/shard_map/ppermute | solution.py:288
  39.9 2.2 %collective-permute-start.16 = (f32[256,128]{1,0:T(8,128)S(1)}, f32[256,128]{1,0:T(8,128)S(1)}, u32[]{:S(2)}, u32[]{:S(2)}) collective-permute-start(f32[256,128]{1,0:T(8,128)S(1)} %collective-permute-done.14.near_ref), channel_id=1, source_target_pairs={{0,4},{4,0},{8,12},{12,8},{16,20},{20,16},{24,28},{28,24},{1,5},{5... | collective-permute-start | bytes 393224 | tf_op jit(solution)/shard_map/ppermute | solution.py:291
  40.9 1.3 %collective-permute-start.17 = (f32[128,128]{1,0:T(8,128)S(1)}, f32[128,128]{1,0:T(8,128)S(1)}, u32[]{:S(2)}, u32[]{:S(2)}) collective-permute-start(f32[128,128]{1,0:T(8,128)S(1)} %collective-permute-done.15.far_ref), channel_id=1, source_target_pairs={{0,4},{4,0},{8,12},{12,8},{16,20},{20,16},{24,28},{28,24},{1,5},{5... | collective-permute-start | bytes 196616 | tf_op jit(solution)/shard_map/ppermute | solution.py:291
  44.0 5.7 %collective-permute-start.18 = (f32[256,128]{1,0:T(8,128)S(1)}, f32[256,128]{1,0:T(8,128)S(1)}, u32[]{:S(2)}, u32[]{:S(2)}) collective-permute-start(f32[256,128]{1,0:T(8,128)S(1)} %get-tuple-element.22), channel_id=1, source_target_pairs={{0,8},{4,20},{8,0},{12,28},{16,24},{20,4},{24,16},{28,12},{1,9},{5... | collective-permute-start | bytes 393224 | tf_op jit(solution)/shard_map/ppermute | solution.py:288
  45.2 5.8 %collective-permute-start.19 = (f32[128,128]{1,0:T(8,128)S(1)}, f32[128,128]{1,0:T(8,128)S(1)}, u32[]{:S(2)}, u32[]{:S(2)}) collective-permute-start(f32[128,128]{1,0:T(8,128)S(1)} %get-tuple-element.23), channel_id=1, source_target_pairs={{0,24},{4,28},{8,16},{12,20},{16,8},{20,12},{24,0},{28,4},{1,25},{... | collective-permute-start | bytes 196616 | tf_op jit(solution)/shard_map/ppermute | solution.py:288
  49.7 2.6 %collective-permute-start.20 = (f32[256,128]{1,0:T(8,128)S(1)}, f32[256,128]{1,0:T(8,128)S(1)}, u32[]{:S(2)}, u32[]{:S(2)}) collective-permute-start(f32[256,128]{1,0:T(8,128)S(1)} %collective-permute-done.18.near_ref), channel_id=1, source_target_pairs={{0,4},{4,0},{8,12},{12,8},{16,20},{20,16},{24,28},{28,24},{1,5},{5... | collective-permute-start | bytes 393224 | tf_op jit(solution)/shard_map/ppermute | solution.py:291
  51.1 1.3 %collective-permute-start.21 = (f32[128,128]{1,0:T(8,128)S(1)}, f32[128,128]{1,0:T(8,128)S(1)}, u32[]{:S(2)}, u32[]{:S(2)}) collective-permute-start(f32[128,128]{1,0:T(8,128)S(1)} %collective-permute-done.19.far_ref), channel_id=1, source_target_pairs={{0,4},{4,0},{8,12},{12,8},{16,20},{20,16},{24,28},{28,24},{1,5},{5... | collective-permute-start | bytes 196616 | tf_op jit(solution)/shard_map/ppermute | solution.py:291

commit v4 on v3

--- a/solution.py
+++ b/solution.py
@@ -135,84 +135,128 @@
         out_ref[g] = jnp.where(orow == ocol, 1.0, 0.0) - moved
 
 
-def payloads(node, core, fixed, lead, near_ref, far_ref):
-    block = lead.shape[1]
-    up, down = slice(0, block), slice(2 * block, None)
+def pick_near(node, core, value):
+    block = value.shape[0] // 3
     send_up = (core == 0) & ((node & 1) == 1)
-    near_ref[:block] = jnp.where(send_up, fixed[up], fixed[down])
-    near_ref[block:] = jnp.where(send_up, lead[up], lead[down])
-    low_half = (node & 2) == 0
-    far_ref[...] = jnp.where(
-        core == 0,
-        jnp.where(low_half, fixed[down], fixed[up]),
-        jnp.where(low_half, lead[down], lead[up]),
-    )
+    return jnp.where(send_up, value[:block], value[2 * block :])
+
+
+def pick_far(node, value):
+    block = value.shape[0] // 3
+    return jnp.where((node & 2) == 0, value[2 * block :], value[:block])
+
+
+def half_of(core, value):
+    rows = value.shape[0] // PAIR
+    return jnp.where(core == 0, value[:rows], value[rows:])
+
+
+def assemble(place_ref, mine, theirs, groups, refl_ref):
+    core, vec = place_ref[1], place_ref[2]
+    rows = mine[0].shape[1]
+    for step, (own, other) in enumerate(zip(mine, theirs)):
+        at = pl.ds(pl.multiple_of((step ^ vec) * rows, rows), rows)
+        for slot, group in enumerate(groups):
+            refl_ref[core, slot, at, :] = own[group]
+            refl_ref[1 - core, slot, at, :] = other[group]
 
 
 def first_kernel(count, nodes, place_ref, *refs):
     mine, theirs = refs[:count], refs[count : 2 * count]
-    own_ref, other_ref, near_ref, far_ref = refs[2 * count : 2 * count + 4]
+    top_ref, low_ref, near_ref, far_ref = refs[2 * count : 2 * count + 4]
     oper_ref, fixed_ref, out_near, out_far, refl_ref = refs[2 * count + 4 :]
-    block = own_ref.shape[0]
-    node, core, vec = place_ref[0], place_ref[1], place_ref[2]
-    groups, rows, _ = mine[0].shape
-    for step in range(count):
-        at = pl.ds(pl.multiple_of((step ^ vec) * rows, rows), rows)
-        for group in range(groups):
-            refl_ref[core, group, at, :] = mine[step][group]
-            refl_ref[1 - core, group, at, :] = theirs[step][group]
+    block = top_ref.shape[0]
+    node, core = place_ref[0], place_ref[1]
+    assemble(place_ref, mine, theirs, [0], refl_ref)
     pair_operators(refl_ref, node != nodes - 1, oper_ref)
-    own, other = own_ref[...], other_ref[...]
-    top = jnp.where(core == 0, own, other)
-    low = jnp.where(core == 0, other, own)
     below = jnp.where((node & 1) == 0, near_ref[...], far_ref[...])
     window = jnp.concatenate(
         [
-            jnp.where(node == 0, top, 0.0),
-            low,
+            jnp.where(node == 0, top_ref[...], 0.0),
+            low_ref[...],
             jnp.where(node == nodes - 1, 0.0, below),
         ],
         0,
     )
     fixed = mm(oper_ref[0], window)
     fixed_ref[...] = fixed
-    payloads(node, core, fixed, oper_ref[0, :, :block], out_near, out_far)
-
-
-def next_kernel(group, place_ref, near_ref, far_ref, near2_ref, far2_ref, fixed_ref, oper_ref, *outs):
-    block = far_ref.shape[0]
+    lead = oper_ref[0, :, :block]
+    out_near[:block] = pick_near(node, core, fixed)
+    out_near[block:] = pick_near(node, core, lead)
+    out_far[...] = jnp.where(core == 0, pick_far(node, fixed), pick_far(node, lead))
+
+
+def later_kernel(count, nodes, place_ref, *refs):
+    mine, theirs = refs[:count], refs[count : 2 * count]
+    oper_ref, map_near, map_far, refl_ref = refs[2 * count :]
+    node, core = place_ref[0], place_ref[1]
+    later, _, size = oper_ref.shape
+    assemble(place_ref, mine, theirs, range(1, 1 + later), refl_ref)
+    pair_operators(refl_ref, node != nodes - 1, oper_ref)
+    leads = [oper_ref[slot, :, : size // 3] for slot in range(later)]
+    map_near[...] = jnp.concatenate([pick_near(node, core, lead) for lead in leads], 0)
+    map_far[...] = half_of(core, jnp.concatenate([pick_far(node, lead) for lead in leads], 0))
+
+
+def next_kernel(group, place_ref, *refs):
+    (near_ref, far_ref, near2_ref, far2_ref), refs = refs[:4], refs[4:]
     node, core = place_ref[0], place_ref[1]
     here = core == 0
+    odd, high = (node & 1) == 1, (node & 2) == 2
     near, near2, far, far2 = near_ref[...], near2_ref[...], far_ref[...], far2_ref[...]
     came1 = jnp.where(here, near, near2)
     came2 = jnp.where(here, near2, near)
-    came3 = jnp.where(here, far, far2), jnp.where(here, far2, far)
-    odd, high = (node & 1) == 1, (node & 2) == 2
-    carry = jnp.where(high, jnp.where(odd, came3[0], came2[:block]), came1[:block])
+    came3 = jnp.concatenate([jnp.where(here, far, far2), jnp.where(here, far2, far)], 0)
+    if group == 0:
+        block = came1.shape[0] // 2
+        map1, map2, map3 = came1[block:], came2[block:], came3[block:]
+        came1, came2, came3 = came1[:block], came2[:block], came3[:block]
+    else:
+        (mnear_ref, mfar_ref, mnear2_ref, mfar2_ref), refs = refs[:4], refs[4:]
+        block = came1.shape[0]
+        at = slice((group - 1) * block, group * block)
+        map1 = jnp.where(here, mnear_ref[at], mnear2_ref[at])
+        map2 = jnp.where(here, mnear2_ref[at], mnear_ref[at])
+        mfar, mfar2 = mfar_ref[...], mfar2_ref[...]
+        map3 = jnp.concatenate(
+            [jnp.where(here, mfar, mfar2), jnp.where(here, mfar2, mfar)], 0
+        )[at]
+    (fixed_ref, first_ref, later_ref), outs = refs[:3], refs[3:]
+    oper = first_ref.at[0] if group == 0 else later_ref.at[group - 1]
+    carry = jnp.where(high, jnp.where(odd, came3, came2), came1)
     carry = jnp.where(node == 0, 0.0, carry)
-    step = jnp.where(odd, came2[:block], came3[0]) + mm(
-        jnp.where(odd, came2[block:], came3[1]), carry
-    )
+    step = jnp.where(odd, came2, came3) + mm(jnp.where(odd, map2, map3), carry)
     carry = jnp.where(high, step, carry)
-    step = came1[:block] + mm(came1[block:], carry)
+    step = came1 + mm(map1, carry)
     carry = jnp.where(node == 3, step, carry)
-    result = fixed_ref[...] + mm(oper_ref[group, :, :block], carry)
-    top, low, out = result[:block], result[block : 2 * block], result[2 * block :]
     if len(outs) == 1:
-        outs[0][...] = jnp.where(here, top, low)
+        at = pl.ds(pl.multiple_of(core * block, block), block)
+        outs[0][...] = fixed_ref[at, :] + mm(oper[at, :block], carry)
         return
-    below = jnp.where(odd, came3[0], came1[:block]) + mm(
-        jnp.where(odd, came3[1], came1[block:]), out
-    )
+    fixed, lead = fixed_ref[...], oper[:, :block]
+    cols = fixed.shape[1]
+    below = mm(
+        jnp.where(odd, map3, map1), jnp.concatenate([fixed[2 * block :], lead[2 * block :]], 1)
+    )
+    offset = jnp.where(odd, came3, came1)
+    below = jnp.where(node == 3, 0.0, below + jnp.concatenate([offset, jnp.zeros_like(lead[:block])], 1))
+    first = jnp.where(node == 0, fixed[:block], 0.0)
     window = jnp.concatenate(
-        [jnp.where(node == 0, top, 0.0), low, jnp.where(node == 3, 0.0, below)], 0
-    )
-    fixed = mm(oper_ref[group + 1], window)
+        [
+            jnp.concatenate([first, jnp.zeros_like(lead[:block])], 1),
+            jnp.concatenate([fixed[block : 2 * block], lead[block : 2 * block]], 1),
+            below,
+        ],
+        0,
+    )
+    moved = mm(later_ref[group], window)
+    fixed = moved[:, :cols] + mm(moved[:, cols:], carry)
     outs[0][...] = fixed
-    payloads(node, core, fixed, oper_ref[group + 1, :, :block], outs[1], outs[2])
-
-
-def call(kernel, outs, operands, scratch=()):
+    outs[1][...] = pick_near(node, core, fixed)
+    outs[2][...] = half_of(core, pick_far(node, fixed))
+
+
+def call(kernel, outs, operands, scratch=(), work=0):
     vmem = pl.BlockSpec(memory_space=pltpu.VMEM)
     return pl.pallas_call(
         kernel,
@@ -220,6 +264,7 @@
         in_specs=[pl.BlockSpec(memory_space=pltpu.SMEM)] + [vmem] * (len(operands) - 1),
         out_specs=[vmem] * len(outs),
         scratch_shapes=list(scratch),
+        cost_estimate=pl.CostEstimate(flops=work, bytes_accessed=0, transcendentals=0),
         compiler_params=pltpu.CompilerParams(vmem_limit_bytes=16 << 20),
     )(*operands)
 
@@ -239,7 +284,7 @@
 
 
 def many_pairs(fixed, operators, node, nodes, row_count):
-    groups, _, block = operators.shape[0], None, operators.shape[1] // 3
+    groups, block = len(operators), fixed.shape[0] // 3
     members = [[place * PAIR + core for place in range(nodes)] for core in range(PAIR)]
     for group in range(groups):
         lead = operators[group][:, :block]
@@ -293,6 +338,7 @@
     mine, mixed = spread(reflectors[:, 0], "vecs", vec_count)
     other = across(vectors)
     top = jnp.where(core == 0, vectors, other)
+    low = jnp.where(core == 0, other, vectors)
     if nodes == 4:
         below = [swap(top, (1, 1)), swap(top, (3, 3))]
     else:
@@ -302,29 +348,54 @@
             )
         ] * 2
     theirs = [across(piece) for piece in mine]
+    mine[0] = jnp.where(vec_index < 0, 0.0, mine[0])
     place = jnp.stack([node, core, vec_index if mixed else 0]).astype(jnp.int32)
-    operators, fixed, near, far = call(
+    later = groups - 1
+    work = 16 * (3 * block) ** 3
+    pieces = [place, *mine, *theirs]
+    first_oper, fixed, near, far = call(
         functools.partial(first_kernel, len(mine), nodes),
         [
-            (groups, 3 * block, 3 * block),
+            (1, 3 * block, 3 * block),
             (3 * block, cols),
             (2 * block, cols),
             (block, cols),
         ],
-        [place, *mine, *theirs, vectors, other, *below],
-        [pltpu.VMEM((PAIR, groups, block, window), F32)],
+        [*pieces, top, low, *below],
+        [pltpu.VMEM((PAIR, 1, block, window), F32)],
+        work,
+    )
+    later_oper, *maps = call(
+        functools.partial(later_kernel, len(mine), nodes),
+        [
+            (later, 3 * block, 3 * block),
+            (later * block, block),
+            (later * block // PAIR, block),
+        ],
+        pieces,
+        [pltpu.VMEM((PAIR, later, block, window), F32)],
+        work * later,
     )
     if nodes != 4:
+        operators = [first_oper[0]] + [later_oper[slot] for slot in range(later)]
         result = many_pairs(fixed, operators, node, nodes, row_count)
         return jnp.where(core == 0, result[:block], result[block : 2 * block])
+    hold = lax.optimization_barrier
     for group in range(groups):
         near = swap(near, (1, 2))
         far = swap(far, (3, 3))
-        operands = [place, near, far, across(near), across(far), fixed, operators]
+        if group == 0:
+            near, *maps = hold((near, *maps))
+            maps = [swap(maps[0], (1, 2)), swap(maps[1], (3, 3))]
+        elif group == 1:
+            far, *maps = hold((far, *maps))
+            maps += [across(part) for part in maps]
+        came = [near, far, across(near), across(far)]
+        operands = [place, *came, *(maps if group else []), fixed, first_oper, later_oper]
         if group < groups - 1:
             fixed, near, far = call(
                 functools.partial(next_kernel, group),
-                [(3 * block, cols), (2 * block, cols), (block, cols)],
+                [(3 * block, cols), (block, cols), (block // PAIR, cols)],
                 operands,
             )
         else:

time: 54.3 us -> 49.9 us (0.919)
  waiting for transfers between devices: 21.6 us -> 12.2 us
  starting transfers between devices: 18.1 us -> 21.6 us
  Pallas kernels: 11.7 us -> 14.1 us
  local copies, waits for them, and re-layouts: 1.73 us -> 0 us
  other arithmetic: 0.93 us -> 1.83 us
    ppermute x8 -> x10, waiting for transfers between devices: 13 us -> 7.18 us  [swap(): return lax.ppermute(value, 'rows', moves)]
    pallas_call x4 -> x5, Pallas kernels: 11.7 us -> 14.1 us  [call(): pl.pallas_call(kernel, out_shape=[jax.ShapeDtypeStruct(shape, F32) for sh...]
    ppermute x8 -> x10, starting transfers between devices: 11.4 us -> 13.7 us  [swap(): return lax.ppermute(value, 'rows', moves)]
    ppermute x11 -> x13, waiting for transfers between devices: 4.62 us -> 2.7 us  [across(): lax.ppermute(value, 'rows', [(place, place ^ 1) for place in range(row_co...]
    unnamed x4 -> x0, local copies, waits for them, and re-layouts: 1.73 us -> none
    ppermute x3, waiting for transfers between devices: 3.95 us -> 2.31 us  [spread(): lax.ppermute(value, axis, [(place, place ^ mask) for place in range(size)])]
    ppermute x11 -> x13, starting transfers between devices: 1.04 us -> 2.19 us  [across(): lax.ppermute(value, 'rows', [(place, place ^ 1) for place in range(row_co...]
    select_n x1 -> x2, other arithmetic: 0.85 us -> 1.75 us  [the longest x1 0.9 us: local(): mine[0] = jnp.where(vec_index < 0, 0.0, mine[0])]
  transfers between devices with their start and end apart: 22 -> 26, of which waited for: 12 -> 11; matrix products, arithmetic and copies ran while one was open for 2% -> 4% of each run, Pallas kernels for 0% -> 13%
where the time goes in v4:
time: 49.9 us; the launch traced here: 49.7 us
  starting transfers between devices  21.6 us (43%)
  Pallas kernels  14.1 us (28%)
  waiting for transfers between devices  12.2 us (24%)
  other arithmetic  1.83 us (4%)
    pallas_call x5, Pallas kernels, call(): pl.pallas_call(kernel, out_shape=[jax.ShapeDtypeStruct(shape, F32) for sh...  14.1 us
    ppermute x10, starting transfers between devices, swap(): return lax.ppermute(value, 'rows', moves)  13.7 us
    ppermute x10, waiting for transfers between devices, swap(): return lax.ppermute(value, 'rows', moves)  7.18 us
    ppermute x3, starting transfers between devices, spread(): lax.ppermute(value, axis, [(place, place ^ mask) for place in range(size)])  5.62 us
    ppermute x13, waiting for transfers between devices, across(): lax.ppermute(value, 'rows', [(place, place ^ 1) for place in range(row_co...  2.7 us
    ppermute x3, waiting for transfers between devices, spread(): lax.ppermute(value, axis, [(place, place ^ mask) for place in range(size)])  2.31 us
    ppermute x13, starting transfers between devices, across(): lax.ppermute(value, 'rows', [(place, place ^ 1) for place in range(row_co...  2.19 us
  transfers between devices with their start and end apart: 26, of which 11 were waited for; matrix products, arithmetic and copies ran while one was open for 4% of the time, Pallas kernels for 13%

profile of v4, /device:TPU:0, one launch (start us, length us, event | category | flops | bytes accessed | tf_op | source)
XLA Modules:
  0.0 49.7 jit_solution(8927963811478215904)
XLA Ops:
  0.0 3.0 %collective-permute-start = (f32[3,32,256]{2,1,0:T(8,128)}, f32[3,32,256]{2,1,0:T(8,128)S(1)}, u32[]{:S(2)}, u32[]{:S(2)}) collective-permute-start(f32[3,32,256]{2,1,0:T(8,128)} %bitcast.5), channel_id=1, source_target_pairs={{0,1},{1,0},{2,3},{3,2},{4,5},{5,4},{6,7},{7,6},{8,9},{9,8},{10,11... | collective-permute-start | bytes 294920 | tf_op jit(solution)/shard_map/ppermute | solution.py:281
  3.0 2.6 %collective-permute-start.1 = (f32[3,32,256]{2,1,0:T(8,128)}, f32[3,32,256]{2,1,0:T(8,128)S(1)}, u32[]{:S(2)}, u32[]{:S(2)}) collective-permute-start(f32[3,32,256]{2,1,0:T(8,128)} %bitcast.6), channel_id=1, source_target_pairs={{0,2},{1,3},{2,0},{3,1},{4,6},{5,7},{6,4},{7,5},{8,10},{9,11},{10,... | collective-permute-start | bytes 294920 | tf_op jit(solution)/shard_map/ppermute | solution.py:281
  6.1 0.9 %broadcast_select_fusion.refs_0_ = f32[3,32,256]{2,1,0:T(8,128)S(1)} fusion(pred[]{:T(512)S(6)} %lt.10, f32[3,1,32,256]{3,2,1,0:T(8,128)} %param.3), kind=kLoop, calls=%fused_computation | loop fusion | flops 24576 | bytes 196609 | tf_op jit(solution)/shard_map/jit(_where)/select_n | solution.py:351
  7.2 0.8 %broadcast_select_fusion.1 = (f32[128,128]{1,0:T(8,128)S(1)}, f32[128,128]{1,0:T(8,128)S(1)}) fusion(f32[128,128]{1,0:T(8,128)S(1)} %collective-permute-done.7, f32[128,128]{1,0:T(8,128)} %param.2, pred[]{:T(512)S(6)} %eq.6), kind=kLoop, calls=%fused_computation.1 | loop fusion | flops 32768 | bytes 262145 | tf_op jit(solution)/shard_map/jit(_where)/select_n | solution.py:341
  8.1 1.8 %collective-permute-start.8 = (f32[128,128]{1,0:T(8,128)S(1)}, f32[128,128]{1,0:T(8,128)S(1)}, u32[]{:S(2)}, u32[]{:S(2)}) collective-permute-start(f32[128,128]{1,0:T(8,128)S(1)} %get-tuple-element.44.refs_8_), channel_id=1, source_target_pairs={{0,8},{4,12},{8,0},{12,4},{16,24},{20,28},{24,16},{28,20},{1,9},{5... | collective-permute-start | bytes 196616 | tf_op jit(solution)/shard_map/ppermute | solution.py:333
  9.9 1.5 %collective-permute-start.9 = (f32[128,128]{1,0:T(8,128)S(1)}, f32[128,128]{1,0:T(8,128)S(1)}, u32[]{:S(2)}, u32[]{:S(2)}) collective-permute-start(f32[128,128]{1,0:T(8,128)S(1)} %get-tuple-element.44.refs_8_), channel_id=1, source_target_pairs={{0,24},{4,28},{8,16},{12,20},{16,8},{20,12},{24,0},{28,4},{1,25},{... | collective-permute-start | bytes 196616 | tf_op jit(solution)/shard_map/ppermute | solution.py:333
  11.4 2.3 %collective-permute-done.1.refs_2_ = f32[3,32,256]{2,1,0:T(8,128)S(1)} collective-permute-done((f32[3,32,256]{2,1,0:T(8,128)}, f32[3,32,256]{2,1,0:T(8,128)S(1)}, u32[]{:S(2)}, u32[]{:S(2)}) %collective-permute-start.1) | collective-permute-done | bytes 98336 | tf_op jit(solution)/shard_map/ppermute | solution.py:281
  14.3 0.7 %collective-permute-done.9.refs_11_ = f32[128,128]{1,0:T(8,128)S(1)} collective-permute-done((f32[128,128]{1,0:T(8,128)S(1)}, f32[128,128]{1,0:T(8,128)S(1)}, u32[]{:S(2)}, u32[]{:S(2)}) %collective-permute-start.9) | collective-permute-done | bytes 65568 | tf_op jit(solution)/shard_map/ppermute | solution.py:333
  15.5 4.3 %shard_map.28 = (f32[1,384,384]{2,1,0:T(8,128)S(1)}, f32[384,128]{1,0:T(8,128)S(1)}, f32[256,128]{1,0:T(8,128)S(1)}, f32[128,128]{1,0:T(8,128)S(1)}) custom-call(s32[3]{0:T(128)S(1)} %pad_add_fusion.place_ref, f32[3,32,256]{2,1,0:T(8,128)S(1)} %broadcast_select_fusion.refs_0_, f32[3,32,256]{2,1,0:T(8,128)S(1)} %collective-permute-done.refs_1_, ...), custom_call_target="tpu_custom_call" | custom-call | flops 905969664 | tf_op jit(solution)/shard_map/pallas_call | solution.py:261
  19.8 1.6 %collective-permute-start.10 = (f32[256,128]{1,0:T(8,128)S(1)}, f32[256,128]{1,0:T(8,128)S(1)}, u32[]{:S(2)}, u32[]{:S(2)}) collective-permute-start(f32[256,128]{1,0:T(8,128)S(1)} %get-tuple-element.24), channel_id=1, source_target_pairs={{0,8},{4,20},{8,0},{12,28},{16,24},{20,4},{24,16},{28,12},{1,9},{5... | collective-permute-start | bytes 393224 | tf_op jit(solution)/shard_map/ppermute | solution.py:333
  21.3 1.5 %collective-permute-start.11 = (f32[128,128]{1,0:T(8,128)S(1)}, f32[128,128]{1,0:T(8,128)S(1)}, u32[]{:S(2)}, u32[]{:S(2)}) collective-permute-start(f32[128,128]{1,0:T(8,128)S(1)} %get-tuple-element.28), channel_id=1, source_target_pairs={{0,24},{4,28},{8,16},{12,20},{16,8},{20,12},{24,0},{28,4},{1,25},{... | collective-permute-start | bytes 196616 | tf_op jit(solution)/shard_map/ppermute | solution.py:333
  22.8 4.9 %shard_map.29 = (f32[2,384,384]{2,1,0:T(8,128)S(1)}, f32[256,128]{1,0:T(8,128)S(1)}, f32[128,128]{1,0:T(8,128)S(1)}) custom-call(s32[3]{0:T(128)S(1)} %pad_add_fusion.place_ref, f32[3,32,256]{2,1,0:T(8,128)S(1)} %broadcast_select_fusion.refs_0_, f32[3,32,256]{2,1,0:T(8,128)S(1)} %collective-permute-done.refs_1_, ...), custom_call_target="tpu_custom_call" | custom-call | flops 1811939328 | tf_op jit(solution)/shard_map/pallas_call | solution.py:261
  27.8 1.6 %collective-permute-start.16 = (f32[256,128]{1,0:T(8,128)S(1)}, f32[256,128]{1,0:T(8,128)S(1)}, u32[]{:S(2)}, u32[]{:S(2)}) collective-permute-start(f32[256,128]{1,0:T(8,128)S(1)} %get-tuple-element.34), channel_id=1, source_target_pairs={{0,8},{4,20},{8,0},{12,28},{16,24},{20,4},{24,16},{28,12},{1,9},{5... | collective-permute-start | bytes 393224 | tf_op jit(solution)/shard_map/ppermute | solution.py:333
  29.4 1.6 %collective-permute-start.17 = (f32[128,128]{1,0:T(8,128)S(1)}, f32[128,128]{1,0:T(8,128)S(1)}, u32[]{:S(2)}, u32[]{:S(2)}) collective-permute-start(f32[128,128]{1,0:T(8,128)S(1)} %get-tuple-element.35), channel_id=1, source_target_pairs={{0,24},{4,28},{8,16},{12,20},{16,8},{20,12},{24,0},{28,4},{1,25},{... | collective-permute-start | bytes 196616 | tf_op jit(solution)/shard_map/ppermute | solution.py:333
  31.0 1.6 %shard_map.30 = (f32[384,128]{1,0:T(8,128)S(1)}, f32[128,128]{1,0:T(8,128)S(1)}, f32[64,128]{1,0:T(8,128)S(1)}) custom-call(s32[3]{0:T(128)S(1)} %pad_add_fusion.place_ref, f32[256,128]{1,0:T(8,128)S(1)} %collective-permute-done.10.refs_0_, f32[128,128]{1,0:T(8,128)S(1)} %collective-permute-done.11.refs_1_, f32[256,128]{1,0:T(8,128)S(1)} %collective-permute-done.12.refs_2_, ...), custom_call_target="tpu_custom_call" | custom-call | tf_op jit(solution)/shard_map/pallas_call | solution.py:261
  32.6 1.4 %collective-permute-start.15 = (f32[64,128]{1,0:T(8,128)S(1)}, f32[64,128]{1,0:T(8,128)S(1)}, u32[]{:S(2)}, u32[]{:S(2)}) collective-permute-start(f32[64,128]{1,0:T(8,128)S(1)} %get-tuple-element.33), channel_id=1, source_target_pairs={{0,24},{4,28},{8,16},{12,20},{16,8},{20,12},{24,0},{28,4},{1,25},{... | collective-permute-start | bytes 98312 | tf_op jit(solution)/shard_map/ppermute | solution.py:333
  34.8 2.8 %collective-permute-done.15.refs_1_ = f32[64,128]{1,0:T(8,128)S(1)} collective-permute-done((f32[64,128]{1,0:T(8,128)S(1)}, f32[64,128]{1,0:T(8,128)S(1)}, u32[]{:S(2)}, u32[]{:S(2)}) %collective-permute-start.15) | collective-permute-done | bytes 32800 | tf_op jit(solution)/shard_map/ppermute | solution.py:333
  38.8 0.9 %collective-permute-done.19.refs_3_ = f32[64,128]{1,0:T(8,128)S(1)} collective-permute-done((f32[64,128]{1,0:T(8,128)S(1)}, f32[64,128]{1,0:T(8,128)S(1)}, u32[]{:S(2)}, u32[]{:S(2)}) %collective-permute-start.19) | collective-permute-done | bytes 32800 | tf_op jit(solution)/shard_map/ppermute | solution.py:336
  39.6 1.6 %shard_map.31 = (f32[384,128]{1,0:T(8,128)S(1)}, f32[128,128]{1,0:T(8,128)S(1)}, f32[64,128]{1,0:T(8,128)S(1)}) custom-call(s32[3]{0:T(128)S(1)} %pad_add_fusion.place_ref, f32[128,128]{1,0:T(8,128)S(1)} %collective-permute-done.14.refs_0_, f32[64,128]{1,0:T(8,128)S(1)} %collective-permute-done.15.refs_1_, f32[128,128]{1,0:T(8,128)S(1)} %collective-permute-done.18.refs_2_, ...), custom_call_target="tpu_custom_call" | custom-call | tf_op jit(solution)/shard_map/pallas_call | solution.py:261
  42.0 1.5 %collective-permute-start.23 = (f32[64,128]{1,0:T(8,128)S(1)}, f32[64,128]{1,0:T(8,128)S(1)}, u32[]{:S(2)}, u32[]{:S(2)}) collective-permute-start(f32[64,128]{1,0:T(8,128)S(1)} %get-tuple-element.41), channel_id=1, source_target_pairs={{0,24},{4,28},{8,16},{12,20},{16,8},{20,12},{24,0},{28,4},{1,25},{... | collective-permute-start | bytes 98312 | tf_op jit(solution)/shard_map/ppermute | solution.py:333
  43.5 2.3 %collective-permute-done.22.refs_0_ = f32[128,128]{1,0:T(8,128)S(1)} collective-permute-done((f32[128,128]{1,0:T(8,128)S(1)}, f32[128,128]{1,0:T(8,128)S(1)}, u32[]{:S(2)}, u32[]{:S(2)}) %collective-permute-start.22) | collective-permute-done | bytes 65568 | tf_op jit(solution)/shard_map/ppermute | solution.py:333
  45.8 1.0 %collective-permute-done.23.refs_1_ = f32[64,128]{1,0:T(8,128)S(1)} collective-permute-done((f32[64,128]{1,0:T(8,128)S(1)}, f32[64,128]{1,0:T(8,128)S(1)}, u32[]{:S(2)}, u32[]{:S(2)}) %collective-permute-start.23) | collective-permute-done | bytes 32800 | tf_op jit(solution)/shard_map/ppermute | solution.py:333
  46.8 1.2 %collective-permute-done.25.refs_3_ = f32[64,128]{1,0:T(8,128)S(1)} collective-permute-done((f32[64,128]{1,0:T(8,128)S(1)}, f32[64,128]{1,0:T(8,128)S(1)}, u32[]{:S(2)}, u32[]{:S(2)}) %collective-permute-start.25) | collective-permute-done | bytes 32800 | tf_op jit(solution)/shard_map/ppermute | solution.py:336
  48.0 1.7 %shard_map.32 = f32[128,128]{1,0:T(8,128)} custom-call(s32[3]{0:T(128)S(1)} %pad_add_fusion.place_ref, f32[128,128]{1,0:T(8,128)S(1)} %collective-permute-done.22.refs_0_, f32[64,128]{1,0:T(8,128)S(1)} %collective-permute-done.23.refs_1_, f32[128,128]{1,0:T(8,128)S(1)} %collective-permute-done.24.refs_2_, f32[64,128]{1,0:T(8,128)S(1)} %collective-permute-done.25.refs_3_, ...), custom_call_target="tpu_custom_call" | custom-call | tf_op jit(solution)/shard_map/pallas_call | solution.py:261
  (36 shorter events, 4.6 us)
Async XLA Ops:
  0.0 9.9 %collective-permute-start = (f32[3,32,256]{2,1,0:T(8,128)}, f32[3,32,256]{2,1,0:T(8,128)S(1)}, u32[]{:S(2)}, u32[]{:S(2)}) collective-permute-start(f32[3,32,256]{2,1,0:T(8,128)} %bitcast.5), channel_id=1, source_target_pairs={{0,1},{1,0},{2,3},{3,2},{4,5},{5,4},{6,7},{7,6},{8,9},{9,8},{10,11... | collective-permute-start | bytes 294920 | tf_op jit(solution)/shard_map/ppermute | solution.py:281
  3.0 10.6 %collective-permute-start.1 = (f32[3,32,256]{2,1,0:T(8,128)}, f32[3,32,256]{2,1,0:T(8,128)S(1)}, u32[]{:S(2)}, u32[]{:S(2)}) collective-permute-start(f32[3,32,256]{2,1,0:T(8,128)} %bitcast.6), channel_id=1, source_target_pairs={{0,2},{1,3},{2,0},{3,1},{4,6},{5,7},{6,4},{7,5},{8,10},{9,11},{10,... | collective-permute-start | bytes 294920 | tf_op jit(solution)/shard_map/ppermute | solution.py:281
  5.6 8.1 %collective-permute-start.2 = (f32[3,32,256]{2,1,0:T(8,128)}, f32[3,32,256]{2,1,0:T(8,128)S(1)}, u32[]{:S(2)}, u32[]{:S(2)}) collective-permute-start(f32[3,32,256]{2,1,0:T(8,128)} %bitcast.7), channel_id=1, source_target_pairs={{0,3},{1,2},{2,1},{3,0},{4,7},{5,6},{6,5},{7,4},{8,11},{9,10},{10,... | collective-permute-start | bytes 294920 | tf_op jit(solution)/shard_map/ppermute | solution.py:281
  5.6 8.6 %collective-permute-start.3 = (f32[3,32,256]{2,1,0:T(8,128)}, f32[3,32,256]{2,1,0:T(8,128)S(1)}, u32[]{:S(2)}, u32[]{:S(2)}) collective-permute-start(f32[3,32,256]{2,1,0:T(8,128)} %bitcast.8), channel_id=1, source_target_pairs={{0,4},{4,0},{8,12},{12,8},{16,20},{20,16},{24,28},{28,24},{1,5},{5... | collective-permute-start | bytes 294920 | tf_op jit(solution)/shard_map/ppermute | solution.py:336
  5.6 1.6 %collective-permute-start.7 = (f32[128,128]{1,0:T(8,128)}, f32[128,128]{1,0:T(8,128)S(1)}, u32[]{:S(2)}, u32[]{:S(2)}) collective-permute-start(f32[128,128]{1,0:T(8,128)} %param.2), channel_id=1, source_target_pairs={{0,4},{4,0},{8,12},{12,8},{16,20},{20,16},{24,28},{28,24},{1,5},{5... | collective-permute-start | bytes 196616 | tf_op jit(solution)/shard_map/ppermute | solution.py:336
  8.1 6.2 %collective-permute-start.8 = (f32[128,128]{1,0:T(8,128)S(1)}, f32[128,128]{1,0:T(8,128)S(1)}, u32[]{:S(2)}, u32[]{:S(2)}) collective-permute-start(f32[128,128]{1,0:T(8,128)S(1)} %get-tuple-element.44.refs_8_), channel_id=1, source_target_pairs={{0,8},{4,12},{8,0},{12,4},{16,24},{20,28},{24,16},{28,20},{1,9},{5... | collective-permute-start | bytes 196616 | tf_op jit(solution)/shard_map/ppermute | solution.py:333
  9.9 5.2 %collective-permute-start.9 = (f32[128,128]{1,0:T(8,128)S(1)}, f32[128,128]{1,0:T(8,128)S(1)}, u32[]{:S(2)}, u32[]{:S(2)}) collective-permute-start(f32[128,128]{1,0:T(8,128)S(1)} %get-tuple-element.44.refs_8_), channel_id=1, source_target_pairs={{0,24},{4,28},{8,16},{12,20},{16,8},{20,12},{24,0},{28,4},{1,25},{... | collective-permute-start | bytes 196616 | tf_op jit(solution)/shard_map/ppermute | solution.py:333
  13.7 1.4 %collective-permute-start.4 = (f32[3,32,256]{2,1,0:T(8,128)S(1)}, f32[3,32,256]{2,1,0:T(8,128)S(1)}, u32[]{:S(2)}, u32[]{:S(2)}) collective-permute-start(f32[3,32,256]{2,1,0:T(8,128)S(1)} %collective-permute-done.refs_1_), channel_id=1, source_target_pairs={{0,4},{4,0},{8,12},{12,8},{16,20},{20,16},{24,28},{28,24},{1,5},{5... | collective-permute-start | bytes 294920 | tf_op jit(solution)/shard_map/ppermute | solution.py:336
  13.7 1.5 %collective-permute-start.5 = (f32[3,32,256]{2,1,0:T(8,128)S(1)}, f32[3,32,256]{2,1,0:T(8,128)S(1)}, u32[]{:S(2)}, u32[]{:S(2)}) collective-permute-start(f32[3,32,256]{2,1,0:T(8,128)S(1)} %collective-permute-done.1.refs_2_), channel_id=1, source_target_pairs={{0,4},{4,0},{8,12},{12,8},{16,20},{20,16},{24,28},{28,24},{1,5},{5... | collective-permute-start | bytes 294920 | tf_op jit(solution)/shard_map/ppermute | solution.py:336
  19.8 8.0 %collective-permute-start.10 = (f32[256,128]{1,0:T(8,128)S(1)}, f32[256,128]{1,0:T(8,128)S(1)}, u32[]{:S(2)}, u32[]{:S(2)}) collective-permute-start(f32[256,128]{1,0:T(8,128)S(1)} %get-tuple-element.24), channel_id=1, source_target_pairs={{0,8},{4,20},{8,0},{12,28},{16,24},{20,4},{24,16},{28,12},{1,9},{5... | collective-permute-start | bytes 393224 | tf_op jit(solution)/shard_map/ppermute | solution.py:333
  21.3 8.1 %collective-permute-start.11 = (f32[128,128]{1,0:T(8,128)S(1)}, f32[128,128]{1,0:T(8,128)S(1)}, u32[]{:S(2)}, u32[]{:S(2)}) collective-permute-start(f32[128,128]{1,0:T(8,128)S(1)} %get-tuple-element.28), channel_id=1, source_target_pairs={{0,24},{4,28},{8,16},{12,20},{16,8},{20,12},{24,0},{28,4},{1,25},{... | collective-permute-start | bytes 196616 | tf_op jit(solution)/shard_map/ppermute | solution.py:333
  27.8 3.3 %collective-permute-start.12 = (f32[256,128]{1,0:T(8,128)S(1)}, f32[256,128]{1,0:T(8,128)S(1)}, u32[]{:S(2)}, u32[]{:S(2)}) collective-permute-start(f32[256,128]{1,0:T(8,128)S(1)} %collective-permute-done.10.refs_0_), channel_id=1, source_target_pairs={{0,4},{4,0},{8,12},{12,8},{16,20},{20,16},{24,28},{28,24},{1,5},{5... | collective-permute-start | bytes 393224 | tf_op jit(solution)/shard_map/ppermute | solution.py:336
  27.8 7.0 %collective-permute-start.16 = (f32[256,128]{1,0:T(8,128)S(1)}, f32[256,128]{1,0:T(8,128)S(1)}, u32[]{:S(2)}, u32[]{:S(2)}) collective-permute-start(f32[256,128]{1,0:T(8,128)S(1)} %get-tuple-element.34), channel_id=1, source_target_pairs={{0,8},{4,20},{8,0},{12,28},{16,24},{20,4},{24,16},{28,12},{1,9},{5... | collective-permute-start | bytes 393224 | tf_op jit(solution)/shard_map/ppermute | solution.py:333
  29.4 1.6 %collective-permute-start.13 = (f32[128,128]{1,0:T(8,128)S(1)}, f32[128,128]{1,0:T(8,128)S(1)}, u32[]{:S(2)}, u32[]{:S(2)}) collective-permute-start(f32[128,128]{1,0:T(8,128)S(1)} %collective-permute-done.11.refs_1_), channel_id=1, source_target_pairs={{0,4},{4,0},{8,12},{12,8},{16,20},{20,16},{24,28},{28,24},{1,5},{5... | collective-permute-start | bytes 196616 | tf_op jit(solution)/shard_map/ppermute | solution.py:336
  29.4 5.4 %collective-permute-start.17 = (f32[128,128]{1,0:T(8,128)S(1)}, f32[128,128]{1,0:T(8,128)S(1)}, u32[]{:S(2)}, u32[]{:S(2)}) collective-permute-start(f32[128,128]{1,0:T(8,128)S(1)} %get-tuple-element.35), channel_id=1, source_target_pairs={{0,24},{4,28},{8,16},{12,20},{16,8},{20,12},{24,0},{28,4},{1,25},{... | collective-permute-start | bytes 196616 | tf_op jit(solution)/shard_map/ppermute | solution.py:333
  32.6 5.0 %collective-permute-start.15 = (f32[64,128]{1,0:T(8,128)S(1)}, f32[64,128]{1,0:T(8,128)S(1)}, u32[]{:S(2)}, u32[]{:S(2)}) collective-permute-start(f32[64,128]{1,0:T(8,128)S(1)} %get-tuple-element.33), channel_id=1, source_target_pairs={{0,24},{4,28},{8,16},{12,20},{16,8},{20,12},{24,0},{28,4},{1,25},{... | collective-permute-start | bytes 98312 | tf_op jit(solution)/shard_map/ppermute | solution.py:333
  34.0 4.3 %collective-permute-start.14 = (f32[128,128]{1,0:T(8,128)S(1)}, f32[128,128]{1,0:T(8,128)S(1)}, u32[]{:S(2)}, u32[]{:S(2)}) collective-permute-start(f32[128,128]{1,0:T(8,128)S(1)} %get-tuple-element.32), channel_id=1, source_target_pairs={{0,8},{4,20},{8,0},{12,28},{16,24},{20,4},{24,16},{28,12},{1,9},{5... | collective-permute-start | bytes 196616 | tf_op jit(solution)/shard_map/ppermute | solution.py:333
  37.6 2.1 %collective-permute-start.20 = (f32[256,128]{1,0:T(8,128)S(1)}, f32[256,128]{1,0:T(8,128)S(1)}, u32[]{:S(2)}, u32[]{:S(2)}) collective-permute-start(f32[256,128]{1,0:T(8,128)S(1)} %collective-permute-done.16.refs_4_), channel_id=1, source_target_pairs={{0,4},{4,0},{8,12},{12,8},{16,20},{20,16},{24,28},{28,24},{1,5},{5... | collective-permute-start | bytes 393224 | tf_op jit(solution)/shard_map/ppermute | solution.py:336
  37.6 2.0 %collective-permute-start.21 = (f32[128,128]{1,0:T(8,128)S(1)}, f32[128,128]{1,0:T(8,128)S(1)}, u32[]{:S(2)}, u32[]{:S(2)}) collective-permute-start(f32[128,128]{1,0:T(8,128)S(1)} %collective-permute-done.17.refs_5_), channel_id=1, source_target_pairs={{0,4},{4,0},{8,12},{12,8},{16,20},{20,16},{24,28},{28,24},{1,5},{5... | collective-permute-start | bytes 196616 | tf_op jit(solution)/shard_map/ppermute | solution.py:336
  38.3 1.4 %collective-permute-start.18 = (f32[128,128]{1,0:T(8,128)S(1)}, f32[128,128]{1,0:T(8,128)S(1)}, u32[]{:S(2)}, u32[]{:S(2)}) collective-permute-start(f32[128,128]{1,0:T(8,128)S(1)} %collective-permute-done.14.refs_0_), channel_id=1, source_target_pairs={{0,4},{4,0},{8,12},{12,8},{16,20},{20,16},{24,28},{28,24},{1,5},{5... | collective-permute-start | bytes 196616 | tf_op jit(solution)/shard_map/ppermute | solution.py:336
  38.3 1.4 %collective-permute-start.19 = (f32[64,128]{1,0:T(8,128)S(1)}, f32[64,128]{1,0:T(8,128)S(1)}, u32[]{:S(2)}, u32[]{:S(2)}) collective-permute-start(f32[64,128]{1,0:T(8,128)S(1)} %collective-permute-done.15.refs_1_), channel_id=1, source_target_pairs={{0,4},{4,0},{8,12},{12,8},{16,20},{20,16},{24,28},{28,24},{1,5},{5... | collective-permute-start | bytes 98312 | tf_op jit(solution)/shard_map/ppermute | solution.py:336
  41.2 4.5 %collective-permute-start.22 = (f32[128,128]{1,0:T(8,128)S(1)}, f32[128,128]{1,0:T(8,128)S(1)}, u32[]{:S(2)}, u32[]{:S(2)}) collective-permute-start(f32[128,128]{1,0:T(8,128)S(1)} %get-tuple-element.40), channel_id=1, source_target_pairs={{0,8},{4,20},{8,0},{12,28},{16,24},{20,4},{24,16},{28,12},{1,9},{5... | collective-permute-start | bytes 196616 | tf_op jit(solution)/shard_map/ppermute | solution.py:333
  42.0 4.8 %collective-permute-start.23 = (f32[64,128]{1,0:T(8,128)S(1)}, f32[64,128]{1,0:T(8,128)S(1)}, u32[]{:S(2)}, u32[]{:S(2)}) collective-permute-start(f32[64,128]{1,0:T(8,128)S(1)} %get-tuple-element.41), channel_id=1, source_target_pairs={{0,24},{4,28},{8,16},{12,20},{16,8},{20,12},{24,0},{28,4},{1,25},{... | collective-permute-start | bytes 98312 | tf_op jit(solution)/shard_map/ppermute | solution.py:333
  45.8 2.2 %collective-permute-start.24 = (f32[128,128]{1,0:T(8,128)S(1)}, f32[128,128]{1,0:T(8,128)S(1)}, u32[]{:S(2)}, u32[]{:S(2)}) collective-permute-start(f32[128,128]{1,0:T(8,128)S(1)} %collective-permute-done.22.refs_0_), channel_id=1, source_target_pairs={{0,4},{4,0},{8,12},{12,8},{16,20},{20,16},{24,28},{28,24},{1,5},{5... | collective-permute-start | bytes 196616 | tf_op jit(solution)/shard_map/ppermute | solution.py:336
  (2 other events, 2.5 us)

commit v5 on v4

--- a/solution.py
+++ b/solution.py
@@ -151,14 +151,15 @@
     return jnp.where(core == 0, value[:rows], value[rows:])
 
 
-def assemble(place_ref, mine, theirs, groups, refl_ref):
+def assemble(place_ref, mine, theirs, skip, refl_ref):
     core, vec = place_ref[1], place_ref[2]
-    rows = mine[0].shape[1]
+    count, rows = refl_ref.shape[1], mine[0].shape[1]
     for step, (own, other) in enumerate(zip(mine, theirs)):
         at = pl.ds(pl.multiple_of((step ^ vec) * rows, rows), rows)
-        for slot, group in enumerate(groups):
-            refl_ref[core, slot, at, :] = own[group]
-            refl_ref[1 - core, slot, at, :] = other[group]
+        first = min(skip, own.shape[0] - count)
+        for slot in range(count):
+            refl_ref[core, slot, at, :] = own[first + slot]
+            refl_ref[1 - core, slot, at, :] = other[first + slot]
 
 
 def first_kernel(count, nodes, place_ref, *refs):
@@ -167,7 +168,7 @@
     oper_ref, fixed_ref, out_near, out_far, refl_ref = refs[2 * count + 4 :]
     block = top_ref.shape[0]
     node, core = place_ref[0], place_ref[1]
-    assemble(place_ref, mine, theirs, [0], refl_ref)
+    assemble(place_ref, mine, theirs, 0, refl_ref)
     pair_operators(refl_ref, node != nodes - 1, oper_ref)
     below = jnp.where((node & 1) == 0, near_ref[...], far_ref[...])
     window = jnp.concatenate(
@@ -191,7 +192,7 @@
     oper_ref, map_near, map_far, refl_ref = refs[2 * count :]
     node, core = place_ref[0], place_ref[1]
     later, _, size = oper_ref.shape
-    assemble(place_ref, mine, theirs, range(1, 1 + later), refl_ref)
+    assemble(place_ref, mine, theirs, 1, refl_ref)
     pair_operators(refl_ref, node != nodes - 1, oper_ref)
     leads = [oper_ref[slot, :, : size // 3] for slot in range(later)]
     map_near[...] = jnp.concatenate([pick_near(node, core, lead) for lead in leads], 0)
@@ -273,16 +274,6 @@
     return jnp.matmul(left, right, precision=lax.Precision.HIGHEST)
 
 
-def spread(value, axis, size):
-    if size & (size - 1) or size > 8:
-        gathered = lax.all_gather(value, axis)
-        return [gathered[place] for place in range(size)], False
-    return [value] + [
-        lax.ppermute(value, axis, [(place, place ^ mask) for place in range(size)])
-        for mask in range(1, size)
-    ], True
-
-
 def many_pairs(fixed, operators, node, nodes, row_count):
     groups, block = len(operators), fixed.shape[0] // 3
     members = [[place * PAIR + core for place in range(nodes)] for core in range(PAIR)]
@@ -335,8 +326,28 @@
     def across(value):
         return lax.ppermute(value, "rows", [(place, place ^ 1) for place in range(row_count)])
 
-    mine, mixed = spread(reflectors[:, 0], "vecs", vec_count)
+    hold = lax.optimization_barrier
+    later = groups - 1
+    blocks = reflectors[:, 0]
     other = across(vectors)
+    if vec_count & (vec_count - 1) or vec_count > 8:
+        gathered = lax.all_gather(blocks, "vecs")
+        mine = rest = [gathered[step] for step in range(vec_count)]
+        start = 0
+    else:
+
+        def partners(value, mask):
+            return lax.ppermute(
+                value, "vecs", [(step, step ^ mask) for step in range(vec_count)]
+            )
+
+        mine = [blocks, partners(blocks, 1)]
+        mine += [partners(blocks[:1], mask) for mask in range(vec_count - 1, 1, -1)]
+        behind, other = hold((blocks[1:], other))
+        rest = mine[:2] + [partners(behind, mask) for mask in range(vec_count - 1, 1, -1)]
+        order = [0, 1] + list(range(vec_count - 1, 1, -1))
+        mine, rest = ([part[order.index(step)] for step in range(vec_count)] for part in (mine, rest))
+        start = vec_index
     top = jnp.where(core == 0, vectors, other)
     low = jnp.where(core == 0, other, vectors)
     if nodes == 4:
@@ -348,31 +359,31 @@
             )
         ] * 2
     theirs = [across(piece) for piece in mine]
-    mine[0] = jnp.where(vec_index < 0, 0.0, mine[0])
-    place = jnp.stack([node, core, vec_index if mixed else 0]).astype(jnp.int32)
-    later = groups - 1
+    whole = jnp.where(vec_index < 0, 0.0, blocks)
+    place = jnp.stack([node, core, start]).astype(jnp.int32)
     work = 16 * (3 * block) ** 3
-    pieces = [place, *mine, *theirs]
     first_oper, fixed, near, far = call(
-        functools.partial(first_kernel, len(mine), nodes),
+        functools.partial(first_kernel, vec_count, nodes),
         [
             (1, 3 * block, 3 * block),
             (3 * block, cols),
             (2 * block, cols),
             (block, cols),
         ],
-        [*pieces, top, low, *below],
+        [place, *([whole] + mine[1:]), *theirs, top, low, *below],
         [pltpu.VMEM((PAIR, 1, block, window), F32)],
-        work,
-    )
+        0,
+    )
+    far, *rest[2:] = hold((far, *rest[2:]))
+    theirs = theirs[:2] + [across(piece) for piece in rest[2:]]
     later_oper, *maps = call(
-        functools.partial(later_kernel, len(mine), nodes),
+        functools.partial(later_kernel, vec_count, nodes),
         [
             (later, 3 * block, 3 * block),
             (later * block, block),
             (later * block // PAIR, block),
         ],
-        pieces,
+        [place, *([whole] + rest[1:]), *theirs],
         [pltpu.VMEM((PAIR, later, block, window), F32)],
         work * later,
     )
@@ -380,7 +391,6 @@
         operators = [first_oper[0]] + [later_oper[slot] for slot in range(later)]
         result = many_pairs(fixed, operators, node, nodes, row_count)
         return jnp.where(core == 0, result[:block], result[block : 2 * block])
-    hold = lax.optimization_barrier
     for group in range(groups):
         near = swap(near, (1, 2))
         far = swap(far, (3, 3))

time: 49.9 us -> 53.6 us (1.074)
  starting transfers between devices: 21.6 us -> 24.6 us
  local copies, waits for them, and re-layouts: 0 us -> 1.6 us
  waiting for transfers between devices: 12.2 us -> 11.1 us
    ppermute x3 -> x5, starting transfers between devices: 5.62 us -> 8.22 us  [partners(): lax.ppermute(value, 'vecs', [(step, step ^ mask) for step in range(vec_co...]
    slice x0 -> x2, local copies, waits for them, and re-layouts: none -> 1.6 us  [the longest x1 0.84 us: local(): behind, other = hold((blocks[1:], other))]
    ppermute x13 -> x15, waiting for transfers between devices: 2.7 us -> 2.13 us  [across(): lax.ppermute(value, 'rows', [(place, place ^ 1) for place in range(row_co...]
    ppermute x3 -> x5, waiting for transfers between devices: 2.31 us -> 2.06 us  [partners(): lax.ppermute(value, 'vecs', [(step, step ^ mask) for step in range(vec_co...]
    ppermute x13 -> x15, starting transfers between devices: 2.19 us -> 2.43 us  [across(): lax.ppermute(value, 'rows', [(place, place ^ 1) for place in range(row_co...]
  transfers between devices with their start and end apart: 26 -> 30, of which waited for: 11 -> 8; matrix products, arithmetic and copies ran while one was open for 4% -> 5% of each run, Pallas kernels for 13% -> 20%
where the time goes in v5:
time: 53.6 us; the launch traced here: 53.3 us
  starting transfers between devices  24.6 us (46%)
  Pallas kernels  14.1 us (26%)
  waiting for transfers between devices  11.1 us (21%)
  other arithmetic  1.83 us (3%)
  local copies, waits for them, and re-layouts  1.6 us (3%)
    pallas_call x5, Pallas kernels, call(): pl.pallas_call(kernel, out_shape=[jax.ShapeDtypeStruct(shape, F32) for sh...  14.1 us
    ppermute x10, starting transfers between devices, swap(): return lax.ppermute(value, 'rows', moves)  13.9 us
    ppermute x5, starting transfers between devices, partners(): lax.ppermute(value, 'vecs', [(step, step ^ mask) for step in range(vec_co...  8.22 us
    ppermute x10, waiting for transfers between devices, swap(): return lax.ppermute(value, 'rows', moves)  6.95 us
    ppermute x15, starting transfers between devices, across(): lax.ppermute(value, 'rows', [(place, place ^ 1) for place in range(row_co...  2.43 us
    ppermute x15, waiting for transfers between devices, across(): lax.ppermute(value, 'rows', [(place, place ^ 1) for place in range(row_co...  2.13 us
    ppermute x5, waiting for transfers between devices, partners(): lax.ppermute(value, 'vecs', [(step, step ^ mask) for step in range(vec_co...  2.06 us
  transfers between devices with their start and end apart: 30, of which 8 were waited for; matrix products, arithmetic and copies ran while one was open for 5% of the time, Pallas kernels for 20%

profile of v5, /device:TPU:0, one launch (start us, length us, event | category | flops | bytes accessed | tf_op | source)
XLA Modules:
  0.0 53.3 jit_solution(11876613716652348281)
XLA Ops:
  0.8 4.0 %collective-permute-start.1 = (f32[1,32,256]{2,1,0:T(8,128)S(1)}, f32[1,32,256]{2,1,0:T(8,128)S(1)}, u32[]{:S(2)}, u32[]{:S(2)}) collective-permute-start(f32[1,32,256]{2,1,0:T(8,128)S(1)} %slice_bitcast_fusion.1), channel_id=1, source_target_pairs={{0,2},{1,3},{2,0},{3,1},{4,6},{5,7},{6,4},{7,5},{8,10},{9,11},{10,... | collective-permute-start | bytes 98312 | tf_op jit(solution)/shard_map/ppermute | solution.py:340
  4.8 1.3 %collective-permute-start.2 = (f32[1,32,256]{2,1,0:T(8,128)S(1)}, f32[1,32,256]{2,1,0:T(8,128)S(1)}, u32[]{:S(2)}, u32[]{:S(2)}) collective-permute-start(f32[1,32,256]{2,1,0:T(8,128)S(1)} %slice_bitcast_fusion.1), channel_id=1, source_target_pairs={{0,3},{1,2},{2,1},{3,0},{4,7},{5,6},{6,5},{7,4},{8,11},{9,10},{10,... | collective-permute-start | bytes 98312 | tf_op jit(solution)/shard_map/ppermute | solution.py:340
  8.7 2.1 %collective-permute-done.2.refs_3_ = f32[1,32,256]{2,1,0:T(8,128)S(1)} collective-permute-done((f32[1,32,256]{2,1,0:T(8,128)S(1)}, f32[1,32,256]{2,1,0:T(8,128)S(1)}, u32[]{:S(2)}, u32[]{:S(2)}) %collective-permute-start.2) | collective-permute-done | bytes 32800 | tf_op jit(solution)/shard_map/ppermute | solution.py:340
  11.6 1.6 %collective-permute-start.8 = (f32[128,128]{1,0:T(8,128)S(1)}, f32[128,128]{1,0:T(8,128)S(1)}, u32[]{:S(2)}, u32[]{:S(2)}) collective-permute-start(f32[128,128]{1,0:T(8,128)S(1)} %get-tuple-element.54.refs_8_), channel_id=1, source_target_pairs={{0,8},{4,12},{8,0},{12,4},{16,24},{20,28},{24,16},{28,20},{1,9},{5... | collective-permute-start | bytes 196616 | tf_op jit(solution)/shard_map/ppermute | solution.py:324
  13.2 1.5 %collective-permute-start.9 = (f32[128,128]{1,0:T(8,128)S(1)}, f32[128,128]{1,0:T(8,128)S(1)}, u32[]{:S(2)}, u32[]{:S(2)}) collective-permute-start(f32[128,128]{1,0:T(8,128)S(1)} %get-tuple-element.54.refs_8_), channel_id=1, source_target_pairs={{0,24},{4,28},{8,16},{12,20},{16,8},{20,12},{24,0},{28,4},{1,25},{... | collective-permute-start | bytes 196616 | tf_op jit(solution)/shard_map/ppermute | solution.py:324
  14.7 1.3 %collective-permute-start.11 = (f32[2,32,256]{2,1,0:T(8,128)S(1)}, f32[2,32,256]{2,1,0:T(8,128)S(1)}, u32[]{:S(2)}, u32[]{:S(2)}) collective-permute-start(f32[2,32,256]{2,1,0:T(8,128)S(1)} %slice_bitcast_fusion), channel_id=1, source_target_pairs={{0,2},{1,3},{2,0},{3,1},{4,6},{5,7},{6,4},{7,5},{8,10},{9,11},{10,... | collective-permute-start | bytes 196616 | tf_op jit(solution)/shard_map/ppermute | solution.py:340
  15.9 1.3 %collective-permute-start.12 = (f32[2,32,256]{2,1,0:T(8,128)S(1)}, f32[2,32,256]{2,1,0:T(8,128)S(1)}, u32[]{:S(2)}, u32[]{:S(2)}) collective-permute-start(f32[2,32,256]{2,1,0:T(8,128)S(1)} %slice_bitcast_fusion), channel_id=1, source_target_pairs={{0,3},{1,2},{2,1},{3,0},{4,7},{5,6},{6,5},{7,4},{8,11},{9,10},{10,... | collective-permute-start | bytes 196616 | tf_op jit(solution)/shard_map/ppermute | solution.py:340
  17.4 1.2 %collective-permute-done.9.refs_11_ = f32[128,128]{1,0:T(8,128)S(1)} collective-permute-done((f32[128,128]{1,0:T(8,128)S(1)}, f32[128,128]{1,0:T(8,128)S(1)}, u32[]{:S(2)}, u32[]{:S(2)}) %collective-permute-start.9) | collective-permute-done | bytes 65568 | tf_op jit(solution)/shard_map/ppermute | solution.py:324
  18.6 4.3 %shard_map.28 = (f32[1,384,384]{2,1,0:T(8,128)S(1)}, f32[384,128]{1,0:T(8,128)S(1)}, f32[256,128]{1,0:T(8,128)S(1)}, f32[128,128]{1,0:T(8,128)S(1)}) custom-call(s32[3]{0:T(128)S(1)} %pad_add_fusion.place_ref, f32[3,32,256]{2,1,0:T(8,128)S(1)} %broadcast_select_fusion.refs_0_, f32[3,32,256]{2,1,0:T(8,128)S(1)} %collective-permute-done.refs_1_, ...), custom_call_target="tpu_custom_call" | custom-call | tf_op jit(solution)/shard_map/pallas_call | solution.py:262
  23.5 1.5 %collective-permute-start.10 = (f32[256,128]{1,0:T(8,128)S(1)}, f32[256,128]{1,0:T(8,128)S(1)}, u32[]{:S(2)}, u32[]{:S(2)}) collective-permute-start(f32[256,128]{1,0:T(8,128)S(1)} %get-tuple-element.30), channel_id=1, source_target_pairs={{0,8},{4,20},{8,0},{12,28},{16,24},{20,4},{24,16},{28,12},{1,9},{5... | collective-permute-start | bytes 393224 | tf_op jit(solution)/shard_map/ppermute | solution.py:324
  25.0 1.3 %collective-permute-start.15 = (f32[128,128]{1,0:T(8,128)S(1)}, f32[128,128]{1,0:T(8,128)S(1)}, u32[]{:S(2)}, u32[]{:S(2)}) collective-permute-start(f32[128,128]{1,0:T(8,128)S(1)} %get-tuple-element.38), channel_id=1, source_target_pairs={{0,24},{4,28},{8,16},{12,20},{16,8},{20,12},{24,0},{28,4},{1,25},{... | collective-permute-start | bytes 196616 | tf_op jit(solution)/shard_map/ppermute | solution.py:324
  26.2 4.9 %shard_map.29 = (f32[2,384,384]{2,1,0:T(8,128)S(1)}, f32[256,128]{1,0:T(8,128)S(1)}, f32[128,128]{1,0:T(8,128)S(1)}) custom-call(s32[3]{0:T(128)S(1)} %pad_add_fusion.place_ref, f32[3,32,256]{2,1,0:T(8,128)S(1)} %broadcast_select_fusion.refs_0_, f32[3,32,256]{2,1,0:T(8,128)S(1)} %collective-permute-done.refs_1_, ...), custom_call_target="tpu_custom_call" | custom-call | flops 1811939328 | tf_op jit(solution)/shard_map/pallas_call | solution.py:262
  32.2 1.5 %collective-permute-start.21 = (f32[128,128]{1,0:T(8,128)S(1)}, f32[128,128]{1,0:T(8,128)S(1)}, u32[]{:S(2)}, u32[]{:S(2)}) collective-permute-start(f32[128,128]{1,0:T(8,128)S(1)} %get-tuple-element.45), channel_id=1, source_target_pairs={{0,24},{4,28},{8,16},{12,20},{16,8},{20,12},{24,0},{28,4},{1,25},{... | collective-permute-start | bytes 196616 | tf_op jit(solution)/shard_map/ppermute | solution.py:324
  33.7 1.6 %shard_map.30 = (f32[384,128]{1,0:T(8,128)S(1)}, f32[128,128]{1,0:T(8,128)S(1)}, f32[64,128]{1,0:T(8,128)S(1)}) custom-call(s32[3]{0:T(128)S(1)} %pad_add_fusion.place_ref, f32[256,128]{1,0:T(8,128)S(1)} %collective-permute-done.10.refs_0_, f32[128,128]{1,0:T(8,128)S(1)} %collective-permute-done.15.refs_1_, f32[256,128]{1,0:T(8,128)S(1)} %collective-permute-done.16.refs_2_, ...), custom_call_target="tpu_custom_call" | custom-call | tf_op jit(solution)/shard_map/pallas_call | solution.py:262
  35.3 1.5 %collective-permute-start.19 = (f32[64,128]{1,0:T(8,128)S(1)}, f32[64,128]{1,0:T(8,128)S(1)}, u32[]{:S(2)}, u32[]{:S(2)}) collective-permute-start(f32[64,128]{1,0:T(8,128)S(1)} %get-tuple-element.43), channel_id=1, source_target_pairs={{0,24},{4,28},{8,16},{12,20},{16,8},{20,12},{24,0},{28,4},{1,25},{... | collective-permute-start | bytes 98312 | tf_op jit(solution)/shard_map/ppermute | solution.py:324
  36.8 1.5 %collective-permute-start.18 = (f32[128,128]{1,0:T(8,128)S(1)}, f32[128,128]{1,0:T(8,128)S(1)}, u32[]{:S(2)}, u32[]{:S(2)}) collective-permute-start(f32[128,128]{1,0:T(8,128)S(1)} %get-tuple-element.42), channel_id=1, source_target_pairs={{0,8},{4,20},{8,0},{12,28},{16,24},{20,4},{24,16},{28,12},{1,9},{5... | collective-permute-start | bytes 196616 | tf_op jit(solution)/shard_map/ppermute | solution.py:324
  38.3 2.0 %collective-permute-done.19.refs_1_ = f32[64,128]{1,0:T(8,128)S(1)} collective-permute-done((f32[64,128]{1,0:T(8,128)S(1)}, f32[64,128]{1,0:T(8,128)S(1)}, u32[]{:S(2)}, u32[]{:S(2)}) %collective-permute-start.19) | collective-permute-done | bytes 32800 | tf_op jit(solution)/shard_map/ppermute | solution.py:324
  42.5 1.6 %shard_map.31 = (f32[384,128]{1,0:T(8,128)S(1)}, f32[128,128]{1,0:T(8,128)S(1)}, f32[64,128]{1,0:T(8,128)S(1)}) custom-call(s32[3]{0:T(128)S(1)} %pad_add_fusion.place_ref, f32[128,128]{1,0:T(8,128)S(1)} %collective-permute-done.18.refs_0_, f32[64,128]{1,0:T(8,128)S(1)} %collective-permute-done.19.refs_1_, f32[128,128]{1,0:T(8,128)S(1)} %collective-permute-done.22.refs_2_, ...), custom_call_target="tpu_custom_call" | custom-call | tf_op jit(solution)/shard_map/pallas_call | solution.py:262
  44.1 1.6 %collective-permute-start.26 = (f32[128,128]{1,0:T(8,128)S(1)}, f32[128,128]{1,0:T(8,128)S(1)}, u32[]{:S(2)}, u32[]{:S(2)}) collective-permute-start(f32[128,128]{1,0:T(8,128)S(1)} %get-tuple-element.50), channel_id=1, source_target_pairs={{0,8},{4,20},{8,0},{12,28},{16,24},{20,4},{24,16},{28,12},{1,9},{5... | collective-permute-start | bytes 196616 | tf_op jit(solution)/shard_map/ppermute | solution.py:324
  45.6 1.3 %collective-permute-start.27 = (f32[64,128]{1,0:T(8,128)S(1)}, f32[64,128]{1,0:T(8,128)S(1)}, u32[]{:S(2)}, u32[]{:S(2)}) collective-permute-start(f32[64,128]{1,0:T(8,128)S(1)} %get-tuple-element.51), channel_id=1, source_target_pairs={{0,24},{4,28},{8,16},{12,20},{16,8},{20,12},{24,0},{28,4},{1,25},{... | collective-permute-start | bytes 98312 | tf_op jit(solution)/shard_map/ppermute | solution.py:324
  46.9 1.7 %collective-permute-done.26.refs_0_ = f32[128,128]{1,0:T(8,128)S(1)} collective-permute-done((f32[128,128]{1,0:T(8,128)S(1)}, f32[128,128]{1,0:T(8,128)S(1)}, u32[]{:S(2)}, u32[]{:S(2)}) %collective-permute-start.26) | collective-permute-done | bytes 65568 | tf_op jit(solution)/shard_map/ppermute | solution.py:324
  48.6 1.8 %collective-permute-done.27.refs_1_ = f32[64,128]{1,0:T(8,128)S(1)} collective-permute-done((f32[64,128]{1,0:T(8,128)S(1)}, f32[64,128]{1,0:T(8,128)S(1)}, u32[]{:S(2)}, u32[]{:S(2)}) %collective-permute-start.27) | collective-permute-done | bytes 32800 | tf_op jit(solution)/shard_map/ppermute | solution.py:324
  50.4 1.2 %collective-permute-done.29.refs_3_ = f32[64,128]{1,0:T(8,128)S(1)} collective-permute-done((f32[64,128]{1,0:T(8,128)S(1)}, f32[64,128]{1,0:T(8,128)S(1)}, u32[]{:S(2)}, u32[]{:S(2)}) %collective-permute-start.29) | collective-permute-done | bytes 32800 | tf_op jit(solution)/shard_map/ppermute | solution.py:327
  51.6 1.7 %shard_map.32 = f32[128,128]{1,0:T(8,128)} custom-call(s32[3]{0:T(128)S(1)} %pad_add_fusion.place_ref, f32[128,128]{1,0:T(8,128)S(1)} %collective-permute-done.26.refs_0_, f32[64,128]{1,0:T(8,128)S(1)} %collective-permute-done.27.refs_1_, f32[128,128]{1,0:T(8,128)S(1)} %collective-permute-done.28.refs_2_, f32[64,128]{1,0:T(8,128)S(1)} %collective-permute-done.29.refs_3_, ...), custom_call_target="tpu_custom_call" | custom-call | tf_op jit(solution)/shard_map/pallas_call | solution.py:262
  (46 shorter events, 8.1 us)
Async XLA Ops:
  0.8 7.9 %collective-permute-start.1 = (f32[1,32,256]{2,1,0:T(8,128)S(1)}, f32[1,32,256]{2,1,0:T(8,128)S(1)}, u32[]{:S(2)}, u32[]{:S(2)}) collective-permute-start(f32[1,32,256]{2,1,0:T(8,128)S(1)} %slice_bitcast_fusion.1), channel_id=1, source_target_pairs={{0,2},{1,3},{2,0},{3,1},{4,6},{5,7},{6,4},{7,5},{8,10},{9,11},{10,... | collective-permute-start | bytes 98312 | tf_op jit(solution)/shard_map/ppermute | solution.py:340
  4.8 6.0 %collective-permute-start.2 = (f32[1,32,256]{2,1,0:T(8,128)S(1)}, f32[1,32,256]{2,1,0:T(8,128)S(1)}, u32[]{:S(2)}, u32[]{:S(2)}) collective-permute-start(f32[1,32,256]{2,1,0:T(8,128)S(1)} %slice_bitcast_fusion.1), channel_id=1, source_target_pairs={{0,3},{1,2},{2,1},{3,0},{4,7},{5,6},{6,5},{7,4},{8,11},{9,10},{10,... | collective-permute-start | bytes 98312 | tf_op jit(solution)/shard_map/ppermute | solution.py:340
  6.1 9.8 %collective-permute-start = (f32[3,32,256]{2,1,0:T(8,128)}, f32[3,32,256]{2,1,0:T(8,128)S(1)}, u32[]{:S(2)}, u32[]{:S(2)}) collective-permute-start(f32[3,32,256]{2,1,0:T(8,128)} %bitcast.10), channel_id=1, source_target_pairs={{0,1},{1,0},{2,3},{3,2},{4,5},{5,4},{6,7},{7,6},{8,9},{9,8},{10,11... | collective-permute-start | bytes 294920 | tf_op jit(solution)/shard_map/ppermute | solution.py:340
  6.4 10.9 %collective-permute-start.3 = (f32[3,32,256]{2,1,0:T(8,128)}, f32[3,32,256]{2,1,0:T(8,128)S(1)}, u32[]{:S(2)}, u32[]{:S(2)}) collective-permute-start(f32[3,32,256]{2,1,0:T(8,128)} %bitcast.11), channel_id=1, source_target_pairs={{0,4},{4,0},{8,12},{12,8},{16,20},{20,16},{24,28},{28,24},{1,5},{5... | collective-permute-start | bytes 294920 | tf_op jit(solution)/shard_map/ppermute | solution.py:327
  6.4 4.4 %collective-permute-start.7 = (f32[128,128]{1,0:T(8,128)}, f32[128,128]{1,0:T(8,128)S(1)}, u32[]{:S(2)}, u32[]{:S(2)}) collective-permute-start(f32[128,128]{1,0:T(8,128)} %param.2), channel_id=1, source_target_pairs={{0,4},{4,0},{8,12},{12,8},{16,20},{20,16},{24,28},{28,24},{1,5},{5... | collective-permute-start | bytes 196616 | tf_op jit(solution)/shard_map/ppermute | solution.py:327
  8.6 4.5 %collective-permute-start.5 = (f32[1,32,256]{2,1,0:T(8,128)S(1)}, f32[1,32,256]{2,1,0:T(8,128)S(1)}, u32[]{:S(2)}, u32[]{:S(2)}) collective-permute-start(f32[1,32,256]{2,1,0:T(8,128)S(1)} %collective-permute-done.1.refs_2_), channel_id=1, source_target_pairs={{0,4},{4,0},{8,12},{12,8},{16,20},{20,16},{24,28},{28,24},{1,5},{5... | collective-permute-start | bytes 98312 | tf_op jit(solution)/shard_map/ppermute | solution.py:327
  10.8 3.9 %collective-permute-start.6 = (f32[1,32,256]{2,1,0:T(8,128)S(1)}, f32[1,32,256]{2,1,0:T(8,128)S(1)}, u32[]{:S(2)}, u32[]{:S(2)}) collective-permute-start(f32[1,32,256]{2,1,0:T(8,128)S(1)} %collective-permute-done.2.refs_3_), channel_id=1, source_target_pairs={{0,4},{4,0},{8,12},{12,8},{16,20},{20,16},{24,28},{28,24},{1,5},{5... | collective-permute-start | bytes 98312 | tf_op jit(solution)/shard_map/ppermute | solution.py:327
  11.6 5.7 %collective-permute-start.8 = (f32[128,128]{1,0:T(8,128)S(1)}, f32[128,128]{1,0:T(8,128)S(1)}, u32[]{:S(2)}, u32[]{:S(2)}) collective-permute-start(f32[128,128]{1,0:T(8,128)S(1)} %get-tuple-element.54.refs_8_), channel_id=1, source_target_pairs={{0,8},{4,12},{8,0},{12,4},{16,24},{20,28},{24,16},{28,20},{1,9},{5... | collective-permute-start | bytes 196616 | tf_op jit(solution)/shard_map/ppermute | solution.py:324
  13.2 5.4 %collective-permute-start.9 = (f32[128,128]{1,0:T(8,128)S(1)}, f32[128,128]{1,0:T(8,128)S(1)}, u32[]{:S(2)}, u32[]{:S(2)}) collective-permute-start(f32[128,128]{1,0:T(8,128)S(1)} %get-tuple-element.54.refs_8_), channel_id=1, source_target_pairs={{0,24},{4,28},{8,16},{12,20},{16,8},{20,12},{24,0},{28,4},{1,25},{... | collective-permute-start | bytes 196616 | tf_op jit(solution)/shard_map/ppermute | solution.py:324
  14.7 8.2 %collective-permute-start.11 = (f32[2,32,256]{2,1,0:T(8,128)S(1)}, f32[2,32,256]{2,1,0:T(8,128)S(1)}, u32[]{:S(2)}, u32[]{:S(2)}) collective-permute-start(f32[2,32,256]{2,1,0:T(8,128)S(1)} %slice_bitcast_fusion), channel_id=1, source_target_pairs={{0,2},{1,3},{2,0},{3,1},{4,6},{5,7},{6,4},{7,5},{8,10},{9,11},{10,... | collective-permute-start | bytes 196616 | tf_op jit(solution)/shard_map/ppermute | solution.py:340
  15.9 7.0 %collective-permute-start.12 = (f32[2,32,256]{2,1,0:T(8,128)S(1)}, f32[2,32,256]{2,1,0:T(8,128)S(1)}, u32[]{:S(2)}, u32[]{:S(2)}) collective-permute-start(f32[2,32,256]{2,1,0:T(8,128)S(1)} %slice_bitcast_fusion), channel_id=1, source_target_pairs={{0,3},{1,2},{2,1},{3,0},{4,7},{5,6},{6,5},{7,4},{8,11},{9,10},{10,... | collective-permute-start | bytes 196616 | tf_op jit(solution)/shard_map/ppermute | solution.py:340
  22.9 3.3 %collective-permute-start.13 = (f32[2,32,256]{2,1,0:T(8,128)S(1)}, f32[2,32,256]{2,1,0:T(8,128)S(1)}, u32[]{:S(2)}, u32[]{:S(2)}) collective-permute-start(f32[2,32,256]{2,1,0:T(8,128)S(1)} %collective-permute-done.11.refs_2_), channel_id=1, source_target_pairs={{0,4},{4,0},{8,12},{12,8},{16,20},{20,16},{24,28},{28,24},{1,5},{5... | collective-permute-start | bytes 196616 | tf_op jit(solution)/shard_map/ppermute | solution.py:327
  23.1 3.1 %collective-permute-start.14 = (f32[2,32,256]{2,1,0:T(8,128)S(1)}, f32[2,32,256]{2,1,0:T(8,128)S(1)}, u32[]{:S(2)}, u32[]{:S(2)}) collective-permute-start(f32[2,32,256]{2,1,0:T(8,128)S(1)} %collective-permute-done.12.refs_3_), channel_id=1, source_target_pairs={{0,4},{4,0},{8,12},{12,8},{16,20},{20,16},{24,28},{28,24},{1,5},{5... | collective-permute-start | bytes 196616 | tf_op jit(solution)/shard_map/ppermute | solution.py:327
  23.5 7.7 %collective-permute-start.10 = (f32[256,128]{1,0:T(8,128)S(1)}, f32[256,128]{1,0:T(8,128)S(1)}, u32[]{:S(2)}, u32[]{:S(2)}) collective-permute-start(f32[256,128]{1,0:T(8,128)S(1)} %get-tuple-element.30), channel_id=1, source_target_pairs={{0,8},{4,20},{8,0},{12,28},{16,24},{20,4},{24,16},{28,12},{1,9},{5... | collective-permute-start | bytes 393224 | tf_op jit(solution)/shard_map/ppermute | solution.py:324
  25.0 7.1 %collective-permute-start.15 = (f32[128,128]{1,0:T(8,128)S(1)}, f32[128,128]{1,0:T(8,128)S(1)}, u32[]{:S(2)}, u32[]{:S(2)}) collective-permute-start(f32[128,128]{1,0:T(8,128)S(1)} %get-tuple-element.38), channel_id=1, source_target_pairs={{0,24},{4,28},{8,16},{12,20},{16,8},{20,12},{24,0},{28,4},{1,25},{... | collective-permute-start | bytes 196616 | tf_op jit(solution)/shard_map/ppermute | solution.py:324
  31.2 2.5 %collective-permute-start.16 = (f32[256,128]{1,0:T(8,128)S(1)}, f32[256,128]{1,0:T(8,128)S(1)}, u32[]{:S(2)}, u32[]{:S(2)}) collective-permute-start(f32[256,128]{1,0:T(8,128)S(1)} %collective-permute-done.10.refs_0_), channel_id=1, source_target_pairs={{0,4},{4,0},{8,12},{12,8},{16,20},{20,16},{24,28},{28,24},{1,5},{5... | collective-permute-start | bytes 393224 | tf_op jit(solution)/shard_map/ppermute | solution.py:327
  31.2 7.1 %collective-permute-start.20 = (f32[256,128]{1,0:T(8,128)S(1)}, f32[256,128]{1,0:T(8,128)S(1)}, u32[]{:S(2)}, u32[]{:S(2)}) collective-permute-start(f32[256,128]{1,0:T(8,128)S(1)} %get-tuple-element.44), channel_id=1, source_target_pairs={{0,8},{4,20},{8,0},{12,28},{16,24},{20,4},{24,16},{28,12},{1,9},{5... | collective-permute-start | bytes 393224 | tf_op jit(solution)/shard_map/ppermute | solution.py:324
  32.2 6.1 %collective-permute-start.21 = (f32[128,128]{1,0:T(8,128)S(1)}, f32[128,128]{1,0:T(8,128)S(1)}, u32[]{:S(2)}, u32[]{:S(2)}) collective-permute-start(f32[128,128]{1,0:T(8,128)S(1)} %get-tuple-element.45), channel_id=1, source_target_pairs={{0,24},{4,28},{8,16},{12,20},{16,8},{20,12},{24,0},{28,4},{1,25},{... | collective-permute-start | bytes 196616 | tf_op jit(solution)/shard_map/ppermute | solution.py:324
  35.3 5.0 %collective-permute-start.19 = (f32[64,128]{1,0:T(8,128)S(1)}, f32[64,128]{1,0:T(8,128)S(1)}, u32[]{:S(2)}, u32[]{:S(2)}) collective-permute-start(f32[64,128]{1,0:T(8,128)S(1)} %get-tuple-element.43), channel_id=1, source_target_pairs={{0,24},{4,28},{8,16},{12,20},{16,8},{20,12},{24,0},{28,4},{1,25},{... | collective-permute-start | bytes 98312 | tf_op jit(solution)/shard_map/ppermute | solution.py:324
  36.8 4.3 %collective-permute-start.18 = (f32[128,128]{1,0:T(8,128)S(1)}, f32[128,128]{1,0:T(8,128)S(1)}, u32[]{:S(2)}, u32[]{:S(2)}) collective-permute-start(f32[128,128]{1,0:T(8,128)S(1)} %get-tuple-element.42), channel_id=1, source_target_pairs={{0,8},{4,20},{8,0},{12,28},{16,24},{20,4},{24,16},{28,12},{1,9},{5... | collective-permute-start | bytes 196616 | tf_op jit(solution)/shard_map/ppermute | solution.py:324
  40.3 2.2 %collective-permute-start.24 = (f32[256,128]{1,0:T(8,128)S(1)}, f32[256,128]{1,0:T(8,128)S(1)}, u32[]{:S(2)}, u32[]{:S(2)}) collective-permute-start(f32[256,128]{1,0:T(8,128)S(1)} %collective-permute-done.20.refs_4_), channel_id=1, source_target_pairs={{0,4},{4,0},{8,12},{12,8},{16,20},{20,16},{24,28},{28,24},{1,5},{5... | collective-permute-start | bytes 393224 | tf_op jit(solution)/shard_map/ppermute | solution.py:327
  44.1 4.5 %collective-permute-start.26 = (f32[128,128]{1,0:T(8,128)S(1)}, f32[128,128]{1,0:T(8,128)S(1)}, u32[]{:S(2)}, u32[]{:S(2)}) collective-permute-start(f32[128,128]{1,0:T(8,128)S(1)} %get-tuple-element.50), channel_id=1, source_target_pairs={{0,8},{4,20},{8,0},{12,28},{16,24},{20,4},{24,16},{28,12},{1,9},{5... | collective-permute-start | bytes 196616 | tf_op jit(solution)/shard_map/ppermute | solution.py:324
  45.6 4.8 %collective-permute-start.27 = (f32[64,128]{1,0:T(8,128)S(1)}, f32[64,128]{1,0:T(8,128)S(1)}, u32[]{:S(2)}, u32[]{:S(2)}) collective-permute-start(f32[64,128]{1,0:T(8,128)S(1)} %get-tuple-element.51), channel_id=1, source_target_pairs={{0,24},{4,28},{8,16},{12,20},{16,8},{20,12},{24,0},{28,4},{1,25},{... | collective-permute-start | bytes 98312 | tf_op jit(solution)/shard_map/ppermute | solution.py:324
  48.6 3.0 %collective-permute-start.28 = (f32[128,128]{1,0:T(8,128)S(1)}, f32[128,128]{1,0:T(8,128)S(1)}, u32[]{:S(2)}, u32[]{:S(2)}) collective-permute-start(f32[128,128]{1,0:T(8,128)S(1)} %collective-permute-done.26.refs_0_), channel_id=1, source_target_pairs={{0,4},{4,0},{8,12},{12,8},{16,20},{20,16},{24,28},{28,24},{1,5},{5... | collective-permute-start | bytes 196616 | tf_op jit(solution)/shard_map/ppermute | solution.py:327
  (6 other events, 9.1 us)

commit v6 on v4

--- a/solution.py
+++ b/solution.py
@@ -151,23 +151,18 @@
     return jnp.where(core == 0, value[:rows], value[rows:])
 
 
-def assemble(place_ref, mine, theirs, groups, refl_ref):
-    core, vec = place_ref[1], place_ref[2]
-    rows = mine[0].shape[1]
-    for step, (own, other) in enumerate(zip(mine, theirs)):
-        at = pl.ds(pl.multiple_of((step ^ vec) * rows, rows), rows)
-        for slot, group in enumerate(groups):
-            refl_ref[core, slot, at, :] = own[group]
-            refl_ref[1 - core, slot, at, :] = other[group]
-
-
 def first_kernel(count, nodes, place_ref, *refs):
     mine, theirs = refs[:count], refs[count : 2 * count]
     top_ref, low_ref, near_ref, far_ref = refs[2 * count : 2 * count + 4]
     oper_ref, fixed_ref, out_near, out_far, refl_ref = refs[2 * count + 4 :]
     block = top_ref.shape[0]
-    node, core = place_ref[0], place_ref[1]
-    assemble(place_ref, mine, theirs, [0], refl_ref)
+    node, core, vec = place_ref[0], place_ref[1], place_ref[2]
+    groups, rows, _ = mine[0].shape
+    for step in range(count):
+        at = pl.ds(pl.multiple_of((step ^ vec) * rows, rows), rows)
+        for group in range(groups):
+            refl_ref[core, group, at, :] = mine[step][group]
+            refl_ref[1 - core, group, at, :] = theirs[step][group]
     pair_operators(refl_ref, node != nodes - 1, oper_ref)
     below = jnp.where((node & 1) == 0, near_ref[...], far_ref[...])
     window = jnp.concatenate(
@@ -186,16 +181,22 @@
     out_far[...] = jnp.where(core == 0, pick_far(node, fixed), pick_far(node, lead))
 
 
-def later_kernel(count, nodes, place_ref, *refs):
-    mine, theirs = refs[:count], refs[count : 2 * count]
-    oper_ref, map_near, map_far, refl_ref = refs[2 * count :]
+def between_kernel(group, place_ref, fixed_ref, oper_ref, base_ref, low_ref, *maps):
     node, core = place_ref[0], place_ref[1]
-    later, _, size = oper_ref.shape
-    assemble(place_ref, mine, theirs, range(1, 1 + later), refl_ref)
-    pair_operators(refl_ref, node != nodes - 1, oper_ref)
-    leads = [oper_ref[slot, :, : size // 3] for slot in range(later)]
-    map_near[...] = jnp.concatenate([pick_near(node, core, lead) for lead in leads], 0)
-    map_far[...] = half_of(core, jnp.concatenate([pick_far(node, lead) for lead in leads], 0))
+    groups, size, _ = oper_ref.shape
+    block = size // 3
+    own = slice(block, 2 * block)
+    first = jnp.where(node == 0, fixed_ref[:block], 0.0)
+    base_ref[...] = mm(
+        oper_ref[group + 1, :, : 2 * block], jnp.concatenate([first, fixed_ref[own]], 0)
+    )
+    low_ref[...] = mm(oper_ref[group + 1, :, own], oper_ref[group, own, :block])
+    if maps:
+        leads = [oper_ref[later, :, :block] for later in range(1, groups)]
+        maps[0][...] = jnp.concatenate([pick_near(node, core, lead) for lead in leads], 0)
+        maps[1][...] = half_of(
+            core, jnp.concatenate([pick_far(node, lead) for lead in leads], 0)
+        )
 
 
 def next_kernel(group, place_ref, *refs):
@@ -221,39 +222,33 @@
         map3 = jnp.concatenate(
             [jnp.where(here, mfar, mfar2), jnp.where(here, mfar2, mfar)], 0
         )[at]
-    (fixed_ref, first_ref, later_ref), outs = refs[:3], refs[3:]
-    oper = first_ref.at[0] if group == 0 else later_ref.at[group - 1]
+    fixed_ref, oper_ref, refs = refs[0], refs[1], refs[2:]
     carry = jnp.where(high, jnp.where(odd, came3, came2), came1)
     carry = jnp.where(node == 0, 0.0, carry)
     step = jnp.where(odd, came2, came3) + mm(jnp.where(odd, map2, map3), carry)
     carry = jnp.where(high, step, carry)
     step = came1 + mm(map1, carry)
     carry = jnp.where(node == 3, step, carry)
-    if len(outs) == 1:
+    if len(refs) == 1:
         at = pl.ds(pl.multiple_of(core * block, block), block)
-        outs[0][...] = fixed_ref[at, :] + mm(oper[at, :block], carry)
+        refs[0][...] = fixed_ref[at, :] + mm(oper_ref[group, at, :block], carry)
         return
-    fixed, lead = fixed_ref[...], oper[:, :block]
-    cols = fixed.shape[1]
-    below = mm(
-        jnp.where(odd, map3, map1), jnp.concatenate([fixed[2 * block :], lead[2 * block :]], 1)
-    )
-    offset = jnp.where(odd, came3, came1)
-    below = jnp.where(node == 3, 0.0, below + jnp.concatenate([offset, jnp.zeros_like(lead[:block])], 1))
-    first = jnp.where(node == 0, fixed[:block], 0.0)
-    window = jnp.concatenate(
-        [
-            jnp.concatenate([first, jnp.zeros_like(lead[:block])], 1),
-            jnp.concatenate([fixed[block : 2 * block], lead[block : 2 * block]], 1),
-            below,
-        ],
-        0,
-    )
-    moved = mm(later_ref[group], window)
-    fixed = moved[:, :cols] + mm(moved[:, cols:], carry)
-    outs[0][...] = fixed
-    outs[1][...] = pick_near(node, core, fixed)
-    outs[2][...] = half_of(core, pick_far(node, fixed))
+    base_ref, low_ref, out_fixed, out_near, out_far = refs
+    cols = fixed_ref.shape[1]
+    out = slice(2 * block, 3 * block)
+    reach = mm(
+        jnp.where(odd, map3, map1),
+        jnp.concatenate([fixed_ref[out], oper_ref[group, out, :block]], 1),
+    )
+    below = jnp.where(odd, came3, came1) + reach[:, :cols] + mm(reach[:, cols:], carry)
+    below = jnp.where(node == 3, 0.0, below)
+    fixed = base_ref[...] + mm(
+        jnp.concatenate([oper_ref[group + 1, :, out], low_ref[...]], 1),
+        jnp.concatenate([below, carry], 0),
+    )
+    out_fixed[...] = fixed
+    out_near[...] = pick_near(node, core, fixed)
+    out_far[...] = half_of(core, pick_far(node, fixed))
 
 
 def call(kernel, outs, operands, scratch=(), work=0):
@@ -284,7 +279,7 @@
 
 
 def many_pairs(fixed, operators, node, nodes, row_count):
-    groups, block = len(operators), fixed.shape[0] // 3
+    groups, block = operators.shape[0], fixed.shape[0] // 3
     members = [[place * PAIR + core for place in range(nodes)] for core in range(PAIR)]
     for group in range(groups):
         lead = operators[group][:, :block]
@@ -350,57 +345,44 @@
     theirs = [across(piece) for piece in mine]
     mine[0] = jnp.where(vec_index < 0, 0.0, mine[0])
     place = jnp.stack([node, core, vec_index if mixed else 0]).astype(jnp.int32)
-    later = groups - 1
-    work = 16 * (3 * block) ** 3
-    pieces = [place, *mine, *theirs]
-    first_oper, fixed, near, far = call(
+    later = (groups - 1) * block
+    size = 3 * block
+    operators, fixed, near, far = call(
         functools.partial(first_kernel, len(mine), nodes),
-        [
-            (1, 3 * block, 3 * block),
-            (3 * block, cols),
-            (2 * block, cols),
-            (block, cols),
-        ],
-        [*pieces, top, low, *below],
-        [pltpu.VMEM((PAIR, 1, block, window), F32)],
-        work,
-    )
-    later_oper, *maps = call(
-        functools.partial(later_kernel, len(mine), nodes),
-        [
-            (later, 3 * block, 3 * block),
-            (later * block, block),
-            (later * block // PAIR, block),
-        ],
-        pieces,
-        [pltpu.VMEM((PAIR, later, block, window), F32)],
-        work * later,
+        [(groups, size, size), (size, cols), (2 * block, cols), (block, cols)],
+        [place, *mine, *theirs, top, low, *below],
+        [pltpu.VMEM((PAIR, groups, block, window), F32)],
     )
     if nodes != 4:
-        operators = [first_oper[0]] + [later_oper[slot] for slot in range(later)]
         result = many_pairs(fixed, operators, node, nodes, row_count)
         return jnp.where(core == 0, result[:block], result[block : 2 * block])
     hold = lax.optimization_barrier
+    maps = []
     for group in range(groups):
+        last_group = group == groups - 1
         near = swap(near, (1, 2))
         far = swap(far, (3, 3))
-        if group == 0:
-            near, *maps = hold((near, *maps))
-            maps = [swap(maps[0], (1, 2)), swap(maps[1], (3, 3))]
-        elif group == 1:
+        if not last_group:
+            shapes = [(later, block), (later // PAIR, block)] if group == 0 else []
+            base, onto, *sent = call(
+                functools.partial(between_kernel, group),
+                [(size, cols), (size, block), *shapes],
+                [place, fixed, operators],
+                work=4 * size * size * cols,
+            )
+        if group == 1:
             far, *maps = hold((far, *maps))
             maps += [across(part) for part in maps]
-        came = [near, far, across(near), across(far)]
-        operands = [place, *came, *(maps if group else []), fixed, first_oper, later_oper]
-        if group < groups - 1:
+        operands = [place, near, far, across(near), across(far), *maps, fixed, operators]
+        if group == 0:
+            maps = [swap(sent[0], (1, 2)), swap(sent[1], (3, 3))]
+        if last_group:
+            (result,) = call(functools.partial(next_kernel, group), [(block, cols)], operands)
+        else:
             fixed, near, far = call(
                 functools.partial(next_kernel, group),
-                [(3 * block, cols), (block, cols), (block // PAIR, cols)],
-                operands,
-            )
-        else:
-            (result,) = call(
-                functools.partial(next_kernel, group), [(block, cols)], operands
+                [(size, cols), (block, cols), (block // PAIR, cols)],
+                [*operands, base, onto],
             )
     return result
 

time: 49.9 us -> 51.3 us (1.028)
  starting transfers between devices: 21.6 us -> 23.1 us
  Pallas kernels: 14.1 us -> 12.8 us
  waiting for transfers between devices: 12.2 us -> 13.3 us
    ppermute x10, waiting for transfers between devices: 7.18 us -> 9.43 us  [swap(): return lax.ppermute(value, 'rows', moves)]
    ppermute x10, starting transfers between devices: 13.7 us -> 15.1 us  [swap(): return lax.ppermute(value, 'rows', moves)]
    pallas_call x5 -> x6, Pallas kernels: 14.1 us -> 12.8 us  [call(): pl.pallas_call(kernel, out_shape=[jax.ShapeDtypeStruct(shape, F32) for sh...]
    ppermute x13, waiting for transfers between devices: 2.7 us -> 1.69 us  [across(): lax.ppermute(value, 'rows', [(place, place ^ 1) for place in range(row_co...]
  transfers between devices with their start and end apart: 26 -> 26, of which waited for: 11 -> 10; matrix products, arithmetic and copies ran while one was open for 4% -> 4% of each run, Pallas kernels for 13% -> 7%
where the time goes in v6:
time: 51.3 us; the launch traced here: 51.1 us
  starting transfers between devices  23.1 us (45%)
  waiting for transfers between devices  13.3 us (26%)
  Pallas kernels  12.8 us (25%)
  other arithmetic  1.83 us (4%)
    ppermute x10, starting transfers between devices, swap(): return lax.ppermute(value, 'rows', moves)  15.1 us
    pallas_call x6, Pallas kernels, call(): pl.pallas_call(kernel, out_shape=[jax.ShapeDtypeStruct(shape, F32) for sh...  12.8 us
    ppermute x10, waiting for transfers between devices, swap(): return lax.ppermute(value, 'rows', moves)  9.43 us
    ppermute x3, starting transfers between devices, spread(): lax.ppermute(value, axis, [(place, place ^ mask) for place in range(size)])  5.62 us
    ppermute x13, starting transfers between devices, across(): lax.ppermute(value, 'rows', [(place, place ^ 1) for place in range(row_co...  2.37 us
    ppermute x3, waiting for transfers between devices, spread(): lax.ppermute(value, axis, [(place, place ^ mask) for place in range(size)])  2.16 us
    ppermute x13, waiting for transfers between devices, across(): lax.ppermute(value, 'rows', [(place, place ^ 1) for place in range(row_co...  1.69 us
  transfers between devices with their start and end apart: 26, of which 10 were waited for; matrix products, arithmetic and copies ran while one was open for 4% of the time, Pallas kernels for 7%

profile of v6, /device:TPU:0, one launch (start us, length us, event | category | flops | bytes accessed | tf_op | source)
XLA Modules:
  0.0 51.1 jit_solution(18239726343045867128)
XLA Ops:
  0.0 5.0 %collective-permute-start.2 = (f32[3,32,256]{2,1,0:T(8,128)}, f32[3,32,256]{2,1,0:T(8,128)S(1)}, u32[]{:S(2)}, u32[]{:S(2)}) collective-permute-start(f32[3,32,256]{2,1,0:T(8,128)} %bitcast.5), channel_id=1, source_target_pairs={{0,3},{1,2},{2,1},{3,0},{4,7},{5,6},{6,5},{7,4},{8,11},{9,10},{10,... | collective-permute-start | bytes 294920 | tf_op jit(solution)/shard_map/ppermute | solution.py:276
  6.1 0.9 %broadcast_select_fusion.refs_0_ = f32[3,32,256]{2,1,0:T(8,128)S(1)} fusion(pred[]{:T(512)S(6)} %lt.10, f32[3,1,32,256]{3,2,1,0:T(8,128)} %param.3), kind=kLoop, calls=%fused_computation | loop fusion | flops 24576 | bytes 196609 | tf_op jit(solution)/shard_map/jit(_where)/select_n | solution.py:346
  8.1 2.7 %collective-permute-start.9 = (f32[128,128]{1,0:T(8,128)S(1)}, f32[128,128]{1,0:T(8,128)S(1)}, u32[]{:S(2)}, u32[]{:S(2)}) collective-permute-start(f32[128,128]{1,0:T(8,128)S(1)} %get-tuple-element.44.refs_8_), channel_id=1, source_target_pairs={{0,24},{4,28},{8,16},{12,20},{16,8},{20,12},{24,0},{28,4},{1,25},{... | collective-permute-start | bytes 196616 | tf_op jit(solution)/shard_map/ppermute | solution.py:328
  11.4 2.2 %collective-permute-done.1.refs_2_ = f32[3,32,256]{2,1,0:T(8,128)S(1)} collective-permute-done((f32[3,32,256]{2,1,0:T(8,128)}, f32[3,32,256]{2,1,0:T(8,128)S(1)}, u32[]{:S(2)}, u32[]{:S(2)}) %collective-permute-start.1) | collective-permute-done | bytes 98336 | tf_op jit(solution)/shard_map/ppermute | solution.py:276
  14.2 0.9 %collective-permute-done.8.refs_10_ = f32[128,128]{1,0:T(8,128)S(1)} collective-permute-done((f32[128,128]{1,0:T(8,128)S(1)}, f32[128,128]{1,0:T(8,128)S(1)}, u32[]{:S(2)}, u32[]{:S(2)}) %collective-permute-start.8) | collective-permute-done | bytes 65568 | tf_op jit(solution)/shard_map/ppermute | solution.py:328
  15.3 6.3 %shard_map.28 = (f32[3,384,384]{2,1,0:T(8,128)S(1)}, f32[384,128]{1,0:T(8,128)S(1)}, f32[256,128]{1,0:T(8,128)S(1)}, f32[128,128]{1,0:T(8,128)S(1)}) custom-call(s32[3]{0:T(128)S(1)} %pad_add_fusion.place_ref, f32[3,32,256]{2,1,0:T(8,128)S(1)} %broadcast_select_fusion.refs_0_, f32[3,32,256]{2,1,0:T(8,128)S(1)} %collective-permute-done.refs_1_, ...), custom_call_target="tpu_custom_call" | custom-call | tf_op jit(solution)/shard_map/pallas_call | solution.py:256
  21.7 1.6 %collective-permute-start.10 = (f32[256,128]{1,0:T(8,128)S(1)}, f32[256,128]{1,0:T(8,128)S(1)}, u32[]{:S(2)}, u32[]{:S(2)}) collective-permute-start(f32[256,128]{1,0:T(8,128)S(1)} %get-tuple-element.24), channel_id=1, source_target_pairs={{0,8},{4,20},{8,0},{12,28},{16,24},{20,4},{24,16},{28,12},{1,9},{5... | collective-permute-start | bytes 393224 | tf_op jit(solution)/shard_map/ppermute | solution.py:328
  23.2 1.5 %collective-permute-start.11 = (f32[128,128]{1,0:T(8,128)S(1)}, f32[128,128]{1,0:T(8,128)S(1)}, u32[]{:S(2)}, u32[]{:S(2)}) collective-permute-start(f32[128,128]{1,0:T(8,128)S(1)} %get-tuple-element.25), channel_id=1, source_target_pairs={{0,24},{4,28},{8,16},{12,20},{16,8},{20,12},{24,0},{28,4},{1,25},{... | collective-permute-start | bytes 196616 | tf_op jit(solution)/shard_map/ppermute | solution.py:328
  24.7 2.7 %collective-permute-done.10.refs_0_ = f32[256,128]{1,0:T(8,128)S(1)} collective-permute-done((f32[256,128]{1,0:T(8,128)S(1)}, f32[256,128]{1,0:T(8,128)S(1)}, u32[]{:S(2)}, u32[]{:S(2)}) %collective-permute-start.10) | collective-permute-done | bytes 131104 | tf_op jit(solution)/shard_map/ppermute | solution.py:328
  27.4 1.0 %shard_map.29 = (f32[384,128]{1,0:T(8,128)S(1)}, f32[384,128]{1,0:T(8,128)S(1)}, f32[256,128]{1,0:T(8,128)S(1)}, f32[128,128]{1,0:T(8,128)S(1)}) custom-call(s32[3]{0:T(128)S(1)} %pad_add_fusion.place_ref, f32[384,128]{1,0:T(8,128)S(1)} %get-tuple-element.26.fixed_ref.refs_4_, f32[3,384,384]{2,1,0:T(8,128)S(1)} %get-tuple-element.27.oper_ref.refs_5_.refs_9_), custom_call_target="tpu_custom_call" | custom-call | flops 75497472 | tf_op jit(solution)/shard_map/pallas_call | solution.py:256
  28.4 1.6 %collective-permute-start.16 = (f32[256,128]{1,0:T(8,128)S(1)}, f32[256,128]{1,0:T(8,128)S(1)}, u32[]{:S(2)}, u32[]{:S(2)}) collective-permute-start(f32[256,128]{1,0:T(8,128)S(1)} %get-tuple-element.32), channel_id=1, source_target_pairs={{0,8},{4,20},{8,0},{12,28},{16,24},{20,4},{24,16},{28,12},{1,9},{5... | collective-permute-start | bytes 393224 | tf_op jit(solution)/shard_map/ppermute | solution.py:328
  30.2 1.4 %collective-permute-start.17 = (f32[128,128]{1,0:T(8,128)S(1)}, f32[128,128]{1,0:T(8,128)S(1)}, u32[]{:S(2)}, u32[]{:S(2)}) collective-permute-start(f32[128,128]{1,0:T(8,128)S(1)} %get-tuple-element.33), channel_id=1, source_target_pairs={{0,24},{4,28},{8,16},{12,20},{16,8},{20,12},{24,0},{28,4},{1,25},{... | collective-permute-start | bytes 196616 | tf_op jit(solution)/shard_map/ppermute | solution.py:328
  31.7 1.4 %shard_map.30 = (f32[384,128]{1,0:T(8,128)S(1)}, f32[128,128]{1,0:T(8,128)S(1)}, f32[64,128]{1,0:T(8,128)S(1)}) custom-call(s32[3]{0:T(128)S(1)} %pad_add_fusion.place_ref, f32[256,128]{1,0:T(8,128)S(1)} %collective-permute-done.10.refs_0_, f32[128,128]{1,0:T(8,128)S(1)} %collective-permute-done.11.refs_1_, f32[256,128]{1,0:T(8,128)S(1)} %collective-permute-done.12.refs_2_, ...), custom_call_target="tpu_custom_call" | custom-call | tf_op jit(solution)/shard_map/pallas_call | solution.py:256
  33.1 1.6 %collective-permute-start.15 = (f32[64,128]{1,0:T(8,128)S(1)}, f32[64,128]{1,0:T(8,128)S(1)}, u32[]{:S(2)}, u32[]{:S(2)}) collective-permute-start(f32[64,128]{1,0:T(8,128)S(1)} %get-tuple-element.31), channel_id=1, source_target_pairs={{0,24},{4,28},{8,16},{12,20},{16,8},{20,12},{24,0},{28,4},{1,25},{... | collective-permute-start | bytes 98312 | tf_op jit(solution)/shard_map/ppermute | solution.py:328
  34.6 1.5 %collective-permute-start.14 = (f32[128,128]{1,0:T(8,128)S(1)}, f32[128,128]{1,0:T(8,128)S(1)}, u32[]{:S(2)}, u32[]{:S(2)}) collective-permute-start(f32[128,128]{1,0:T(8,128)S(1)} %get-tuple-element.30), channel_id=1, source_target_pairs={{0,8},{4,20},{8,0},{12,28},{16,24},{20,4},{24,16},{28,12},{1,9},{5... | collective-permute-start | bytes 196616 | tf_op jit(solution)/shard_map/ppermute | solution.py:328
  36.1 1.9 %collective-permute-done.15.refs_1_ = f32[64,128]{1,0:T(8,128)S(1)} collective-permute-done((f32[64,128]{1,0:T(8,128)S(1)}, f32[64,128]{1,0:T(8,128)S(1)}, u32[]{:S(2)}, u32[]{:S(2)}) %collective-permute-start.15) | collective-permute-done | bytes 32800 | tf_op jit(solution)/shard_map/ppermute | solution.py:328
  39.4 1.0 %shard_map.31 = (f32[384,128]{1,0:T(8,128)S(1)}, f32[384,128]{1,0:T(8,128)S(1)}) custom-call(s32[3]{0:T(128)S(1)} %pad_add_fusion.place_ref, f32[384,128]{1,0:T(8,128)S(1)} %get-tuple-element.37.fixed_ref.refs_8_, f32[3,384,384]{2,1,0:T(8,128)S(1)} %get-tuple-element.27.oper_ref.refs_5_.refs_9_), custom_call_target="tpu_custom_call" | custom-call | flops 75497472 | tf_op jit(solution)/shard_map/pallas_call | solution.py:256
  40.4 1.4 %shard_map.32 = (f32[384,128]{1,0:T(8,128)S(1)}, f32[128,128]{1,0:T(8,128)S(1)}, f32[64,128]{1,0:T(8,128)S(1)}) custom-call(s32[3]{0:T(128)S(1)} %pad_add_fusion.place_ref, f32[128,128]{1,0:T(8,128)S(1)} %collective-permute-done.14.refs_0_, f32[64,128]{1,0:T(8,128)S(1)} %collective-permute-done.15.refs_1_, f32[128,128]{1,0:T(8,128)S(1)} %collective-permute-done.18.refs_2_, ...), custom_call_target="tpu_custom_call" | custom-call | tf_op jit(solution)/shard_map/pallas_call | solution.py:256
  41.8 1.6 %collective-permute-start.22 = (f32[128,128]{1,0:T(8,128)S(1)}, f32[128,128]{1,0:T(8,128)S(1)}, u32[]{:S(2)}, u32[]{:S(2)}) collective-permute-start(f32[128,128]{1,0:T(8,128)S(1)} %get-tuple-element.40), channel_id=1, source_target_pairs={{0,8},{4,20},{8,0},{12,28},{16,24},{20,4},{24,16},{28,12},{1,9},{5... | collective-permute-start | bytes 196616 | tf_op jit(solution)/shard_map/ppermute | solution.py:328
  43.4 1.2 %collective-permute-start.23 = (f32[64,128]{1,0:T(8,128)S(1)}, f32[64,128]{1,0:T(8,128)S(1)}, u32[]{:S(2)}, u32[]{:S(2)}) collective-permute-start(f32[64,128]{1,0:T(8,128)S(1)} %get-tuple-element.41), channel_id=1, source_target_pairs={{0,24},{4,28},{8,16},{12,20},{16,8},{20,12},{24,0},{28,4},{1,25},{... | collective-permute-start | bytes 98312 | tf_op jit(solution)/shard_map/ppermute | solution.py:328
  44.6 1.9 %collective-permute-done.22.refs_0_ = f32[128,128]{1,0:T(8,128)S(1)} collective-permute-done((f32[128,128]{1,0:T(8,128)S(1)}, f32[128,128]{1,0:T(8,128)S(1)}, u32[]{:S(2)}, u32[]{:S(2)}) %collective-permute-start.22) | collective-permute-done | bytes 65568 | tf_op jit(solution)/shard_map/ppermute | solution.py:328
  46.5 1.7 %collective-permute-done.23.refs_1_ = f32[64,128]{1,0:T(8,128)S(1)} collective-permute-done((f32[64,128]{1,0:T(8,128)S(1)}, f32[64,128]{1,0:T(8,128)S(1)}, u32[]{:S(2)}, u32[]{:S(2)}) %collective-permute-start.23) | collective-permute-done | bytes 32800 | tf_op jit(solution)/shard_map/ppermute | solution.py:328
  48.2 1.2 %collective-permute-done.25.refs_3_ = f32[64,128]{1,0:T(8,128)S(1)} collective-permute-done((f32[64,128]{1,0:T(8,128)S(1)}, f32[64,128]{1,0:T(8,128)S(1)}, u32[]{:S(2)}, u32[]{:S(2)}) %collective-permute-start.25) | collective-permute-done | bytes 32800 | tf_op jit(solution)/shard_map/ppermute | solution.py:331
  49.4 1.7 %shard_map.33 = f32[128,128]{1,0:T(8,128)} custom-call(s32[3]{0:T(128)S(1)} %pad_add_fusion.place_ref, f32[128,128]{1,0:T(8,128)S(1)} %collective-permute-done.22.refs_0_, f32[64,128]{1,0:T(8,128)S(1)} %collective-permute-done.23.refs_1_, f32[128,128]{1,0:T(8,128)S(1)} %collective-permute-done.24.refs_2_, f32[64,128]{1,0:T(8,128)S(1)} %collective-permute-done.25.refs_3_, ...), custom_call_target="tpu_custom_call" | custom-call | tf_op jit(solution)/shard_map/pallas_call | solution.py:256
  (37 shorter events, 5.2 us)
Async XLA Ops:
  0.0 10.8 %collective-permute-start.2 = (f32[3,32,256]{2,1,0:T(8,128)}, f32[3,32,256]{2,1,0:T(8,128)S(1)}, u32[]{:S(2)}, u32[]{:S(2)}) collective-permute-start(f32[3,32,256]{2,1,0:T(8,128)} %bitcast.5), channel_id=1, source_target_pairs={{0,3},{1,2},{2,1},{3,0},{4,7},{5,6},{6,5},{7,4},{8,11},{9,10},{10,... | collective-permute-start | bytes 294920 | tf_op jit(solution)/shard_map/ppermute | solution.py:276
  5.0 8.5 %collective-permute-start.1 = (f32[3,32,256]{2,1,0:T(8,128)}, f32[3,32,256]{2,1,0:T(8,128)S(1)}, u32[]{:S(2)}, u32[]{:S(2)}) collective-permute-start(f32[3,32,256]{2,1,0:T(8,128)} %bitcast.6), channel_id=1, source_target_pairs={{0,2},{1,3},{2,0},{3,1},{4,6},{5,7},{6,4},{7,5},{8,10},{9,11},{10,... | collective-permute-start | bytes 294920 | tf_op jit(solution)/shard_map/ppermute | solution.py:276
  5.1 8.5 %collective-permute-start = (f32[3,32,256]{2,1,0:T(8,128)}, f32[3,32,256]{2,1,0:T(8,128)S(1)}, u32[]{:S(2)}, u32[]{:S(2)}) collective-permute-start(f32[3,32,256]{2,1,0:T(8,128)} %bitcast.7), channel_id=1, source_target_pairs={{0,1},{1,0},{2,3},{3,2},{4,5},{5,4},{6,7},{7,6},{8,9},{9,8},{10,11... | collective-permute-start | bytes 294920 | tf_op jit(solution)/shard_map/ppermute | solution.py:276
  5.6 8.4 %collective-permute-start.3 = (f32[3,32,256]{2,1,0:T(8,128)}, f32[3,32,256]{2,1,0:T(8,128)S(1)}, u32[]{:S(2)}, u32[]{:S(2)}) collective-permute-start(f32[3,32,256]{2,1,0:T(8,128)} %bitcast.8), channel_id=1, source_target_pairs={{0,4},{4,0},{8,12},{12,8},{16,20},{20,16},{24,28},{28,24},{1,5},{5... | collective-permute-start | bytes 294920 | tf_op jit(solution)/shard_map/ppermute | solution.py:331
  5.6 1.6 %collective-permute-start.7 = (f32[128,128]{1,0:T(8,128)}, f32[128,128]{1,0:T(8,128)S(1)}, u32[]{:S(2)}, u32[]{:S(2)}) collective-permute-start(f32[128,128]{1,0:T(8,128)} %param.2), channel_id=1, source_target_pairs={{0,4},{4,0},{8,12},{12,8},{16,20},{20,16},{24,28},{28,24},{1,5},{5... | collective-permute-start | bytes 196616 | tf_op jit(solution)/shard_map/ppermute | solution.py:331
  8.1 6.1 %collective-permute-start.9 = (f32[128,128]{1,0:T(8,128)S(1)}, f32[128,128]{1,0:T(8,128)S(1)}, u32[]{:S(2)}, u32[]{:S(2)}) collective-permute-start(f32[128,128]{1,0:T(8,128)S(1)} %get-tuple-element.44.refs_8_), channel_id=1, source_target_pairs={{0,24},{4,28},{8,16},{12,20},{16,8},{20,12},{24,0},{28,4},{1,25},{... | collective-permute-start | bytes 196616 | tf_op jit(solution)/shard_map/ppermute | solution.py:328
  10.8 4.3 %collective-permute-start.8 = (f32[128,128]{1,0:T(8,128)S(1)}, f32[128,128]{1,0:T(8,128)S(1)}, u32[]{:S(2)}, u32[]{:S(2)}) collective-permute-start(f32[128,128]{1,0:T(8,128)S(1)} %get-tuple-element.44.refs_8_), channel_id=1, source_target_pairs={{0,8},{4,12},{8,0},{12,4},{16,24},{20,28},{24,16},{28,20},{1,9},{5... | collective-permute-start | bytes 196616 | tf_op jit(solution)/shard_map/ppermute | solution.py:328
  13.5 1.6 %collective-permute-start.6 = (f32[3,32,256]{2,1,0:T(8,128)S(1)}, f32[3,32,256]{2,1,0:T(8,128)S(1)}, u32[]{:S(2)}, u32[]{:S(2)}) collective-permute-start(f32[3,32,256]{2,1,0:T(8,128)S(1)} %collective-permute-done.2.refs_3_), channel_id=1, source_target_pairs={{0,4},{4,0},{8,12},{12,8},{16,20},{20,16},{24,28},{28,24},{1,5},{5... | collective-permute-start | bytes 294920 | tf_op jit(solution)/shard_map/ppermute | solution.py:331
  13.5 1.6 %collective-permute-start.5 = (f32[3,32,256]{2,1,0:T(8,128)S(1)}, f32[3,32,256]{2,1,0:T(8,128)S(1)}, u32[]{:S(2)}, u32[]{:S(2)}) collective-permute-start(f32[3,32,256]{2,1,0:T(8,128)S(1)} %collective-permute-done.1.refs_2_), channel_id=1, source_target_pairs={{0,4},{4,0},{8,12},{12,8},{16,20},{20,16},{24,28},{28,24},{1,5},{5... | collective-permute-start | bytes 294920 | tf_op jit(solution)/shard_map/ppermute | solution.py:331
  21.7 5.7 %collective-permute-start.10 = (f32[256,128]{1,0:T(8,128)S(1)}, f32[256,128]{1,0:T(8,128)S(1)}, u32[]{:S(2)}, u32[]{:S(2)}) collective-permute-start(f32[256,128]{1,0:T(8,128)S(1)} %get-tuple-element.24), channel_id=1, source_target_pairs={{0,8},{4,20},{8,0},{12,28},{16,24},{20,4},{24,16},{28,12},{1,9},{5... | collective-permute-start | bytes 393224 | tf_op jit(solution)/shard_map/ppermute | solution.py:328
  23.2 6.7 %collective-permute-start.11 = (f32[128,128]{1,0:T(8,128)S(1)}, f32[128,128]{1,0:T(8,128)S(1)}, u32[]{:S(2)}, u32[]{:S(2)}) collective-permute-start(f32[128,128]{1,0:T(8,128)S(1)} %get-tuple-element.25), channel_id=1, source_target_pairs={{0,24},{4,28},{8,16},{12,20},{16,8},{20,12},{24,0},{28,4},{1,25},{... | collective-permute-start | bytes 196616 | tf_op jit(solution)/shard_map/ppermute | solution.py:328
  27.4 4.2 %collective-permute-start.12 = (f32[256,128]{1,0:T(8,128)S(1)}, f32[256,128]{1,0:T(8,128)S(1)}, u32[]{:S(2)}, u32[]{:S(2)}) collective-permute-start(f32[256,128]{1,0:T(8,128)S(1)} %collective-permute-done.10.refs_0_), channel_id=1, source_target_pairs={{0,4},{4,0},{8,12},{12,8},{16,20},{20,16},{24,28},{28,24},{1,5},{5... | collective-permute-start | bytes 393224 | tf_op jit(solution)/shard_map/ppermute | solution.py:331
  28.4 7.7 %collective-permute-start.16 = (f32[256,128]{1,0:T(8,128)S(1)}, f32[256,128]{1,0:T(8,128)S(1)}, u32[]{:S(2)}, u32[]{:S(2)}) collective-permute-start(f32[256,128]{1,0:T(8,128)S(1)} %get-tuple-element.32), channel_id=1, source_target_pairs={{0,8},{4,20},{8,0},{12,28},{16,24},{20,4},{24,16},{28,12},{1,9},{5... | collective-permute-start | bytes 393224 | tf_op jit(solution)/shard_map/ppermute | solution.py:328
  30.0 1.7 %collective-permute-start.13 = (f32[128,128]{1,0:T(8,128)S(1)}, f32[128,128]{1,0:T(8,128)S(1)}, u32[]{:S(2)}, u32[]{:S(2)}) collective-permute-start(f32[128,128]{1,0:T(8,128)S(1)} %collective-permute-done.11.refs_1_), channel_id=1, source_target_pairs={{0,4},{4,0},{8,12},{12,8},{16,20},{20,16},{24,28},{28,24},{1,5},{5... | collective-permute-start | bytes 196616 | tf_op jit(solution)/shard_map/ppermute | solution.py:331
  30.2 5.9 %collective-permute-start.17 = (f32[128,128]{1,0:T(8,128)S(1)}, f32[128,128]{1,0:T(8,128)S(1)}, u32[]{:S(2)}, u32[]{:S(2)}) collective-permute-start(f32[128,128]{1,0:T(8,128)S(1)} %get-tuple-element.33), channel_id=1, source_target_pairs={{0,24},{4,28},{8,16},{12,20},{16,8},{20,12},{24,0},{28,4},{1,25},{... | collective-permute-start | bytes 196616 | tf_op jit(solution)/shard_map/ppermute | solution.py:328
  33.1 5.0 %collective-permute-start.15 = (f32[64,128]{1,0:T(8,128)S(1)}, f32[64,128]{1,0:T(8,128)S(1)}, u32[]{:S(2)}, u32[]{:S(2)}) collective-permute-start(f32[64,128]{1,0:T(8,128)S(1)} %get-tuple-element.31), channel_id=1, source_target_pairs={{0,24},{4,28},{8,16},{12,20},{16,8},{20,12},{24,0},{28,4},{1,25},{... | collective-permute-start | bytes 98312 | tf_op jit(solution)/shard_map/ppermute | solution.py:328
  34.6 4.3 %collective-permute-start.14 = (f32[128,128]{1,0:T(8,128)S(1)}, f32[128,128]{1,0:T(8,128)S(1)}, u32[]{:S(2)}, u32[]{:S(2)}) collective-permute-start(f32[128,128]{1,0:T(8,128)S(1)} %get-tuple-element.30), channel_id=1, source_target_pairs={{0,8},{4,20},{8,0},{12,28},{16,24},{20,4},{24,16},{28,12},{1,9},{5... | collective-permute-start | bytes 196616 | tf_op jit(solution)/shard_map/ppermute | solution.py:328
  38.1 2.3 %collective-permute-start.20 = (f32[256,128]{1,0:T(8,128)S(1)}, f32[256,128]{1,0:T(8,128)S(1)}, u32[]{:S(2)}, u32[]{:S(2)}) collective-permute-start(f32[256,128]{1,0:T(8,128)S(1)} %collective-permute-done.16.refs_4_), channel_id=1, source_target_pairs={{0,4},{4,0},{8,12},{12,8},{16,20},{20,16},{24,28},{28,24},{1,5},{5... | collective-permute-start | bytes 393224 | tf_op jit(solution)/shard_map/ppermute | solution.py:331
  38.1 2.3 %collective-permute-start.21 = (f32[128,128]{1,0:T(8,128)S(1)}, f32[128,128]{1,0:T(8,128)S(1)}, u32[]{:S(2)}, u32[]{:S(2)}) collective-permute-start(f32[128,128]{1,0:T(8,128)S(1)} %collective-permute-done.17.refs_5_), channel_id=1, source_target_pairs={{0,4},{4,0},{8,12},{12,8},{16,20},{20,16},{24,28},{28,24},{1,5},{5... | collective-permute-start | bytes 196616 | tf_op jit(solution)/shard_map/ppermute | solution.py:331
  38.9 1.5 %collective-permute-start.18 = (f32[128,128]{1,0:T(8,128)S(1)}, f32[128,128]{1,0:T(8,128)S(1)}, u32[]{:S(2)}, u32[]{:S(2)}) collective-permute-start(f32[128,128]{1,0:T(8,128)S(1)} %collective-permute-done.14.refs_0_), channel_id=1, source_target_pairs={{0,4},{4,0},{8,12},{12,8},{16,20},{20,16},{24,28},{28,24},{1,5},{5... | collective-permute-start | bytes 196616 | tf_op jit(solution)/shard_map/ppermute | solution.py:331
  38.9 1.5 %collective-permute-start.19 = (f32[64,128]{1,0:T(8,128)S(1)}, f32[64,128]{1,0:T(8,128)S(1)}, u32[]{:S(2)}, u32[]{:S(2)}) collective-permute-start(f32[64,128]{1,0:T(8,128)S(1)} %collective-permute-done.15.refs_1_), channel_id=1, source_target_pairs={{0,4},{4,0},{8,12},{12,8},{16,20},{20,16},{24,28},{28,24},{1,5},{5... | collective-permute-start | bytes 98312 | tf_op jit(solution)/shard_map/ppermute | solution.py:331
  41.8 4.7 %collective-permute-start.22 = (f32[128,128]{1,0:T(8,128)S(1)}, f32[128,128]{1,0:T(8,128)S(1)}, u32[]{:S(2)}, u32[]{:S(2)}) collective-permute-start(f32[128,128]{1,0:T(8,128)S(1)} %get-tuple-element.40), channel_id=1, source_target_pairs={{0,8},{4,20},{8,0},{12,28},{16,24},{20,4},{24,16},{28,12},{1,9},{5... | collective-permute-start | bytes 196616 | tf_op jit(solution)/shard_map/ppermute | solution.py:328
  43.4 4.8 %collective-permute-start.23 = (f32[64,128]{1,0:T(8,128)S(1)}, f32[64,128]{1,0:T(8,128)S(1)}, u32[]{:S(2)}, u32[]{:S(2)}) collective-permute-start(f32[64,128]{1,0:T(8,128)S(1)} %get-tuple-element.41), channel_id=1, source_target_pairs={{0,24},{4,28},{8,16},{12,20},{16,8},{20,12},{24,0},{28,4},{1,25},{... | collective-permute-start | bytes 98312 | tf_op jit(solution)/shard_map/ppermute | solution.py:328
  46.5 2.9 %collective-permute-start.24 = (f32[128,128]{1,0:T(8,128)S(1)}, f32[128,128]{1,0:T(8,128)S(1)}, u32[]{:S(2)}, u32[]{:S(2)}) collective-permute-start(f32[128,128]{1,0:T(8,128)S(1)} %collective-permute-done.22.refs_0_), channel_id=1, source_target_pairs={{0,4},{4,0},{8,12},{12,8},{16,20},{20,16},{24,28},{28,24},{1,5},{5... | collective-permute-start | bytes 196616 | tf_op jit(solution)/shard_map/ppermute | solution.py:331
  (2 other events, 2.5 us)

commit v7 on v4

--- a/solution.py
+++ b/solution.py
@@ -37,7 +37,7 @@
     return (row // rows_block) == ((col % wrap) // cols_block)
 
 
-def pair_operators(refl_ref, keep, out_ref):
+def pair_inverses(refl_ref, keep):
     _, groups, block, window = refl_ref.shape
     wide = 2 * block
     groups = range(groups)
@@ -110,29 +110,64 @@
     bmask = same_block((block, wide), 64, 64, block)
     across = [mm(r, diagonal(jnp.where(bmask, 0.0, n), block)) for r, n in zip(result, near)]
     result = [r - mm(x, diagonal(r, block)) for r, x in zip(result, across)]
-    for g in groups:
-        q, p = halves(result[g][:, :block]), halves(result[g][:, block:])
-        link = mm(q, cross[g])
-        link = mm(link, p)
-        solved_p = mm(p, sfirst[g])
-        low = halves(sfirst[g])
-        solved_q = mm(q, ssecond[g])
-        reach = mm(link, low)
-        zero = jnp.zeros((block, block), F32)
-        sq = jnp.concatenate([-reach[:, :block], solved_q[:, :block] - reach[:, block:], solved_q[:, block:]], 1)
-        sp = jnp.concatenate([solved_p, zero], 1)
-        solved = jnp.concatenate([sq, sp], 0)
-        joined = jnp.concatenate(
+    return [
+        (
+            firsts[g],
+            seconds[g],
+            sfirst[g],
+            ssecond[g],
+            cross[g],
+            halves(result[g][:, :block]),
+            halves(result[g][:, block:]),
+        )
+        for g in groups
+    ]
+
+
+def joined(first, second):
+    block = first.shape[0]
+    none = jnp.zeros((block, block), F32)
+    return jnp.concatenate(
+        [jnp.concatenate([none, second], 1), jnp.concatenate([first, none], 1)], 0
+    )
+
+
+def pair_operators(refl_ref, keep, out_ref):
+    block = refl_ref.shape[2]
+    for g, (first, second, sfirst, ssecond, cross, q, p) in enumerate(pair_inverses(refl_ref, keep)):
+        link = mm(mm(q, cross), p)
+        solved_p = mm(p, sfirst)
+        solved_q = mm(q, ssecond)
+        reach = mm(link, sfirst)
+        none = jnp.zeros((block, block), F32)
+        solved = jnp.concatenate(
             [
-                jnp.concatenate([zero, seconds[g]], 1),
-                jnp.concatenate([firsts[g], zero], 1),
+                jnp.concatenate(
+                    [-reach[:, :block], solved_q[:, :block] - reach[:, block:], solved_q[:, block:]], 1
+                ),
+                jnp.concatenate([solved_p, none], 1),
             ],
             0,
         )
-        moved = mm(joined, solved, TN)
-        orow = lax.broadcasted_iota(jnp.int32, moved.shape, 0)
-        ocol = lax.broadcasted_iota(jnp.int32, moved.shape, 1)
-        out_ref[g] = jnp.where(orow == ocol, 1.0, 0.0) - moved
+        moved = mm(joined(first, second), solved, TN)
+        row = lax.broadcasted_iota(jnp.int32, moved.shape, 0)
+        col = lax.broadcasted_iota(jnp.int32, moved.shape, 1)
+        out_ref[g] = jnp.where(row == col, 1.0, 0.0) - moved
+
+
+def pair_action(refl_ref, keep, window):
+    block = refl_ref.shape[2]
+    cols = window.shape[1]
+    ((first, second, sfirst, ssecond, cross, q, p),) = pair_inverses(refl_ref, keep)
+    weights_p = jnp.concatenate([mm(sfirst, window[: 2 * block]), sfirst[:, :block]], 1)
+    weights_q = mm(ssecond, window[block:])
+    weights_q = jnp.concatenate([weights_q, jnp.zeros((block, block), F32)], 1)
+    solved_p = mm(p, weights_p)
+    solved_q = mm(q, weights_q - mm(cross, solved_p))
+    moved = mm(joined(first, second), jnp.concatenate([solved_q, solved_p], 0), TN)
+    row = lax.broadcasted_iota(jnp.int32, (3 * block, block), 0)
+    col = lax.broadcasted_iota(jnp.int32, (3 * block, block), 1)
+    return window - moved[:, :cols], jnp.where(row == col, 1.0, 0.0) - moved[:, cols:]
 
 
 def pick_near(node, core, value):
@@ -146,9 +181,9 @@
     return jnp.where((node & 2) == 0, value[2 * block :], value[:block])
 
 
-def half_of(core, value):
-    rows = value.shape[0] // PAIR
-    return jnp.where(core == 0, value[:rows], value[rows:])
+def half_of(core, ref):
+    rows = ref.shape[0] // PAIR
+    return ref[pl.ds(pl.multiple_of(core * rows, rows), rows), :]
 
 
 def assemble(place_ref, mine, theirs, groups, refl_ref):
@@ -164,11 +199,10 @@
 def first_kernel(count, nodes, place_ref, *refs):
     mine, theirs = refs[:count], refs[count : 2 * count]
     top_ref, low_ref, near_ref, far_ref = refs[2 * count : 2 * count + 4]
-    oper_ref, fixed_ref, out_near, out_far, refl_ref = refs[2 * count + 4 :]
+    fixed_ref, lead_ref, out_near, out_far, refl_ref = refs[2 * count + 4 :]
     block = top_ref.shape[0]
     node, core = place_ref[0], place_ref[1]
     assemble(place_ref, mine, theirs, [0], refl_ref)
-    pair_operators(refl_ref, node != nodes - 1, oper_ref)
     below = jnp.where((node & 1) == 0, near_ref[...], far_ref[...])
     window = jnp.concatenate(
         [
@@ -178,9 +212,9 @@
         ],
         0,
     )
-    fixed = mm(oper_ref[0], window)
+    fixed, lead = pair_action(refl_ref, node != nodes - 1, window)
     fixed_ref[...] = fixed
-    lead = oper_ref[0, :, :block]
+    lead_ref[...] = lead
     out_near[:block] = pick_near(node, core, fixed)
     out_near[block:] = pick_near(node, core, lead)
     out_far[...] = jnp.where(core == 0, pick_far(node, fixed), pick_far(node, lead))
@@ -188,72 +222,123 @@
 
 def later_kernel(count, nodes, place_ref, *refs):
     mine, theirs = refs[:count], refs[count : 2 * count]
-    oper_ref, map_near, map_far, refl_ref = refs[2 * count :]
+    oper_ref, map_ref, map_half, refl_ref = refs[2 * count :]
     node, core = place_ref[0], place_ref[1]
-    later, _, size = oper_ref.shape
+    later, size, _ = oper_ref.shape
+    block = size // 3
     assemble(place_ref, mine, theirs, range(1, 1 + later), refl_ref)
     pair_operators(refl_ref, node != nodes - 1, oper_ref)
-    leads = [oper_ref[slot, :, : size // 3] for slot in range(later)]
-    map_near[...] = jnp.concatenate([pick_near(node, core, lead) for lead in leads], 0)
-    map_far[...] = half_of(core, jnp.concatenate([pick_far(node, lead) for lead in leads], 0))
-
-
-def next_kernel(group, place_ref, *refs):
-    (near_ref, far_ref, near2_ref, far2_ref), refs = refs[:4], refs[4:]
+    if later != 2:
+        return
+    up, own, out = (slice(part * block, (part + 1) * block) for part in range(3))
+    map_ref[:block] = oper_ref[0, out, :block]
+    map_ref[block : 2 * block] = oper_ref[0, up, :block]
+    map_ref[2 * block : 3 * block] = mm(oper_ref[1, out, own], oper_ref[0, own, :block])
+    map_ref[3 * block : 4 * block] = oper_ref[1, out, out]
+    map_ref[4 * block :] = oper_ref[1, out, :block]
+    map_half[...] = half_of(core, map_ref)
+
+
+def next_kernel(place_ref, near_ref, far_ref, near2_ref, far2_ref, fixed_ref, lead_ref, oper_ref, *outs):
+    out_fixed, out_vec, out_half = outs
+    block = far_ref.shape[0]
     node, core = place_ref[0], place_ref[1]
     here = core == 0
     odd, high = (node & 1) == 1, (node & 2) == 2
     near, near2, far, far2 = near_ref[...], near2_ref[...], far_ref[...], far2_ref[...]
-    came1 = jnp.where(here, near, near2)
-    came2 = jnp.where(here, near2, near)
-    came3 = jnp.concatenate([jnp.where(here, far, far2), jnp.where(here, far2, far)], 0)
-    if group == 0:
-        block = came1.shape[0] // 2
-        map1, map2, map3 = came1[block:], came2[block:], came3[block:]
-        came1, came2, came3 = came1[:block], came2[:block], came3[:block]
-    else:
-        (mnear_ref, mfar_ref, mnear2_ref, mfar2_ref), refs = refs[:4], refs[4:]
-        block = came1.shape[0]
-        at = slice((group - 1) * block, group * block)
-        map1 = jnp.where(here, mnear_ref[at], mnear2_ref[at])
-        map2 = jnp.where(here, mnear2_ref[at], mnear_ref[at])
-        mfar, mfar2 = mfar_ref[...], mfar2_ref[...]
-        map3 = jnp.concatenate(
-            [jnp.where(here, mfar, mfar2), jnp.where(here, mfar2, mfar)], 0
-        )[at]
-    (fixed_ref, first_ref, later_ref), outs = refs[:3], refs[3:]
-    oper = first_ref.at[0] if group == 0 else later_ref.at[group - 1]
+    came1, map1 = (jnp.where(here, near[at], near2[at]) for at in (slice(0, block), slice(block, None)))
+    came2, map2 = (jnp.where(here, near2[at], near[at]) for at in (slice(0, block), slice(block, None)))
+    came3, map3 = jnp.where(here, far, far2), jnp.where(here, far2, far)
     carry = jnp.where(high, jnp.where(odd, came3, came2), came1)
     carry = jnp.where(node == 0, 0.0, carry)
     step = jnp.where(odd, came2, came3) + mm(jnp.where(odd, map2, map3), carry)
     carry = jnp.where(high, step, carry)
     step = came1 + mm(map1, carry)
     carry = jnp.where(node == 3, step, carry)
-    if len(outs) == 1:
-        at = pl.ds(pl.multiple_of(core * block, block), block)
-        outs[0][...] = fixed_ref[at, :] + mm(oper[at, :block], carry)
-        return
-    fixed, lead = fixed_ref[...], oper[:, :block]
+    up, own, out = (slice(part * block, (part + 1) * block) for part in range(3))
+    fixed, lead = fixed_ref[...], lead_ref[...]
     cols = fixed.shape[1]
-    below = mm(
-        jnp.where(odd, map3, map1), jnp.concatenate([fixed[2 * block :], lead[2 * block :]], 1)
-    )
-    offset = jnp.where(odd, came3, came1)
-    below = jnp.where(node == 3, 0.0, below + jnp.concatenate([offset, jnp.zeros_like(lead[:block])], 1))
-    first = jnp.where(node == 0, fixed[:block], 0.0)
+    none = jnp.zeros((block, block), F32)
+    below = mm(jnp.where(odd, map3, map1), jnp.concatenate([fixed[out], lead[out]], 1))
+    below += jnp.concatenate([jnp.where(odd, came3, came1), none], 1)
     window = jnp.concatenate(
         [
-            jnp.concatenate([first, jnp.zeros_like(lead[:block])], 1),
-            jnp.concatenate([fixed[block : 2 * block], lead[block : 2 * block]], 1),
-            below,
+            jnp.concatenate([jnp.where(node == 0, fixed[up], 0.0), none], 1),
+            jnp.concatenate([fixed[own], lead[own]], 1),
+            jnp.where(node == 3, 0.0, below),
         ],
         0,
     )
-    moved = mm(later_ref[group], window)
+    moved = mm(oper_ref[0], window)
     fixed = moved[:, :cols] + mm(moved[:, cols:], carry)
-    outs[0][...] = fixed
-    outs[1][...] = pick_near(node, core, fixed)
-    outs[2][...] = half_of(core, pick_far(node, fixed))
+    out_fixed[...] = fixed
+    out_vec[:block] = fixed[out]
+    out_vec[block : 2 * block] = fixed[up]
+    part = mm(oper_ref[1, out, own], fixed[own])
+    first = mm(oper_ref[1, out, up], fixed[up])
+    out_vec[2 * block :] = part + jnp.where(node == 0, first, 0.0)
+    out_half[...] = half_of(core, out_vec)
+
+
+def last_kernel(place_ref, *refs):
+    vecs, maps, (fixed_ref, oper_ref, out_ref) = refs[:5], refs[5:10], refs[10:]
+    block = out_ref.shape[0]
+    own, out = slice(block, 2 * block), slice(2 * block, 3 * block)
+    here = place_ref[1] == 0
+
+    def either(one_ref, two_ref, first, last):
+        return jnp.where(here, one_ref[first:last], two_ref[first:last])
+
+    def fetch(arrays, mask, part):
+        near_ref, far_ref, near2_ref, far2_ref, own_ref = arrays
+        first, last = part * block, (part + 1) * block
+        if mask == 0:
+            return own_ref[first:last]
+        if mask == 1:
+            return either(near_ref, near2_ref, first, last)
+        if mask == 2:
+            return either(near2_ref, near_ref, first, last)
+        half = far_ref.shape[0]
+        pieces = []
+        if first < half:
+            pieces.append(either(far_ref, far2_ref, first, min(last, half)))
+        if last > half:
+            pieces.append(either(far2_ref, far_ref, max(first, half) - half, last - half))
+        return jnp.concatenate(pieces, 0)
+
+    def finish(node):
+        offset = lambda pair, part: fetch(vecs, node ^ pair, part)
+        matrix = lambda pair, part: fetch(maps, node ^ pair, part)
+        at = pl.ds(pl.multiple_of(place_ref[1] * block, block), block)
+        reach = min(node + 1, 3)
+        carries = [None]
+        for pair in range(reach):
+            carry = offset(pair, 0)
+            if pair:
+                carry = carry + mm(matrix(pair, 0), carries[pair])
+            carries.append(carry)
+        belows = [
+            offset(pair + 1, 1) + mm(matrix(pair + 1, 1), carries[pair + 1])
+            for pair in range(reach)
+        ]
+        final = None
+        for pair in range(node):
+            end = mm(matrix(pair, 3), belows[pair])
+            if pair:
+                end = end + mm(matrix(pair, 2), carries[pair]) + mm(matrix(pair, 4), final)
+            final = offset(pair, 2) + end
+        reached = fixed_ref[: 2 * block]
+        if node:
+            reached = reached + mm(oper_ref[0, : 2 * block, :block], carries[node])
+        else:
+            final = reached[:block]
+        total = mm(oper_ref[1, at, own], reached[own])
+        if node < 3:
+            total = total + mm(oper_ref[1, at, out], belows[node])
+        out_ref[...] = total + mm(oper_ref[1, at, :block], final)
+
+    for node in range(4):
+        pl.when(place_ref[0] == node)(functools.partial(finish, node))
 
 
 def call(kernel, outs, operands, scratch=(), work=0):
@@ -283,11 +368,10 @@
     ], True
 
 
-def many_pairs(fixed, operators, node, nodes, row_count):
-    groups, block = len(operators), fixed.shape[0] // 3
+def many_pairs(fixed, lead, operators, node, nodes, row_count):
+    groups, block = 1 + operators.shape[0], fixed.shape[0] // 3
     members = [[place * PAIR + core for place in range(nodes)] for core in range(PAIR)]
     for group in range(groups):
-        lead = operators[group][:, :block]
         down = jnp.concatenate([fixed[2 * block :], lead[2 * block :]], 0)
         up = jnp.concatenate([fixed[:block], lead[:block]], 0)
         earlier = lax.all_gather(down, "rows", axis_index_groups=members)
@@ -309,7 +393,8 @@
                 ],
                 0,
             )
-            fixed = dot(operators[group + 1], window)
+            lead = operators[group][:, :block]
+            fixed = dot(operators[group], window)
     return result
 
 
@@ -350,58 +435,48 @@
     theirs = [across(piece) for piece in mine]
     mine[0] = jnp.where(vec_index < 0, 0.0, mine[0])
     place = jnp.stack([node, core, vec_index if mixed else 0]).astype(jnp.int32)
+    hold = lax.optimization_barrier
     later = groups - 1
-    work = 16 * (3 * block) ** 3
+    size = 3 * block
+    maps = 5 * block
+    work = 16 * size**3
     pieces = [place, *mine, *theirs]
-    first_oper, fixed, near, far = call(
+    fixed, lead, near, far = call(
         functools.partial(first_kernel, len(mine), nodes),
-        [
-            (1, 3 * block, 3 * block),
-            (3 * block, cols),
-            (2 * block, cols),
-            (block, cols),
-        ],
+        [(size, cols), (size, block), (2 * block, cols), (block, cols)],
         [*pieces, top, low, *below],
         [pltpu.VMEM((PAIR, 1, block, window), F32)],
         work,
     )
-    later_oper, *maps = call(
+    operators, sent, sent_half = call(
         functools.partial(later_kernel, len(mine), nodes),
-        [
-            (later, 3 * block, 3 * block),
-            (later * block, block),
-            (later * block // PAIR, block),
-        ],
+        [(later, size, size), (maps, block), (maps // PAIR, block)],
         pieces,
         [pltpu.VMEM((PAIR, later, block, window), F32)],
         work * later,
     )
-    if nodes != 4:
-        operators = [first_oper[0]] + [later_oper[slot] for slot in range(later)]
-        result = many_pairs(fixed, operators, node, nodes, row_count)
+    if nodes != 4 or groups != 3:
+        result = many_pairs(fixed, lead, operators, node, nodes, row_count)
         return jnp.where(core == 0, result[:block], result[block : 2 * block])
-    hold = lax.optimization_barrier
-    for group in range(groups):
-        near = swap(near, (1, 2))
-        far = swap(far, (3, 3))
-        if group == 0:
-            near, *maps = hold((near, *maps))
-            maps = [swap(maps[0], (1, 2)), swap(maps[1], (3, 3))]
-        elif group == 1:
-            far, *maps = hold((far, *maps))
-            maps += [across(part) for part in maps]
-        came = [near, far, across(near), across(far)]
-        operands = [place, *came, *(maps if group else []), fixed, first_oper, later_oper]
-        if group < groups - 1:
-            fixed, near, far = call(
-                functools.partial(next_kernel, group),
-                [(3 * block, cols), (block, cols), (block // PAIR, cols)],
-                operands,
-            )
-        else:
-            (result,) = call(
-                functools.partial(next_kernel, group), [(block, cols)], operands
-            )
+
+    def shared(near, far):
+        return [place, near, far, across(near), across(far)]
+
+    near, far = swap(near, (1, 2)), swap(far, (3, 3))
+    near, far, sent, sent_half = hold((near, far, sent, sent_half))
+    known = [swap(sent, (1, 2)), swap(sent_half, (3, 3))]
+    fixed, vec, vec_half = call(
+        next_kernel,
+        [(size, cols), (size, cols), (size // PAIR, cols)],
+        [*shared(near, far), fixed, lead, operators],
+    )
+    near, far = swap(vec, (1, 2)), swap(vec_half, (3, 3))
+    far, *known = hold((far, *known))
+    (result,) = call(
+        last_kernel,
+        [(block, cols)],
+        [*shared(near, far), vec, *shared(*known)[1:], sent, fixed, operators],
+    )
     return result
 
 

time: 49.9 us -> 45.9 us (0.920)
  starting transfers between devices: 21.6 us -> 18.7 us
  Pallas kernels: 14.1 us -> 12.5 us
    ppermute x10 -> x8, starting transfers between devices: 13.7 us -> 10.9 us  [swap(): return lax.ppermute(value, 'rows', moves)]
    pallas_call x5 -> x4, Pallas kernels: 14.1 us -> 12.5 us  [call(): pl.pallas_call(kernel, out_shape=[jax.ShapeDtypeStruct(shape, F32) for sh...]
    ppermute x10 -> x8, waiting for transfers between devices: 7.18 us -> 8.29 us  [swap(): return lax.ppermute(value, 'rows', moves)]
    ppermute x13 -> x11, waiting for transfers between devices: 2.7 us -> 2.17 us  [across(): lax.ppermute(value, 'rows', [(place, place ^ 1) for place in range(row_co...]
    ppermute x13 -> x11, starting transfers between devices: 2.19 us -> 2.17 us  [across(): lax.ppermute(value, 'rows', [(place, place ^ 1) for place in range(row_co...]
  transfers between devices with their start and end apart: 26 -> 22, of which waited for: 11 -> 9; matrix products, arithmetic and copies ran while one was open for 4% -> 4% of each run, Pallas kernels for 13% -> 15%
where the time goes in v7:
time: 45.9 us; the launch traced here: 45.8 us
  starting transfers between devices  18.7 us (41%)
  waiting for transfers between devices  12.6 us (27%)
  Pallas kernels  12.5 us (27%)
  other arithmetic  1.83 us (4%)
    pallas_call x4, Pallas kernels, call(): pl.pallas_call(kernel, out_shape=[jax.ShapeDtypeStruct(shape, F32) for sh...  12.5 us
    ppermute x8, starting transfers between devices, swap(): return lax.ppermute(value, 'rows', moves)  10.9 us
    ppermute x8, waiting for transfers between devices, swap(): return lax.ppermute(value, 'rows', moves)  8.29 us
    ppermute x3, starting transfers between devices, spread(): lax.ppermute(value, axis, [(place, place ^ mask) for place in range(size)])  5.62 us
    ppermute x11, starting transfers between devices, across(): lax.ppermute(value, 'rows', [(place, place ^ 1) for place in range(row_co...  2.17 us
    ppermute x11, waiting for transfers between devices, across(): lax.ppermute(value, 'rows', [(place, place ^ 1) for place in range(row_co...  2.17 us
    ppermute x3, waiting for transfers between devices, spread(): lax.ppermute(value, axis, [(place, place ^ mask) for place in range(size)])  2.16 us
  transfers between devices with their start and end apart: 22, of which 9 were waited for; matrix products, arithmetic and copies ran while one was open for 4% of the time, Pallas kernels for 15%

profile of v7, /device:TPU:0, one launch (start us, length us, event | category | flops | bytes accessed | tf_op | source)
XLA Modules:
  0.0 45.8 jit_solution(12098739053072856076)
XLA Ops:
  0.0 5.0 %collective-permute-start.2 = (f32[3,32,256]{2,1,0:T(8,128)}, f32[3,32,256]{2,1,0:T(8,128)S(1)}, u32[]{:S(2)}, u32[]{:S(2)}) collective-permute-start(f32[3,32,256]{2,1,0:T(8,128)} %bitcast.5), channel_id=1, source_target_pairs={{0,3},{1,2},{2,1},{3,0},{4,7},{5,6},{6,5},{7,4},{8,11},{9,10},{10,... | collective-permute-start | bytes 294920 | tf_op jit(solution)/shard_map/ppermute | solution.py:366
  5.1 0.6 %collective-permute-start = (f32[3,32,256]{2,1,0:T(8,128)}, f32[3,32,256]{2,1,0:T(8,128)S(1)}, u32[]{:S(2)}, u32[]{:S(2)}) collective-permute-start(f32[3,32,256]{2,1,0:T(8,128)} %bitcast.7), channel_id=1, source_target_pairs={{0,1},{1,0},{2,3},{3,2},{4,5},{5,4},{6,7},{7,6},{8,9},{9,8},{10,11... | collective-permute-start | bytes 294920 | tf_op jit(solution)/shard_map/ppermute | solution.py:366
  5.6 0.5 %collective-permute-start.7 = (f32[128,128]{1,0:T(8,128)}, f32[128,128]{1,0:T(8,128)S(1)}, u32[]{:S(2)}, u32[]{:S(2)}) collective-permute-start(f32[128,128]{1,0:T(8,128)} %param.2), channel_id=1, source_target_pairs={{0,4},{4,0},{8,12},{12,8},{16,20},{20,16},{24,28},{28,24},{1,5},{5... | collective-permute-start | bytes 196616 | tf_op jit(solution)/shard_map/ppermute | solution.py:421
  6.1 0.9 %broadcast_select_fusion.refs_0_ = f32[3,32,256]{2,1,0:T(8,128)S(1)} fusion(pred[]{:T(512)S(6)} %lt.10, f32[3,1,32,256]{3,2,1,0:T(8,128)} %param.3), kind=kLoop, calls=%fused_computation | loop fusion | flops 24576 | bytes 196609 | tf_op jit(solution)/shard_map/jit(_where)/select_n | solution.py:436
  7.2 0.8 %broadcast_select_fusion.1 = (f32[128,128]{1,0:T(8,128)S(1)}, f32[128,128]{1,0:T(8,128)S(1)}) fusion(f32[128,128]{1,0:T(8,128)S(1)} %collective-permute-done.7, f32[128,128]{1,0:T(8,128)} %param.2, pred[]{:T(512)S(6)} %eq.6), kind=kLoop, calls=%fused_computation.1 | loop fusion | flops 32768 | bytes 262145 | tf_op jit(solution)/shard_map/jit(_where)/select_n | solution.py:426
  8.1 2.7 %collective-permute-start.9 = (f32[128,128]{1,0:T(8,128)S(1)}, f32[128,128]{1,0:T(8,128)S(1)}, u32[]{:S(2)}, u32[]{:S(2)}) collective-permute-start(f32[128,128]{1,0:T(8,128)S(1)} %get-tuple-element.40.refs_8_), channel_id=1, source_target_pairs={{0,24},{4,28},{8,16},{12,20},{16,8},{20,12},{24,0},{28,4},{1,25},{... | collective-permute-start | bytes 196616 | tf_op jit(solution)/shard_map/ppermute | solution.py:418
  10.8 0.5 %collective-permute-start.8 = (f32[128,128]{1,0:T(8,128)S(1)}, f32[128,128]{1,0:T(8,128)S(1)}, u32[]{:S(2)}, u32[]{:S(2)}) collective-permute-start(f32[128,128]{1,0:T(8,128)S(1)} %get-tuple-element.40.refs_8_), channel_id=1, source_target_pairs={{0,8},{4,12},{8,0},{12,4},{16,24},{20,28},{24,16},{28,20},{1,9},{5... | collective-permute-start | bytes 196616 | tf_op jit(solution)/shard_map/ppermute | solution.py:418
  11.4 2.2 %collective-permute-done.1.refs_2_ = f32[3,32,256]{2,1,0:T(8,128)S(1)} collective-permute-done((f32[3,32,256]{2,1,0:T(8,128)}, f32[3,32,256]{2,1,0:T(8,128)S(1)}, u32[]{:S(2)}, u32[]{:S(2)}) %collective-permute-start.1) | collective-permute-done | bytes 98336 | tf_op jit(solution)/shard_map/ppermute | solution.py:366
  13.5 0.5 %collective-permute-start.5 = (f32[3,32,256]{2,1,0:T(8,128)S(1)}, f32[3,32,256]{2,1,0:T(8,128)S(1)}, u32[]{:S(2)}, u32[]{:S(2)}) collective-permute-start(f32[3,32,256]{2,1,0:T(8,128)S(1)} %collective-permute-done.1.refs_2_), channel_id=1, source_target_pairs={{0,4},{4,0},{8,12},{12,8},{16,20},{20,16},{24,28},{28,24},{1,5},{5... | collective-permute-start | bytes 294920 | tf_op jit(solution)/shard_map/ppermute | solution.py:421
  14.2 0.9 %collective-permute-done.8.refs_10_ = f32[128,128]{1,0:T(8,128)S(1)} collective-permute-done((f32[128,128]{1,0:T(8,128)S(1)}, f32[128,128]{1,0:T(8,128)S(1)}, u32[]{:S(2)}, u32[]{:S(2)}) %collective-permute-start.8) | collective-permute-done | bytes 65568 | tf_op jit(solution)/shard_map/ppermute | solution.py:418
  15.3 4.0 %shard_map.28 = (f32[384,128]{1,0:T(8,128)S(1)}, f32[384,128]{1,0:T(8,128)S(1)}, f32[256,128]{1,0:T(8,128)S(1)}, f32[128,128]{1,0:T(8,128)S(1)}) custom-call(s32[3]{0:T(128)S(1)} %pad_add_fusion.place_ref, f32[3,32,256]{2,1,0:T(8,128)S(1)} %broadcast_select_fusion.refs_0_, f32[3,32,256]{2,1,0:T(8,128)S(1)} %collective-permute-done.refs_1_, ...), custom_call_target="tpu_custom_call" | custom-call | flops 905969664 | tf_op jit(solution)/shard_map/pallas_call | solution.py:346
  19.3 2.5 %collective-permute-start.11 = (f32[128,128]{1,0:T(8,128)S(1)}, f32[128,128]{1,0:T(8,128)S(1)}, u32[]{:S(2)}, u32[]{:S(2)}) collective-permute-start(f32[128,128]{1,0:T(8,128)S(1)} %get-tuple-element.23), channel_id=1, source_target_pairs={{0,24},{4,28},{8,16},{12,20},{16,8},{20,12},{24,0},{28,4},{1,25},{... | collective-permute-start | bytes 196616 | tf_op jit(solution)/shard_map/ppermute | solution.py:418
  21.8 0.5 %collective-permute-start.10 = (f32[256,128]{1,0:T(8,128)S(1)}, f32[256,128]{1,0:T(8,128)S(1)}, u32[]{:S(2)}, u32[]{:S(2)}) collective-permute-start(f32[256,128]{1,0:T(8,128)S(1)} %get-tuple-element.22), channel_id=1, source_target_pairs={{0,8},{4,20},{8,0},{12,28},{16,24},{20,4},{24,16},{28,12},{1,9},{5... | collective-permute-start | bytes 393224 | tf_op jit(solution)/shard_map/ppermute | solution.py:418
  22.4 5.0 %shard_map.29 = (f32[2,384,384]{2,1,0:T(8,128)S(1)}, f32[640,128]{1,0:T(8,128)S(1)}, f32[320,128]{1,0:T(8,128)S(1)}) custom-call(s32[3]{0:T(128)S(1)} %pad_add_fusion.place_ref, f32[3,32,256]{2,1,0:T(8,128)S(1)} %broadcast_select_fusion.refs_0_, f32[3,32,256]{2,1,0:T(8,128)S(1)} %collective-permute-done.refs_1_, ...), custom_call_target="tpu_custom_call" | custom-call | flops 1811939328 | tf_op jit(solution)/shard_map/pallas_call | solution.py:346
  27.5 1.6 %collective-permute-start.16 = (f32[640,128]{1,0:T(8,128)S(1)}, f32[640,128]{1,0:T(8,128)S(1)}, u32[]{:S(2)}, u32[]{:S(2)}) collective-permute-start(f32[640,128]{1,0:T(8,128)S(1)} %get-tuple-element.33.refs_9_), channel_id=1, source_target_pairs={{0,8},{4,20},{8,0},{12,28},{16,24},{20,4},{24,16},{28,12},{1,9},{5... | collective-permute-start | bytes 983048 | tf_op jit(solution)/shard_map/ppermute | solution.py:418
  29.0 0.5 %collective-permute-start.13 = (f32[128,128]{1,0:T(8,128)S(1)}, f32[128,128]{1,0:T(8,128)S(1)}, u32[]{:S(2)}, u32[]{:S(2)}) collective-permute-start(f32[128,128]{1,0:T(8,128)S(1)} %collective-permute-done.11.far_ref), channel_id=1, source_target_pairs={{0,4},{4,0},{8,12},{12,8},{16,20},{20,16},{24,28},{28,24},{1,5},{5... | collective-permute-start | bytes 196616 | tf_op jit(solution)/shard_map/ppermute | solution.py:421
  30.5 1.9 %shard_map.30 = (f32[384,128]{1,0:T(8,128)S(1)}, f32[384,128]{1,0:T(8,128)S(1)}, f32[192,128]{1,0:T(8,128)S(1)}) custom-call(s32[3]{0:T(128)S(1)} %pad_add_fusion.place_ref, f32[256,128]{1,0:T(8,128)S(1)} %collective-permute-done.10.near_ref, f32[128,128]{1,0:T(8,128)S(1)} %collective-permute-done.11.far_ref, ...), custom_call_target="tpu_custom_call" | custom-call | tf_op jit(solution)/shard_map/pallas_call | solution.py:346
  32.3 2.1 %collective-permute-start.15 = (f32[192,128]{1,0:T(8,128)S(1)}, f32[192,128]{1,0:T(8,128)S(1)}, u32[]{:S(2)}, u32[]{:S(2)}) collective-permute-start(f32[192,128]{1,0:T(8,128)S(1)} %get-tuple-element.32), channel_id=1, source_target_pairs={{0,24},{4,28},{8,16},{12,20},{16,8},{20,12},{24,0},{28,4},{1,25},{... | collective-permute-start | bytes 294920 | tf_op jit(solution)/shard_map/ppermute | solution.py:418
  34.4 0.5 %collective-permute-start.14 = (f32[384,128]{1,0:T(8,128)S(1)}, f32[384,128]{1,0:T(8,128)S(1)}, u32[]{:S(2)}, u32[]{:S(2)}) collective-permute-start(f32[384,128]{1,0:T(8,128)S(1)} %get-tuple-element.31.refs_4_), channel_id=1, source_target_pairs={{0,8},{4,20},{8,0},{12,28},{16,24},{20,4},{24,16},{28,12},{1,9},{5... | collective-permute-start | bytes 589832 | tf_op jit(solution)/shard_map/ppermute | solution.py:418
  34.9 4.3 %collective-permute-done.17.refs_6_ = f32[320,128]{1,0:T(8,128)S(1)} collective-permute-done((f32[320,128]{1,0:T(8,128)S(1)}, f32[320,128]{1,0:T(8,128)S(1)}, u32[]{:S(2)}, u32[]{:S(2)}) %collective-permute-start.17) | collective-permute-done | bytes 163872 | tf_op jit(solution)/shard_map/ppermute | solution.py:418
  39.2 1.1 %collective-permute-done.15.refs_1_ = f32[192,128]{1,0:T(8,128)S(1)} collective-permute-done((f32[192,128]{1,0:T(8,128)S(1)}, f32[192,128]{1,0:T(8,128)S(1)}, u32[]{:S(2)}, u32[]{:S(2)}) %collective-permute-start.15) | collective-permute-done | bytes 98336 | tf_op jit(solution)/shard_map/ppermute | solution.py:418
  40.3 2.1 %collective-permute-done.14.refs_0_ = f32[384,128]{1,0:T(8,128)S(1)} collective-permute-done((f32[384,128]{1,0:T(8,128)S(1)}, f32[384,128]{1,0:T(8,128)S(1)}, u32[]{:S(2)}, u32[]{:S(2)}) %collective-permute-start.14) | collective-permute-done | bytes 196640 | tf_op jit(solution)/shard_map/ppermute | solution.py:418
  42.9 1.2 %collective-permute-done.19.refs_3_ = f32[192,128]{1,0:T(8,128)S(1)} collective-permute-done((f32[192,128]{1,0:T(8,128)S(1)}, f32[192,128]{1,0:T(8,128)S(1)}, u32[]{:S(2)}, u32[]{:S(2)}) %collective-permute-start.19) | collective-permute-done | bytes 98336 | tf_op jit(solution)/shard_map/ppermute | solution.py:421
  44.2 1.6 %shard_map.31 = f32[128,128]{1,0:T(8,128)} custom-call(s32[3]{0:T(128)S(1)} %pad_add_fusion.place_ref, f32[384,128]{1,0:T(8,128)S(1)} %collective-permute-done.14.refs_0_, f32[192,128]{1,0:T(8,128)S(1)} %collective-permute-done.15.refs_1_, f32[384,128]{1,0:T(8,128)S(1)} %collective-permute-done.18.refs_2_, f32[192,128]{1,0:T(8,128)S(1)} %collective-permute-done.19.refs_3_, ...), custom_call_target="tpu_custom_call" | custom-call | tf_op jit(solution)/shard_map/pallas_call | solution.py:346
  (27 shorter events, 2.1 us)
Async XLA Ops:
  0.0 10.8 %collective-permute-start.2 = (f32[3,32,256]{2,1,0:T(8,128)}, f32[3,32,256]{2,1,0:T(8,128)S(1)}, u32[]{:S(2)}, u32[]{:S(2)}) collective-permute-start(f32[3,32,256]{2,1,0:T(8,128)} %bitcast.5), channel_id=1, source_target_pairs={{0,3},{1,2},{2,1},{3,0},{4,7},{5,6},{6,5},{7,4},{8,11},{9,10},{10,... | collective-permute-start | bytes 294920 | tf_op jit(solution)/shard_map/ppermute | solution.py:366
  5.0 8.5 %collective-permute-start.1 = (f32[3,32,256]{2,1,0:T(8,128)}, f32[3,32,256]{2,1,0:T(8,128)S(1)}, u32[]{:S(2)}, u32[]{:S(2)}) collective-permute-start(f32[3,32,256]{2,1,0:T(8,128)} %bitcast.6), channel_id=1, source_target_pairs={{0,2},{1,3},{2,0},{3,1},{4,6},{5,7},{6,4},{7,5},{8,10},{9,11},{10,... | collective-permute-start | bytes 294920 | tf_op jit(solution)/shard_map/ppermute | solution.py:366
  5.1 8.5 %collective-permute-start = (f32[3,32,256]{2,1,0:T(8,128)}, f32[3,32,256]{2,1,0:T(8,128)S(1)}, u32[]{:S(2)}, u32[]{:S(2)}) collective-permute-start(f32[3,32,256]{2,1,0:T(8,128)} %bitcast.7), channel_id=1, source_target_pairs={{0,1},{1,0},{2,3},{3,2},{4,5},{5,4},{6,7},{7,6},{8,9},{9,8},{10,11... | collective-permute-start | bytes 294920 | tf_op jit(solution)/shard_map/ppermute | solution.py:366
  5.6 8.4 %collective-permute-start.3 = (f32[3,32,256]{2,1,0:T(8,128)}, f32[3,32,256]{2,1,0:T(8,128)S(1)}, u32[]{:S(2)}, u32[]{:S(2)}) collective-permute-start(f32[3,32,256]{2,1,0:T(8,128)} %bitcast.8), channel_id=1, source_target_pairs={{0,4},{4,0},{8,12},{12,8},{16,20},{20,16},{24,28},{28,24},{1,5},{5... | collective-permute-start | bytes 294920 | tf_op jit(solution)/shard_map/ppermute | solution.py:421
  5.6 1.6 %collective-permute-start.7 = (f32[128,128]{1,0:T(8,128)}, f32[128,128]{1,0:T(8,128)S(1)}, u32[]{:S(2)}, u32[]{:S(2)}) collective-permute-start(f32[128,128]{1,0:T(8,128)} %param.2), channel_id=1, source_target_pairs={{0,4},{4,0},{8,12},{12,8},{16,20},{20,16},{24,28},{28,24},{1,5},{5... | collective-permute-start | bytes 196616 | tf_op jit(solution)/shard_map/ppermute | solution.py:421
  8.1 6.1 %collective-permute-start.9 = (f32[128,128]{1,0:T(8,128)S(1)}, f32[128,128]{1,0:T(8,128)S(1)}, u32[]{:S(2)}, u32[]{:S(2)}) collective-permute-start(f32[128,128]{1,0:T(8,128)S(1)} %get-tuple-element.40.refs_8_), channel_id=1, source_target_pairs={{0,24},{4,28},{8,16},{12,20},{16,8},{20,12},{24,0},{28,4},{1,25},{... | collective-permute-start | bytes 196616 | tf_op jit(solution)/shard_map/ppermute | solution.py:418
  10.8 4.3 %collective-permute-start.8 = (f32[128,128]{1,0:T(8,128)S(1)}, f32[128,128]{1,0:T(8,128)S(1)}, u32[]{:S(2)}, u32[]{:S(2)}) collective-permute-start(f32[128,128]{1,0:T(8,128)S(1)} %get-tuple-element.40.refs_8_), channel_id=1, source_target_pairs={{0,8},{4,12},{8,0},{12,4},{16,24},{20,28},{24,16},{28,20},{1,9},{5... | collective-permute-start | bytes 196616 | tf_op jit(solution)/shard_map/ppermute | solution.py:418
  13.5 1.6 %collective-permute-start.6 = (f32[3,32,256]{2,1,0:T(8,128)S(1)}, f32[3,32,256]{2,1,0:T(8,128)S(1)}, u32[]{:S(2)}, u32[]{:S(2)}) collective-permute-start(f32[3,32,256]{2,1,0:T(8,128)S(1)} %collective-permute-done.2.refs_3_), channel_id=1, source_target_pairs={{0,4},{4,0},{8,12},{12,8},{16,20},{20,16},{24,28},{28,24},{1,5},{5... | collective-permute-start | bytes 294920 | tf_op jit(solution)/shard_map/ppermute | solution.py:421
  13.5 1.6 %collective-permute-start.5 = (f32[3,32,256]{2,1,0:T(8,128)S(1)}, f32[3,32,256]{2,1,0:T(8,128)S(1)}, u32[]{:S(2)}, u32[]{:S(2)}) collective-permute-start(f32[3,32,256]{2,1,0:T(8,128)S(1)} %collective-permute-done.1.refs_2_), channel_id=1, source_target_pairs={{0,4},{4,0},{8,12},{12,8},{16,20},{20,16},{24,28},{28,24},{1,5},{5... | collective-permute-start | bytes 294920 | tf_op jit(solution)/shard_map/ppermute | solution.py:421
  14.0 1.3 %collective-permute-start.4 = (f32[3,32,256]{2,1,0:T(8,128)S(1)}, f32[3,32,256]{2,1,0:T(8,128)S(1)}, u32[]{:S(2)}, u32[]{:S(2)}) collective-permute-start(f32[3,32,256]{2,1,0:T(8,128)S(1)} %collective-permute-done.refs_1_), channel_id=1, source_target_pairs={{0,4},{4,0},{8,12},{12,8},{16,20},{20,16},{24,28},{28,24},{1,5},{5... | collective-permute-start | bytes 294920 | tf_op jit(solution)/shard_map/ppermute | solution.py:421
  19.3 8.1 %collective-permute-start.11 = (f32[128,128]{1,0:T(8,128)S(1)}, f32[128,128]{1,0:T(8,128)S(1)}, u32[]{:S(2)}, u32[]{:S(2)}) collective-permute-start(f32[128,128]{1,0:T(8,128)S(1)} %get-tuple-element.23), channel_id=1, source_target_pairs={{0,24},{4,28},{8,16},{12,20},{16,8},{20,12},{24,0},{28,4},{1,25},{... | collective-permute-start | bytes 196616 | tf_op jit(solution)/shard_map/ppermute | solution.py:418
  21.8 5.6 %collective-permute-start.10 = (f32[256,128]{1,0:T(8,128)S(1)}, f32[256,128]{1,0:T(8,128)S(1)}, u32[]{:S(2)}, u32[]{:S(2)}) collective-permute-start(f32[256,128]{1,0:T(8,128)S(1)} %get-tuple-element.22), channel_id=1, source_target_pairs={{0,8},{4,20},{8,0},{12,28},{16,24},{20,4},{24,16},{28,12},{1,9},{5... | collective-permute-start | bytes 393224 | tf_op jit(solution)/shard_map/ppermute | solution.py:418
  27.5 12.8 %collective-permute-start.16 = (f32[640,128]{1,0:T(8,128)S(1)}, f32[640,128]{1,0:T(8,128)S(1)}, u32[]{:S(2)}, u32[]{:S(2)}) collective-permute-start(f32[640,128]{1,0:T(8,128)S(1)} %get-tuple-element.33.refs_9_), channel_id=1, source_target_pairs={{0,8},{4,20},{8,0},{12,28},{16,24},{20,4},{24,16},{28,12},{1,9},{5... | collective-permute-start | bytes 983048 | tf_op jit(solution)/shard_map/ppermute | solution.py:418
  29.0 1.4 %collective-permute-start.12 = (f32[256,128]{1,0:T(8,128)S(1)}, f32[256,128]{1,0:T(8,128)S(1)}, u32[]{:S(2)}, u32[]{:S(2)}) collective-permute-start(f32[256,128]{1,0:T(8,128)S(1)} %collective-permute-done.10.near_ref), channel_id=1, source_target_pairs={{0,4},{4,0},{8,12},{12,8},{16,20},{20,16},{24,28},{28,24},{1,5},{5... | collective-permute-start | bytes 393224 | tf_op jit(solution)/shard_map/ppermute | solution.py:421
  29.0 1.4 %collective-permute-start.13 = (f32[128,128]{1,0:T(8,128)S(1)}, f32[128,128]{1,0:T(8,128)S(1)}, u32[]{:S(2)}, u32[]{:S(2)}) collective-permute-start(f32[128,128]{1,0:T(8,128)S(1)} %collective-permute-done.11.far_ref), channel_id=1, source_target_pairs={{0,4},{4,0},{8,12},{12,8},{16,20},{20,16},{24,28},{28,24},{1,5},{5... | collective-permute-start | bytes 196616 | tf_op jit(solution)/shard_map/ppermute | solution.py:421
  29.5 9.7 %collective-permute-start.17 = (f32[320,128]{1,0:T(8,128)S(1)}, f32[320,128]{1,0:T(8,128)S(1)}, u32[]{:S(2)}, u32[]{:S(2)}) collective-permute-start(f32[320,128]{1,0:T(8,128)S(1)} %get-tuple-element.34), channel_id=1, source_target_pairs={{0,24},{4,28},{8,16},{12,20},{16,8},{20,12},{24,0},{28,4},{1,25},{... | collective-permute-start | bytes 491528 | tf_op jit(solution)/shard_map/ppermute | solution.py:418
  32.3 7.9 %collective-permute-start.15 = (f32[192,128]{1,0:T(8,128)S(1)}, f32[192,128]{1,0:T(8,128)S(1)}, u32[]{:S(2)}, u32[]{:S(2)}) collective-permute-start(f32[192,128]{1,0:T(8,128)S(1)} %get-tuple-element.32), channel_id=1, source_target_pairs={{0,24},{4,28},{8,16},{12,20},{16,8},{20,12},{24,0},{28,4},{1,25},{... | collective-permute-start | bytes 294920 | tf_op jit(solution)/shard_map/ppermute | solution.py:418
  34.4 7.9 %collective-permute-start.14 = (f32[384,128]{1,0:T(8,128)S(1)}, f32[384,128]{1,0:T(8,128)S(1)}, u32[]{:S(2)}, u32[]{:S(2)}) collective-permute-start(f32[384,128]{1,0:T(8,128)S(1)} %get-tuple-element.31.refs_4_), channel_id=1, source_target_pairs={{0,8},{4,20},{8,0},{12,28},{16,24},{20,4},{24,16},{28,12},{1,9},{5... | collective-permute-start | bytes 589832 | tf_op jit(solution)/shard_map/ppermute | solution.py:418
  40.3 3.9 %collective-permute-start.20 = (f32[640,128]{1,0:T(8,128)S(1)}, f32[640,128]{1,0:T(8,128)S(1)}, u32[]{:S(2)}, u32[]{:S(2)}) collective-permute-start(f32[640,128]{1,0:T(8,128)S(1)} %collective-permute-done.16.refs_5_), channel_id=1, source_target_pairs={{0,4},{4,0},{8,12},{12,8},{16,20},{20,16},{24,28},{28,24},{1,5},{5... | collective-permute-start | bytes 983048 | tf_op jit(solution)/shard_map/ppermute | solution.py:421
  42.3 1.8 %collective-permute-start.18 = (f32[384,128]{1,0:T(8,128)S(1)}, f32[384,128]{1,0:T(8,128)S(1)}, u32[]{:S(2)}, u32[]{:S(2)}) collective-permute-start(f32[384,128]{1,0:T(8,128)S(1)} %collective-permute-done.14.refs_0_), channel_id=1, source_target_pairs={{0,4},{4,0},{8,12},{12,8},{16,20},{20,16},{24,28},{28,24},{1,5},{5... | collective-permute-start | bytes 589832 | tf_op jit(solution)/shard_map/ppermute | solution.py:421
  42.4 1.8 %collective-permute-start.21 = (f32[320,128]{1,0:T(8,128)S(1)}, f32[320,128]{1,0:T(8,128)S(1)}, u32[]{:S(2)}, u32[]{:S(2)}) collective-permute-start(f32[320,128]{1,0:T(8,128)S(1)} %collective-permute-done.17.refs_6_), channel_id=1, source_target_pairs={{0,4},{4,0},{8,12},{12,8},{16,20},{20,16},{24,28},{28,24},{1,5},{5... | collective-permute-start | bytes 491528 | tf_op jit(solution)/shard_map/ppermute | solution.py:421
  42.8 1.3 %collective-permute-start.19 = (f32[192,128]{1,0:T(8,128)S(1)}, f32[192,128]{1,0:T(8,128)S(1)}, u32[]{:S(2)}, u32[]{:S(2)}) collective-permute-start(f32[192,128]{1,0:T(8,128)S(1)} %collective-permute-done.15.refs_1_), channel_id=1, source_target_pairs={{0,4},{4,0},{8,12},{12,8},{16,20},{20,16},{24,28},{28,24},{1,5},{5... | collective-permute-start | bytes 294920 | tf_op jit(solution)/shard_map/ppermute | solution.py:421

commit v8 on v7

--- a/solution.py
+++ b/solution.py
@@ -132,33 +132,33 @@
     )
 
 
-def pair_operators(refl_ref, keep, out_ref):
-    block = refl_ref.shape[2]
-    for g, (first, second, sfirst, ssecond, cross, q, p) in enumerate(pair_inverses(refl_ref, keep)):
-        link = mm(mm(q, cross), p)
-        solved_p = mm(p, sfirst)
-        solved_q = mm(q, ssecond)
-        reach = mm(link, sfirst)
-        none = jnp.zeros((block, block), F32)
-        solved = jnp.concatenate(
-            [
-                jnp.concatenate(
-                    [-reach[:, :block], solved_q[:, :block] - reach[:, block:], solved_q[:, block:]], 1
-                ),
-                jnp.concatenate([solved_p, none], 1),
-            ],
-            0,
-        )
-        moved = mm(joined(first, second), solved, TN)
-        row = lax.broadcasted_iota(jnp.int32, moved.shape, 0)
-        col = lax.broadcasted_iota(jnp.int32, moved.shape, 1)
-        out_ref[g] = jnp.where(row == col, 1.0, 0.0) - moved
-
-
-def pair_action(refl_ref, keep, window):
-    block = refl_ref.shape[2]
+def whole_operator(parts, out_ref):
+    first, second, sfirst, ssecond, cross, q, p = parts
+    block = first.shape[0]
+    link = mm(mm(q, cross), p)
+    solved_p = mm(p, sfirst)
+    solved_q = mm(q, ssecond)
+    reach = mm(link, sfirst)
+    none = jnp.zeros((block, block), F32)
+    solved = jnp.concatenate(
+        [
+            jnp.concatenate(
+                [-reach[:, :block], solved_q[:, :block] - reach[:, block:], solved_q[:, block:]], 1
+            ),
+            jnp.concatenate([solved_p, none], 1),
+        ],
+        0,
+    )
+    moved = mm(joined(first, second), solved, TN)
+    row = lax.broadcasted_iota(jnp.int32, moved.shape, 0)
+    col = lax.broadcasted_iota(jnp.int32, moved.shape, 1)
+    out_ref[...] = jnp.where(row == col, 1.0, 0.0) - moved
+
+
+def pair_action(parts, window):
+    first, second, sfirst, ssecond, cross, q, p = parts
+    block = first.shape[0]
     cols = window.shape[1]
-    ((first, second, sfirst, ssecond, cross, q, p),) = pair_inverses(refl_ref, keep)
     weights_p = jnp.concatenate([mm(sfirst, window[: 2 * block]), sfirst[:, :block]], 1)
     weights_q = mm(ssecond, window[block:])
     weights_q = jnp.concatenate([weights_q, jnp.zeros((block, block), F32)], 1)
@@ -186,23 +186,19 @@
     return ref[pl.ds(pl.multiple_of(core * rows, rows), rows), :]
 
 
-def assemble(place_ref, mine, theirs, groups, refl_ref):
-    core, vec = place_ref[1], place_ref[2]
-    rows = mine[0].shape[1]
-    for step, (own, other) in enumerate(zip(mine, theirs)):
-        at = pl.ds(pl.multiple_of((step ^ vec) * rows, rows), rows)
-        for slot, group in enumerate(groups):
-            refl_ref[core, slot, at, :] = own[group]
-            refl_ref[1 - core, slot, at, :] = other[group]
-
-
 def first_kernel(count, nodes, place_ref, *refs):
     mine, theirs = refs[:count], refs[count : 2 * count]
     top_ref, low_ref, near_ref, far_ref = refs[2 * count : 2 * count + 4]
-    fixed_ref, lead_ref, out_near, out_far, refl_ref = refs[2 * count + 4 :]
+    fixed_ref, lead_ref, out_near, out_far, oper_ref, map_ref, map_half, refl_ref = refs[2 * count + 4 :]
     block = top_ref.shape[0]
-    node, core = place_ref[0], place_ref[1]
-    assemble(place_ref, mine, theirs, [0], refl_ref)
+    node, core, vec = place_ref[0], place_ref[1], place_ref[2]
+    groups, rows, _ = mine[0].shape
+    for step in range(count):
+        at = pl.ds(pl.multiple_of((step ^ vec) * rows, rows), rows)
+        for group in range(groups):
+            refl_ref[core, group, at, :] = mine[step][group]
+            refl_ref[1 - core, group, at, :] = theirs[step][group]
+    parts = pair_inverses(refl_ref, node != nodes - 1)
     below = jnp.where((node & 1) == 0, near_ref[...], far_ref[...])
     window = jnp.concatenate(
         [
@@ -212,23 +208,15 @@
         ],
         0,
     )
-    fixed, lead = pair_action(refl_ref, node != nodes - 1, window)
+    fixed, lead = pair_action(parts[0], window)
     fixed_ref[...] = fixed
     lead_ref[...] = lead
     out_near[:block] = pick_near(node, core, fixed)
     out_near[block:] = pick_near(node, core, lead)
     out_far[...] = jnp.where(core == 0, pick_far(node, fixed), pick_far(node, lead))
-
-
-def later_kernel(count, nodes, place_ref, *refs):
-    mine, theirs = refs[:count], refs[count : 2 * count]
-    oper_ref, map_ref, map_half, refl_ref = refs[2 * count :]
-    node, core = place_ref[0], place_ref[1]
-    later, size, _ = oper_ref.shape
-    block = size // 3
-    assemble(place_ref, mine, theirs, range(1, 1 + later), refl_ref)
-    pair_operators(refl_ref, node != nodes - 1, oper_ref)
-    if later != 2:
+    for group in range(1, groups):
+        whole_operator(parts[group], oper_ref.at[group - 1])
+    if groups != 3:
         return
     up, own, out = (slice(part * block, (part + 1) * block) for part in range(3))
     map_ref[:block] = oper_ref[0, out, :block]
@@ -239,7 +227,18 @@
     map_half[...] = half_of(core, map_ref)
 
 
-def next_kernel(place_ref, near_ref, far_ref, near2_ref, far2_ref, fixed_ref, lead_ref, oper_ref, *outs):
+def between_kernel(place_ref, fixed_ref, lead_ref, oper_ref, base_ref, onto_ref):
+    block = fixed_ref.shape[0] // 3
+    own = slice(block, 2 * block)
+    first = jnp.where(place_ref[0] == 0, fixed_ref[:block], 0.0)
+    operator = oper_ref.at[0]
+    base_ref[...] = mm(
+        operator[:, : 2 * block], jnp.concatenate([first, fixed_ref[own]], 0)
+    )
+    onto_ref[...] = mm(operator[:, own], lead_ref[own])
+
+
+def next_kernel(place_ref, near_ref, far_ref, near2_ref, far2_ref, fixed_ref, lead_ref, oper_ref, base_ref, onto_ref, *outs):
     out_fixed, out_vec, out_half = outs
     block = far_ref.shape[0]
     node, core = place_ref[0], place_ref[1]
@@ -256,27 +255,23 @@
     step = came1 + mm(map1, carry)
     carry = jnp.where(node == 3, step, carry)
     up, own, out = (slice(part * block, (part + 1) * block) for part in range(3))
-    fixed, lead = fixed_ref[...], lead_ref[...]
-    cols = fixed.shape[1]
-    none = jnp.zeros((block, block), F32)
-    below = mm(jnp.where(odd, map3, map1), jnp.concatenate([fixed[out], lead[out]], 1))
-    below += jnp.concatenate([jnp.where(odd, came3, came1), none], 1)
-    window = jnp.concatenate(
-        [
-            jnp.concatenate([jnp.where(node == 0, fixed[up], 0.0), none], 1),
-            jnp.concatenate([fixed[own], lead[own]], 1),
-            jnp.where(node == 3, 0.0, below),
-        ],
-        0,
-    )
-    moved = mm(oper_ref[0], window)
-    fixed = moved[:, :cols] + mm(moved[:, cols:], carry)
+    cols = carry.shape[1]
+    reach = mm(
+        jnp.where(odd, map3, map1), jnp.concatenate([fixed_ref[out], lead_ref[out]], 1)
+    )
+    below = jnp.where(odd, came3, came1) + reach[:, :cols] + mm(reach[:, cols:], carry)
+    below = jnp.where(node == 3, 0.0, below)
+    fixed = base_ref[...] + mm(
+        jnp.concatenate([oper_ref[0, :, out], onto_ref[...]], 1),
+        jnp.concatenate([below, carry], 0),
+    )
     out_fixed[...] = fixed
     out_vec[:block] = fixed[out]
     out_vec[block : 2 * block] = fixed[up]
-    part = mm(oper_ref[1, out, own], fixed[own])
-    first = mm(oper_ref[1, out, up], fixed[up])
-    out_vec[2 * block :] = part + jnp.where(node == 0, first, 0.0)
+    first = jnp.where(node == 0, fixed[up], 0.0)
+    out_vec[2 * block :] = mm(
+        oper_ref[1, out, : 2 * block], jnp.concatenate([first, fixed[own]], 0)
+    )
     out_half[...] = half_of(core, out_vec)
 
 
@@ -439,21 +434,19 @@
     later = groups - 1
     size = 3 * block
     maps = 5 * block
-    work = 16 * size**3
-    pieces = [place, *mine, *theirs]
-    fixed, lead, near, far = call(
+    fixed, lead, near, far, operators, sent, sent_half = call(
         functools.partial(first_kernel, len(mine), nodes),
-        [(size, cols), (size, block), (2 * block, cols), (block, cols)],
-        [*pieces, top, low, *below],
-        [pltpu.VMEM((PAIR, 1, block, window), F32)],
-        work,
-    )
-    operators, sent, sent_half = call(
-        functools.partial(later_kernel, len(mine), nodes),
-        [(later, size, size), (maps, block), (maps // PAIR, block)],
-        pieces,
-        [pltpu.VMEM((PAIR, later, block, window), F32)],
-        work * later,
+        [
+            (size, cols),
+            (size, block),
+            (2 * block, cols),
+            (block, cols),
+            (later, size, size),
+            (maps, block),
+            (maps // PAIR, block),
+        ],
+        [place, *mine, *theirs, top, low, *below],
+        [pltpu.VMEM((PAIR, groups, block, window), F32)],
     )
     if nodes != 4 or groups != 3:
         result = many_pairs(fixed, lead, operators, node, nodes, row_count)
@@ -462,13 +455,19 @@
     def shared(near, far):
         return [place, near, far, across(near), across(far)]
 
+    base, onto = call(
+        between_kernel,
+        [(size, cols), (size, block)],
+        [place, fixed, lead, operators],
+        work=32 * size**3,
+    )
     near, far = swap(near, (1, 2)), swap(far, (3, 3))
-    near, far, sent, sent_half = hold((near, far, sent, sent_half))
+    near, far, base = hold((near, far, base))
     known = [swap(sent, (1, 2)), swap(sent_half, (3, 3))]
     fixed, vec, vec_half = call(
         next_kernel,
         [(size, cols), (size, cols), (size // PAIR, cols)],
-        [*shared(near, far), fixed, lead, operators],
+        [*shared(near, far), fixed, lead, operators, base, onto],
     )
     near, far = swap(vec, (1, 2)), swap(vec_half, (3, 3))
     far, *known = hold((far, *known))

time: 45.9 us -> 44.1 us (0.961)
  Pallas kernels: 12.5 us -> 10.4 us
  starting transfers between devices: 18.7 us -> 20.2 us
  waiting for transfers between devices: 12.6 us -> 11.5 us
    pallas_call x4, Pallas kernels: 12.5 us -> 10.4 us  [call(): pl.pallas_call(kernel, out_shape=[jax.ShapeDtypeStruct(shape, F32) for sh...]
    ppermute x8, starting transfers between devices: 10.9 us -> 12.2 us  [swap(): return lax.ppermute(value, 'rows', moves)]
    ppermute x8, waiting for transfers between devices: 8.29 us -> 7.45 us  [swap(): return lax.ppermute(value, 'rows', moves)]
    ppermute x11, waiting for transfers between devices: 2.17 us -> 1.69 us  [across(): lax.ppermute(value, 'rows', [(place, place ^ 1) for place in range(row_co...]
  transfers between devices with their start and end apart: 22 -> 22, of which waited for: 9 -> 9; matrix products, arithmetic and copies ran while one was open for 4% -> 4% of each run, Pallas kernels for 15% -> 6%
where the time goes in v8:
time: 44.1 us; the launch traced here: 43.9 us
  starting transfers between devices  20.2 us (46%)
  waiting for transfers between devices  11.5 us (26%)
  Pallas kernels  10.4 us (24%)
  other arithmetic  1.83 us (4%)
    ppermute x8, starting transfers between devices, swap(): return lax.ppermute(value, 'rows', moves)  12.2 us
    pallas_call x4, Pallas kernels, call(): pl.pallas_call(kernel, out_shape=[jax.ShapeDtypeStruct(shape, F32) for sh...  10.4 us
    ppermute x8, waiting for transfers between devices, swap(): return lax.ppermute(value, 'rows', moves)  7.45 us
    ppermute x3, starting transfers between devices, spread(): lax.ppermute(value, axis, [(place, place ^ mask) for place in range(size)])  5.62 us
    ppermute x11, starting transfers between devices, across(): lax.ppermute(value, 'rows', [(place, place ^ 1) for place in range(row_co...  2.36 us
    ppermute x3, waiting for transfers between devices, spread(): lax.ppermute(value, axis, [(place, place ^ mask) for place in range(size)])  2.31 us
    ppermute x11, waiting for transfers between devices, across(): lax.ppermute(value, 'rows', [(place, place ^ 1) for place in range(row_co...  1.69 us
    select_n x1, other arithmetic, local(): mine[0] = jnp.where(vec_index < 0, 0.0, mine[0])  0.9 us
  transfers between devices with their start and end apart: 22, of which 9 were waited for; matrix products, arithmetic and copies ran while one was open for 4% of the time, Pallas kernels for 6%

profile of v8, /device:TPU:0, one launch (start us, length us, event | category | flops | bytes accessed | tf_op | source)
XLA Modules:
  0.0 43.9 jit_solution(5227137294949645166)
XLA Ops:
  0.0 3.0 %collective-permute-start = (f32[3,32,256]{2,1,0:T(8,128)}, f32[3,32,256]{2,1,0:T(8,128)S(1)}, u32[]{:S(2)}, u32[]{:S(2)}) collective-permute-start(f32[3,32,256]{2,1,0:T(8,128)} %bitcast.5), channel_id=1, source_target_pairs={{0,1},{1,0},{2,3},{3,2},{4,5},{5,4},{6,7},{7,6},{8,9},{9,8},{10,11... | collective-permute-start | bytes 294920 | tf_op jit(solution)/shard_map/ppermute | solution.py:361
  3.0 2.6 %collective-permute-start.1 = (f32[3,32,256]{2,1,0:T(8,128)}, f32[3,32,256]{2,1,0:T(8,128)S(1)}, u32[]{:S(2)}, u32[]{:S(2)}) collective-permute-start(f32[3,32,256]{2,1,0:T(8,128)} %bitcast.6), channel_id=1, source_target_pairs={{0,2},{1,3},{2,0},{3,1},{4,6},{5,7},{6,4},{7,5},{8,10},{9,11},{10,... | collective-permute-start | bytes 294920 | tf_op jit(solution)/shard_map/ppermute | solution.py:361
  6.1 0.9 %broadcast_select_fusion.refs_0_ = f32[3,32,256]{2,1,0:T(8,128)S(1)} fusion(pred[]{:T(512)S(6)} %lt.10, f32[3,1,32,256]{3,2,1,0:T(8,128)} %param.3), kind=kLoop, calls=%fused_computation | loop fusion | flops 24576 | bytes 196609 | tf_op jit(solution)/shard_map/jit(_where)/select_n | solution.py:431
  7.2 0.8 %broadcast_select_fusion.1 = (f32[128,128]{1,0:T(8,128)S(1)}, f32[128,128]{1,0:T(8,128)S(1)}) fusion(f32[128,128]{1,0:T(8,128)S(1)} %collective-permute-done.7, f32[128,128]{1,0:T(8,128)} %param.2, pred[]{:T(512)S(6)} %eq.6), kind=kLoop, calls=%fused_computation.1 | loop fusion | flops 32768 | bytes 262145 | tf_op jit(solution)/shard_map/jit(_where)/select_n | solution.py:421
  8.1 1.8 %collective-permute-start.8 = (f32[128,128]{1,0:T(8,128)S(1)}, f32[128,128]{1,0:T(8,128)S(1)}, u32[]{:S(2)}, u32[]{:S(2)}) collective-permute-start(f32[128,128]{1,0:T(8,128)S(1)} %get-tuple-element.42.refs_8_), channel_id=1, source_target_pairs={{0,8},{4,12},{8,0},{12,4},{16,24},{20,28},{24,16},{28,20},{1,9},{5... | collective-permute-start | bytes 196616 | tf_op jit(solution)/shard_map/ppermute | solution.py:413
  9.9 1.5 %collective-permute-start.9 = (f32[128,128]{1,0:T(8,128)S(1)}, f32[128,128]{1,0:T(8,128)S(1)}, u32[]{:S(2)}, u32[]{:S(2)}) collective-permute-start(f32[128,128]{1,0:T(8,128)S(1)} %get-tuple-element.42.refs_8_), channel_id=1, source_target_pairs={{0,24},{4,28},{8,16},{12,20},{16,8},{20,12},{24,0},{28,4},{1,25},{... | collective-permute-start | bytes 196616 | tf_op jit(solution)/shard_map/ppermute | solution.py:413
  11.4 2.3 %collective-permute-done.1.refs_2_ = f32[3,32,256]{2,1,0:T(8,128)S(1)} collective-permute-done((f32[3,32,256]{2,1,0:T(8,128)}, f32[3,32,256]{2,1,0:T(8,128)S(1)}, u32[]{:S(2)}, u32[]{:S(2)}) %collective-permute-start.1) | collective-permute-done | bytes 98336 | tf_op jit(solution)/shard_map/ppermute | solution.py:361
  14.3 0.7 %collective-permute-done.9.refs_11_ = f32[128,128]{1,0:T(8,128)S(1)} collective-permute-done((f32[128,128]{1,0:T(8,128)S(1)}, f32[128,128]{1,0:T(8,128)S(1)}, u32[]{:S(2)}, u32[]{:S(2)}) %collective-permute-start.9) | collective-permute-done | bytes 65568 | tf_op jit(solution)/shard_map/ppermute | solution.py:413
  15.5 6.2 %shard_map.28 = (f32[384,128]{1,0:T(8,128)S(1)}, f32[384,128]{1,0:T(8,128)S(1)}, f32[256,128]{1,0:T(8,128)S(1)}, f32[128,128]{1,0:T(8,128)S(1)}, f32[2,384,384]{...) custom-call(s32[3]{0:T(128)S(1)} %pad_add_fusion.place_ref, ...), custom_call_target="tpu_custom_call" | custom-call | tf_op jit(solution)/shard_map/pallas_call | solution.py:341
  21.7 1.6 %collective-permute-start.10 = (f32[256,128]{1,0:T(8,128)S(1)}, f32[256,128]{1,0:T(8,128)S(1)}, u32[]{:S(2)}, u32[]{:S(2)}) collective-permute-start(f32[256,128]{1,0:T(8,128)S(1)} %get-tuple-element.23), channel_id=1, source_target_pairs={{0,8},{4,20},{8,0},{12,28},{16,24},{20,4},{24,16},{28,12},{1,9},{5... | collective-permute-start | bytes 393224 | tf_op jit(solution)/shard_map/ppermute | solution.py:413
  23.2 1.5 %collective-permute-start.11 = (f32[128,128]{1,0:T(8,128)S(1)}, f32[128,128]{1,0:T(8,128)S(1)}, u32[]{:S(2)}, u32[]{:S(2)}) collective-permute-start(f32[128,128]{1,0:T(8,128)S(1)} %get-tuple-element.24), channel_id=1, source_target_pairs={{0,24},{4,28},{8,16},{12,20},{16,8},{20,12},{24,0},{28,4},{1,25},{... | collective-permute-start | bytes 196616 | tf_op jit(solution)/shard_map/ppermute | solution.py:413
  24.7 1.5 %collective-permute-start.16 = (f32[640,128]{1,0:T(8,128)S(1)}, f32[640,128]{1,0:T(8,128)S(1)}, u32[]{:S(2)}, u32[]{:S(2)}) collective-permute-start(f32[640,128]{1,0:T(8,128)S(1)} %get-tuple-element.35.refs_9_), channel_id=1, source_target_pairs={{0,8},{4,20},{8,0},{12,28},{16,24},{20,4},{24,16},{28,12},{1,9},{5... | collective-permute-start | bytes 983048 | tf_op jit(solution)/shard_map/ppermute | solution.py:413
  26.2 0.9 %shard_map.29 = (f32[384,128]{1,0:T(8,128)S(1)}, f32[384,128]{1,0:T(8,128)S(1)}) custom-call(s32[3]{0:T(128)S(1)} %pad_add_fusion.place_ref, f32[384,128]{1,0:T(8,128)S(1)} %get-tuple-element.25.fixed_ref, f32[384,128]{1,0:T(8,128)S(1)} %get-tuple-element.26.lead_ref, f32[2,384,384]{2,1,0:T(8,128)S(1)} %get-tuple-element.27.oper_ref.refs_11_), custom_call_target="tpu_custom_call" | custom-call | flops 1811939328 | tf_op jit(solution)/shard_map/pallas_call | solution.py:341
  27.2 2.0 %collective-permute-done.11.far_ref = f32[128,128]{1,0:T(8,128)S(1)} collective-permute-done((f32[128,128]{1,0:T(8,128)S(1)}, f32[128,128]{1,0:T(8,128)S(1)}, u32[]{:S(2)}, u32[]{:S(2)}) %collective-permute-start.11) | collective-permute-done | bytes 65568 | tf_op jit(solution)/shard_map/ppermute | solution.py:413
  29.2 0.5 %collective-permute-start.13 = (f32[128,128]{1,0:T(8,128)S(1)}, f32[128,128]{1,0:T(8,128)S(1)}, u32[]{:S(2)}, u32[]{:S(2)}) collective-permute-start(f32[128,128]{1,0:T(8,128)S(1)} %collective-permute-done.11.far_ref), channel_id=1, source_target_pairs={{0,4},{4,0},{8,12},{12,8},{16,20},{20,16},{24,28},{28,24},{1,5},{5... | collective-permute-start | bytes 196616 | tf_op jit(solution)/shard_map/ppermute | solution.py:416
  29.7 1.4 %collective-permute-start.17 = (f32[320,128]{1,0:T(8,128)S(1)}, f32[320,128]{1,0:T(8,128)S(1)}, u32[]{:S(2)}, u32[]{:S(2)}) collective-permute-start(f32[320,128]{1,0:T(8,128)S(1)} %get-tuple-element.36), channel_id=1, source_target_pairs={{0,24},{4,28},{8,16},{12,20},{16,8},{20,12},{24,0},{28,4},{1,25},{... | collective-permute-start | bytes 491528 | tf_op jit(solution)/shard_map/ppermute | solution.py:413
  31.1 1.7 %shard_map.30 = (f32[384,128]{1,0:T(8,128)S(1)}, f32[384,128]{1,0:T(8,128)S(1)}, f32[192,128]{1,0:T(8,128)S(1)}) custom-call(s32[3]{0:T(128)S(1)} %pad_add_fusion.place_ref, f32[256,128]{1,0:T(8,128)S(1)} %collective-permute-done.10.near_ref, f32[128,128]{1,0:T(8,128)S(1)} %collective-permute-done.11.far_ref, ...), custom_call_target="tpu_custom_call" | custom-call | tf_op jit(solution)/shard_map/pallas_call | solution.py:341
  32.7 1.6 %collective-permute-start.15 = (f32[192,128]{1,0:T(8,128)S(1)}, f32[192,128]{1,0:T(8,128)S(1)}, u32[]{:S(2)}, u32[]{:S(2)}) collective-permute-start(f32[192,128]{1,0:T(8,128)S(1)} %get-tuple-element.34), channel_id=1, source_target_pairs={{0,24},{4,28},{8,16},{12,20},{16,8},{20,12},{24,0},{28,4},{1,25},{... | collective-permute-start | bytes 294920 | tf_op jit(solution)/shard_map/ppermute | solution.py:413
  34.3 1.4 %collective-permute-start.14 = (f32[384,128]{1,0:T(8,128)S(1)}, f32[384,128]{1,0:T(8,128)S(1)}, u32[]{:S(2)}, u32[]{:S(2)}) collective-permute-start(f32[384,128]{1,0:T(8,128)S(1)} %get-tuple-element.33.refs_4_), channel_id=1, source_target_pairs={{0,8},{4,20},{8,0},{12,28},{16,24},{20,4},{24,16},{28,12},{1,9},{5... | collective-permute-start | bytes 589832 | tf_op jit(solution)/shard_map/ppermute | solution.py:413
  35.8 1.4 %collective-permute-done.17.refs_6_ = f32[320,128]{1,0:T(8,128)S(1)} collective-permute-done((f32[320,128]{1,0:T(8,128)S(1)}, f32[320,128]{1,0:T(8,128)S(1)}, u32[]{:S(2)}, u32[]{:S(2)}) %collective-permute-start.17) | collective-permute-done | bytes 163872 | tf_op jit(solution)/shard_map/ppermute | solution.py:413
  37.2 1.7 %collective-permute-done.15.refs_1_ = f32[192,128]{1,0:T(8,128)S(1)} collective-permute-done((f32[192,128]{1,0:T(8,128)S(1)}, f32[192,128]{1,0:T(8,128)S(1)}, u32[]{:S(2)}, u32[]{:S(2)}) %collective-permute-start.15) | collective-permute-done | bytes 98336 | tf_op jit(solution)/shard_map/ppermute | solution.py:413
  38.9 1.6 %collective-permute-done.14.refs_0_ = f32[384,128]{1,0:T(8,128)S(1)} collective-permute-done((f32[384,128]{1,0:T(8,128)S(1)}, f32[384,128]{1,0:T(8,128)S(1)}, u32[]{:S(2)}, u32[]{:S(2)}) %collective-permute-start.14) | collective-permute-done | bytes 196640 | tf_op jit(solution)/shard_map/ppermute | solution.py:413
  41.2 1.1 %collective-permute-done.19.refs_3_ = f32[192,128]{1,0:T(8,128)S(1)} collective-permute-done((f32[192,128]{1,0:T(8,128)S(1)}, f32[192,128]{1,0:T(8,128)S(1)}, u32[]{:S(2)}, u32[]{:S(2)}) %collective-permute-start.19) | collective-permute-done | bytes 98336 | tf_op jit(solution)/shard_map/ppermute | solution.py:416
  42.3 1.6 %shard_map.31 = f32[128,128]{1,0:T(8,128)} custom-call(s32[3]{0:T(128)S(1)} %pad_add_fusion.place_ref, f32[384,128]{1,0:T(8,128)S(1)} %collective-permute-done.14.refs_0_, f32[192,128]{1,0:T(8,128)S(1)} %collective-permute-done.15.refs_1_, f32[384,128]{1,0:T(8,128)S(1)} %collective-permute-done.18.refs_2_, f32[192,128]{1,0:T(8,128)S(1)} %collective-permute-done.19.refs_3_, ...), custom_call_target="tpu_custom_call" | custom-call | tf_op jit(solution)/shard_map/pallas_call | solution.py:341
  (27 shorter events, 2.6 us)
Async XLA Ops:
  0.0 9.9 %collective-permute-start = (f32[3,32,256]{2,1,0:T(8,128)}, f32[3,32,256]{2,1,0:T(8,128)S(1)}, u32[]{:S(2)}, u32[]{:S(2)}) collective-permute-start(f32[3,32,256]{2,1,0:T(8,128)} %bitcast.5), channel_id=1, source_target_pairs={{0,1},{1,0},{2,3},{3,2},{4,5},{5,4},{6,7},{7,6},{8,9},{9,8},{10,11... | collective-permute-start | bytes 294920 | tf_op jit(solution)/shard_map/ppermute | solution.py:361
  3.0 10.6 %collective-permute-start.1 = (f32[3,32,256]{2,1,0:T(8,128)}, f32[3,32,256]{2,1,0:T(8,128)S(1)}, u32[]{:S(2)}, u32[]{:S(2)}) collective-permute-start(f32[3,32,256]{2,1,0:T(8,128)} %bitcast.6), channel_id=1, source_target_pairs={{0,2},{1,3},{2,0},{3,1},{4,6},{5,7},{6,4},{7,5},{8,10},{9,11},{10,... | collective-permute-start | bytes 294920 | tf_op jit(solution)/shard_map/ppermute | solution.py:361
  5.6 8.1 %collective-permute-start.2 = (f32[3,32,256]{2,1,0:T(8,128)}, f32[3,32,256]{2,1,0:T(8,128)S(1)}, u32[]{:S(2)}, u32[]{:S(2)}) collective-permute-start(f32[3,32,256]{2,1,0:T(8,128)} %bitcast.7), channel_id=1, source_target_pairs={{0,3},{1,2},{2,1},{3,0},{4,7},{5,6},{6,5},{7,4},{8,11},{9,10},{10,... | collective-permute-start | bytes 294920 | tf_op jit(solution)/shard_map/ppermute | solution.py:361
  5.6 8.6 %collective-permute-start.3 = (f32[3,32,256]{2,1,0:T(8,128)}, f32[3,32,256]{2,1,0:T(8,128)S(1)}, u32[]{:S(2)}, u32[]{:S(2)}) collective-permute-start(f32[3,32,256]{2,1,0:T(8,128)} %bitcast.8), channel_id=1, source_target_pairs={{0,4},{4,0},{8,12},{12,8},{16,20},{20,16},{24,28},{28,24},{1,5},{5... | collective-permute-start | bytes 294920 | tf_op jit(solution)/shard_map/ppermute | solution.py:416
  5.6 1.6 %collective-permute-start.7 = (f32[128,128]{1,0:T(8,128)}, f32[128,128]{1,0:T(8,128)S(1)}, u32[]{:S(2)}, u32[]{:S(2)}) collective-permute-start(f32[128,128]{1,0:T(8,128)} %param.2), channel_id=1, source_target_pairs={{0,4},{4,0},{8,12},{12,8},{16,20},{20,16},{24,28},{28,24},{1,5},{5... | collective-permute-start | bytes 196616 | tf_op jit(solution)/shard_map/ppermute | solution.py:416
  8.1 6.2 %collective-permute-start.8 = (f32[128,128]{1,0:T(8,128)S(1)}, f32[128,128]{1,0:T(8,128)S(1)}, u32[]{:S(2)}, u32[]{:S(2)}) collective-permute-start(f32[128,128]{1,0:T(8,128)S(1)} %get-tuple-element.42.refs_8_), channel_id=1, source_target_pairs={{0,8},{4,12},{8,0},{12,4},{16,24},{20,28},{24,16},{28,20},{1,9},{5... | collective-permute-start | bytes 196616 | tf_op jit(solution)/shard_map/ppermute | solution.py:413
  9.9 5.2 %collective-permute-start.9 = (f32[128,128]{1,0:T(8,128)S(1)}, f32[128,128]{1,0:T(8,128)S(1)}, u32[]{:S(2)}, u32[]{:S(2)}) collective-permute-start(f32[128,128]{1,0:T(8,128)S(1)} %get-tuple-element.42.refs_8_), channel_id=1, source_target_pairs={{0,24},{4,28},{8,16},{12,20},{16,8},{20,12},{24,0},{28,4},{1,25},{... | collective-permute-start | bytes 196616 | tf_op jit(solution)/shard_map/ppermute | solution.py:413
  13.7 1.4 %collective-permute-start.4 = (f32[3,32,256]{2,1,0:T(8,128)S(1)}, f32[3,32,256]{2,1,0:T(8,128)S(1)}, u32[]{:S(2)}, u32[]{:S(2)}) collective-permute-start(f32[3,32,256]{2,1,0:T(8,128)S(1)} %collective-permute-done.refs_1_), channel_id=1, source_target_pairs={{0,4},{4,0},{8,12},{12,8},{16,20},{20,16},{24,28},{28,24},{1,5},{5... | collective-permute-start | bytes 294920 | tf_op jit(solution)/shard_map/ppermute | solution.py:416
  13.7 1.5 %collective-permute-start.5 = (f32[3,32,256]{2,1,0:T(8,128)S(1)}, f32[3,32,256]{2,1,0:T(8,128)S(1)}, u32[]{:S(2)}, u32[]{:S(2)}) collective-permute-start(f32[3,32,256]{2,1,0:T(8,128)S(1)} %collective-permute-done.1.refs_2_), channel_id=1, source_target_pairs={{0,4},{4,0},{8,12},{12,8},{16,20},{20,16},{24,28},{28,24},{1,5},{5... | collective-permute-start | bytes 294920 | tf_op jit(solution)/shard_map/ppermute | solution.py:416
  14.2 1.3 %collective-permute-start.6 = (f32[3,32,256]{2,1,0:T(8,128)S(1)}, f32[3,32,256]{2,1,0:T(8,128)S(1)}, u32[]{:S(2)}, u32[]{:S(2)}) collective-permute-start(f32[3,32,256]{2,1,0:T(8,128)S(1)} %collective-permute-done.2.refs_3_), channel_id=1, source_target_pairs={{0,4},{4,0},{8,12},{12,8},{16,20},{20,16},{24,28},{28,24},{1,5},{5... | collective-permute-start | bytes 294920 | tf_op jit(solution)/shard_map/ppermute | solution.py:416
  21.7 7.5 %collective-permute-start.10 = (f32[256,128]{1,0:T(8,128)S(1)}, f32[256,128]{1,0:T(8,128)S(1)}, u32[]{:S(2)}, u32[]{:S(2)}) collective-permute-start(f32[256,128]{1,0:T(8,128)S(1)} %get-tuple-element.23), channel_id=1, source_target_pairs={{0,8},{4,20},{8,0},{12,28},{16,24},{20,4},{24,16},{28,12},{1,9},{5... | collective-permute-start | bytes 393224 | tf_op jit(solution)/shard_map/ppermute | solution.py:413
  23.2 5.9 %collective-permute-start.11 = (f32[128,128]{1,0:T(8,128)S(1)}, f32[128,128]{1,0:T(8,128)S(1)}, u32[]{:S(2)}, u32[]{:S(2)}) collective-permute-start(f32[128,128]{1,0:T(8,128)S(1)} %get-tuple-element.24), channel_id=1, source_target_pairs={{0,24},{4,28},{8,16},{12,20},{16,8},{20,12},{24,0},{28,4},{1,25},{... | collective-permute-start | bytes 196616 | tf_op jit(solution)/shard_map/ppermute | solution.py:413
  24.7 12.5 %collective-permute-start.16 = (f32[640,128]{1,0:T(8,128)S(1)}, f32[640,128]{1,0:T(8,128)S(1)}, u32[]{:S(2)}, u32[]{:S(2)}) collective-permute-start(f32[640,128]{1,0:T(8,128)S(1)} %get-tuple-element.35.refs_9_), channel_id=1, source_target_pairs={{0,8},{4,20},{8,0},{12,28},{16,24},{20,4},{24,16},{28,12},{1,9},{5... | collective-permute-start | bytes 983048 | tf_op jit(solution)/shard_map/ppermute | solution.py:413
  29.2 1.9 %collective-permute-start.12 = (f32[256,128]{1,0:T(8,128)S(1)}, f32[256,128]{1,0:T(8,128)S(1)}, u32[]{:S(2)}, u32[]{:S(2)}) collective-permute-start(f32[256,128]{1,0:T(8,128)S(1)} %collective-permute-done.10.near_ref), channel_id=1, source_target_pairs={{0,4},{4,0},{8,12},{12,8},{16,20},{20,16},{24,28},{28,24},{1,5},{5... | collective-permute-start | bytes 393224 | tf_op jit(solution)/shard_map/ppermute | solution.py:416
  29.2 1.9 %collective-permute-start.13 = (f32[128,128]{1,0:T(8,128)S(1)}, f32[128,128]{1,0:T(8,128)S(1)}, u32[]{:S(2)}, u32[]{:S(2)}) collective-permute-start(f32[128,128]{1,0:T(8,128)S(1)} %collective-permute-done.11.far_ref), channel_id=1, source_target_pairs={{0,4},{4,0},{8,12},{12,8},{16,20},{20,16},{24,28},{28,24},{1,5},{5... | collective-permute-start | bytes 196616 | tf_op jit(solution)/shard_map/ppermute | solution.py:416
  29.7 7.5 %collective-permute-start.17 = (f32[320,128]{1,0:T(8,128)S(1)}, f32[320,128]{1,0:T(8,128)S(1)}, u32[]{:S(2)}, u32[]{:S(2)}) collective-permute-start(f32[320,128]{1,0:T(8,128)S(1)} %get-tuple-element.36), channel_id=1, source_target_pairs={{0,24},{4,28},{8,16},{12,20},{16,8},{20,12},{24,0},{28,4},{1,25},{... | collective-permute-start | bytes 491528 | tf_op jit(solution)/shard_map/ppermute | solution.py:413
  32.7 6.2 %collective-permute-start.15 = (f32[192,128]{1,0:T(8,128)S(1)}, f32[192,128]{1,0:T(8,128)S(1)}, u32[]{:S(2)}, u32[]{:S(2)}) collective-permute-start(f32[192,128]{1,0:T(8,128)S(1)} %get-tuple-element.34), channel_id=1, source_target_pairs={{0,24},{4,28},{8,16},{12,20},{16,8},{20,12},{24,0},{28,4},{1,25},{... | collective-permute-start | bytes 294920 | tf_op jit(solution)/shard_map/ppermute | solution.py:413
  34.3 6.1 %collective-permute-start.14 = (f32[384,128]{1,0:T(8,128)S(1)}, f32[384,128]{1,0:T(8,128)S(1)}, u32[]{:S(2)}, u32[]{:S(2)}) collective-permute-start(f32[384,128]{1,0:T(8,128)S(1)} %get-tuple-element.33.refs_4_), channel_id=1, source_target_pairs={{0,8},{4,20},{8,0},{12,28},{16,24},{20,4},{24,16},{28,12},{1,9},{5... | collective-permute-start | bytes 589832 | tf_op jit(solution)/shard_map/ppermute | solution.py:413
  38.9 3.4 %collective-permute-start.20 = (f32[640,128]{1,0:T(8,128)S(1)}, f32[640,128]{1,0:T(8,128)S(1)}, u32[]{:S(2)}, u32[]{:S(2)}) collective-permute-start(f32[640,128]{1,0:T(8,128)S(1)} %collective-permute-done.16.refs_5_), channel_id=1, source_target_pairs={{0,4},{4,0},{8,12},{12,8},{16,20},{20,16},{24,28},{28,24},{1,5},{5... | collective-permute-start | bytes 983048 | tf_op jit(solution)/shard_map/ppermute | solution.py:416
  40.5 1.8 %collective-permute-start.18 = (f32[384,128]{1,0:T(8,128)S(1)}, f32[384,128]{1,0:T(8,128)S(1)}, u32[]{:S(2)}, u32[]{:S(2)}) collective-permute-start(f32[384,128]{1,0:T(8,128)S(1)} %collective-permute-done.14.refs_0_), channel_id=1, source_target_pairs={{0,4},{4,0},{8,12},{12,8},{16,20},{20,16},{24,28},{28,24},{1,5},{5... | collective-permute-start | bytes 589832 | tf_op jit(solution)/shard_map/ppermute | solution.py:416
  40.7 1.6 %collective-permute-start.21 = (f32[320,128]{1,0:T(8,128)S(1)}, f32[320,128]{1,0:T(8,128)S(1)}, u32[]{:S(2)}, u32[]{:S(2)}) collective-permute-start(f32[320,128]{1,0:T(8,128)S(1)} %collective-permute-done.17.refs_6_), channel_id=1, source_target_pairs={{0,4},{4,0},{8,12},{12,8},{16,20},{20,16},{24,28},{28,24},{1,5},{5... | collective-permute-start | bytes 491528 | tf_op jit(solution)/shard_map/ppermute | solution.py:416
  41.0 1.3 %collective-permute-start.19 = (f32[192,128]{1,0:T(8,128)S(1)}, f32[192,128]{1,0:T(8,128)S(1)}, u32[]{:S(2)}, u32[]{:S(2)}) collective-permute-start(f32[192,128]{1,0:T(8,128)S(1)} %collective-permute-done.15.refs_1_), channel_id=1, source_target_pairs={{0,4},{4,0},{8,12},{12,8},{16,20},{20,16},{24,28},{28,24},{1,5},{5... | collective-permute-start | bytes 294920 | tf_op jit(solution)/shard_map/ppermute | solution.py:416

commit v9 on v8

--- a/solution.py
+++ b/solution.py
@@ -117,8 +117,8 @@
             sfirst[g],
             ssecond[g],
             cross[g],
-            halves(result[g][:, :block]),
-            halves(result[g][:, block:]),
+            result[g][:, :block],
+            result[g][:, block:],
         )
         for g in groups
     ]
@@ -134,6 +134,7 @@
 
 def whole_operator(parts, out_ref):
     first, second, sfirst, ssecond, cross, q, p = parts
+    q, p = halves(q), halves(p)
     block = first.shape[0]
     link = mm(mm(q, cross), p)
     solved_p = mm(p, sfirst)
@@ -149,7 +150,16 @@
         ],
         0,
     )
-    moved = mm(joined(first, second), solved, TN)
+    top = mm(first[:, :block], solved[block:, : 2 * block], TN)
+    both = jnp.concatenate([second[:, :block], first[:, block:]], 0)
+    moved = jnp.concatenate(
+        [
+            jnp.concatenate([top, none], 1),
+            mm(both, solved, TN),
+            mm(second[:, block:], solved[:block], TN),
+        ],
+        0,
+    )
     row = lax.broadcasted_iota(jnp.int32, moved.shape, 0)
     col = lax.broadcasted_iota(jnp.int32, moved.shape, 1)
     out_ref[...] = jnp.where(row == col, 1.0, 0.0) - moved
@@ -157,6 +167,7 @@
 
 def pair_action(parts, window):
     first, second, sfirst, ssecond, cross, q, p = parts
+    q, p = halves(q), halves(p)
     block = first.shape[0]
     cols = window.shape[1]
     weights_p = jnp.concatenate([mm(sfirst, window[: 2 * block]), sfirst[:, :block]], 1)
@@ -189,7 +200,8 @@
 def first_kernel(count, nodes, place_ref, *refs):
     mine, theirs = refs[:count], refs[count : 2 * count]
     top_ref, low_ref, near_ref, far_ref = refs[2 * count : 2 * count + 4]
-    fixed_ref, lead_ref, out_near, out_far, oper_ref, map_ref, map_half, refl_ref = refs[2 * count + 4 :]
+    (fixed_ref, lead_ref, out_near, out_far), keep_refs = refs[2 * count + 4 : 2 * count + 8], refs[2 * count + 8 : -1]
+    refl_ref = refs[-1]
     block = top_ref.shape[0]
     node, core, vec = place_ref[0], place_ref[1], place_ref[2]
     groups, rows, _ = mine[0].shape
@@ -215,8 +227,18 @@
     out_near[block:] = pick_near(node, core, lead)
     out_far[...] = jnp.where(core == 0, pick_far(node, fixed), pick_far(node, lead))
     for group in range(1, groups):
-        whole_operator(parts[group], oper_ref.at[group - 1])
-    if groups != 3:
+        for part, array in enumerate(parts[group]):
+            keep_refs[part][group - 1] = array
+
+
+def later_kernel(place_ref, *refs):
+    parts, (oper_ref, map_ref, map_half) = refs[:7], refs[7:]
+    core = place_ref[1]
+    later, size, _ = oper_ref.shape
+    block = size // 3
+    for group in range(later):
+        whole_operator([part[group] for part in parts], oper_ref.at[group])
+    if later != 2:
         return
     up, own, out = (slice(part * block, (part + 1) * block) for part in range(3))
     map_ref[:block] = oper_ref[0, out, :block]
@@ -232,13 +254,20 @@
     own = slice(block, 2 * block)
     first = jnp.where(place_ref[0] == 0, fixed_ref[:block], 0.0)
     operator = oper_ref.at[0]
-    base_ref[...] = mm(
-        operator[:, : 2 * block], jnp.concatenate([first, fixed_ref[own]], 0)
-    )
-    onto_ref[...] = mm(operator[:, own], lead_ref[own])
-
-
-def next_kernel(place_ref, near_ref, far_ref, near2_ref, far2_ref, fixed_ref, lead_ref, oper_ref, base_ref, onto_ref, *outs):
+    base = mm(operator[:, : 2 * block], jnp.concatenate([first, fixed_ref[own]], 0))
+    onto = jnp.concatenate([operator[:, 2 * block :], mm(operator[:, own], lead_ref[own])], 1)
+    rows = oper_ref[1, 2 * block :, : 2 * block]
+    cols = base.shape[1]
+    both = jnp.concatenate([base[: 2 * block], onto[: 2 * block]], 1)
+    both = jnp.concatenate([jnp.where(place_ref[0] == 0, both[:block], 0.0), both[block:]], 0)
+    both = mm(rows, both)
+    base_ref[: 3 * block] = base
+    base_ref[3 * block :] = both[:, :cols]
+    onto_ref[: 3 * block] = onto
+    onto_ref[3 * block :] = both[:, cols:]
+
+
+def next_kernel(place_ref, near_ref, far_ref, near2_ref, far2_ref, fixed_ref, lead_ref, base_ref, onto_ref, *outs):
     out_fixed, out_vec, out_half = outs
     block = far_ref.shape[0]
     node, core = place_ref[0], place_ref[1]
@@ -261,17 +290,11 @@
     )
     below = jnp.where(odd, came3, came1) + reach[:, :cols] + mm(reach[:, cols:], carry)
     below = jnp.where(node == 3, 0.0, below)
-    fixed = base_ref[...] + mm(
-        jnp.concatenate([oper_ref[0, :, out], onto_ref[...]], 1),
-        jnp.concatenate([below, carry], 0),
-    )
-    out_fixed[...] = fixed
+    fixed = base_ref[...] + mm(onto_ref[...], jnp.concatenate([below, carry], 0))
+    out_fixed[...] = fixed[: 3 * block]
     out_vec[:block] = fixed[out]
     out_vec[block : 2 * block] = fixed[up]
-    first = jnp.where(node == 0, fixed[up], 0.0)
-    out_vec[2 * block :] = mm(
-        oper_ref[1, out, : 2 * block], jnp.concatenate([first, fixed[own]], 0)
-    )
+    out_vec[2 * block :] = fixed[3 * block :]
     out_half[...] = half_of(core, out_vec)
 
 
@@ -434,20 +457,25 @@
     later = groups - 1
     size = 3 * block
     maps = 5 * block
-    fixed, lead, near, far, operators, sent, sent_half = call(
+    fixed, lead, near, far, *parts = call(
         functools.partial(first_kernel, len(mine), nodes),
         [
             (size, cols),
             (size, block),
             (2 * block, cols),
             (block, cols),
-            (later, size, size),
-            (maps, block),
-            (maps // PAIR, block),
+            *[(later, block, window)] * 4,
+            *[(later, block, block)] * 3,
         ],
         [place, *mine, *theirs, top, low, *below],
         [pltpu.VMEM((PAIR, groups, block, window), F32)],
     )
+    operators, sent, sent_half = call(
+        later_kernel,
+        [(later, size, size), (maps, block), (maps // PAIR, block)],
+        [place, *parts],
+        work=32 * size**3,
+    )
     if nodes != 4 or groups != 3:
         result = many_pairs(fixed, lead, operators, node, nodes, row_count)
         return jnp.where(core == 0, result[:block], result[block : 2 * block])
@@ -457,7 +485,7 @@
 
     base, onto = call(
         between_kernel,
-        [(size, cols), (size, block)],
+        [(4 * block, cols), (4 * block, 2 * block)],
         [place, fixed, lead, operators],
         work=32 * size**3,
     )
@@ -467,7 +495,7 @@
     fixed, vec, vec_half = call(
         next_kernel,
         [(size, cols), (size, cols), (size // PAIR, cols)],
-        [*shared(near, far), fixed, lead, operators, base, onto],
+        [*shared(near, far), fixed, lead, base, onto],
     )
     near, far = swap(vec, (1, 2)), swap(vec_half, (3, 3))
     far, *known = hold((far, *known))

time: 44.1 us -> 43.8 us (level)
  starting transfers between devices: 20.2 us -> 19.5 us
  Pallas kernels: 10.4 us -> 11 us
    pallas_call x4 -> x5, Pallas kernels: 10.4 us -> 11 us  [call(): pl.pallas_call(kernel, out_shape=[jax.ShapeDtypeStruct(shape, F32) for sh...]
    ppermute x8, waiting for transfers between devices: 7.45 us -> 6.79 us  [swap(): return lax.ppermute(value, 'rows', moves)]
    ppermute x8, starting transfers between devices: 12.2 us -> 11.7 us  [swap(): return lax.ppermute(value, 'rows', moves)]
  transfers between devices with their start and end apart: 22 -> 22, of which waited for: 9 -> 9; matrix products, arithmetic and copies ran while one was open for 4% -> 4% of each run, Pallas kernels for 6% -> 11%
where the time goes in v9:
time: 43.8 us; the launch traced here: 43.6 us
  starting transfers between devices  19.5 us (45%)
  waiting for transfers between devices  11.2 us (26%)
  Pallas kernels  11 us (25%)
  other arithmetic  1.83 us (4%)
    ppermute x8, starting transfers between devices, swap(): return lax.ppermute(value, 'rows', moves)  11.7 us
    pallas_call x5, Pallas kernels, call(): pl.pallas_call(kernel, out_shape=[jax.ShapeDtypeStruct(shape, F32) for sh...  11 us
    ppermute x8, waiting for transfers between devices, swap(): return lax.ppermute(value, 'rows', moves)  6.79 us
    ppermute x3, starting transfers between devices, spread(): lax.ppermute(value, axis, [(place, place ^ mask) for place in range(size)])  5.62 us
    ppermute x3, waiting for transfers between devices, spread(): lax.ppermute(value, axis, [(place, place ^ mask) for place in range(size)])  2.31 us
    ppermute x11, starting transfers between devices, across(): lax.ppermute(value, 'rows', [(place, place ^ 1) for place in range(row_co...  2.19 us
    ppermute x11, waiting for transfers between devices, across(): lax.ppermute(value, 'rows', [(place, place ^ 1) for place in range(row_co...  2.07 us
    select_n x1, other arithmetic, local(): mine[0] = jnp.where(vec_index < 0, 0.0, mine[0])  0.9 us
  transfers between devices with their start and end apart: 22, of which 9 were waited for; matrix products, arithmetic and copies ran while one was open for 4% of the time, Pallas kernels for 11%

profile of v9, /device:TPU:0, one launch (start us, length us, event | category | flops | bytes accessed | tf_op | source)
XLA Modules:
  0.0 43.6 jit_solution(877571438989525535)
XLA Ops:
  0.0 3.0 %collective-permute-start = (f32[3,32,256]{2,1,0:T(8,128)}, f32[3,32,256]{2,1,0:T(8,128)S(1)}, u32[]{:S(2)}, u32[]{:S(2)}) collective-permute-start(f32[3,32,256]{2,1,0:T(8,128)} %bitcast.5), channel_id=1, source_target_pairs={{0,1},{1,0},{2,3},{3,2},{4,5},{5,4},{6,7},{7,6},{8,9},{9,8},{10,11... | collective-permute-start | bytes 294920 | tf_op jit(solution)/shard_map/ppermute | solution.py:384
  3.0 2.6 %collective-permute-start.1 = (f32[3,32,256]{2,1,0:T(8,128)}, f32[3,32,256]{2,1,0:T(8,128)S(1)}, u32[]{:S(2)}, u32[]{:S(2)}) collective-permute-start(f32[3,32,256]{2,1,0:T(8,128)} %bitcast.6), channel_id=1, source_target_pairs={{0,2},{1,3},{2,0},{3,1},{4,6},{5,7},{6,4},{7,5},{8,10},{9,11},{10,... | collective-permute-start | bytes 294920 | tf_op jit(solution)/shard_map/ppermute | solution.py:384
  6.1 0.9 %broadcast_select_fusion.refs_0_ = f32[3,32,256]{2,1,0:T(8,128)S(1)} fusion(pred[]{:T(512)S(6)} %lt.10, f32[3,1,32,256]{3,2,1,0:T(8,128)} %param.3), kind=kLoop, calls=%fused_computation | loop fusion | flops 24576 | bytes 196609 | tf_op jit(solution)/shard_map/jit(_where)/select_n | solution.py:454
  7.2 0.8 %broadcast_select_fusion.1 = (f32[128,128]{1,0:T(8,128)S(1)}, f32[128,128]{1,0:T(8,128)S(1)}) fusion(f32[128,128]{1,0:T(8,128)S(1)} %collective-permute-done.7, f32[128,128]{1,0:T(8,128)} %param.2, pred[]{:T(512)S(6)} %eq.6), kind=kLoop, calls=%fused_computation.1 | loop fusion | flops 32768 | bytes 262145 | tf_op jit(solution)/shard_map/jit(_where)/select_n | solution.py:444
  8.1 1.8 %collective-permute-start.8 = (f32[128,128]{1,0:T(8,128)S(1)}, f32[128,128]{1,0:T(8,128)S(1)}, u32[]{:S(2)}, u32[]{:S(2)}) collective-permute-start(f32[128,128]{1,0:T(8,128)S(1)} %get-tuple-element.56.refs_8_), channel_id=1, source_target_pairs={{0,8},{4,12},{8,0},{12,4},{16,24},{20,28},{24,16},{28,20},{1,9},{5... | collective-permute-start | bytes 196616 | tf_op jit(solution)/shard_map/ppermute | solution.py:436
  9.9 1.5 %collective-permute-start.9 = (f32[128,128]{1,0:T(8,128)S(1)}, f32[128,128]{1,0:T(8,128)S(1)}, u32[]{:S(2)}, u32[]{:S(2)}) collective-permute-start(f32[128,128]{1,0:T(8,128)S(1)} %get-tuple-element.56.refs_8_), channel_id=1, source_target_pairs={{0,24},{4,28},{8,16},{12,20},{16,8},{20,12},{24,0},{28,4},{1,25},{... | collective-permute-start | bytes 196616 | tf_op jit(solution)/shard_map/ppermute | solution.py:436
  11.4 2.3 %collective-permute-done.1.refs_2_ = f32[3,32,256]{2,1,0:T(8,128)S(1)} collective-permute-done((f32[3,32,256]{2,1,0:T(8,128)}, f32[3,32,256]{2,1,0:T(8,128)S(1)}, u32[]{:S(2)}, u32[]{:S(2)}) %collective-permute-start.1) | collective-permute-done | bytes 98336 | tf_op jit(solution)/shard_map/ppermute | solution.py:384
  13.7 0.5 %collective-permute-start.5 = (f32[3,32,256]{2,1,0:T(8,128)S(1)}, f32[3,32,256]{2,1,0:T(8,128)S(1)}, u32[]{:S(2)}, u32[]{:S(2)}) collective-permute-start(f32[3,32,256]{2,1,0:T(8,128)S(1)} %collective-permute-done.1.refs_2_), channel_id=1, source_target_pairs={{0,4},{4,0},{8,12},{12,8},{16,20},{20,16},{24,28},{28,24},{1,5},{5... | collective-permute-start | bytes 294920 | tf_op jit(solution)/shard_map/ppermute | solution.py:439
  14.3 0.7 %collective-permute-done.9.refs_11_ = f32[128,128]{1,0:T(8,128)S(1)} collective-permute-done((f32[128,128]{1,0:T(8,128)S(1)}, f32[128,128]{1,0:T(8,128)S(1)}, u32[]{:S(2)}, u32[]{:S(2)}) %collective-permute-start.9) | collective-permute-done | bytes 65568 | tf_op jit(solution)/shard_map/ppermute | solution.py:436
  15.5 4.6 %shard_map.28 = (f32[384,128]{1,0:T(8,128)S(1)}, f32[384,128]{1,0:T(8,128)S(1)}, f32[256,128]{1,0:T(8,128)S(1)}, f32[128,128]{1,0:T(8,128)S(1)}, f32[2,128,256]{...) custom-call(s32[3]{0:T(128)S(1)} %pad_add_fusion.place_ref, ...), custom_call_target="tpu_custom_call" | custom-call | tf_op jit(solution)/shard_map/pallas_call | solution.py:364
  20.1 1.6 %collective-permute-start.10 = (f32[256,128]{1,0:T(8,128)S(1)}, f32[256,128]{1,0:T(8,128)S(1)}, u32[]{:S(2)}, u32[]{:S(2)}) collective-permute-start(f32[256,128]{1,0:T(8,128)S(1)} %get-tuple-element.30), channel_id=1, source_target_pairs={{0,8},{4,20},{8,0},{12,28},{16,24},{20,4},{24,16},{28,12},{1,9},{5... | collective-permute-start | bytes 393224 | tf_op jit(solution)/shard_map/ppermute | solution.py:436
  21.7 1.5 %collective-permute-start.11 = (f32[128,128]{1,0:T(8,128)S(1)}, f32[128,128]{1,0:T(8,128)S(1)}, u32[]{:S(2)}, u32[]{:S(2)}) collective-permute-start(f32[128,128]{1,0:T(8,128)S(1)} %get-tuple-element.31), channel_id=1, source_target_pairs={{0,24},{4,28},{8,16},{12,20},{16,8},{20,12},{24,0},{28,4},{1,25},{... | collective-permute-start | bytes 196616 | tf_op jit(solution)/shard_map/ppermute | solution.py:436
  23.2 2.1 %shard_map.29 = (f32[2,384,384]{2,1,0:T(8,128)S(1)}, f32[640,128]{1,0:T(8,128)S(1)}, f32[320,128]{1,0:T(8,128)S(1)}) custom-call(s32[3]{0:T(128)S(1)} %pad_add_fusion.place_ref, f32[2,128,256]{2,1,0:T(8,128)S(1)} %get-tuple-element.34.refs_0_, f32[2,128,256]{2,1,0:T(8,128)S(1)} %get-tuple-element.35.refs_1_, f32[2,128,256]{2,1,0:T(8,128)S(1)} %get-tuple-element.36.refs_2_, ...), custom_call_target="tpu_custom_call" | custom-call | flops 1811939328 | tf_op jit(solution)/shard_map/pallas_call | solution.py:364
  25.3 1.6 %collective-permute-start.16 = (f32[640,128]{1,0:T(8,128)S(1)}, f32[640,128]{1,0:T(8,128)S(1)}, u32[]{:S(2)}, u32[]{:S(2)}) collective-permute-start(f32[640,128]{1,0:T(8,128)S(1)} %get-tuple-element.49.refs_9_), channel_id=1, source_target_pairs={{0,8},{4,20},{8,0},{12,28},{16,24},{20,4},{24,16},{28,12},{1,9},{5... | collective-permute-start | bytes 983048 | tf_op jit(solution)/shard_map/ppermute | solution.py:436
  26.8 1.3 %shard_map.30 = (f32[512,128]{1,0:T(8,128)S(1)}, f32[512,256]{1,0:T(8,128)S(1)}) custom-call(s32[3]{0:T(128)S(1)} %pad_add_fusion.place_ref, f32[384,128]{1,0:T(8,128)S(1)} %get-tuple-element.32.fixed_ref, f32[384,128]{1,0:T(8,128)S(1)} %get-tuple-element.33.lead_ref, f32[2,384,384]{2,1,0:T(8,128)S(1)} %get-tuple-element.41.oper_ref.refs_11_), custom_call_target="tpu_custom_call" | custom-call | flops 1811939328 | tf_op jit(solution)/shard_map/pallas_call | solution.py:364
  28.7 0.8 %collective-permute-start.17 = (f32[320,128]{1,0:T(8,128)S(1)}, f32[320,128]{1,0:T(8,128)S(1)}, u32[]{:S(2)}, u32[]{:S(2)}) collective-permute-start(f32[320,128]{1,0:T(8,128)S(1)} %get-tuple-element.50), channel_id=1, source_target_pairs={{0,24},{4,28},{8,16},{12,20},{16,8},{20,12},{24,0},{28,4},{1,25},{... | collective-permute-start | bytes 491528 | tf_op jit(solution)/shard_map/ppermute | solution.py:436
  29.6 1.5 %shard_map.31 = (f32[384,128]{1,0:T(8,128)S(1)}, f32[384,128]{1,0:T(8,128)S(1)}, f32[192,128]{1,0:T(8,128)S(1)}) custom-call(s32[3]{0:T(128)S(1)} %pad_add_fusion.place_ref, f32[256,128]{1,0:T(8,128)S(1)} %collective-permute-done.10.near_ref, f32[128,128]{1,0:T(8,128)S(1)} %collective-permute-done.11.far_ref, ...), custom_call_target="tpu_custom_call" | custom-call | tf_op jit(solution)/shard_map/pallas_call | solution.py:364
  31.1 2.1 %collective-permute-start.15 = (f32[192,128]{1,0:T(8,128)S(1)}, f32[192,128]{1,0:T(8,128)S(1)}, u32[]{:S(2)}, u32[]{:S(2)}) collective-permute-start(f32[192,128]{1,0:T(8,128)S(1)} %get-tuple-element.48), channel_id=1, source_target_pairs={{0,24},{4,28},{8,16},{12,20},{16,8},{20,12},{24,0},{28,4},{1,25},{... | collective-permute-start | bytes 294920 | tf_op jit(solution)/shard_map/ppermute | solution.py:436
  33.2 0.9 %collective-permute-start.14 = (f32[384,128]{1,0:T(8,128)S(1)}, f32[384,128]{1,0:T(8,128)S(1)}, u32[]{:S(2)}, u32[]{:S(2)}) collective-permute-start(f32[384,128]{1,0:T(8,128)S(1)} %get-tuple-element.47.refs_4_), channel_id=1, source_target_pairs={{0,8},{4,20},{8,0},{12,28},{16,24},{20,4},{24,16},{28,12},{1,9},{5... | collective-permute-start | bytes 589832 | tf_op jit(solution)/shard_map/ppermute | solution.py:436
  34.1 2.6 %collective-permute-done.17.refs_6_ = f32[320,128]{1,0:T(8,128)S(1)} collective-permute-done((f32[320,128]{1,0:T(8,128)S(1)}, f32[320,128]{1,0:T(8,128)S(1)}, u32[]{:S(2)}, u32[]{:S(2)}) %collective-permute-start.17) | collective-permute-done | bytes 163872 | tf_op jit(solution)/shard_map/ppermute | solution.py:436
  36.8 1.3 %collective-permute-done.15.refs_1_ = f32[192,128]{1,0:T(8,128)S(1)} collective-permute-done((f32[192,128]{1,0:T(8,128)S(1)}, f32[192,128]{1,0:T(8,128)S(1)}, u32[]{:S(2)}, u32[]{:S(2)}) %collective-permute-start.15) | collective-permute-done | bytes 98336 | tf_op jit(solution)/shard_map/ppermute | solution.py:436
  38.1 2.1 %collective-permute-done.14.refs_0_ = f32[384,128]{1,0:T(8,128)S(1)} collective-permute-done((f32[384,128]{1,0:T(8,128)S(1)}, f32[384,128]{1,0:T(8,128)S(1)}, u32[]{:S(2)}, u32[]{:S(2)}) %collective-permute-start.14) | collective-permute-done | bytes 196640 | tf_op jit(solution)/shard_map/ppermute | solution.py:436
  40.7 1.3 %collective-permute-done.19.refs_3_ = f32[192,128]{1,0:T(8,128)S(1)} collective-permute-done((f32[192,128]{1,0:T(8,128)S(1)}, f32[192,128]{1,0:T(8,128)S(1)}, u32[]{:S(2)}, u32[]{:S(2)}) %collective-permute-start.19) | collective-permute-done | bytes 98336 | tf_op jit(solution)/shard_map/ppermute | solution.py:439
  42.0 1.6 %shard_map.32 = f32[128,128]{1,0:T(8,128)} custom-call(s32[3]{0:T(128)S(1)} %pad_add_fusion.place_ref, f32[384,128]{1,0:T(8,128)S(1)} %collective-permute-done.14.refs_0_, f32[192,128]{1,0:T(8,128)S(1)} %collective-permute-done.15.refs_1_, f32[384,128]{1,0:T(8,128)S(1)} %collective-permute-done.18.refs_2_, f32[192,128]{1,0:T(8,128)S(1)} %collective-permute-done.19.refs_3_, ...), custom_call_target="tpu_custom_call" | custom-call | tf_op jit(solution)/shard_map/pallas_call | solution.py:364
  (28 shorter events, 2.6 us)
Async XLA Ops:
  0.0 9.9 %collective-permute-start = (f32[3,32,256]{2,1,0:T(8,128)}, f32[3,32,256]{2,1,0:T(8,128)S(1)}, u32[]{:S(2)}, u32[]{:S(2)}) collective-permute-start(f32[3,32,256]{2,1,0:T(8,128)} %bitcast.5), channel_id=1, source_target_pairs={{0,1},{1,0},{2,3},{3,2},{4,5},{5,4},{6,7},{7,6},{8,9},{9,8},{10,11... | collective-permute-start | bytes 294920 | tf_op jit(solution)/shard_map/ppermute | solution.py:384
  3.0 10.6 %collective-permute-start.1 = (f32[3,32,256]{2,1,0:T(8,128)}, f32[3,32,256]{2,1,0:T(8,128)S(1)}, u32[]{:S(2)}, u32[]{:S(2)}) collective-permute-start(f32[3,32,256]{2,1,0:T(8,128)} %bitcast.6), channel_id=1, source_target_pairs={{0,2},{1,3},{2,0},{3,1},{4,6},{5,7},{6,4},{7,5},{8,10},{9,11},{10,... | collective-permute-start | bytes 294920 | tf_op jit(solution)/shard_map/ppermute | solution.py:384
  5.6 8.1 %collective-permute-start.2 = (f32[3,32,256]{2,1,0:T(8,128)}, f32[3,32,256]{2,1,0:T(8,128)S(1)}, u32[]{:S(2)}, u32[]{:S(2)}) collective-permute-start(f32[3,32,256]{2,1,0:T(8,128)} %bitcast.7), channel_id=1, source_target_pairs={{0,3},{1,2},{2,1},{3,0},{4,7},{5,6},{6,5},{7,4},{8,11},{9,10},{10,... | collective-permute-start | bytes 294920 | tf_op jit(solution)/shard_map/ppermute | solution.py:384
  5.6 8.6 %collective-permute-start.3 = (f32[3,32,256]{2,1,0:T(8,128)}, f32[3,32,256]{2,1,0:T(8,128)S(1)}, u32[]{:S(2)}, u32[]{:S(2)}) collective-permute-start(f32[3,32,256]{2,1,0:T(8,128)} %bitcast.8), channel_id=1, source_target_pairs={{0,4},{4,0},{8,12},{12,8},{16,20},{20,16},{24,28},{28,24},{1,5},{5... | collective-permute-start | bytes 294920 | tf_op jit(solution)/shard_map/ppermute | solution.py:439
  5.6 1.6 %collective-permute-start.7 = (f32[128,128]{1,0:T(8,128)}, f32[128,128]{1,0:T(8,128)S(1)}, u32[]{:S(2)}, u32[]{:S(2)}) collective-permute-start(f32[128,128]{1,0:T(8,128)} %param.2), channel_id=1, source_target_pairs={{0,4},{4,0},{8,12},{12,8},{16,20},{20,16},{24,28},{28,24},{1,5},{5... | collective-permute-start | bytes 196616 | tf_op jit(solution)/shard_map/ppermute | solution.py:439
  8.1 6.2 %collective-permute-start.8 = (f32[128,128]{1,0:T(8,128)S(1)}, f32[128,128]{1,0:T(8,128)S(1)}, u32[]{:S(2)}, u32[]{:S(2)}) collective-permute-start(f32[128,128]{1,0:T(8,128)S(1)} %get-tuple-element.56.refs_8_), channel_id=1, source_target_pairs={{0,8},{4,12},{8,0},{12,4},{16,24},{20,28},{24,16},{28,20},{1,9},{5... | collective-permute-start | bytes 196616 | tf_op jit(solution)/shard_map/ppermute | solution.py:436
  9.9 5.2 %collective-permute-start.9 = (f32[128,128]{1,0:T(8,128)S(1)}, f32[128,128]{1,0:T(8,128)S(1)}, u32[]{:S(2)}, u32[]{:S(2)}) collective-permute-start(f32[128,128]{1,0:T(8,128)S(1)} %get-tuple-element.56.refs_8_), channel_id=1, source_target_pairs={{0,24},{4,28},{8,16},{12,20},{16,8},{20,12},{24,0},{28,4},{1,25},{... | collective-permute-start | bytes 196616 | tf_op jit(solution)/shard_map/ppermute | solution.py:436
  13.7 1.4 %collective-permute-start.4 = (f32[3,32,256]{2,1,0:T(8,128)S(1)}, f32[3,32,256]{2,1,0:T(8,128)S(1)}, u32[]{:S(2)}, u32[]{:S(2)}) collective-permute-start(f32[3,32,256]{2,1,0:T(8,128)S(1)} %collective-permute-done.refs_1_), channel_id=1, source_target_pairs={{0,4},{4,0},{8,12},{12,8},{16,20},{20,16},{24,28},{28,24},{1,5},{5... | collective-permute-start | bytes 294920 | tf_op jit(solution)/shard_map/ppermute | solution.py:439
  13.7 1.5 %collective-permute-start.5 = (f32[3,32,256]{2,1,0:T(8,128)S(1)}, f32[3,32,256]{2,1,0:T(8,128)S(1)}, u32[]{:S(2)}, u32[]{:S(2)}) collective-permute-start(f32[3,32,256]{2,1,0:T(8,128)S(1)} %collective-permute-done.1.refs_2_), channel_id=1, source_target_pairs={{0,4},{4,0},{8,12},{12,8},{16,20},{20,16},{24,28},{28,24},{1,5},{5... | collective-permute-start | bytes 294920 | tf_op jit(solution)/shard_map/ppermute | solution.py:439
  14.2 1.3 %collective-permute-start.6 = (f32[3,32,256]{2,1,0:T(8,128)S(1)}, f32[3,32,256]{2,1,0:T(8,128)S(1)}, u32[]{:S(2)}, u32[]{:S(2)}) collective-permute-start(f32[3,32,256]{2,1,0:T(8,128)S(1)} %collective-permute-done.2.refs_3_), channel_id=1, source_target_pairs={{0,4},{4,0},{8,12},{12,8},{16,20},{20,16},{24,28},{28,24},{1,5},{5... | collective-permute-start | bytes 294920 | tf_op jit(solution)/shard_map/ppermute | solution.py:439
  20.1 8.0 %collective-permute-start.10 = (f32[256,128]{1,0:T(8,128)S(1)}, f32[256,128]{1,0:T(8,128)S(1)}, u32[]{:S(2)}, u32[]{:S(2)}) collective-permute-start(f32[256,128]{1,0:T(8,128)S(1)} %get-tuple-element.30), channel_id=1, source_target_pairs={{0,8},{4,20},{8,0},{12,28},{16,24},{20,4},{24,16},{28,12},{1,9},{5... | collective-permute-start | bytes 393224 | tf_op jit(solution)/shard_map/ppermute | solution.py:436
  21.7 6.4 %collective-permute-start.11 = (f32[128,128]{1,0:T(8,128)S(1)}, f32[128,128]{1,0:T(8,128)S(1)}, u32[]{:S(2)}, u32[]{:S(2)}) collective-permute-start(f32[128,128]{1,0:T(8,128)S(1)} %get-tuple-element.31), channel_id=1, source_target_pairs={{0,24},{4,28},{8,16},{12,20},{16,8},{20,12},{24,0},{28,4},{1,25},{... | collective-permute-start | bytes 196616 | tf_op jit(solution)/shard_map/ppermute | solution.py:436
  25.3 11.5 %collective-permute-start.16 = (f32[640,128]{1,0:T(8,128)S(1)}, f32[640,128]{1,0:T(8,128)S(1)}, u32[]{:S(2)}, u32[]{:S(2)}) collective-permute-start(f32[640,128]{1,0:T(8,128)S(1)} %get-tuple-element.49.refs_9_), channel_id=1, source_target_pairs={{0,8},{4,20},{8,0},{12,28},{16,24},{20,4},{24,16},{28,12},{1,9},{5... | collective-permute-start | bytes 983048 | tf_op jit(solution)/shard_map/ppermute | solution.py:436
  28.1 1.5 %collective-permute-start.12 = (f32[256,128]{1,0:T(8,128)S(1)}, f32[256,128]{1,0:T(8,128)S(1)}, u32[]{:S(2)}, u32[]{:S(2)}) collective-permute-start(f32[256,128]{1,0:T(8,128)S(1)} %collective-permute-done.10.near_ref), channel_id=1, source_target_pairs={{0,4},{4,0},{8,12},{12,8},{16,20},{20,16},{24,28},{28,24},{1,5},{5... | collective-permute-start | bytes 393224 | tf_op jit(solution)/shard_map/ppermute | solution.py:439
  28.2 1.4 %collective-permute-start.13 = (f32[128,128]{1,0:T(8,128)S(1)}, f32[128,128]{1,0:T(8,128)S(1)}, u32[]{:S(2)}, u32[]{:S(2)}) collective-permute-start(f32[128,128]{1,0:T(8,128)S(1)} %collective-permute-done.11.far_ref), channel_id=1, source_target_pairs={{0,4},{4,0},{8,12},{12,8},{16,20},{20,16},{24,28},{28,24},{1,5},{5... | collective-permute-start | bytes 196616 | tf_op jit(solution)/shard_map/ppermute | solution.py:439
  28.7 8.1 %collective-permute-start.17 = (f32[320,128]{1,0:T(8,128)S(1)}, f32[320,128]{1,0:T(8,128)S(1)}, u32[]{:S(2)}, u32[]{:S(2)}) collective-permute-start(f32[320,128]{1,0:T(8,128)S(1)} %get-tuple-element.50), channel_id=1, source_target_pairs={{0,24},{4,28},{8,16},{12,20},{16,8},{20,12},{24,0},{28,4},{1,25},{... | collective-permute-start | bytes 491528 | tf_op jit(solution)/shard_map/ppermute | solution.py:436
  31.1 6.9 %collective-permute-start.15 = (f32[192,128]{1,0:T(8,128)S(1)}, f32[192,128]{1,0:T(8,128)S(1)}, u32[]{:S(2)}, u32[]{:S(2)}) collective-permute-start(f32[192,128]{1,0:T(8,128)S(1)} %get-tuple-element.48), channel_id=1, source_target_pairs={{0,24},{4,28},{8,16},{12,20},{16,8},{20,12},{24,0},{28,4},{1,25},{... | collective-permute-start | bytes 294920 | tf_op jit(solution)/shard_map/ppermute | solution.py:436
  33.2 7.0 %collective-permute-start.14 = (f32[384,128]{1,0:T(8,128)S(1)}, f32[384,128]{1,0:T(8,128)S(1)}, u32[]{:S(2)}, u32[]{:S(2)}) collective-permute-start(f32[384,128]{1,0:T(8,128)S(1)} %get-tuple-element.47.refs_4_), channel_id=1, source_target_pairs={{0,8},{4,20},{8,0},{12,28},{16,24},{20,4},{24,16},{28,12},{1,9},{5... | collective-permute-start | bytes 589832 | tf_op jit(solution)/shard_map/ppermute | solution.py:436
  38.1 3.9 %collective-permute-start.20 = (f32[640,128]{1,0:T(8,128)S(1)}, f32[640,128]{1,0:T(8,128)S(1)}, u32[]{:S(2)}, u32[]{:S(2)}) collective-permute-start(f32[640,128]{1,0:T(8,128)S(1)} %collective-permute-done.16.refs_5_), channel_id=1, source_target_pairs={{0,4},{4,0},{8,12},{12,8},{16,20},{20,16},{24,28},{28,24},{1,5},{5... | collective-permute-start | bytes 983048 | tf_op jit(solution)/shard_map/ppermute | solution.py:439
  40.2 1.8 %collective-permute-start.18 = (f32[384,128]{1,0:T(8,128)S(1)}, f32[384,128]{1,0:T(8,128)S(1)}, u32[]{:S(2)}, u32[]{:S(2)}) collective-permute-start(f32[384,128]{1,0:T(8,128)S(1)} %collective-permute-done.14.refs_0_), channel_id=1, source_target_pairs={{0,4},{4,0},{8,12},{12,8},{16,20},{20,16},{24,28},{28,24},{1,5},{5... | collective-permute-start | bytes 589832 | tf_op jit(solution)/shard_map/ppermute | solution.py:439
  40.2 1.8 %collective-permute-start.21 = (f32[320,128]{1,0:T(8,128)S(1)}, f32[320,128]{1,0:T(8,128)S(1)}, u32[]{:S(2)}, u32[]{:S(2)}) collective-permute-start(f32[320,128]{1,0:T(8,128)S(1)} %collective-permute-done.17.refs_6_), channel_id=1, source_target_pairs={{0,4},{4,0},{8,12},{12,8},{16,20},{20,16},{24,28},{28,24},{1,5},{5... | collective-permute-start | bytes 491528 | tf_op jit(solution)/shard_map/ppermute | solution.py:439
  40.7 1.3 %collective-permute-start.19 = (f32[192,128]{1,0:T(8,128)S(1)}, f32[192,128]{1,0:T(8,128)S(1)}, u32[]{:S(2)}, u32[]{:S(2)}) collective-permute-start(f32[192,128]{1,0:T(8,128)S(1)} %collective-permute-done.15.refs_1_), channel_id=1, source_target_pairs={{0,4},{4,0},{8,12},{12,8},{16,20},{20,16},{24,28},{28,24},{1,5},{5... | collective-permute-start | bytes 294920 | tf_op jit(solution)/shard_map/ppermute | solution.py:439

commit v10 on v9

--- a/solution.py
+++ b/solution.py
@@ -499,10 +499,12 @@
     )
     near, far = swap(vec, (1, 2)), swap(vec_half, (3, 3))
     far, *known = hold((far, *known))
+    far2, known2 = across(far), across(known[1])
+    near, far2, known2 = hold((near, far2, known2))
     (result,) = call(
         last_kernel,
         [(block, cols)],
-        [*shared(near, far), vec, *shared(*known)[1:], sent, fixed, operators],
+        [place, near, far, across(near), far2, vec, *known, across(known[0]), known2, sent, fixed, operators],
     )
     return result
 

time: 43.8 us -> 43.4 us (level)
  waiting for transfers between devices: 11.2 us -> 10.6 us
    ppermute x8, waiting for transfers between devices: 6.79 us -> 4.79 us  [swap(): return lax.ppermute(value, 'rows', moves)]
    ppermute x11, waiting for transfers between devices: 2.07 us -> 3.53 us  [across(): lax.ppermute(value, 'rows', [(place, place ^ 1) for place in range(row_co...]
  transfers between devices with their start and end apart: 22 -> 22, of which waited for: 9 -> 10; matrix products, arithmetic and copies ran while one was open for 4% -> 4% of each run, Pallas kernels for 11% -> 11%
where the time goes in v10:
time: 43.4 us; the launch traced here: 43.2 us
  starting transfers between devices  19.6 us (45%)
  Pallas kernels  11 us (25%)
  waiting for transfers between devices  10.6 us (24%)
  other arithmetic  1.83 us (4%)
    ppermute x8, starting transfers between devices, swap(): return lax.ppermute(value, 'rows', moves)  11.7 us
    pallas_call x5, Pallas kernels, call(): pl.pallas_call(kernel, out_shape=[jax.ShapeDtypeStruct(shape, F32) for sh...  11 us
    ppermute x3, starting transfers between devices, spread(): lax.ppermute(value, axis, [(place, place ^ mask) for place in range(size)])  5.62 us
    ppermute x8, waiting for transfers between devices, swap(): return lax.ppermute(value, 'rows', moves)  4.79 us
    ppermute x11, waiting for transfers between devices, across(): lax.ppermute(value, 'rows', [(place, place ^ 1) for place in range(row_co...  3.53 us
    ppermute x11, starting transfers between devices, across(): lax.ppermute(value, 'rows', [(place, place ^ 1) for place in range(row_co...  2.36 us
    ppermute x3, waiting for transfers between devices, spread(): lax.ppermute(value, axis, [(place, place ^ mask) for place in range(size)])  2.31 us
    select_n x1, other arithmetic, local(): mine[0] = jnp.where(vec_index < 0, 0.0, mine[0])  0.9 us
  transfers between devices with their start and end apart: 22, of which 10 were waited for; matrix products, arithmetic and copies ran while one was open for 4% of the time, Pallas kernels for 11%

profile of v10, /device:TPU:0, one launch (start us, length us, event | category | flops | bytes accessed | tf_op | source)
XLA Modules:
  0.0 43.2 jit_solution(4441779429604661935)
XLA Ops:
  0.0 3.0 %collective-permute-start = (f32[3,32,256]{2,1,0:T(8,128)}, f32[3,32,256]{2,1,0:T(8,128)S(1)}, u32[]{:S(2)}, u32[]{:S(2)}) collective-permute-start(f32[3,32,256]{2,1,0:T(8,128)} %bitcast.5), channel_id=1, source_target_pairs={{0,1},{1,0},{2,3},{3,2},{4,5},{5,4},{6,7},{7,6},{8,9},{9,8},{10,11... | collective-permute-start | bytes 294920 | tf_op jit(solution)/shard_map/ppermute | solution.py:384
  3.0 2.6 %collective-permute-start.1 = (f32[3,32,256]{2,1,0:T(8,128)}, f32[3,32,256]{2,1,0:T(8,128)S(1)}, u32[]{:S(2)}, u32[]{:S(2)}) collective-permute-start(f32[3,32,256]{2,1,0:T(8,128)} %bitcast.6), channel_id=1, source_target_pairs={{0,2},{1,3},{2,0},{3,1},{4,6},{5,7},{6,4},{7,5},{8,10},{9,11},{10,... | collective-permute-start | bytes 294920 | tf_op jit(solution)/shard_map/ppermute | solution.py:384
  6.1 0.9 %broadcast_select_fusion.refs_0_ = f32[3,32,256]{2,1,0:T(8,128)S(1)} fusion(pred[]{:T(512)S(6)} %lt.10, f32[3,1,32,256]{3,2,1,0:T(8,128)} %param.3), kind=kLoop, calls=%fused_computation | loop fusion | flops 24576 | bytes 196609 | tf_op jit(solution)/shard_map/jit(_where)/select_n | solution.py:454
  7.2 0.8 %broadcast_select_fusion.1 = (f32[128,128]{1,0:T(8,128)S(1)}, f32[128,128]{1,0:T(8,128)S(1)}) fusion(f32[128,128]{1,0:T(8,128)S(1)} %collective-permute-done.7, f32[128,128]{1,0:T(8,128)} %param.2, pred[]{:T(512)S(6)} %eq.6), kind=kLoop, calls=%fused_computation.1 | loop fusion | flops 32768 | bytes 262145 | tf_op jit(solution)/shard_map/jit(_where)/select_n | solution.py:444
  8.1 1.8 %collective-permute-start.8 = (f32[128,128]{1,0:T(8,128)S(1)}, f32[128,128]{1,0:T(8,128)S(1)}, u32[]{:S(2)}, u32[]{:S(2)}) collective-permute-start(f32[128,128]{1,0:T(8,128)S(1)} %get-tuple-element.62.refs_8_), channel_id=1, source_target_pairs={{0,8},{4,12},{8,0},{12,4},{16,24},{20,28},{24,16},{28,20},{1,9},{5... | collective-permute-start | bytes 196616 | tf_op jit(solution)/shard_map/ppermute | solution.py:436
  9.9 1.5 %collective-permute-start.9 = (f32[128,128]{1,0:T(8,128)S(1)}, f32[128,128]{1,0:T(8,128)S(1)}, u32[]{:S(2)}, u32[]{:S(2)}) collective-permute-start(f32[128,128]{1,0:T(8,128)S(1)} %get-tuple-element.62.refs_8_), channel_id=1, source_target_pairs={{0,24},{4,28},{8,16},{12,20},{16,8},{20,12},{24,0},{28,4},{1,25},{... | collective-permute-start | bytes 196616 | tf_op jit(solution)/shard_map/ppermute | solution.py:436
  11.4 2.3 %collective-permute-done.1.refs_2_ = f32[3,32,256]{2,1,0:T(8,128)S(1)} collective-permute-done((f32[3,32,256]{2,1,0:T(8,128)}, f32[3,32,256]{2,1,0:T(8,128)S(1)}, u32[]{:S(2)}, u32[]{:S(2)}) %collective-permute-start.1) | collective-permute-done | bytes 98336 | tf_op jit(solution)/shard_map/ppermute | solution.py:384
  13.7 0.5 %collective-permute-start.5 = (f32[3,32,256]{2,1,0:T(8,128)S(1)}, f32[3,32,256]{2,1,0:T(8,128)S(1)}, u32[]{:S(2)}, u32[]{:S(2)}) collective-permute-start(f32[3,32,256]{2,1,0:T(8,128)S(1)} %collective-permute-done.1.refs_2_), channel_id=1, source_target_pairs={{0,4},{4,0},{8,12},{12,8},{16,20},{20,16},{24,28},{28,24},{1,5},{5... | collective-permute-start | bytes 294920 | tf_op jit(solution)/shard_map/ppermute | solution.py:439
  14.3 0.7 %collective-permute-done.9.refs_11_ = f32[128,128]{1,0:T(8,128)S(1)} collective-permute-done((f32[128,128]{1,0:T(8,128)S(1)}, f32[128,128]{1,0:T(8,128)S(1)}, u32[]{:S(2)}, u32[]{:S(2)}) %collective-permute-start.9) | collective-permute-done | bytes 65568 | tf_op jit(solution)/shard_map/ppermute | solution.py:436
  15.5 4.6 %shard_map.28 = (f32[384,128]{1,0:T(8,128)S(1)}, f32[384,128]{1,0:T(8,128)S(1)}, f32[256,128]{1,0:T(8,128)S(1)}, f32[128,128]{1,0:T(8,128)S(1)}, f32[2,128,256]{...) custom-call(s32[3]{0:T(128)S(1)} %pad_add_fusion.place_ref, ...), custom_call_target="tpu_custom_call" | custom-call | tf_op jit(solution)/shard_map/pallas_call | solution.py:364
  20.1 1.6 %collective-permute-start.10 = (f32[256,128]{1,0:T(8,128)S(1)}, f32[256,128]{1,0:T(8,128)S(1)}, u32[]{:S(2)}, u32[]{:S(2)}) collective-permute-start(f32[256,128]{1,0:T(8,128)S(1)} %get-tuple-element.33), channel_id=1, source_target_pairs={{0,8},{4,20},{8,0},{12,28},{16,24},{20,4},{24,16},{28,12},{1,9},{5... | collective-permute-start | bytes 393224 | tf_op jit(solution)/shard_map/ppermute | solution.py:436
  21.7 1.5 %collective-permute-start.11 = (f32[128,128]{1,0:T(8,128)S(1)}, f32[128,128]{1,0:T(8,128)S(1)}, u32[]{:S(2)}, u32[]{:S(2)}) collective-permute-start(f32[128,128]{1,0:T(8,128)S(1)} %get-tuple-element.34), channel_id=1, source_target_pairs={{0,24},{4,28},{8,16},{12,20},{16,8},{20,12},{24,0},{28,4},{1,25},{... | collective-permute-start | bytes 196616 | tf_op jit(solution)/shard_map/ppermute | solution.py:436
  23.2 2.1 %shard_map.29 = (f32[2,384,384]{2,1,0:T(8,128)S(1)}, f32[640,128]{1,0:T(8,128)S(1)}, f32[320,128]{1,0:T(8,128)S(1)}) custom-call(s32[3]{0:T(128)S(1)} %pad_add_fusion.place_ref, f32[2,128,256]{2,1,0:T(8,128)S(1)} %get-tuple-element.37.refs_0_, f32[2,128,256]{2,1,0:T(8,128)S(1)} %get-tuple-element.38.refs_1_, f32[2,128,256]{2,1,0:T(8,128)S(1)} %get-tuple-element.39.refs_2_, ...), custom_call_target="tpu_custom_call" | custom-call | flops 1811939328 | tf_op jit(solution)/shard_map/pallas_call | solution.py:364
  25.3 1.6 %collective-permute-start.16 = (f32[640,128]{1,0:T(8,128)S(1)}, f32[640,128]{1,0:T(8,128)S(1)}, u32[]{:S(2)}, u32[]{:S(2)}) collective-permute-start(f32[640,128]{1,0:T(8,128)S(1)} %get-tuple-element.52.refs_9_), channel_id=1, source_target_pairs={{0,8},{4,20},{8,0},{12,28},{16,24},{20,4},{24,16},{28,12},{1,9},{5... | collective-permute-start | bytes 983048 | tf_op jit(solution)/shard_map/ppermute | solution.py:436
  26.8 1.3 %shard_map.30 = (f32[512,128]{1,0:T(8,128)S(1)}, f32[512,256]{1,0:T(8,128)S(1)}) custom-call(s32[3]{0:T(128)S(1)} %pad_add_fusion.place_ref, f32[384,128]{1,0:T(8,128)S(1)} %get-tuple-element.35.fixed_ref, f32[384,128]{1,0:T(8,128)S(1)} %get-tuple-element.36.lead_ref, f32[2,384,384]{2,1,0:T(8,128)S(1)} %get-tuple-element.44.oper_ref.refs_11_), custom_call_target="tpu_custom_call" | custom-call | flops 1811939328 | tf_op jit(solution)/shard_map/pallas_call | solution.py:364
  28.7 0.8 %collective-permute-start.17 = (f32[320,128]{1,0:T(8,128)S(1)}, f32[320,128]{1,0:T(8,128)S(1)}, u32[]{:S(2)}, u32[]{:S(2)}) collective-permute-start(f32[320,128]{1,0:T(8,128)S(1)} %get-tuple-element.53), channel_id=1, source_target_pairs={{0,24},{4,28},{8,16},{12,20},{16,8},{20,12},{24,0},{28,4},{1,25},{... | collective-permute-start | bytes 491528 | tf_op jit(solution)/shard_map/ppermute | solution.py:436
  29.6 1.5 %shard_map.31 = (f32[384,128]{1,0:T(8,128)S(1)}, f32[384,128]{1,0:T(8,128)S(1)}, f32[192,128]{1,0:T(8,128)S(1)}) custom-call(s32[3]{0:T(128)S(1)} %pad_add_fusion.place_ref, f32[256,128]{1,0:T(8,128)S(1)} %collective-permute-done.10.near_ref, f32[128,128]{1,0:T(8,128)S(1)} %collective-permute-done.11.far_ref, ...), custom_call_target="tpu_custom_call" | custom-call | tf_op jit(solution)/shard_map/pallas_call | solution.py:364
  31.1 2.1 %collective-permute-start.15 = (f32[192,128]{1,0:T(8,128)S(1)}, f32[192,128]{1,0:T(8,128)S(1)}, u32[]{:S(2)}, u32[]{:S(2)}) collective-permute-start(f32[192,128]{1,0:T(8,128)S(1)} %get-tuple-element.51), channel_id=1, source_target_pairs={{0,24},{4,28},{8,16},{12,20},{16,8},{20,12},{24,0},{28,4},{1,25},{... | collective-permute-start | bytes 294920 | tf_op jit(solution)/shard_map/ppermute | solution.py:436
  33.2 0.9 %collective-permute-start.14 = (f32[384,128]{1,0:T(8,128)S(1)}, f32[384,128]{1,0:T(8,128)S(1)}, u32[]{:S(2)}, u32[]{:S(2)}) collective-permute-start(f32[384,128]{1,0:T(8,128)S(1)} %get-tuple-element.50.refs_4_), channel_id=1, source_target_pairs={{0,8},{4,20},{8,0},{12,28},{16,24},{20,4},{24,16},{28,12},{1,9},{5... | collective-permute-start | bytes 589832 | tf_op jit(solution)/shard_map/ppermute | solution.py:436
  34.1 2.6 %collective-permute-done.17.refs_6_ = f32[320,128]{1,0:T(8,128)S(1)} collective-permute-done((f32[320,128]{1,0:T(8,128)S(1)}, f32[320,128]{1,0:T(8,128)S(1)}, u32[]{:S(2)}, u32[]{:S(2)}) %collective-permute-start.17) | collective-permute-done | bytes 163872 | tf_op jit(solution)/shard_map/ppermute | solution.py:436
  36.8 1.3 %collective-permute-done.15.refs_1_ = f32[192,128]{1,0:T(8,128)S(1)} collective-permute-done((f32[192,128]{1,0:T(8,128)S(1)}, f32[192,128]{1,0:T(8,128)S(1)}, u32[]{:S(2)}, u32[]{:S(2)}) %collective-permute-start.15) | collective-permute-done | bytes 98336 | tf_op jit(solution)/shard_map/ppermute | solution.py:436
  38.6 1.5 %collective-permute-done.18.refs_3_ = f32[192,128]{1,0:T(8,128)S(1)} collective-permute-done((f32[192,128]{1,0:T(8,128)S(1)}, f32[192,128]{1,0:T(8,128)S(1)}, u32[]{:S(2)}, u32[]{:S(2)}) %collective-permute-start.18) | collective-permute-done | bytes 98336 | tf_op jit(solution)/shard_map/ppermute | solution.py:439
  40.4 1.3 %collective-permute-done.20.refs_2_ = f32[384,128]{1,0:T(8,128)S(1)} collective-permute-done((f32[384,128]{1,0:T(8,128)S(1)}, f32[384,128]{1,0:T(8,128)S(1)}, u32[]{:S(2)}, u32[]{:S(2)}) %collective-permute-start.20) | collective-permute-done | bytes 196640 | tf_op jit(solution)/shard_map/ppermute | solution.py:439
  41.6 1.6 %shard_map.32 = f32[128,128]{1,0:T(8,128)} custom-call(s32[3]{0:T(128)S(1)} %pad_add_fusion.place_ref, f32[384,128]{1,0:T(8,128)S(1)} %collective-permute-done.14.refs_0_, f32[192,128]{1,0:T(8,128)S(1)} %collective-permute-done.15.refs_1_, f32[384,128]{1,0:T(8,128)S(1)} %collective-permute-done.20.refs_2_, f32[192,128]{1,0:T(8,128)S(1)} %collective-permute-done.18.refs_3_, ...), custom_call_target="tpu_custom_call" | custom-call | tf_op jit(solution)/shard_map/pallas_call | solution.py:364
  (28 shorter events, 2.8 us)
Async XLA Ops:
  0.0 9.9 %collective-permute-start = (f32[3,32,256]{2,1,0:T(8,128)}, f32[3,32,256]{2,1,0:T(8,128)S(1)}, u32[]{:S(2)}, u32[]{:S(2)}) collective-permute-start(f32[3,32,256]{2,1,0:T(8,128)} %bitcast.5), channel_id=1, source_target_pairs={{0,1},{1,0},{2,3},{3,2},{4,5},{5,4},{6,7},{7,6},{8,9},{9,8},{10,11... | collective-permute-start | bytes 294920 | tf_op jit(solution)/shard_map/ppermute | solution.py:384
  3.0 10.6 %collective-permute-start.1 = (f32[3,32,256]{2,1,0:T(8,128)}, f32[3,32,256]{2,1,0:T(8,128)S(1)}, u32[]{:S(2)}, u32[]{:S(2)}) collective-permute-start(f32[3,32,256]{2,1,0:T(8,128)} %bitcast.6), channel_id=1, source_target_pairs={{0,2},{1,3},{2,0},{3,1},{4,6},{5,7},{6,4},{7,5},{8,10},{9,11},{10,... | collective-permute-start | bytes 294920 | tf_op jit(solution)/shard_map/ppermute | solution.py:384
  5.6 8.1 %collective-permute-start.2 = (f32[3,32,256]{2,1,0:T(8,128)}, f32[3,32,256]{2,1,0:T(8,128)S(1)}, u32[]{:S(2)}, u32[]{:S(2)}) collective-permute-start(f32[3,32,256]{2,1,0:T(8,128)} %bitcast.7), channel_id=1, source_target_pairs={{0,3},{1,2},{2,1},{3,0},{4,7},{5,6},{6,5},{7,4},{8,11},{9,10},{10,... | collective-permute-start | bytes 294920 | tf_op jit(solution)/shard_map/ppermute | solution.py:384
  5.6 8.6 %collective-permute-start.3 = (f32[3,32,256]{2,1,0:T(8,128)}, f32[3,32,256]{2,1,0:T(8,128)S(1)}, u32[]{:S(2)}, u32[]{:S(2)}) collective-permute-start(f32[3,32,256]{2,1,0:T(8,128)} %bitcast.8), channel_id=1, source_target_pairs={{0,4},{4,0},{8,12},{12,8},{16,20},{20,16},{24,28},{28,24},{1,5},{5... | collective-permute-start | bytes 294920 | tf_op jit(solution)/shard_map/ppermute | solution.py:439
  5.6 1.6 %collective-permute-start.7 = (f32[128,128]{1,0:T(8,128)}, f32[128,128]{1,0:T(8,128)S(1)}, u32[]{:S(2)}, u32[]{:S(2)}) collective-permute-start(f32[128,128]{1,0:T(8,128)} %param.2), channel_id=1, source_target_pairs={{0,4},{4,0},{8,12},{12,8},{16,20},{20,16},{24,28},{28,24},{1,5},{5... | collective-permute-start | bytes 196616 | tf_op jit(solution)/shard_map/ppermute | solution.py:439
  8.1 6.2 %collective-permute-start.8 = (f32[128,128]{1,0:T(8,128)S(1)}, f32[128,128]{1,0:T(8,128)S(1)}, u32[]{:S(2)}, u32[]{:S(2)}) collective-permute-start(f32[128,128]{1,0:T(8,128)S(1)} %get-tuple-element.62.refs_8_), channel_id=1, source_target_pairs={{0,8},{4,12},{8,0},{12,4},{16,24},{20,28},{24,16},{28,20},{1,9},{5... | collective-permute-start | bytes 196616 | tf_op jit(solution)/shard_map/ppermute | solution.py:436
  9.9 5.2 %collective-permute-start.9 = (f32[128,128]{1,0:T(8,128)S(1)}, f32[128,128]{1,0:T(8,128)S(1)}, u32[]{:S(2)}, u32[]{:S(2)}) collective-permute-start(f32[128,128]{1,0:T(8,128)S(1)} %get-tuple-element.62.refs_8_), channel_id=1, source_target_pairs={{0,24},{4,28},{8,16},{12,20},{16,8},{20,12},{24,0},{28,4},{1,25},{... | collective-permute-start | bytes 196616 | tf_op jit(solution)/shard_map/ppermute | solution.py:436
  13.7 1.4 %collective-permute-start.4 = (f32[3,32,256]{2,1,0:T(8,128)S(1)}, f32[3,32,256]{2,1,0:T(8,128)S(1)}, u32[]{:S(2)}, u32[]{:S(2)}) collective-permute-start(f32[3,32,256]{2,1,0:T(8,128)S(1)} %collective-permute-done.refs_1_), channel_id=1, source_target_pairs={{0,4},{4,0},{8,12},{12,8},{16,20},{20,16},{24,28},{28,24},{1,5},{5... | collective-permute-start | bytes 294920 | tf_op jit(solution)/shard_map/ppermute | solution.py:439
  13.7 1.5 %collective-permute-start.5 = (f32[3,32,256]{2,1,0:T(8,128)S(1)}, f32[3,32,256]{2,1,0:T(8,128)S(1)}, u32[]{:S(2)}, u32[]{:S(2)}) collective-permute-start(f32[3,32,256]{2,1,0:T(8,128)S(1)} %collective-permute-done.1.refs_2_), channel_id=1, source_target_pairs={{0,4},{4,0},{8,12},{12,8},{16,20},{20,16},{24,28},{28,24},{1,5},{5... | collective-permute-start | bytes 294920 | tf_op jit(solution)/shard_map/ppermute | solution.py:439
  14.2 1.3 %collective-permute-start.6 = (f32[3,32,256]{2,1,0:T(8,128)S(1)}, f32[3,32,256]{2,1,0:T(8,128)S(1)}, u32[]{:S(2)}, u32[]{:S(2)}) collective-permute-start(f32[3,32,256]{2,1,0:T(8,128)S(1)} %collective-permute-done.2.refs_3_), channel_id=1, source_target_pairs={{0,4},{4,0},{8,12},{12,8},{16,20},{20,16},{24,28},{28,24},{1,5},{5... | collective-permute-start | bytes 294920 | tf_op jit(solution)/shard_map/ppermute | solution.py:439
  20.1 8.0 %collective-permute-start.10 = (f32[256,128]{1,0:T(8,128)S(1)}, f32[256,128]{1,0:T(8,128)S(1)}, u32[]{:S(2)}, u32[]{:S(2)}) collective-permute-start(f32[256,128]{1,0:T(8,128)S(1)} %get-tuple-element.33), channel_id=1, source_target_pairs={{0,8},{4,20},{8,0},{12,28},{16,24},{20,4},{24,16},{28,12},{1,9},{5... | collective-permute-start | bytes 393224 | tf_op jit(solution)/shard_map/ppermute | solution.py:436
  21.7 6.4 %collective-permute-start.11 = (f32[128,128]{1,0:T(8,128)S(1)}, f32[128,128]{1,0:T(8,128)S(1)}, u32[]{:S(2)}, u32[]{:S(2)}) collective-permute-start(f32[128,128]{1,0:T(8,128)S(1)} %get-tuple-element.34), channel_id=1, source_target_pairs={{0,24},{4,28},{8,16},{12,20},{16,8},{20,12},{24,0},{28,4},{1,25},{... | collective-permute-start | bytes 196616 | tf_op jit(solution)/shard_map/ppermute | solution.py:436
  25.3 11.5 %collective-permute-start.16 = (f32[640,128]{1,0:T(8,128)S(1)}, f32[640,128]{1,0:T(8,128)S(1)}, u32[]{:S(2)}, u32[]{:S(2)}) collective-permute-start(f32[640,128]{1,0:T(8,128)S(1)} %get-tuple-element.52.refs_9_), channel_id=1, source_target_pairs={{0,8},{4,20},{8,0},{12,28},{16,24},{20,4},{24,16},{28,12},{1,9},{5... | collective-permute-start | bytes 983048 | tf_op jit(solution)/shard_map/ppermute | solution.py:436
  28.1 1.5 %collective-permute-start.12 = (f32[256,128]{1,0:T(8,128)S(1)}, f32[256,128]{1,0:T(8,128)S(1)}, u32[]{:S(2)}, u32[]{:S(2)}) collective-permute-start(f32[256,128]{1,0:T(8,128)S(1)} %collective-permute-done.10.near_ref), channel_id=1, source_target_pairs={{0,4},{4,0},{8,12},{12,8},{16,20},{20,16},{24,28},{28,24},{1,5},{5... | collective-permute-start | bytes 393224 | tf_op jit(solution)/shard_map/ppermute | solution.py:439
  28.2 1.4 %collective-permute-start.13 = (f32[128,128]{1,0:T(8,128)S(1)}, f32[128,128]{1,0:T(8,128)S(1)}, u32[]{:S(2)}, u32[]{:S(2)}) collective-permute-start(f32[128,128]{1,0:T(8,128)S(1)} %collective-permute-done.11.far_ref), channel_id=1, source_target_pairs={{0,4},{4,0},{8,12},{12,8},{16,20},{20,16},{24,28},{28,24},{1,5},{5... | collective-permute-start | bytes 196616 | tf_op jit(solution)/shard_map/ppermute | solution.py:439
  28.7 8.1 %collective-permute-start.17 = (f32[320,128]{1,0:T(8,128)S(1)}, f32[320,128]{1,0:T(8,128)S(1)}, u32[]{:S(2)}, u32[]{:S(2)}) collective-permute-start(f32[320,128]{1,0:T(8,128)S(1)} %get-tuple-element.53), channel_id=1, source_target_pairs={{0,24},{4,28},{8,16},{12,20},{16,8},{20,12},{24,0},{28,4},{1,25},{... | collective-permute-start | bytes 491528 | tf_op jit(solution)/shard_map/ppermute | solution.py:436
  31.1 6.9 %collective-permute-start.15 = (f32[192,128]{1,0:T(8,128)S(1)}, f32[192,128]{1,0:T(8,128)S(1)}, u32[]{:S(2)}, u32[]{:S(2)}) collective-permute-start(f32[192,128]{1,0:T(8,128)S(1)} %get-tuple-element.51), channel_id=1, source_target_pairs={{0,24},{4,28},{8,16},{12,20},{16,8},{20,12},{24,0},{28,4},{1,25},{... | collective-permute-start | bytes 294920 | tf_op jit(solution)/shard_map/ppermute | solution.py:436
  33.2 7.0 %collective-permute-start.14 = (f32[384,128]{1,0:T(8,128)S(1)}, f32[384,128]{1,0:T(8,128)S(1)}, u32[]{:S(2)}, u32[]{:S(2)}) collective-permute-start(f32[384,128]{1,0:T(8,128)S(1)} %get-tuple-element.50.refs_4_), channel_id=1, source_target_pairs={{0,8},{4,20},{8,0},{12,28},{16,24},{20,4},{24,16},{28,12},{1,9},{5... | collective-permute-start | bytes 589832 | tf_op jit(solution)/shard_map/ppermute | solution.py:436
  38.1 2.1 %collective-permute-start.19 = (f32[320,128]{1,0:T(8,128)S(1)}, f32[320,128]{1,0:T(8,128)S(1)}, u32[]{:S(2)}, u32[]{:S(2)}) collective-permute-start(f32[320,128]{1,0:T(8,128)S(1)} %collective-permute-done.17.refs_6_), channel_id=1, source_target_pairs={{0,4},{4,0},{8,12},{12,8},{16,20},{20,16},{24,28},{28,24},{1,5},{5... | collective-permute-start | bytes 491528 | tf_op jit(solution)/shard_map/ppermute | solution.py:439
  38.1 2.3 %collective-permute-start.21 = (f32[640,128]{1,0:T(8,128)S(1)}, f32[640,128]{1,0:T(8,128)S(1)}, u32[]{:S(2)}, u32[]{:S(2)}) collective-permute-start(f32[640,128]{1,0:T(8,128)S(1)} %collective-permute-done.16.refs_5_), channel_id=1, source_target_pairs={{0,4},{4,0},{8,12},{12,8},{16,20},{20,16},{24,28},{28,24},{1,5},{5... | collective-permute-start | bytes 983048 | tf_op jit(solution)/shard_map/ppermute | solution.py:439
  38.6 1.5 %collective-permute-start.18 = (f32[192,128]{1,0:T(8,128)S(1)}, f32[192,128]{1,0:T(8,128)S(1)}, u32[]{:S(2)}, u32[]{:S(2)}) collective-permute-start(f32[192,128]{1,0:T(8,128)S(1)} %collective-permute-done.15.refs_1_), channel_id=1, source_target_pairs={{0,4},{4,0},{8,12},{12,8},{16,20},{20,16},{24,28},{28,24},{1,5},{5... | collective-permute-start | bytes 294920 | tf_op jit(solution)/shard_map/ppermute | solution.py:439
  40.2 1.4 %collective-permute-start.20 = (f32[384,128]{1,0:T(8,128)S(1)}, f32[384,128]{1,0:T(8,128)S(1)}, u32[]{:S(2)}, u32[]{:S(2)}) collective-permute-start(f32[384,128]{1,0:T(8,128)S(1)} %collective-permute-done.14.refs_0_), channel_id=1, source_target_pairs={{0,4},{4,0},{8,12},{12,8},{16,20},{20,16},{24,28},{28,24},{1,5},{5... | collective-permute-start | bytes 589832 | tf_op jit(solution)/shard_map/ppermute | solution.py:439

commit v11 on v10

--- a/solution.py
+++ b/solution.py
@@ -26,6 +26,23 @@
     return lax.dot_general(
         jnp.concatenate([left[0], left[0], left[1]], lc),
         jnp.concatenate([right[0], right[1], right[0]], rc),
+        (dims, ((), ())),
+        preferred_element_type=F32,
+    )
+
+
+def thirds(value):
+    high, rest = halves(value)
+    low = (value - high.astype(F32) - rest.astype(F32)).astype(BF16)
+    return high, rest, low
+
+
+def fine_mm(left, right, dims=NN):
+    (a, b, c), (x, y, z) = thirds(left), thirds(right)
+    (lc,), (rc,) = dims
+    return lax.dot_general(
+        jnp.concatenate([a, a, b, b, a, c], lc),
+        jnp.concatenate([x, y, x, y, z, x], rc),
         (dims, ((), ())),
         preferred_element_type=F32,
     )
@@ -55,12 +72,11 @@
     )
     near, cross = [], []
     for g in groups:
-        ha = halves(firsts[g])
-        gq = mm(ssecond[g], halves(seconds[g]), NT)
-        gp = mm(sfirst[g], ha, NT)
+        gq = fine_mm(ssecond[g], seconds[g], NT)
+        gp = fine_mm(sfirst[g], firsts[g], NT)
         near.append(jnp.where(above, jnp.concatenate([gq, gp], 1), 0.0))
         cross.append(
-            mm(ssecond[g][:, :block], (ha[0][:, block:], ha[1][:, block:]), NT)
+            fine_mm(ssecond[g][:, :block], firsts[g][:, block:], NT)
         )
 
     def diagonal(value, size):

time: 43.4 us -> 43.7 us (level)
  no operation moved by 1% of the time
where the time goes in v11:
time: 43.7 us; the launch traced here: 43.5 us
  starting transfers between devices  19.6 us (45%)
  Pallas kernels  11.4 us (26%)
  waiting for transfers between devices  10.6 us (24%)
  other arithmetic  1.83 us (4%)
    ppermute x8, starting transfers between devices, swap(): return lax.ppermute(value, 'rows', moves)  11.7 us
    pallas_call x5, Pallas kernels, call(): pl.pallas_call(kernel, out_shape=[jax.ShapeDtypeStruct(shape, F32) for sh...  11.4 us
    ppermute x3, starting transfers between devices, spread(): lax.ppermute(value, axis, [(place, place ^ mask) for place in range(size)])  5.62 us
    ppermute x8, waiting for transfers between devices, swap(): return lax.ppermute(value, 'rows', moves)  4.79 us
    ppermute x11, waiting for transfers between devices, across(): lax.ppermute(value, 'rows', [(place, place ^ 1) for place in range(row_co...  3.52 us
    ppermute x11, starting transfers between devices, across(): lax.ppermute(value, 'rows', [(place, place ^ 1) for place in range(row_co...  2.36 us
    ppermute x3, waiting for transfers between devices, spread(): lax.ppermute(value, axis, [(place, place ^ mask) for place in range(size)])  2.31 us
    select_n x1, other arithmetic, local(): mine[0] = jnp.where(vec_index < 0, 0.0, mine[0])  0.9 us
  transfers between devices with their start and end apart: 22, of which 10 were waited for; matrix products, arithmetic and copies ran while one was open for 4% of the time, Pallas kernels for 11%

profile of v11, /device:TPU:0, one launch (start us, length us, event | category | flops | bytes accessed | tf_op | source)
XLA Modules:
  0.0 43.5 jit_solution(17296573085623462274)
XLA Ops:
  0.0 3.0 %collective-permute-start = (f32[3,32,256]{2,1,0:T(8,128)}, f32[3,32,256]{2,1,0:T(8,128)S(1)}, u32[]{:S(2)}, u32[]{:S(2)}) collective-permute-start(f32[3,32,256]{2,1,0:T(8,128)} %bitcast.5), channel_id=1, source_target_pairs={{0,1},{1,0},{2,3},{3,2},{4,5},{5,4},{6,7},{7,6},{8,9},{9,8},{10,11... | collective-permute-start | bytes 294920 | tf_op jit(solution)/shard_map/ppermute | solution.py:400
  3.0 2.6 %collective-permute-start.1 = (f32[3,32,256]{2,1,0:T(8,128)}, f32[3,32,256]{2,1,0:T(8,128)S(1)}, u32[]{:S(2)}, u32[]{:S(2)}) collective-permute-start(f32[3,32,256]{2,1,0:T(8,128)} %bitcast.6), channel_id=1, source_target_pairs={{0,2},{1,3},{2,0},{3,1},{4,6},{5,7},{6,4},{7,5},{8,10},{9,11},{10,... | collective-permute-start | bytes 294920 | tf_op jit(solution)/shard_map/ppermute | solution.py:400
  6.1 0.9 %broadcast_select_fusion.refs_0_ = f32[3,32,256]{2,1,0:T(8,128)S(1)} fusion(pred[]{:T(512)S(6)} %lt.10, f32[3,1,32,256]{3,2,1,0:T(8,128)} %param.3), kind=kLoop, calls=%fused_computation | loop fusion | flops 24576 | bytes 196609 | tf_op jit(solution)/shard_map/jit(_where)/select_n | solution.py:470
  7.2 0.8 %broadcast_select_fusion.1 = (f32[128,128]{1,0:T(8,128)S(1)}, f32[128,128]{1,0:T(8,128)S(1)}) fusion(f32[128,128]{1,0:T(8,128)S(1)} %collective-permute-done.7, f32[128,128]{1,0:T(8,128)} %param.2, pred[]{:T(512)S(6)} %eq.6), kind=kLoop, calls=%fused_computation.1 | loop fusion | flops 32768 | bytes 262145 | tf_op jit(solution)/shard_map/jit(_where)/select_n | solution.py:460
  8.1 1.8 %collective-permute-start.8 = (f32[128,128]{1,0:T(8,128)S(1)}, f32[128,128]{1,0:T(8,128)S(1)}, u32[]{:S(2)}, u32[]{:S(2)}) collective-permute-start(f32[128,128]{1,0:T(8,128)S(1)} %get-tuple-element.62.refs_8_), channel_id=1, source_target_pairs={{0,8},{4,12},{8,0},{12,4},{16,24},{20,28},{24,16},{28,20},{1,9},{5... | collective-permute-start | bytes 196616 | tf_op jit(solution)/shard_map/ppermute | solution.py:452
  9.9 1.5 %collective-permute-start.9 = (f32[128,128]{1,0:T(8,128)S(1)}, f32[128,128]{1,0:T(8,128)S(1)}, u32[]{:S(2)}, u32[]{:S(2)}) collective-permute-start(f32[128,128]{1,0:T(8,128)S(1)} %get-tuple-element.62.refs_8_), channel_id=1, source_target_pairs={{0,24},{4,28},{8,16},{12,20},{16,8},{20,12},{24,0},{28,4},{1,25},{... | collective-permute-start | bytes 196616 | tf_op jit(solution)/shard_map/ppermute | solution.py:452
  11.4 2.3 %collective-permute-done.1.refs_2_ = f32[3,32,256]{2,1,0:T(8,128)S(1)} collective-permute-done((f32[3,32,256]{2,1,0:T(8,128)}, f32[3,32,256]{2,1,0:T(8,128)S(1)}, u32[]{:S(2)}, u32[]{:S(2)}) %collective-permute-start.1) | collective-permute-done | bytes 98336 | tf_op jit(solution)/shard_map/ppermute | solution.py:400
  13.7 0.5 %collective-permute-start.5 = (f32[3,32,256]{2,1,0:T(8,128)S(1)}, f32[3,32,256]{2,1,0:T(8,128)S(1)}, u32[]{:S(2)}, u32[]{:S(2)}) collective-permute-start(f32[3,32,256]{2,1,0:T(8,128)S(1)} %collective-permute-done.1.refs_2_), channel_id=1, source_target_pairs={{0,4},{4,0},{8,12},{12,8},{16,20},{20,16},{24,28},{28,24},{1,5},{5... | collective-permute-start | bytes 294920 | tf_op jit(solution)/shard_map/ppermute | solution.py:455
  14.3 0.7 %collective-permute-done.9.refs_11_ = f32[128,128]{1,0:T(8,128)S(1)} collective-permute-done((f32[128,128]{1,0:T(8,128)S(1)}, f32[128,128]{1,0:T(8,128)S(1)}, u32[]{:S(2)}, u32[]{:S(2)}) %collective-permute-start.9) | collective-permute-done | bytes 65568 | tf_op jit(solution)/shard_map/ppermute | solution.py:452
  15.5 5.0 %shard_map.28 = (f32[384,128]{1,0:T(8,128)S(1)}, f32[384,128]{1,0:T(8,128)S(1)}, f32[256,128]{1,0:T(8,128)S(1)}, f32[128,128]{1,0:T(8,128)S(1)}, f32[2,128,256]{...) custom-call(s32[3]{0:T(128)S(1)} %pad_add_fusion.place_ref, ...), custom_call_target="tpu_custom_call" | custom-call | tf_op jit(solution)/shard_map/pallas_call | solution.py:380
  20.5 1.6 %collective-permute-start.10 = (f32[256,128]{1,0:T(8,128)S(1)}, f32[256,128]{1,0:T(8,128)S(1)}, u32[]{:S(2)}, u32[]{:S(2)}) collective-permute-start(f32[256,128]{1,0:T(8,128)S(1)} %get-tuple-element.33), channel_id=1, source_target_pairs={{0,8},{4,20},{8,0},{12,28},{16,24},{20,4},{24,16},{28,12},{1,9},{5... | collective-permute-start | bytes 393224 | tf_op jit(solution)/shard_map/ppermute | solution.py:452
  22.0 1.5 %collective-permute-start.11 = (f32[128,128]{1,0:T(8,128)S(1)}, f32[128,128]{1,0:T(8,128)S(1)}, u32[]{:S(2)}, u32[]{:S(2)}) collective-permute-start(f32[128,128]{1,0:T(8,128)S(1)} %get-tuple-element.34), channel_id=1, source_target_pairs={{0,24},{4,28},{8,16},{12,20},{16,8},{20,12},{24,0},{28,4},{1,25},{... | collective-permute-start | bytes 196616 | tf_op jit(solution)/shard_map/ppermute | solution.py:452
  23.5 2.1 %shard_map.29 = (f32[2,384,384]{2,1,0:T(8,128)S(1)}, f32[640,128]{1,0:T(8,128)S(1)}, f32[320,128]{1,0:T(8,128)S(1)}) custom-call(s32[3]{0:T(128)S(1)} %pad_add_fusion.place_ref, f32[2,128,256]{2,1,0:T(8,128)S(1)} %get-tuple-element.37.refs_0_, f32[2,128,256]{2,1,0:T(8,128)S(1)} %get-tuple-element.38.refs_1_, f32[2,128,256]{2,1,0:T(8,128)S(1)} %get-tuple-element.39.refs_2_, ...), custom_call_target="tpu_custom_call" | custom-call | flops 1811939328 | tf_op jit(solution)/shard_map/pallas_call | solution.py:380
  25.6 1.6 %collective-permute-start.16 = (f32[640,128]{1,0:T(8,128)S(1)}, f32[640,128]{1,0:T(8,128)S(1)}, u32[]{:S(2)}, u32[]{:S(2)}) collective-permute-start(f32[640,128]{1,0:T(8,128)S(1)} %get-tuple-element.52.refs_9_), channel_id=1, source_target_pairs={{0,8},{4,20},{8,0},{12,28},{16,24},{20,4},{24,16},{28,12},{1,9},{5... | collective-permute-start | bytes 983048 | tf_op jit(solution)/shard_map/ppermute | solution.py:452
  27.1 1.3 %shard_map.30 = (f32[512,128]{1,0:T(8,128)S(1)}, f32[512,256]{1,0:T(8,128)S(1)}) custom-call(s32[3]{0:T(128)S(1)} %pad_add_fusion.place_ref, f32[384,128]{1,0:T(8,128)S(1)} %get-tuple-element.35.fixed_ref, f32[384,128]{1,0:T(8,128)S(1)} %get-tuple-element.36.lead_ref, f32[2,384,384]{2,1,0:T(8,128)S(1)} %get-tuple-element.44.oper_ref.refs_11_), custom_call_target="tpu_custom_call" | custom-call | flops 1811939328 | tf_op jit(solution)/shard_map/pallas_call | solution.py:380
  29.0 0.8 %collective-permute-start.17 = (f32[320,128]{1,0:T(8,128)S(1)}, f32[320,128]{1,0:T(8,128)S(1)}, u32[]{:S(2)}, u32[]{:S(2)}) collective-permute-start(f32[320,128]{1,0:T(8,128)S(1)} %get-tuple-element.53), channel_id=1, source_target_pairs={{0,24},{4,28},{8,16},{12,20},{16,8},{20,12},{24,0},{28,4},{1,25},{... | collective-permute-start | bytes 491528 | tf_op jit(solution)/shard_map/ppermute | solution.py:452
  30.0 1.5 %shard_map.31 = (f32[384,128]{1,0:T(8,128)S(1)}, f32[384,128]{1,0:T(8,128)S(1)}, f32[192,128]{1,0:T(8,128)S(1)}) custom-call(s32[3]{0:T(128)S(1)} %pad_add_fusion.place_ref, f32[256,128]{1,0:T(8,128)S(1)} %collective-permute-done.10.near_ref, f32[128,128]{1,0:T(8,128)S(1)} %collective-permute-done.11.far_ref, ...), custom_call_target="tpu_custom_call" | custom-call | tf_op jit(solution)/shard_map/pallas_call | solution.py:380
  31.4 2.1 %collective-permute-start.15 = (f32[192,128]{1,0:T(8,128)S(1)}, f32[192,128]{1,0:T(8,128)S(1)}, u32[]{:S(2)}, u32[]{:S(2)}) collective-permute-start(f32[192,128]{1,0:T(8,128)S(1)} %get-tuple-element.51), channel_id=1, source_target_pairs={{0,24},{4,28},{8,16},{12,20},{16,8},{20,12},{24,0},{28,4},{1,25},{... | collective-permute-start | bytes 294920 | tf_op jit(solution)/shard_map/ppermute | solution.py:452
  33.5 0.9 %collective-permute-start.14 = (f32[384,128]{1,0:T(8,128)S(1)}, f32[384,128]{1,0:T(8,128)S(1)}, u32[]{:S(2)}, u32[]{:S(2)}) collective-permute-start(f32[384,128]{1,0:T(8,128)S(1)} %get-tuple-element.50.refs_4_), channel_id=1, source_target_pairs={{0,8},{4,20},{8,0},{12,28},{16,24},{20,4},{24,16},{28,12},{1,9},{5... | collective-permute-start | bytes 589832 | tf_op jit(solution)/shard_map/ppermute | solution.py:452
  34.4 2.6 %collective-permute-done.17.refs_6_ = f32[320,128]{1,0:T(8,128)S(1)} collective-permute-done((f32[320,128]{1,0:T(8,128)S(1)}, f32[320,128]{1,0:T(8,128)S(1)}, u32[]{:S(2)}, u32[]{:S(2)}) %collective-permute-start.17) | collective-permute-done | bytes 163872 | tf_op jit(solution)/shard_map/ppermute | solution.py:452
  37.1 1.3 %collective-permute-done.15.refs_1_ = f32[192,128]{1,0:T(8,128)S(1)} collective-permute-done((f32[192,128]{1,0:T(8,128)S(1)}, f32[192,128]{1,0:T(8,128)S(1)}, u32[]{:S(2)}, u32[]{:S(2)}) %collective-permute-start.15) | collective-permute-done | bytes 98336 | tf_op jit(solution)/shard_map/ppermute | solution.py:452
  38.9 1.5 %collective-permute-done.18.refs_3_ = f32[192,128]{1,0:T(8,128)S(1)} collective-permute-done((f32[192,128]{1,0:T(8,128)S(1)}, f32[192,128]{1,0:T(8,128)S(1)}, u32[]{:S(2)}, u32[]{:S(2)}) %collective-permute-start.18) | collective-permute-done | bytes 98336 | tf_op jit(solution)/shard_map/ppermute | solution.py:455
  40.7 1.3 %collective-permute-done.20.refs_2_ = f32[384,128]{1,0:T(8,128)S(1)} collective-permute-done((f32[384,128]{1,0:T(8,128)S(1)}, f32[384,128]{1,0:T(8,128)S(1)}, u32[]{:S(2)}, u32[]{:S(2)}) %collective-permute-start.20) | collective-permute-done | bytes 196640 | tf_op jit(solution)/shard_map/ppermute | solution.py:455
  41.9 1.6 %shard_map.32 = f32[128,128]{1,0:T(8,128)} custom-call(s32[3]{0:T(128)S(1)} %pad_add_fusion.place_ref, f32[384,128]{1,0:T(8,128)S(1)} %collective-permute-done.14.refs_0_, f32[192,128]{1,0:T(8,128)S(1)} %collective-permute-done.15.refs_1_, f32[384,128]{1,0:T(8,128)S(1)} %collective-permute-done.20.refs_2_, f32[192,128]{1,0:T(8,128)S(1)} %collective-permute-done.18.refs_3_, ...), custom_call_target="tpu_custom_call" | custom-call | tf_op jit(solution)/shard_map/pallas_call | solution.py:380
  (28 shorter events, 2.8 us)
Async XLA Ops:
  0.0 9.9 %collective-permute-start = (f32[3,32,256]{2,1,0:T(8,128)}, f32[3,32,256]{2,1,0:T(8,128)S(1)}, u32[]{:S(2)}, u32[]{:S(2)}) collective-permute-start(f32[3,32,256]{2,1,0:T(8,128)} %bitcast.5), channel_id=1, source_target_pairs={{0,1},{1,0},{2,3},{3,2},{4,5},{5,4},{6,7},{7,6},{8,9},{9,8},{10,11... | collective-permute-start | bytes 294920 | tf_op jit(solution)/shard_map/ppermute | solution.py:400
  3.0 10.6 %collective-permute-start.1 = (f32[3,32,256]{2,1,0:T(8,128)}, f32[3,32,256]{2,1,0:T(8,128)S(1)}, u32[]{:S(2)}, u32[]{:S(2)}) collective-permute-start(f32[3,32,256]{2,1,0:T(8,128)} %bitcast.6), channel_id=1, source_target_pairs={{0,2},{1,3},{2,0},{3,1},{4,6},{5,7},{6,4},{7,5},{8,10},{9,11},{10,... | collective-permute-start | bytes 294920 | tf_op jit(solution)/shard_map/ppermute | solution.py:400
  5.6 8.1 %collective-permute-start.2 = (f32[3,32,256]{2,1,0:T(8,128)}, f32[3,32,256]{2,1,0:T(8,128)S(1)}, u32[]{:S(2)}, u32[]{:S(2)}) collective-permute-start(f32[3,32,256]{2,1,0:T(8,128)} %bitcast.7), channel_id=1, source_target_pairs={{0,3},{1,2},{2,1},{3,0},{4,7},{5,6},{6,5},{7,4},{8,11},{9,10},{10,... | collective-permute-start | bytes 294920 | tf_op jit(solution)/shard_map/ppermute | solution.py:400
  5.6 8.6 %collective-permute-start.3 = (f32[3,32,256]{2,1,0:T(8,128)}, f32[3,32,256]{2,1,0:T(8,128)S(1)}, u32[]{:S(2)}, u32[]{:S(2)}) collective-permute-start(f32[3,32,256]{2,1,0:T(8,128)} %bitcast.8), channel_id=1, source_target_pairs={{0,4},{4,0},{8,12},{12,8},{16,20},{20,16},{24,28},{28,24},{1,5},{5... | collective-permute-start | bytes 294920 | tf_op jit(solution)/shard_map/ppermute | solution.py:455
  5.6 1.6 %collective-permute-start.7 = (f32[128,128]{1,0:T(8,128)}, f32[128,128]{1,0:T(8,128)S(1)}, u32[]{:S(2)}, u32[]{:S(2)}) collective-permute-start(f32[128,128]{1,0:T(8,128)} %param.2), channel_id=1, source_target_pairs={{0,4},{4,0},{8,12},{12,8},{16,20},{20,16},{24,28},{28,24},{1,5},{5... | collective-permute-start | bytes 196616 | tf_op jit(solution)/shard_map/ppermute | solution.py:455
  8.1 6.2 %collective-permute-start.8 = (f32[128,128]{1,0:T(8,128)S(1)}, f32[128,128]{1,0:T(8,128)S(1)}, u32[]{:S(2)}, u32[]{:S(2)}) collective-permute-start(f32[128,128]{1,0:T(8,128)S(1)} %get-tuple-element.62.refs_8_), channel_id=1, source_target_pairs={{0,8},{4,12},{8,0},{12,4},{16,24},{20,28},{24,16},{28,20},{1,9},{5... | collective-permute-start | bytes 196616 | tf_op jit(solution)/shard_map/ppermute | solution.py:452
  9.9 5.2 %collective-permute-start.9 = (f32[128,128]{1,0:T(8,128)S(1)}, f32[128,128]{1,0:T(8,128)S(1)}, u32[]{:S(2)}, u32[]{:S(2)}) collective-permute-start(f32[128,128]{1,0:T(8,128)S(1)} %get-tuple-element.62.refs_8_), channel_id=1, source_target_pairs={{0,24},{4,28},{8,16},{12,20},{16,8},{20,12},{24,0},{28,4},{1,25},{... | collective-permute-start | bytes 196616 | tf_op jit(solution)/shard_map/ppermute | solution.py:452
  13.7 1.4 %collective-permute-start.4 = (f32[3,32,256]{2,1,0:T(8,128)S(1)}, f32[3,32,256]{2,1,0:T(8,128)S(1)}, u32[]{:S(2)}, u32[]{:S(2)}) collective-permute-start(f32[3,32,256]{2,1,0:T(8,128)S(1)} %collective-permute-done.refs_1_), channel_id=1, source_target_pairs={{0,4},{4,0},{8,12},{12,8},{16,20},{20,16},{24,28},{28,24},{1,5},{5... | collective-permute-start | bytes 294920 | tf_op jit(solution)/shard_map/ppermute | solution.py:455
  13.7 1.5 %collective-permute-start.5 = (f32[3,32,256]{2,1,0:T(8,128)S(1)}, f32[3,32,256]{2,1,0:T(8,128)S(1)}, u32[]{:S(2)}, u32[]{:S(2)}) collective-permute-start(f32[3,32,256]{2,1,0:T(8,128)S(1)} %collective-permute-done.1.refs_2_), channel_id=1, source_target_pairs={{0,4},{4,0},{8,12},{12,8},{16,20},{20,16},{24,28},{28,24},{1,5},{5... | collective-permute-start | bytes 294920 | tf_op jit(solution)/shard_map/ppermute | solution.py:455
  14.2 1.3 %collective-permute-start.6 = (f32[3,32,256]{2,1,0:T(8,128)S(1)}, f32[3,32,256]{2,1,0:T(8,128)S(1)}, u32[]{:S(2)}, u32[]{:S(2)}) collective-permute-start(f32[3,32,256]{2,1,0:T(8,128)S(1)} %collective-permute-done.2.refs_3_), channel_id=1, source_target_pairs={{0,4},{4,0},{8,12},{12,8},{16,20},{20,16},{24,28},{28,24},{1,5},{5... | collective-permute-start | bytes 294920 | tf_op jit(solution)/shard_map/ppermute | solution.py:455
  20.5 8.0 %collective-permute-start.10 = (f32[256,128]{1,0:T(8,128)S(1)}, f32[256,128]{1,0:T(8,128)S(1)}, u32[]{:S(2)}, u32[]{:S(2)}) collective-permute-start(f32[256,128]{1,0:T(8,128)S(1)} %get-tuple-element.33), channel_id=1, source_target_pairs={{0,8},{4,20},{8,0},{12,28},{16,24},{20,4},{24,16},{28,12},{1,9},{5... | collective-permute-start | bytes 393224 | tf_op jit(solution)/shard_map/ppermute | solution.py:452
  22.0 6.4 %collective-permute-start.11 = (f32[128,128]{1,0:T(8,128)S(1)}, f32[128,128]{1,0:T(8,128)S(1)}, u32[]{:S(2)}, u32[]{:S(2)}) collective-permute-start(f32[128,128]{1,0:T(8,128)S(1)} %get-tuple-element.34), channel_id=1, source_target_pairs={{0,24},{4,28},{8,16},{12,20},{16,8},{20,12},{24,0},{28,4},{1,25},{... | collective-permute-start | bytes 196616 | tf_op jit(solution)/shard_map/ppermute | solution.py:452
  25.6 11.5 %collective-permute-start.16 = (f32[640,128]{1,0:T(8,128)S(1)}, f32[640,128]{1,0:T(8,128)S(1)}, u32[]{:S(2)}, u32[]{:S(2)}) collective-permute-start(f32[640,128]{1,0:T(8,128)S(1)} %get-tuple-element.52.refs_9_), channel_id=1, source_target_pairs={{0,8},{4,20},{8,0},{12,28},{16,24},{20,4},{24,16},{28,12},{1,9},{5... | collective-permute-start | bytes 983048 | tf_op jit(solution)/shard_map/ppermute | solution.py:452
  28.4 1.5 %collective-permute-start.12 = (f32[256,128]{1,0:T(8,128)S(1)}, f32[256,128]{1,0:T(8,128)S(1)}, u32[]{:S(2)}, u32[]{:S(2)}) collective-permute-start(f32[256,128]{1,0:T(8,128)S(1)} %collective-permute-done.10.near_ref), channel_id=1, source_target_pairs={{0,4},{4,0},{8,12},{12,8},{16,20},{20,16},{24,28},{28,24},{1,5},{5... | collective-permute-start | bytes 393224 | tf_op jit(solution)/shard_map/ppermute | solution.py:455
  28.5 1.4 %collective-permute-start.13 = (f32[128,128]{1,0:T(8,128)S(1)}, f32[128,128]{1,0:T(8,128)S(1)}, u32[]{:S(2)}, u32[]{:S(2)}) collective-permute-start(f32[128,128]{1,0:T(8,128)S(1)} %collective-permute-done.11.far_ref), channel_id=1, source_target_pairs={{0,4},{4,0},{8,12},{12,8},{16,20},{20,16},{24,28},{28,24},{1,5},{5... | collective-permute-start | bytes 196616 | tf_op jit(solution)/shard_map/ppermute | solution.py:455
  29.0 8.1 %collective-permute-start.17 = (f32[320,128]{1,0:T(8,128)S(1)}, f32[320,128]{1,0:T(8,128)S(1)}, u32[]{:S(2)}, u32[]{:S(2)}) collective-permute-start(f32[320,128]{1,0:T(8,128)S(1)} %get-tuple-element.53), channel_id=1, source_target_pairs={{0,24},{4,28},{8,16},{12,20},{16,8},{20,12},{24,0},{28,4},{1,25},{... | collective-permute-start | bytes 491528 | tf_op jit(solution)/shard_map/ppermute | solution.py:452
  31.4 7.0 %collective-permute-start.15 = (f32[192,128]{1,0:T(8,128)S(1)}, f32[192,128]{1,0:T(8,128)S(1)}, u32[]{:S(2)}, u32[]{:S(2)}) collective-permute-start(f32[192,128]{1,0:T(8,128)S(1)} %get-tuple-element.51), channel_id=1, source_target_pairs={{0,24},{4,28},{8,16},{12,20},{16,8},{20,12},{24,0},{28,4},{1,25},{... | collective-permute-start | bytes 294920 | tf_op jit(solution)/shard_map/ppermute | solution.py:452
  33.5 7.0 %collective-permute-start.14 = (f32[384,128]{1,0:T(8,128)S(1)}, f32[384,128]{1,0:T(8,128)S(1)}, u32[]{:S(2)}, u32[]{:S(2)}) collective-permute-start(f32[384,128]{1,0:T(8,128)S(1)} %get-tuple-element.50.refs_4_), channel_id=1, source_target_pairs={{0,8},{4,20},{8,0},{12,28},{16,24},{20,4},{24,16},{28,12},{1,9},{5... | collective-permute-start | bytes 589832 | tf_op jit(solution)/shard_map/ppermute | solution.py:452
  38.4 2.1 %collective-permute-start.19 = (f32[320,128]{1,0:T(8,128)S(1)}, f32[320,128]{1,0:T(8,128)S(1)}, u32[]{:S(2)}, u32[]{:S(2)}) collective-permute-start(f32[320,128]{1,0:T(8,128)S(1)} %collective-permute-done.17.refs_6_), channel_id=1, source_target_pairs={{0,4},{4,0},{8,12},{12,8},{16,20},{20,16},{24,28},{28,24},{1,5},{5... | collective-permute-start | bytes 491528 | tf_op jit(solution)/shard_map/ppermute | solution.py:455
  38.4 2.3 %collective-permute-start.21 = (f32[640,128]{1,0:T(8,128)S(1)}, f32[640,128]{1,0:T(8,128)S(1)}, u32[]{:S(2)}, u32[]{:S(2)}) collective-permute-start(f32[640,128]{1,0:T(8,128)S(1)} %collective-permute-done.16.refs_5_), channel_id=1, source_target_pairs={{0,4},{4,0},{8,12},{12,8},{16,20},{20,16},{24,28},{28,24},{1,5},{5... | collective-permute-start | bytes 983048 | tf_op jit(solution)/shard_map/ppermute | solution.py:455
  38.9 1.5 %collective-permute-start.18 = (f32[192,128]{1,0:T(8,128)S(1)}, f32[192,128]{1,0:T(8,128)S(1)}, u32[]{:S(2)}, u32[]{:S(2)}) collective-permute-start(f32[192,128]{1,0:T(8,128)S(1)} %collective-permute-done.15.refs_1_), channel_id=1, source_target_pairs={{0,4},{4,0},{8,12},{12,8},{16,20},{20,16},{24,28},{28,24},{1,5},{5... | collective-permute-start | bytes 294920 | tf_op jit(solution)/shard_map/ppermute | solution.py:455
  40.5 1.4 %collective-permute-start.20 = (f32[384,128]{1,0:T(8,128)S(1)}, f32[384,128]{1,0:T(8,128)S(1)}, u32[]{:S(2)}, u32[]{:S(2)}) collective-permute-start(f32[384,128]{1,0:T(8,128)S(1)} %collective-permute-done.14.refs_0_), channel_id=1, source_target_pairs={{0,4},{4,0},{8,12},{12,8},{16,20},{20,16},{24,28},{28,24},{1,5},{5... | collective-permute-start | bytes 589832 | tf_op jit(solution)/shard_map/ppermute | solution.py:455
